TPU v7x, 32 devices: a whole 2x2x4 slice. The times are simulated.
32 devices in a mesh: row: 4 (over y, core), seq: 8 (over z, x).
Axes of the slice: x: 2, y: 2, z: 4, core: 2. Of those that a mesh axis runs over, the one named last changes fastest.
Arguments:
- tokens: bfloat16 [2, 4, 1024, 1024], P(None, 'row', 'seq'), may hold values from -6 to 6
- cotangent: bfloat16 [2, 4, 1024, 1024], P(None, 'row', 'seq'), may hold values from -6 to 6
- row_lengths: int32 [2, 4], P(None, 'row'), may hold values from 256 to 1024, as said below
- norm1_gain: float32 [1024], replicated, may hold values from 0.5 to 1.5
- w_in: bfloat16 [1024, 6144], P('seq'), may hold values from -0.1875 to 0.1875
- w_router: bfloat16 [1024, 24], replicated, may hold values from -0.25 to 0.25
- conv_weight: float32 [4, 5120], replicated, may hold values from -3 to 3
- a_log: float32 [8], replicated, as said below
- dt_bias: float32 [8], replicated, may hold values from -1 to 1
- head_gain: float32 [128], replicated, may hold values from 0.5 to 1.5
- w_out: bfloat16 [1024, 1024], P('seq'), may hold values from -0.375 to 0.375
- norm2_gain: float32 [1024], replicated, may hold values from 0.5 to 1.5
- w_gu: bfloat16 [1024, 5632], P('seq'), may hold values from -0.1875 to 0.1875
- w_down: bfloat16 [2816, 1024], P('seq'), may hold values from -0.109375 to 0.109375
Outputs:
- out: bfloat16 [2, 4, 1024, 1024], P(None, 'row', 'seq')
- grad_tokens: float32 [2, 4, 1024, 1024], P(None, 'row', 'seq')
- grad_norm1: float32 [1024], replicated
- grad_w_in: float32 [1024, 6144], P('seq')
- grad_w_router: float32 [1024, 24], replicated
- grad_conv: float32 [4, 5120], replicated
- grad_a_log: float32 [8], replicated
- grad_dt_bias: float32 [8], replicated
- grad_head_gain: float32 [128], replicated
- grad_w_out: float32 [1024, 1024], P('seq')
- grad_norm2: float32 [1024], replicated
- grad_w_gu: float32 [1024, 5632], P('seq')
- grad_w_down: float32 [2816, 1024], P('seq')
Inputs may be any that keep to these rules, and one draw needn't show every extreme that they name: `row_lengths`: each length is 1024 or 256; for every index of the rows, some micro-batch's row there has 1024. `a_log`: each entry lies between log(0.05 / 1024) and log(0.05).
All inputs are finite; a program needn't handle non-finite values.
Results may differ from a plain program's by a relative error of at most 0.02.
The roundings to bfloat16 on the way count: a program that leaves them out, or rounds other values in their place, can miss the bound.
Values may be sent and summed in bfloat16 or wider, within the bound.
No kernel may reach another device: no remote copies, remote signals or barrier semaphores. Data moves between devices by JAX's collectives and lax.ppermute only.
A program may use at most 448 MiB of HBM per device.

v0:
```python
from functools import partial

import jax
import jax.numpy as jnp
from jax import lax
from jax.sharding import PartitionSpec as P

GROUP = 64


HIGH = lax.Precision.HIGHEST
EPS_NORM = 1e-05
EPS_UNIT = 1e-06


def shifted(value, axis, steps):
    count = lax.axis_size(axis)
    first, last = (max(0, -steps), min(count, count - steps))
    return lax.ppermute(value, axis, [(source, source + steps) for source in range(first, last)])


def entering(value, axis, join, neutral):
    count, mine = (lax.axis_size(axis), lax.axis_index(axis))
    pieces = jax.tree.map(lambda part: lax.all_gather(part, axis), value)
    total = jax.tree.map(
        lambda part, zero: jnp.full_like(part, 0) + jnp.asarray(zero, part.dtype), value, neutral
    )

    def step(position, total):
        longer = join(total, jax.tree.map(lambda part: part[position], pieces))
        return jax.tree.map(lambda new, old: jnp.where(position < mine, new, old), longer, total)

    return lax.fori_loop(0, count - 1, step, total)


def carried_in(array, axis, join, neutral):
    count = lax.axis_size(axis)
    place = lax.axis_index(axis)
    ahead = count - 1 - place
    gathered = jax.tree.map(
        lambda a, kind: lax.all_gather(a.astype(kind), axis),
        array,
        jax.tree.map(lambda a: jnp.bfloat16 if a.dtype == jnp.float32 else a.dtype, array),
    )
    state = jax.tree.map(lambda a, e: jnp.zeros_like(a) + jnp.asarray(e, a.dtype), array, neutral)

    def one(step, state):
        source = count - 1 - step
        return join(
            state,
            jax.tree.map(
                lambda a, own: lax.dynamic_index_in_dim(a, source, 0, False).astype(own.dtype),
                gathered,
                array,
            ),
        )

    return lax.fori_loop(0, ahead, one, state)


def as_sent(array):
    return jax.tree.map(lambda a: a.astype(jnp.bfloat16) if a.dtype == jnp.float32 else a, array)


def rms_scale(values):
    return lax.rsqrt(jnp.mean(values * values, axis=-1, keepdims=True) + EPS_NORM)


def rms_back(grad_norm, values, inv_scale):
    return inv_scale * grad_norm - values * inv_scale**3 * jnp.mean(
        grad_norm * values, axis=-1, keepdims=True
    )


def to_low(values):
    return lax.optimization_barrier(values.astype(jnp.bfloat16)).astype(jnp.float32)


def mixer_inputs(extended, conv_weight, router, a_log, dt_bias, n_heads, head_dim, n_keys):
    n_taps = conv_weight.shape[0]
    n_rows = extended.shape[0] - n_taps + 1
    conv_sum = conv_weight[0] * extended[0:n_rows]
    for offset in range(1, n_taps):
        conv_sum = conv_sum + conv_weight[offset] * extended[offset : offset + n_rows]
    activated = jax.nn.silu(conv_sum)
    model_width = n_heads * head_dim
    queries = activated[:, :model_width].reshape(n_rows, n_heads, head_dim)
    key_vecs = activated[:, model_width : model_width + n_keys * model_width].reshape(
        n_rows, n_keys, n_heads, head_dim
    )
    val_vecs = activated[:, model_width + n_keys * model_width :].reshape(
        n_rows, n_keys, n_heads, head_dim
    )
    queries = queries * lax.rsqrt(jnp.sum(queries * queries, axis=-1, keepdims=True) + EPS_UNIT)
    key_vecs = key_vecs * lax.rsqrt(jnp.sum(key_vecs * key_vecs, axis=-1, keepdims=True) + EPS_UNIT)
    beta_vals = jax.nn.sigmoid(router[:, : n_keys * n_heads]).reshape(n_rows, n_keys, n_heads)
    decays = -jnp.exp(a_log) * jax.nn.softplus(router[:, n_keys * n_heads :] + dt_bias)
    return (queries, key_vecs, val_vecs, beta_vals, decays)


def head_mix(mixed_out, gate_pre, head_gain):
    n_rows = mixed_out.shape[0]
    normed = (
        mixed_out
        * lax.rsqrt(jnp.mean(mixed_out * mixed_out, axis=-1, keepdims=True) + EPS_NORM)
        * head_gain
    )
    return normed.reshape(n_rows, -1) * jax.nn.silu(gate_pre)


def compose(earlier, latter):
    return (
        jnp.einsum("hkl,hlm->hkm", earlier[0], latter[0], precision=HIGH),
        jnp.einsum("hvl,hlm->hvm", earlier[1], latter[0], precision=HIGH) + latter[1],
    )


def group_maps(queries, key_vecs, val_vecs, beta_vals, decays, group_len):
    n_tok, n_heads, head_dim = queries.shape
    n_keys = key_vecs.shape[1]
    n_groups = n_tok // group_len
    steps_len = group_len * n_keys
    q_blk = queries.reshape(n_groups, group_len, n_heads, head_dim).transpose(0, 2, 1, 3)
    k_blk = (
        key_vecs.reshape(n_groups, group_len, n_keys, n_heads, head_dim)
        .transpose(0, 3, 1, 2, 4)
        .reshape(n_groups, n_heads, steps_len, head_dim)
    )
    v_blk = (
        val_vecs.reshape(n_groups, group_len, n_keys, n_heads, head_dim)
        .transpose(0, 3, 1, 2, 4)
        .reshape(n_groups, n_heads, steps_len, head_dim)
    )
    b_blk = (
        beta_vals.reshape(n_groups, group_len, n_keys, n_heads)
        .transpose(0, 3, 1, 2)
        .reshape(n_groups, n_heads, steps_len)
    )
    g_tok = jnp.cumsum(decays.reshape(n_groups, group_len, n_heads).transpose(0, 2, 1), axis=-1)
    g_step = jnp.repeat(g_tok, n_keys, axis=-1)
    g_last = g_tok[..., -1]
    step_pos = jnp.arange(steps_len)
    tok_pos = jnp.arange(group_len)
    strict = step_pos[:, None] > step_pos[None, :]
    log_gaps = jnp.where(strict, g_step[..., :, None] - g_step[..., None, :], 0.0)
    decay_ratio = jnp.where(strict, jnp.exp(log_gaps), 0.0)
    key_gram = jnp.einsum("chik,chjk->chij", k_blk, k_blk, precision=HIGH)
    lower_part = b_blk[..., :, None] * decay_ratio * key_gram
    eye_steps = jnp.eye(steps_len, dtype=jnp.float32)
    right_side = jnp.concatenate(
        [b_blk[..., None] * v_blk, (b_blk * jnp.exp(g_step))[..., None] * k_blk], axis=-1
    )
    solved = lax.linalg.triangular_solve(
        eye_steps + lower_part, right_side, left_side=True, lower=True, unit_diagonal=True
    )
    new_vals = solved[..., :head_dim]
    new_keys = solved[..., head_dim:]
    k_end = jnp.exp(g_last[..., None] - g_step)[..., None] * k_blk
    eye_head = jnp.eye(head_dim, dtype=jnp.float32)
    transit = jnp.exp(g_last)[..., None, None] * eye_head - jnp.einsum(
        "chik,chil->chkl", new_keys, k_end, precision=HIGH
    )
    state_add = jnp.einsum("chiv,chik->chvk", new_vals, k_end, precision=HIGH)
    visible = step_pos[None, :] // n_keys <= tok_pos[:, None]
    q_gaps = jnp.where(visible, g_tok[..., :, None] - g_step[..., None, :], 0.0)
    weights = jnp.where(visible, jnp.exp(q_gaps), 0.0) * jnp.einsum(
        "chtk,chsk->chts", q_blk, k_blk, precision=HIGH
    )
    q_eff = jnp.exp(g_tok)[..., None] * q_blk - jnp.einsum(
        "chts,chsk->chtk", weights, new_keys, precision=HIGH
    )
    inner_out = jnp.einsum("chts,chsv->chtv", weights, new_vals, precision=HIGH)
    eye_stack = jnp.broadcast_to(eye_head, (n_heads, head_dim, head_dim))

    def advance(carried, step_pair):
        return (compose(carried, step_pair), carried)

    (dev_t, dev_u), (pre_t, pre_u) = lax.scan(
        advance, (eye_stack, jnp.zeros_like(eye_stack)), (transit, state_add)
    )
    return (pre_t, pre_u, q_eff, inner_out, dev_t, dev_u)


def group_apply(state_in, pre_t, pre_u, q_eff, inner_out):
    starts = jnp.einsum("hvk,chkl->chvl", state_in, pre_t, precision=HIGH) + pre_u
    blocks_out = jnp.einsum("chtk,chvk->chtv", q_eff, starts, precision=HIGH) + inner_out
    n_groups, n_heads, group_len, head_dim = blocks_out.shape
    return blocks_out.transpose(0, 2, 1, 3).reshape(n_groups * group_len, n_heads, head_dim)


def group_full(queries, key_vecs, val_vecs, beta_vals, decays, state_in, group_len):
    pre_t, pre_u, q_eff, inner_out, dev_t, dev_u = group_maps(
        queries, key_vecs, val_vecs, beta_vals, decays, group_len
    )
    return (group_apply(state_in, pre_t, pre_u, q_eff, inner_out), dev_t, dev_u)


def weight_terms(
    normed_in, d_proj_low, gated_out, d_res_low, normed_mid, d_gu_low, act_low, d_top_low
):
    term_in = jnp.einsum("td,tc->dc", normed_in, d_proj_low, preferred_element_type=jnp.float32)
    term_out = jnp.einsum("tc,td->cd", gated_out, d_res_low, preferred_element_type=jnp.float32)
    term_gu = jnp.einsum("td,tc->dc", normed_mid, d_gu_low, preferred_element_type=jnp.float32)
    term_down = jnp.einsum("tf,td->fd", act_low, d_top_low, preferred_element_type=jnp.float32)
    return (term_in, term_out, term_gu, term_down)


def local(
    tokens,
    cotangent,
    row_lengths,
    norm1_gain,
    w_in,
    w_router,
    conv_weight,
    a_log,
    dt_bias,
    head_gain,
    w_out,
    norm2_gain,
    w_gu,
    w_down,
):
    full_in, full_out, full_gu, full_down = (
        lax.all_gather(w_in, "seq", axis=0, tiled=True),
        lax.all_gather(w_out, "seq", axis=0, tiled=True),
        lax.all_gather(w_gu, "seq", axis=0, tiled=True),
        lax.all_gather(w_down, "seq", axis=0, tiled=True),
    )
    n_micro = tokens.shape[0]
    n_tok = tokens.shape[2]
    n_heads = a_log.shape[0]
    head_dim = head_gain.shape[0]
    n_keys = (w_router.shape[1] - n_heads) // n_heads
    n_taps = conv_weight.shape[0]
    conv_width = conv_weight.shape[1]
    hidden_units = full_gu.shape[1] // 2
    group_len = GROUP
    n_groups = n_tok // group_len
    position = lax.axis_index("seq") * n_tok + jnp.arange(n_tok, dtype=jnp.int32)
    eye_stack = jnp.broadcast_to(
        jnp.eye(head_dim, dtype=jnp.float32), (n_heads, head_dim, head_dim)
    )
    zero_stack = jnp.zeros_like(eye_stack)
    input_parts = partial(mixer_inputs, n_heads=n_heads, head_dim=head_dim, n_keys=n_keys)
    recur_full = partial(group_full, group_len=group_len)
    out_list = []
    grad_list = []
    kept_list = []
    big_total = None
    small_total = None
    for micro_num in range(n_micro):
        x_vals = tokens[micro_num, 0].astype(jnp.float32)
        scale_in = rms_scale(x_vals)
        normed_in = (x_vals * scale_in * norm1_gain).astype(jnp.bfloat16)
        projected = jnp.dot(normed_in, full_in, preferred_element_type=jnp.float32).astype(
            jnp.bfloat16
        )
        router = jnp.dot(normed_in, w_router, preferred_element_type=jnp.float32)
        conv_in = projected[:, :conv_width]
        gate_pre = projected[:, conv_width:].astype(jnp.float32)
        edge_rows = shifted(conv_in[n_tok - n_taps + 1 :], "seq", 1)
        extended = jnp.concatenate([edge_rows, conv_in], axis=0).astype(jnp.float32)
        queries, key_vecs, val_vecs, beta_vals, decays = input_parts(
            extended, conv_weight, router, a_log, dt_bias
        )
        q_low = to_low(queries)
        k_low = to_low(key_vecs)
        v_low = to_low(val_vecs)
        pre_t, pre_u, q_eff, inner_out, dev_t, dev_u = group_maps(
            q_low, k_low, v_low, beta_vals, decays, group_len
        )
        state_in = entering((dev_t, dev_u), "seq", compose, (eye_stack, zero_stack))[1]
        mixed_out = group_apply(state_in, pre_t, pre_u, q_eff, inner_out)
        gated_out = head_mix(mixed_out, gate_pre, head_gain).astype(jnp.bfloat16)
        residual = x_vals + jnp.dot(gated_out, full_out, preferred_element_type=jnp.float32)
        scale_mid = rms_scale(residual)
        normed_mid = (residual * scale_mid * norm2_gain).astype(jnp.bfloat16)
        gate_up = jnp.dot(normed_mid, full_gu, preferred_element_type=jnp.float32)
        gate_part = gate_up[:, :hidden_units]
        up_part = gate_up[:, hidden_units:]
        act_low = (jax.nn.silu(gate_part) * up_part).astype(jnp.bfloat16)
        mlp_out = jnp.dot(act_low, full_down, preferred_element_type=jnp.float32)
        out_list.append((residual + mlp_out).astype(jnp.bfloat16))
        live_mask = (position < row_lengths[micro_num, 0]).astype(jnp.float32)[:, None]
        d_top = cotangent[micro_num, 0].astype(jnp.float32) * live_mask
        d_top_low = d_top.astype(jnp.bfloat16)
        d_act = jnp.einsum("td,fd->tf", d_top_low, full_down, preferred_element_type=jnp.float32)
        gate_sig = jax.nn.sigmoid(gate_part)
        d_gate = d_act * up_part * gate_sig * (1.0 + gate_part * (1.0 - gate_sig))
        d_up = d_act * gate_part * gate_sig
        d_gu_low = jnp.concatenate([d_gate, d_up], axis=1).astype(jnp.bfloat16)
        d_mid = jnp.einsum("tc,dc->td", d_gu_low, full_gu, preferred_element_type=jnp.float32)
        g_norm2 = jnp.sum(d_mid * residual * scale_mid, axis=0)
        d_residual = d_top + rms_back(d_mid * norm2_gain, residual, scale_mid)
        d_res_low = d_residual.astype(jnp.bfloat16)
        d_gated = jnp.einsum("td,cd->tc", d_res_low, full_out, preferred_element_type=jnp.float32)
        _, head_pull = jax.vjp(head_mix, mixed_out, gate_pre, head_gain)
        d_mixed, d_gate_pre, g_head = head_pull(d_gated)
        _, recur_pull = jax.vjp(recur_full, q_low, k_low, v_low, beta_vals, decays, state_in)
        d_blk = d_mixed.reshape(n_groups, group_len, n_heads, head_dim).transpose(0, 2, 1, 3)
        d_starts = jnp.einsum("chtv,chtk->chvk", d_blk, q_eff, precision=HIGH)
        local_grad = jnp.einsum("chvk,chlk->hvl", d_starts, pre_t, precision=HIGH)
        d_state_out = carried_in(
            (dev_t.transpose(0, 2, 1), local_grad), "seq", compose, (eye_stack, zero_stack)
        )[1]
        d_dev_t = jnp.einsum("hvk,hvl->hkl", state_in, d_state_out, precision=HIGH)
        d_q, d_k, d_v, d_beta, d_decay, _ = recur_pull((d_mixed, d_dev_t, d_state_out))
        _, input_pull = jax.vjp(input_parts, extended, conv_weight, router, a_log, dt_bias)
        d_ext, g_conv, d_router, g_alog, g_dt = input_pull((d_q, d_k, d_v, d_beta, d_decay))
        d_edge = shifted(d_ext[: n_taps - 1].astype(jnp.bfloat16), "seq", -1).astype(jnp.float32)
        d_conv_in = d_ext[n_taps - 1 :].at[n_tok - n_taps + 1 :].add(d_edge)
        d_proj_low = jnp.concatenate([d_conv_in, d_gate_pre], axis=1).astype(jnp.bfloat16)
        d_router_low = d_router.astype(jnp.bfloat16)
        g_router = jnp.einsum(
            "td,tc->dc", normed_in, d_router_low, preferred_element_type=jnp.float32
        )
        d_norm_in = jnp.einsum("tc,dc->td", d_proj_low, full_in, preferred_element_type=jnp.float32)
        d_norm_in = d_norm_in + jnp.einsum(
            "tc,dc->td", d_router_low, w_router, preferred_element_type=jnp.float32
        )
        g_norm1 = jnp.sum(d_norm_in * x_vals * scale_in, axis=0)
        grad_list.append(d_residual + rms_back(d_norm_in * norm1_gain, x_vals, scale_in))
        small_parts = (g_norm1, g_router, g_conv, g_alog, g_dt, g_head, g_norm2)
        small_total = (
            small_parts
            if small_total is None
            else tuple((part_a + part_b for part_a, part_b in zip(small_total, small_parts)))
        )
        kept_parts = (
            normed_in,
            d_proj_low,
            gated_out,
            d_res_low,
            normed_mid,
            d_gu_low,
            act_low,
            d_top_low,
        )
        kept_list.append(kept_parts)
    joined = tuple(
        (jnp.concatenate([kept[index] for kept in kept_list], axis=0) for index in range(8))
    )
    big_total = tuple(
        jax.tree.map(
            lambda part: part.astype(jnp.float32),
            lax.psum_scatter(
                as_sent(weight_terms(*joined)), "seq", scatter_dimension=0, tiled=True
            ),
        )
    )
    grad_in, grad_out, grad_gu, grad_down = jax.tree.map(
        lambda part: part.astype(jnp.float32), lax.psum(as_sent(big_total), "row")
    )
    norm1_sum, router_sum, conv_sum, alog_sum, dt_sum, head_sum, norm2_sum = lax.psum(
        small_total, ("row", "seq")
    )
    out_block = jnp.stack(out_list)[:, None]
    grad_block = jnp.stack(grad_list)[:, None]
    return (
        out_block,
        grad_block,
        norm1_sum,
        grad_in,
        router_sum,
        conv_sum,
        alog_sum,
        dt_sum,
        head_sum,
        grad_out,
        norm2_sum,
        grad_gu,
        grad_down,
    )


def solution(mesh):
    return jax.shard_map(
        local,
        mesh=mesh,
        in_specs=(
            P(None, "row", "seq", None),
            P(None, "row", "seq", None),
            P(None, "row"),
            P(),
            P("seq", None),
            P(),
            P(),
            P(),
            P(),
            P(),
            P("seq", None),
            P(),
            P("seq", None),
            P("seq", None),
        ),
        out_specs=(
            P(None, "row", "seq", None),
            P(None, "row", "seq", None),
            P(),
            P("seq", None),
            P(),
            P(),
            P(),
            P(),
            P(),
            P("seq", None),
            P(),
            P("seq", None),
            P("seq", None),
        ),
        check_vma=False,
    )
```

profile of v0, /device:TPU:0, one launch (start us, length us, event | category | flops | bytes accessed | tf_op | source)
XLA Modules:
  0.0 2061.8 jit_solution(13270942935187892899)
XLA Ops:
  19.8 169.6 %all-gather.21.cloned.1.call-done = bf16[1024,6144]{1,0:T(8,128)(2,1)} async-done(((bf16[128,6144]{1,0:T(8,128)(2,1)}), bf16[1024,6144]{1,0:T(8,128)(2,1)}) %all-gather.21.cloned.1.call-update) | async-done | bytes 12582928 | tf_op jit(solution)/shard_map/all_gather | solution.py:225
  189.4 6.5 convolution_convert_fusion.2
  228.3 158.2 %custom-call.17 = f32[2,8,1,128,128]{3,4,2,1,0:T(8,128)S(1)} custom-call(f32[2,8,1,128,128]{4,3,2,1,0:T(8,128)} %get-tuple-element.1617), custom_call_target="InvertDiagBlocksLowerTriangular" | custom-call | tf_op jit(solution)/shard_map/triangular_solve/custom-call.1 | solution.py:153
  397.8 9.6 while.152
  414.6 159.0 %custom-call.16 = f32[2,8,1,128,128]{3,4,2,1,0:T(8,128)} custom-call(f32[2,8,1,128,128]{4,3,2,1,0:T(8,128)} %get-tuple-element.1616), custom_call_target="InvertDiagBlocksLowerTriangular" | custom-call | tf_op jit(solution)/shard_map/triangular_solve/custom-call.1 | solution.py:153
  585.2 7.1 while.150
  620.4 36.3 %while.153 = (s32[]{:T(128)}, f32[8,128,128]{1,2,0:T(8,128)}, s32[]{:T(128)}, f32[8,8,128,128]{3,2,1,0:T(8,128)}, f32[8,8,128,128]{3,2,1,0:T(8,128)}, /*index=5*/s32[]{:T(128)}, s32[]{:T(128)}) while((s32[]{:T(128)}, f32[8,128,128]{1,2,0:T(8,128)}, s32[]{:T(128)}, f32[8,8,128,128]{3,2,1,0:T(8,128)}, ...), condition=%wide.region_17.19_spmd.clone, body=%wide.region_16.18_spmd.clone.sunk | while | flops 201850880 | bytes 5769315 | solution.py:33
  667.8 73.7 %all-gather.31.cloned.1.call-done = f32[64,128,128]{2,1,0:T(8,128)} async-done(((f32[8,128,128]{2,1,0:T(8,128)}), f32[64,128,128]{2,1,0:T(8,128)}) %all-gather.31.cloned.1.call-update) | async-done | bytes 4194320 | tf_op jit(solution)/shard_map/all_gather | solution.py:24
  741.5 36.6 %while.151 = (s32[]{:T(128)}, f32[8,128,128]{1,2,0:T(8,128)}, s32[]{:T(128)}, f32[8,8,128,128]{3,2,1,0:T(8,128)}, f32[8,8,128,128]{3,2,1,0:T(8,128)}, /*index=5*/s32[]{:T(128)}, s32[]{:T(128)}) while((s32[]{:T(128)}, f32[8,128,128]{1,2,0:T(8,128)}, s32[]{:T(128)}, f32[8,8,128,128]{3,2,1,0:T(8,128)}, f32[8,8,128,128]{3,2,1,0:T(8,128)}, ...), condition=%wide.region_7.9_spmd.clone, body=%wide.region_6.8_spmd.clone.sunk | while | flops 201850880 | bytes 5769315 | solution.py:33
  796.0 159.4 %all-gather.25.cloned.1.call-done = bf16[1024,5632]{1,0:T(8,128)(2,1)} async-done(((bf16[128,5632]{1,0:T(8,128)(2,1)}), bf16[1024,5632]{1,0:T(8,128)(2,1)}) %all-gather.25.cloned.1.call-update) | async-done | bytes 11534352 | tf_op jit(solution)/shard_map/all_gather | solution.py:227
  955.4 7.6 fusion.457
  963.0 85.4 %all-gather.27.cloned.1.call-done = bf16[2816,1024]{1,0:T(8,128)(2,1)} async-done(((bf16[352,1024]{1,0:T(8,128)(2,1)}), bf16[2816,1024]{1,0:T(8,128)(2,1)}) %all-gather.27.cloned.1.call-update) | async-done | bytes 5767184 | tf_op jit(solution)/shard_map/all_gather | solution.py:228
  1048.4 7.4 multiply_convert_fusion.3
  1055.9 5.9 multiply_reduce_fusion.19
  1063.7 6.4 multiply_convert_fusion.1
  1070.1 5.9 multiply_reduce_fusion.18
  1150.5 14.0 convolution_convert_fusion
  1165.4 30.9 %while.146 = (s32[]{:T(128)}, f32[8,128,128]{1,2,0:T(8,128)}, s32[]{:T(128)}, bf16[8,8,128,128]{3,2,1,0:T(8,128)(2,1)}, bf16[8,8,128,128]{3,2,1,0:T(8,128)(2,1)}...) while((s32[]{:T(128)}, f32[8,128,128]{1,2,0:T(8,128)}, s32[]{:T(128)}, ...), condition=%wide.region_23.25_spmd, body=%wide.region_22.24_spmd.sunk | while | flops 201588736 | bytes 3670163 | solution.py:58
  1201.5 29.0 %while.147 = (s32[]{:T(128)}, f32[8,128,128]{1,2,0:T(8,128)}, f32[8,128,128]{1,2,0:T(8,128)}, f32[2,8,128,128]{3,2,1,0:T(8,128)}, f32[2,8,128,128]{2,3,1,0:T(8,1...) while((s32[]{:T(128)}, f32[8,128,128]{1,2,0:T(8,128)}, ...), condition=%wide.region_25.27_spmd, body=%wide.region_24.26_spmd.sunk | while | flops 805699584 | bytes 31983892 | solution.py:178
  1235.4 12.9 all-gather.43.cloned.1.call-done
  1249.2 31.3 %while.148 = (s32[]{:T(128)}, f32[8,128,128]{1,2,0:T(8,128)}, s32[]{:T(128)}, bf16[8,8,128,128]{3,2,1,0:T(8,128)(2,1)}, bf16[8,8,128,128]{3,2,1,0:T(8,128)(2,1)}...) while((s32[]{:T(128)}, f32[8,128,128]{1,2,0:T(8,128)}, s32[]{:T(128)}, ...), condition=%wide.region_45.50_spmd, body=%wide.region_44.49_spmd.sunk | while | flops 201588736 | bytes 3670163 | solution.py:58
  1297.6 29.2 %while.149 = (s32[]{:T(128)}, f32[8,128,128]{1,2,0:T(8,128)}, f32[8,128,128]{1,2,0:T(8,128)}, f32[2,8,128,128]{3,2,1,0:T(8,128)}, f32[2,8,128,128]{2,3,1,0:T(8,1...) while((s32[]{:T(128)}, f32[8,128,128]{1,2,0:T(8,128)}, ...), condition=%wide.region_47.52_spmd, body=%wide.region_46.51_spmd.sunk | while | flops 805699584 | bytes 31983892 | solution.py:178
  1429.3 10.0 broadcast_multiply_fusion
  1439.4 6.2 pad_add_fusion.1
  1459.0 9.5 convolution_convert_fusion.1
  1480.5 146.0 %reduce-scatter.9.cloned.1.call-done = bf16[128,5632]{1,0:T(8,128)(2,1)} async-done(((bf16[1024,5632]{1,0:T(8,128)(2,1)}), bf16[128,5632]{1,0:T(8,128)(2,1)}) %reduce-scatter.9.cloned.1.call-update) | async-done | bytes 1441808 | tf_op jit(solution)/shard_map/reduce_scatter | solution.py:347
  1626.5 209.8 %reduce-scatter.5.cloned.1.call-done = bf16[128,6144]{1,0:T(8,128)(2,1)} async-done(((bf16[1024,6144]{1,0:T(8,128)(2,1)}), bf16[128,6144]{1,0:T(8,128)(2,1)}) %reduce-scatter.5.cloned.1.call-update) | async-done | bytes 1572880 | tf_op jit(solution)/shard_map/reduce_scatter | solution.py:347
  1839.4 9.8 fusion.157
  1849.3 10.0 fusion.256
  1859.3 39.8 %all-reduce.32 = (f32[1024]{0:T(1024)}, f32[8]{0:T(128)}, f32[8]{0:T(128)}, f32[128]{0:T(128)}, f32[1024]{0:T(1024)}) all-reduce(f32[1024]{0:T(1024)S(1)} %add.678, f32[8]{0:T(128)S(1)} %add_multiply_fusion, f32[8]{0:T(128)S(1)} %add.682, f32[128]{0:T(128)S(1)} %add.683, ...), channel_id=1, replica_groups=mesh['row'=4,'seq'=8] {'row','seq'}, use_global_device_ids=true, to_apply=%region_66.71 | all-reduce | flops 2192 | bytes 17536 | tf_op jit(solution)/shard_map/psum | solution.py:355
  1901.6 20.4 all-reduce.40.cloned.1.call-done
  1929.5 122.1 %all-reduce.38.cloned.1.call-done = (f32[1024,24]{0,1:T(8,128)}, f32[4,5120]{1,0:T(4,128)}) async-done(((f32[1024,24]{0,1:T(8,128)}, f32[4,5120]{1,0:T(4,128)}), (f32[1024,24]{0,1:T(8,128)}, f32[4,5120]{1,0:T(4,128)})) %all-reduce.38.cloned.1.call-update) | async-done | bytes 180240 | tf_op jit(solution)/shard_map/psum | solution.py:355
  (1170 shorter events, 585.8 us)
Async XLA Ops:
  7.2 182.2 %all-gather.21.cloned.1.call-start = ((), (), s32[]{:S(2)}) async-start(), calls=%async_computation.4 | async-start | bytes 14155776 | tf_op jit(solution)/shard_map/all_gather | solution.py:225
  7.9 612.4 %all-gather.33.cloned.1.call-start = ((), (), s32[]{:S(2)}) async-start(), calls=%async_computation.14 | async-start | bytes 4718592 | tf_op jit(solution)/shard_map/all_gather | solution.py:24
  11.7 187.0 %copy-start.124 = (bf16[128,1024]{1,0:T(8,128)(2,1)}, bf16[128,1024]{1,0:T(8,128)(2,1)S(1)}, u32[]{:S(2)}) copy-start(bf16[128,1024]{1,0:T(8,128)(2,1)S(1)} %get-tuple-element.1610) | copy-start | bytes 786436
  13.5 396.2 %copy-start.174 = (f32[2,8,64]{2,1,0:T(8,128)}, f32[2,8,64]{2,1,0:T(8,128)S(1)}, u32[]{:S(2)}) copy-start(f32[2,8,64]{2,1,0:T(8,128)S(1)} %reduce_window_sum.37) | copy-start | bytes 12292
  14.1 397.1 %copy-start.158 = (f32[2,64,2,8]{3,2,1,0:T(2,128)}, f32[2,64,2,8]{3,2,1,0:T(2,128)S(1)}, u32[]{:S(2)}) copy-start(f32[2,64,2,8]{3,2,1,0:T(2,128)S(1)} %copy.790) | copy-start | bytes 24580
  17.7 562.9 %copy-start.145 = (f32[128,128]{1,0:T(8,128)}, f32[128,128]{1,0:T(8,128)S(1)}, u32[]{:S(2)}) copy-start(f32[128,128]{1,0:T(8,128)S(1)} %get-tuple-element.1682) | copy-start | bytes 196612
  19.8 186.7 %copy-start.227 = (f32[1,5120]{1,0:T(1,128)}, f32[1,5120]{1,0:T(1,128)S(1)}, u32[]{:S(2)}) copy-start(f32[1,5120]{1,0:T(1,128)S(1)} %get-tuple-element.1628) | copy-start | bytes 61444
  196.0 8.6 collective-permute-start.1
  201.8 4.2 collective-permute-start
  408.6 211.8 %all-gather.35.cloned.1.call-start = ((), (), s32[]{:S(2)}) async-start(), calls=%async_computation.15 | async-start | bytes 4718592 | tf_op jit(solution)/shard_map/all_gather | solution.py:24
  409.7 258.1 %all-gather.29.cloned.1.call-start = ((), (), s32[]{:S(2)}) async-start(), calls=%async_computation.12 | async-start | bytes 4718592 | tf_op jit(solution)/shard_map/all_gather | solution.py:24
  593.4 148.1 %all-gather.31.cloned.1.call-start = ((), (), s32[]{:S(2)}) async-start(), calls=%async_computation.13 | async-start | bytes 4718592 | tf_op jit(solution)/shard_map/all_gather | solution.py:24
  594.4 196.6 %all-gather.23.cloned.1.call-start = ((), (), s32[]{:S(2)}) async-start(), calls=%async_computation.5 | async-start | bytes 2359296 | tf_op jit(solution)/shard_map/all_gather | solution.py:226
  595.0 360.4 %all-gather.25.cloned.1.call-start = ((), (), s32[]{:S(2)}) async-start(), calls=%async_computation.6 | async-start | bytes 12976128 | tf_op jit(solution)/shard_map/all_gather | solution.py:227
  595.8 452.7 %all-gather.27.cloned.1.call-start = ((), (), s32[]{:S(2)}) async-start(), calls=%async_computation.7 | async-start | bytes 6488064 | tf_op jit(solution)/shard_map/all_gather | solution.py:228
  596.5 568.0 %all-gather.37.cloned.1.call-start = ((), (), s32[]{:S(2)}) async-start(), calls=%async_computation.16 | async-start | bytes 2359296 | tf_op jit(solution)/shard_map/all_gather | solution.py:41
  620.3 544.2 %all-gather.39.cloned.1.call-start = ((), (), s32[]{:S(2)}) async-start(), calls=%async_computation.17 | async-start | bytes 2359296 | tf_op jit(solution)/shard_map/all_gather | solution.py:41
  793.4 282.6 %copy-start.63 = (f32[128,1024]{1,0:T(8,128)}, f32[128,1024]{1,0:T(8,128)S(1)}, u32[]{:S(2)}) copy-start(f32[128,1024]{1,0:T(8,128)S(1)} %get-tuple-element.1664) | copy-start | bytes 1572868
  795.1 280.9 %copy-start.61 = (f32[128,1024]{1,0:T(8,128)}, f32[128,1024]{1,0:T(8,128)S(1)}, u32[]{:S(2)}) copy-start(f32[128,1024]{1,0:T(8,128)S(1)} %get-tuple-element.1666) | copy-start | bytes 1572868
  1091.1 144.2 %all-gather.41.cloned.1.call-start = ((), (), s32[]{:S(2)}) async-start(), calls=%async_computation.18 | async-start | bytes 2359296 | tf_op jit(solution)/shard_map/all_gather | solution.py:41
  1092.0 156.3 %all-gather.43.cloned.1.call-start = ((), (), s32[]{:S(2)}) async-start(), calls=%async_computation.19 | async-start | bytes 2359296 | tf_op jit(solution)/shard_map/all_gather | solution.py:41
  1098.1 382.3 %reduce-scatter.7.cloned.1.call-start = ((), (), s32[]{:S(2)}) async-start(), calls=%async_computation.9 | async-start | bytes 2359296 | tf_op jit(solution)/shard_map/reduce_scatter | solution.py:347
  1101.5 378.9 %reduce-scatter.11.cloned.1.call-start = ((), (), s32[]{:S(2)}) async-start(), calls=%async_computation.11 | async-start | bytes 6488064 | tf_op jit(solution)/shard_map/reduce_scatter | solution.py:347
  1107.0 519.5 %reduce-scatter.9.cloned.1.call-start = ((), (), s32[]{:S(2)}) async-start(), calls=%async_computation.10 | async-start | bytes 12976128 | tf_op jit(solution)/shard_map/reduce_scatter | solution.py:347
  1164.5 671.8 %reduce-scatter.5.cloned.1.call-start = ((), (), s32[]{:S(2)}) async-start(), calls=%async_computation.8 | async-start | bytes 14155776 | tf_op jit(solution)/shard_map/reduce_scatter | solution.py:347
  1445.6 7.0 collective-permute-start.2
  1450.6 7.1 collective-permute-start.3
  1468.6 453.5 %all-reduce.40.cloned.1.call-start = ((), (), s32[]{:S(2)}) async-start(), calls=%async_computation.21 | async-start | bytes 7995392 | tf_op jit(solution)/shard_map/psum | solution.py:353
  1477.2 359.4 %copy-start.289 = (f32[8]{0:T(128)S(1)}, f32[8]{0:T(128)}, u32[]{:S(2)}) copy-start(f32[8]{0:T(128)} %param.48) | copy-start | bytes 100
  1477.2 359.4 %copy-start.203 = (f32[2,64,2,8]{3,2,1,0:T(2,128)S(1)}, f32[2,64,2,8]{3,2,1,0:T(2,128)}, u32[]{:S(2)}) copy-start(f32[2,64,2,8]{3,2,1,0:T(2,128)} %get-tuple-element.1614) | copy-start | bytes 24580
  1477.2 359.6 %copy-start.204 = (f32[2,64,2,8]{3,2,1,0:T(2,128)S(1)}, f32[2,64,2,8]{3,2,1,0:T(2,128)}, u32[]{:S(2)}) copy-start(f32[2,64,2,8]{3,2,1,0:T(2,128)} %get-tuple-element.1615) | copy-start | bytes 24580
  1836.3 215.3 %all-reduce.38.cloned.1.call-start = ((), (), s32[]{:S(2)}) async-start(), calls=%async_computation.20 | async-start | bytes 360448 | tf_op jit(solution)/shard_map/psum | solution.py:355
  (299 other events, 3406.8 us)
Sparse Core Ops, SparseCore 0:
  10.2 179.1 all-gather.20
  408.8 74.6 all-gather.32
  485.6 71.2 all-gather.34
  593.5 74.2 all-gather.28
  669.8 71.6 all-gather.30
  743.4 47.5 all-gather.22
  793.2 162.1 all-gather.24
  957.6 90.8 all-gather.26
  1050.6 47.4 all-gather.36
  1100.6 47.7 all-gather.38
  1150.6 47.9 all-gather.40
  1200.5 47.7 all-gather.42
  1251.9 66.0 reduce-scatter.6
  1321.5 108.7 reduce-scatter.10
  1433.8 192.6 reduce-scatter.8
  1629.9 206.3 reduce-scatter.4
  1838.7 83.2 all-reduce.39
  1929.0 122.5 all-reduce.37
where the time goes:
time: 2070 us; the launch traced here: 2060 us
  waiting for transfers between devices  1010 us (49%)
  other arithmetic  411 us (20%)
  matrix products  371 us (18%)
  local copies, waits for them, and re-layouts  198 us (10%)
  blocking collectives  39.8 us (2%)
    reduce_scatter x4, waiting for transfers between devices, local(): lax.psum_scatter(as_sent(weight_terms(*joined)), 'seq', scatter_dimension...  356 us
    another operation x5, other arithmetic, group_maps(): lax.linalg.triangular_solve(eye_steps + lower_part, right_side, left_side...  321 us
    all_gather x1, waiting for transfers between devices, local(): lax.all_gather(w_in, 'seq', axis=0, tiled=True)  170 us
    all_gather x1, waiting for transfers between devices, local(): lax.all_gather(w_gu, 'seq', axis=0, tiled=True)  159 us
    psum x1, waiting for transfers between devices, local(): lax.psum(small_total, ('row', 'seq'))  122 us
    dot_general x40, matrix products, compose(): jnp.einsum('hvl,hlm->hvm', earlier[1], latter[0], precision=HIGH)  96.3 us
    all_gather x1, waiting for transfers between devices, local(): lax.all_gather(w_down, 'seq', axis=0, tiled=True)  85.4 us
    all_gather x4, waiting for transfers between devices, entering(): pieces = jax.tree.map(lambda part: lax.all_gather(part, axis), value)  77.5 us
  transfers between devices with their start and end apart: 22, of which 14 were waited for; matrix products, arithmetic and copies ran while one was open for 36% of the time, Pallas kernels for 0%

commit v1 on v0

v1 whole, which is shorter than its diff:
```python
from functools import partial

import jax
import jax.numpy as jnp
from jax import lax
from jax.experimental import pallas as pl
from jax.experimental.pallas import tpu as pltpu
from jax.sharding import PartitionSpec as P

BF = jnp.bfloat16
F32 = jnp.float32
EPS_NORM = 1e-05
EPS_UNIT = 1e-06
CH = 64
ST = 128
HALO = 16
LANES = 128
VMEM_BYTES = 50 * 1024 * 1024


def halves(value):
    high = value.astype(BF)
    return (high, (value - high.astype(F32)).astype(BF))


def dot(left, right, over_left=1, over_right=0):
    return lax.dot_general(
        left, right, (((over_left,), (over_right,)), ((), ())), preferred_element_type=F32
    )


def mm(left, right, over_left=1, over_right=0):
    left = left if isinstance(left, tuple) else (left,)
    right = right if isinstance(right, tuple) else (right,)
    total = dot(left[0], right[0], over_left, over_right)
    if len(right) > 1:
        total = total + dot(left[0], right[1], over_left, over_right)
    if len(left) > 1:
        total = total + dot(left[1], right[0], over_left, over_right)
    return total


def exact_sum(ones, value):
    high = value.astype(BF)
    rest = value - high.astype(F32)
    mid = rest.astype(BF)
    low = (rest - mid.astype(F32)).astype(BF)
    return dot(ones, high) + dot(ones, mid) + dot(ones, low)


def step_orders():
    row = lax.broadcasted_iota(jnp.int32, (ST, ST), 0)
    col = lax.broadcasted_iota(jnp.int32, (ST, ST), 1)
    order = lambda i: 2 * (i & (CH - 1)) + (i >> 6)
    return order(row), order(col)


def sees():
    row = lax.broadcasted_iota(jnp.int32, (CH, ST), 0)
    col = lax.broadcasted_iota(jnp.int32, (CH, ST), 1)
    return (col & (CH - 1)) <= row


def twice(value):
    return jnp.concatenate([value, value], axis=0)


def log_decays(router, par):
    lane = lax.broadcasted_iota(jnp.int32, (CH, LANES), 1)
    pre = router + par[2:3]
    soft = jnp.maximum(pre, 0.0) + jnp.log1p(jnp.exp(-jnp.abs(pre)))
    decay = -jnp.exp(par[1:2]) * soft
    row = lax.broadcasted_iota(jnp.int32, (CH, CH), 0)
    col = lax.broadcasted_iota(jnp.int32, (CH, CH), 1)
    below = jnp.where(col <= row, 1.0, 0.0).astype(BF)
    total = exact_sum(below, jnp.where(lane == 2, decay, 0.0))
    return decay, total


def gate_columns(router, par):
    strength = jax.nn.sigmoid(router)
    decay, total = log_decays(router, par)
    beta = jnp.concatenate([strength[:, 0:1], strength[:, 1:2]], axis=0)
    doubled = twice(total)
    g_col = doubled[:, 2:3]
    g_row = doubled.T[2:3, :]
    g_last = total[CH - 1 : CH, 2:3]
    return beta, g_col, g_row, g_last, decay


def seen_decay(g_col, g_row, visible):
    return jnp.where(visible, jnp.exp(jnp.where(visible, g_col[:CH] - g_row, 0.0)), 0.0)


def unit(value):
    scale = lax.rsqrt(jnp.sum(value * value, axis=-1, keepdims=True) + EPS_UNIT)
    return value * scale, scale


def taps_sum(window, weight, start):
    total = weight[0:1] * window[pl.ds(start + 5, CH), :]
    for tap in range(1, 4):
        total = total + weight[tap : tap + 1] * window[pl.ds(start + 5 + tap, CH), :]
    return total


def fill_window(window, proj_ref, halo_ref, is_first):
    width = window.shape[1]
    edge = halo_ref[0, :, :width].astype(F32)[HALO - 8 :]
    window[0:8, :] = jnp.where(is_first, 0.0, edge)
    window[8:, :] = proj_ref[0, :, :width].astype(F32)


def prep_kernel(
    count, proj_ref, halo_ref, router_ref, taps_ref, par_ref,
    solve_ref, wmat_ref, umat_ref, seen_ref, q_ref, k_ref, window,
):
    fill_window(window, proj_ref, halo_ref, pl.program_id(1) == 0)
    weight = taps_ref[...]
    par = par_ref[...]
    o_row, o_col = step_orders()
    strict = o_row > o_col
    eye = jnp.where(o_row == o_col, 1.0, 0.0)
    visible = sees()
    many = range(count)
    lower, rights = [], []
    for n in many:
        conv = taps_sum(window, weight, n * CH)
        act = conv * jax.nn.sigmoid(conv)
        q = unit(act[:, 0:128])[0].astype(BF)
        k = jnp.concatenate(
            [unit(act[:, 128:256])[0], unit(act[:, 256:384])[0]], axis=0
        ).astype(BF)
        v = jnp.concatenate([act[:, 384:512], act[:, 512:640]], axis=0).astype(BF)
        beta, g_col, g_row, _, _ = gate_columns(
            router_ref[0, n * CH : (n + 1) * CH, :], par
        )
        gaps = seen_decay(g_col, g_row, visible)
        lower.append(jnp.where(strict, beta * twice(gaps) * dot(k, k, 1, 1), 0.0))
        kf = k.astype(F32)
        rights.append(
            jnp.concatenate([beta * jnp.exp(g_col) * kf, beta * v.astype(F32)], axis=1)
        )
        seen_ref[0, n] = gaps * dot(q, k, 1, 1)
        q_ref[0, n] = q
        k_ref[0, n] = k
    inverse = [eye - jnp.where((o_row >> 1) == (o_col >> 1), part, 0.0) for part in lower]
    for level in range(1, 7):
        at = ((o_row >> level) ^ (o_col >> level)) == 1
        parts = [halves(jnp.where(at, part, 0.0)) for part in lower]
        known = [halves(value) for value in inverse]
        inner = [halves(mm(parts[n], known[n])) for n in many]
        inverse = [inverse[n] - mm(known[n], inner[n]) for n in many]
    for n in many:
        solve_ref[0, n] = inverse[n]
        both = mm(halves(inverse[n]), halves(rights[n]))
        wmat_ref[0, n] = both[:, :128]
        umat_ref[0, n] = both[:, 128:]


def head_norm(mixed):
    return lax.rsqrt(jnp.mean(mixed * mixed, axis=-1, keepdims=True) + EPS_NORM)


def scan_kernel(
    n_micro, count, wmat_ref, umat_ref, seen_ref, q_ref, k_ref, router_ref, gate_ref, par_ref,
    out_ref, mixed_ref, news_ref, state_ref, state,
):
    @pl.when(pl.program_id(0) == 0)
    def _():
        state[...] = jnp.zeros_like(state)

    par = par_ref[...]
    now = [state[m] for m in range(n_micro)]
    for n in range(count):
        rows = slice(n * CH, (n + 1) * CH)
        for m in range(n_micro):
            _, g_col, _, g_last, _ = gate_columns(router_ref[m, rows, :], par)
            held = halves(now[m])
            state_ref[m, n] = now[m]
            news = umat_ref[m, n] - mm(halves(wmat_ref[m, n]), held)
            news_ref[m, n] = news
            news_h = halves(news)
            ends = halves(jnp.exp(g_last - g_col) * k_ref[m, n].astype(F32))
            now[m] = jnp.exp(g_last) * now[m] + mm(ends, news_h, 0, 0)
            mixed = jnp.exp(g_col[:CH]) * mm(q_ref[m, n], held) + mm(halves(seen_ref[m, n]), news_h)
            mixed_ref[m, n] = mixed
            gate = gate_ref[m, rows, :].astype(F32)
            out_ref[m, rows, :] = (
                mixed * head_norm(mixed) * par[0:1] * (gate * jax.nn.sigmoid(gate))
            ).astype(BF)
    for m in range(n_micro):
        state[m] = now[m]


def scan_back_kernel(
    n_micro, count, wmat_ref, seen_ref, q_ref, k_ref, router_ref, gate_ref, par_ref, mixed_ref, d_out_ref,
    d_mixed_ref, d_news_ref, d_state_ref, d_gate_ref, gain_ref, state,
):
    @pl.when(pl.program_id(0) == 0)
    def _():
        state[...] = jnp.zeros_like(state)
        gain_ref[...] = jnp.zeros_like(gain_ref)

    par = par_ref[...]
    now = [state[m] for m in range(n_micro)]
    gain = jnp.zeros((1, LANES), F32)
    for n in reversed(range(count)):
        rows = slice(n * CH, (n + 1) * CH)
        for m in range(n_micro):
            _, g_col, _, g_last, _ = gate_columns(router_ref[m, rows, :], par)
            mixed = mixed_ref[m, n]
            gate = gate_ref[m, rows, :].astype(F32)
            d_out = d_out_ref[m, rows, :].astype(F32)
            scale = head_norm(mixed)
            normed = mixed * scale
            sig = jax.nn.sigmoid(gate)
            silu = gate * sig
            gain = gain + jnp.sum(d_out * normed * silu, axis=0, keepdims=True)
            d_gate = d_out * normed * par[0:1] * (sig * (1.0 + gate * (1.0 - sig)))
            d_gate_ref[m, rows, :] = d_gate.astype(BF)
            d_normed = d_out * par[0:1] * silu
            d_mixed = scale * d_normed - mixed * scale**3 * jnp.mean(
                d_normed * mixed, axis=-1, keepdims=True
            )
            d_mixed_ref[m, n] = d_mixed
            d_mixed_h = halves(d_mixed)
            d_state_ref[m, n] = now[m]
            ends = halves(jnp.exp(g_last - g_col) * k_ref[m, n].astype(F32))
            d_news = mm(halves(seen_ref[m, n]), d_mixed_h, 0, 0) + mm(ends, halves(now[m]))
            d_news_ref[m, n] = d_news
            q_eff = halves(jnp.exp(g_col[:CH]) * q_ref[m, n].astype(F32))
            now[m] = (
                jnp.exp(g_last) * now[m]
                + mm(q_eff, d_mixed_h, 0, 0)
                - mm(halves(wmat_ref[m, n]), halves(d_news), 0, 0)
            )
    gain_ref[0:1, :] += gain
    for m in range(n_micro):
        state[m] = now[m]


def unit_back(grad, value, scale):
    return scale * grad - value * scale**3 * jnp.sum(grad * value, axis=-1, keepdims=True)


def grads_kernel(
    count, proj_ref, halo_ref, router_ref, taps_ref, par_ref, solve_ref, seen_ref, news_ref, state_ref,
    d_mixed_ref, d_news_ref, d_state_ref, d_gate_ref,
    d_ext_ref, g_taps_ref, g_par_ref, window, d_window,
):
    step = pl.program_id(1)
    size = count * CH
    fill_window(window, proj_ref, halo_ref, step == pl.num_programs(1) - 1)

    @pl.when((step == 0) & (pl.program_id(0) == 0))
    def _():
        g_taps_ref[...] = jnp.zeros_like(g_taps_ref)
        g_par_ref[...] = jnp.zeros_like(g_par_ref)

    @pl.when(step == 0)
    def _():
        d_window[size:, :] = jnp.zeros((8, d_window.shape[1]), F32)

    @pl.when(step > 0)
    def _():
        d_window[size:, :] = d_window[0:8, :]

    weight = taps_ref[...]
    par = par_ref[...]
    o_row, o_col = step_orders()
    strict = o_row > o_col
    visible = sees()
    row = lax.broadcasted_iota(jnp.int32, (CH, CH), 0)
    col = lax.broadcasted_iota(jnp.int32, (CH, CH), 1)
    above = jnp.where(col >= row, 1.0, 0.0).astype(BF)
    lane = lax.broadcasted_iota(jnp.int32, (CH, LANES), 1)
    last = lax.broadcasted_iota(jnp.int32, (CH, LANES), 0) == CH - 1
    g_alog = jnp.zeros((1, LANES), F32)
    g_dt = jnp.zeros((1, LANES), F32)
    for n in range(count):
        rows = slice(n * CH, (n + 1) * CH)
        conv = taps_sum(window, weight, n * CH)
        sig = jax.nn.sigmoid(conv)
        act = conv * sig
        qn, q_scale = unit(act[:, 0:128])
        k0n, k0_scale = unit(act[:, 128:256])
        k1n, k1_scale = unit(act[:, 256:384])
        q = qn.astype(BF)
        k = jnp.concatenate([k0n, k1n], axis=0).astype(BF)
        kf, qf = k.astype(F32), q.astype(F32)
        router = router_ref[0, rows, :]
        beta, g_col, g_row, g_last, decay = gate_columns(router, par)
        gaps = seen_decay(g_col, g_row, visible)
        ratio = jnp.where(strict, twice(gaps), 0.0)
        grown = jnp.exp(g_col)
        left = jnp.exp(g_last - g_col)
        gram = dot(k, k, 1, 1)
        state = state_ref[0, n]
        state_h = halves(state)
        news = news_ref[0, n]
        news_h = halves(news)
        d_mixed_h = halves(d_mixed_ref[0, n])
        d_state = d_state_ref[0, n]
        d_right = mm(halves(solve_ref[0, n]), halves(d_news_ref[0, n]), 0, 0)
        d_right_h = halves(d_right)
        d_lower = jnp.where(strict, -mm(d_right_h, news_h, 1, 1), 0.0)
        d_pre = (1.0 - beta) * jnp.sum(d_right * news, axis=-1, keepdims=True)
        d_v = beta * d_right
        d_grown_k = -beta * mm(d_right_h, state_h, 1, 1)
        d_k = grown * d_grown_k
        d_gram = beta * ratio * d_lower
        both = d_gram * gram
        d_g = jnp.sum(both, axis=-1, keepdims=True) + jnp.sum(d_k * kf, axis=-1, keepdims=True)
        d_g_row = -jnp.sum(both, axis=0, keepdims=True)
        d_k = d_k + mm(halves(d_gram + d_gram.T), k)
        d_seen = mm(d_mixed_h, news_h, 1, 1)
        d_scores = halves(d_seen * gaps)
        seen_both = d_seen * seen_ref[0, n]
        d_q_grown = grown[:CH] * mm(d_mixed_h, state_h, 1, 1)
        d_q = d_q_grown + mm(d_scores, k)
        d_k = d_k + mm(d_scores, q, 0, 0)
        d_g_q = jnp.sum(seen_both + d_q_grown * qf, axis=-1, keepdims=True)
        d_g_row = d_g_row - jnp.sum(seen_both, axis=0, keepdims=True)
        d_ends = left * mm(news_h, halves(d_state), 1, 1)
        d_k = d_k + d_ends
        ends_sum = jnp.sum(d_ends * kf, axis=-1, keepdims=True)
        d_g = d_g - ends_sum
        d_last = jnp.sum(ends_sum, axis=0, keepdims=True) + jnp.exp(g_last) * jnp.sum(
            jnp.sum(d_state * state, axis=-1, keepdims=True), axis=0, keepdims=True
        )
        d_g_rows = jnp.broadcast_to(d_g_row, (LANES, ST)).T
        d_g_tok = d_g_q + d_g[:CH] + d_g[CH:] + d_g_rows[:CH] + d_g_rows[CH:]
        d_g_tok = d_g_tok + jnp.where(last, d_last, 0.0)
        d_decay = exact_sum(above, d_g_tok)
        d_soft = -jnp.exp(par[1:2]) * jax.nn.sigmoid(router + par[2:3]) * d_decay
        d_router = jnp.where(
            lane == 0,
            d_pre[:CH],
            jnp.where(lane == 1, d_pre[CH:], jnp.where(lane == 2, d_soft, 0.0)),
        )
        width = window.shape[1]
        d_ext_ref[0, rows, width : width + LANES] = d_gate_ref[0, rows, :]
        d_ext_ref[0, rows, width + LANES :] = d_router.astype(BF)
        g_alog = g_alog + jnp.sum(
            jnp.where(lane == 2, d_decay * decay, 0.0), axis=0, keepdims=True
        )
        g_dt = g_dt + jnp.sum(jnp.where(lane == 2, d_soft, 0.0), axis=0, keepdims=True)
        d_act = jnp.concatenate(
            [
                unit_back(d_q, act[:, 0:128], q_scale),
                unit_back(d_k[:CH], act[:, 128:256], k0_scale),
                unit_back(d_k[CH:], act[:, 256:384], k1_scale),
                d_v[:CH],
                d_v[CH:],
            ],
            axis=1,
        )
        d_window[rows, :] = d_act * (sig * (1.0 + conv * (1.0 - sig)))
    g_par_ref[1:2, :] += g_alog
    g_par_ref[2:3, :] += g_dt
    for n in range(count):
        start = n * CH
        here = d_window[pl.ds(start, CH), :]
        total = weight[3:4] * here
        for tap in range(3):
            total = total + weight[tap : tap + 1] * d_window[pl.ds(start + 3 - tap, CH), :]
        d_ext_ref[0, pl.ds(start, CH), : total.shape[1]] = total.astype(BF)
        for tap in range(4):
            g_taps_ref[tap : tap + 1, :] += jnp.sum(
                here * window[pl.ds(start + 5 + tap, CH), :], axis=0, keepdims=True
            )


def params(*semantics):
    return pltpu.CompilerParams(dimension_semantics=semantics, vmem_limit_bytes=VMEM_BYTES)


def cost(chunks, dots, size):
    return pl.CostEstimate(
        flops=chunks * dots * 2 * 128**3, transcendentals=chunks * 128 * 1024, bytes_accessed=size
    )


def whole(shape):
    return pl.BlockSpec(shape, lambda *_: (0,) * len(shape))


def prepare(projected, router, taps, par, width, count=8):
    n_micro, length, full = projected.shape
    steps = length // (count * CH)
    chunks = length // CH
    size = count * CH
    per = lambda *tail: pl.BlockSpec((1, count) + tail, lambda m, i: (m, i, 0, 0))
    made = lambda kind, *tail: jax.ShapeDtypeStruct((n_micro, chunks) + tail, kind)
    return pl.pallas_call(
        partial(prep_kernel, count),
        grid=(n_micro, steps),
        in_specs=[
            pl.BlockSpec((1, size, full), lambda m, i: (m, i, 0)),
            pl.BlockSpec((1, HALO, full), lambda m, i: (m, jnp.maximum(i * (size // HALO) - 1, 0), 0)),
            pl.BlockSpec((1, size, LANES), lambda m, i: (m, i, 0)),
            whole(taps.shape),
            whole(par.shape),
        ],
        out_specs=[per(ST, ST), per(ST, 128), per(ST, 128), per(CH, ST), per(CH, 128), per(ST, 128)],
        out_shape=[
            made(F32, ST, ST), made(F32, ST, 128), made(F32, ST, 128), made(F32, CH, ST),
            made(BF, CH, 128), made(BF, ST, 128),
        ],
        scratch_shapes=[pltpu.VMEM((size + 8, width), F32)],
        compiler_params=params("arbitrary", "arbitrary"),
        cost_estimate=cost(n_micro * chunks, 44, n_micro * chunks * 400 * 1024),
        name="mixer_prepare",
    )(projected, projected, router, taps, par)


def scan_states(prep, router, projected, par, gate_at, count=4):
    _, wmat, umat, seen, q, k = prep
    n_micro, chunks = wmat.shape[:2]
    length = chunks * CH
    size = count * CH
    per = lambda *tail: pl.BlockSpec((n_micro, count) + tail, lambda i: (0, i, 0, 0))
    made = lambda kind, *tail: jax.ShapeDtypeStruct((n_micro, chunks) + tail, kind)
    return pl.pallas_call(
        partial(scan_kernel, n_micro, count),
        grid=(chunks // count,),
        in_specs=[
            per(ST, 128), per(ST, 128), per(CH, ST), per(CH, 128), per(ST, 128),
            pl.BlockSpec((n_micro, size, LANES), lambda i: (0, i, 0)),
            pl.BlockSpec((n_micro, size, 128), lambda i: (0, i, gate_at)),
            whole(par.shape),
        ],
        out_specs=[
            pl.BlockSpec((n_micro, size, 128), lambda i: (0, i, 0)),
            per(CH, 128), per(ST, 128), per(128, 128),
        ],
        out_shape=[
            jax.ShapeDtypeStruct((n_micro, length, 128), BF),
            made(F32, CH, 128), made(F32, ST, 128), made(F32, 128, 128),
        ],
        scratch_shapes=[pltpu.VMEM((n_micro, 128, 128), F32)],
        compiler_params=params("arbitrary"),
        cost_estimate=cost(n_micro * chunks, 12, n_micro * chunks * 420 * 1024),
        name="mixer_scan",
    )(wmat, umat, seen, q, k, router, projected, par)


def scan_back(prep, router, projected, par, gate_at, mixed, d_out, count=4):
    _, wmat, _, seen, q, k = prep
    n_micro, chunks = wmat.shape[:2]
    length = chunks * CH
    size = count * CH
    blocks = chunks // count
    per = lambda *tail: pl.BlockSpec((n_micro, count) + tail, lambda i: (0, blocks - 1 - i, 0, 0))
    made = lambda kind, *tail: jax.ShapeDtypeStruct((n_micro, chunks) + tail, kind)
    return pl.pallas_call(
        partial(scan_back_kernel, n_micro, count),
        grid=(blocks,),
        in_specs=[
            per(ST, 128), per(CH, ST), per(CH, 128), per(ST, 128),
            pl.BlockSpec((n_micro, size, LANES), lambda i: (0, blocks - 1 - i, 0)),
            pl.BlockSpec((n_micro, size, 128), lambda i: (0, blocks - 1 - i, gate_at)),
            whole(par.shape),
            per(CH, 128),
            pl.BlockSpec((n_micro, size, 128), lambda i: (0, blocks - 1 - i, 0)),
        ],
        out_specs=[
            per(CH, 128), per(ST, 128), per(128, 128),
            pl.BlockSpec((n_micro, size, 128), lambda i: (0, blocks - 1 - i, 0)),
            whole((8, LANES)),
        ],
        out_shape=[
            made(F32, CH, 128), made(F32, ST, 128), made(F32, 128, 128),
            jax.ShapeDtypeStruct((n_micro, length, 128), BF),
            jax.ShapeDtypeStruct((8, LANES), F32),
        ],
        scratch_shapes=[pltpu.VMEM((n_micro, 128, 128), F32)],
        compiler_params=params("arbitrary"),
        cost_estimate=cost(n_micro * chunks, 12, n_micro * chunks * 420 * 1024),
        name="mixer_scan_back",
    )(wmat, seen, q, k, router, projected, par, mixed, d_out)


def mixer_grads(prep, router, projected, taps, par, width, news, state, d_mixed, d_news, d_state, d_gate, count=4):
    solve, _, _, seen, _, _ = prep
    n_micro, chunks = solve.shape[:2]
    length = chunks * CH
    size = count * CH
    blocks = chunks // count
    full = projected.shape[2]
    per = lambda *tail: pl.BlockSpec((1, count) + tail, lambda m, i: (m, blocks - 1 - i, 0, 0))
    rows = lambda n: pl.BlockSpec((1, size, n), lambda m, i: (m, blocks - 1 - i, 0))
    before = lambda m, i: (m, jnp.maximum((blocks - 1 - i) * (size // HALO) - 1, 0), 0)
    return pl.pallas_call(
        partial(grads_kernel, count),
        grid=(n_micro, blocks),
        in_specs=[
            rows(full), pl.BlockSpec((1, HALO, full), before), rows(LANES),
            whole(taps.shape), whole(par.shape),
            per(ST, ST), per(CH, ST), per(ST, 128), per(128, 128),
            per(CH, 128), per(ST, 128), per(128, 128), rows(LANES),
        ],
        out_specs=[rows(width + 2 * LANES), whole((8, width)), whole((8, LANES))],
        out_shape=[
            jax.ShapeDtypeStruct((n_micro, length, width + 2 * LANES), BF),
            jax.ShapeDtypeStruct((8, width), F32),
            jax.ShapeDtypeStruct((8, LANES), F32),
        ],
        scratch_shapes=[pltpu.VMEM((size + 8, width), F32), pltpu.VMEM((size + 8, width), F32)],
        compiler_params=params("arbitrary", "arbitrary"),
        cost_estimate=cost(n_micro * chunks, 32, n_micro * chunks * 600 * 1024),
        name="mixer_grads",
    )(projected, projected, router, taps, par, solve, seen, news, state, d_mixed, d_news, d_state, d_gate)


def exchange(value, bit):
    count = lax.axis_size("row")
    return lax.ppermute(value, "row", [(i, i ^ bit) for i in range(count)])


def row_bits():
    count = lax.axis_size("row")
    return [1 << b for b in range(count.bit_length() - 1)]


def row_gather(value):
    parts = {0: value}
    for bit in reversed(row_bits()):
        places = sorted(parts)
        got = exchange(jnp.stack([parts[j] for j in places]), bit)
        parts.update({j ^ bit: got[n] for n, j in enumerate(places)})
    return [parts[j] for j in range(len(parts))]


def row_scatter(parts):
    parts = dict(enumerate(parts))
    for bit in row_bits():
        away = [j for j in sorted(parts) if j & bit]
        got = exchange(jnp.stack([parts[j].astype(BF) for j in away]), bit).astype(F32)
        parts = {
            j ^ bit: parts[j ^ bit].astype(F32) + got[n] for n, j in enumerate(away)
        }
    return parts[0]


def row_sum(value):
    for bit in row_bits():
        value = value + exchange(value, bit)
    return value


def rms_scale(values):
    return lax.rsqrt(jnp.mean(values * values, axis=-1, keepdims=True) + EPS_NORM)


def rms_back(grad_norm, values, inv_scale):
    return inv_scale * grad_norm - values * inv_scale**3 * jnp.mean(
        grad_norm * values, axis=-1, keepdims=True
    )


def matmul(spec, left, right, kind=F32):
    return jnp.einsum(spec, left, right, preferred_element_type=F32).astype(kind)


def local(
    tokens,
    cotangent,
    row_lengths,
    norm1_gain,
    w_in,
    w_router,
    conv_weight,
    a_log,
    dt_bias,
    head_gain,
    w_out,
    norm2_gain,
    w_gu,
    w_down,
):
    n_seq, n_row = lax.axis_size("seq"), lax.axis_size("row")
    seq, row = lax.axis_index("seq"), lax.axis_index("row")
    n_micro, _, n_tok, model = tokens.shape
    n_heads = a_log.shape[0]
    head_dim = head_gain.shape[0]
    n_taps, conv_width = conv_weight.shape
    slots = w_in.shape[1] // (n_heads * head_dim)
    width = conv_width // n_heads
    length = n_tok * n_seq
    copies = n_seq // n_heads
    head = seq // copies
    gate_at = slots - 1

    def to_heads(value):
        return lax.all_to_all(jnp.repeat(value, copies, axis=0), "seq", 0, 0, tiled=True)

    def from_heads(value):
        got = lax.all_to_all(value, "seq", 0, 0, tiled=True)
        return got if copies == 1 else got[::copies]

    tokens_all = lax.all_gather(tokens[:, 0], "seq", axis=0)
    cut = w_in.shape[0] // n_row
    w_piece = lax.dynamic_index_in_dim(
        w_in.reshape(n_row, cut, slots, n_heads, head_dim), row, 0, False
    )
    w_piece = w_piece.transpose(2, 0, 1, 3).reshape(n_heads, cut, slots * head_dim)
    w_pieces = jnp.stack(row_gather(to_heads(w_piece)))
    w_head = jnp.stack(
        [lax.dynamic_index_in_dim(w_pieces, row ^ j, 0, False) for j in range(n_row)], axis=1
    ).reshape(model, slots * head_dim)
    w_rt = lax.dynamic_index_in_dim(w_router.reshape(model, -1, n_heads), head, 2, False)
    n_rt = w_rt.shape[1]
    w_rt = jnp.pad(w_rt, ((0, 0), (0, LANES - n_rt)))
    taps = lax.dynamic_index_in_dim(
        conv_weight.reshape(n_taps, gate_at, n_heads, head_dim), head, 2, False
    ).reshape(n_taps, width)
    taps = jnp.pad(taps, ((0, 8 - n_taps), (0, 0)))
    par = jnp.concatenate(
        [
            head_gain[None],
            jnp.broadcast_to(lax.dynamic_index_in_dim(a_log, head, 0), (1, LANES)),
            jnp.broadcast_to(lax.dynamic_index_in_dim(dt_bias, head, 0), (1, LANES)),
            jnp.zeros((5, LANES), F32),
        ]
    )
    hidden = w_gu.shape[1] // 2
    unit_cut = hidden // n_seq // n_row
    n_units = unit_cut * n_seq
    gu_piece = lax.dynamic_index_in_dim(
        w_gu.reshape(-1, 2, n_seq, n_row, unit_cut), row, 3, False
    ).reshape(-1, 2 * n_units)
    down_piece = lax.dynamic_slice_in_dim(w_down, row * unit_cut, unit_cut, 0)
    full_out = lax.all_gather(w_out, "seq", axis=0, tiled=True)
    gu = lax.all_gather(gu_piece, "seq", axis=0, tiled=True)
    down = lax.all_gather(down_piece, "seq", axis=0, tiled=True)

    position = seq * n_tok + jnp.arange(n_tok, dtype=jnp.int32)
    live = (position[None, :] < row_lengths[:, :1]).astype(F32)[:, :, None]
    d_top = cotangent[:, 0].astype(F32) * live
    d_top_low = d_top.astype(BF)
    d_top_rows = jnp.concatenate(
        [part.reshape(-1, model) for part in row_gather(d_top_low)], axis=0
    )
    d_act = matmul("td,fd->tf", d_top_rows, down)

    x_all = tokens_all.transpose(1, 0, 2, 3).reshape(n_micro, length, model).astype(F32)
    scale_all = rms_scale(x_all)
    normed_in = (x_all * scale_all * norm1_gain).astype(BF)
    projected = matmul("mtd,dc->mtc", normed_in, w_head, BF)
    router = matmul("mtd,dc->mtc", normed_in, w_rt)
    prep = prepare(projected, router, taps, par, width)
    gated, mixed, news, state = scan_states(prep, router, projected, par, gate_at)

    gated_out = from_heads(
        gated.reshape(n_micro, n_seq, n_tok, head_dim).transpose(1, 0, 2, 3)
    )
    gated_out = gated_out.transpose(1, 2, 0, 3).reshape(n_micro * n_tok, model)
    x_vals = tokens[:, 0].reshape(-1, model).astype(F32)
    residual = x_vals + matmul("tc,cd->td", gated_out, full_out)
    scale_mid = rms_scale(residual)
    normed_mid = (residual * scale_mid * norm2_gain).astype(BF)
    mid_rows = jnp.concatenate(row_gather(normed_mid), axis=0)
    gate_up = matmul("td,dc->tc", mid_rows, gu)
    gate_part = gate_up[:, :n_units]
    up_part = gate_up[:, n_units:]
    gate_sig = jax.nn.sigmoid(gate_part)
    act_low = (gate_part * gate_sig * up_part).astype(BF)
    d_gate = d_act * up_part * gate_sig * (1.0 + gate_part * (1.0 - gate_sig))
    d_up = d_act * gate_part * gate_sig
    d_gu_low = jnp.concatenate([d_gate, d_up], axis=1).astype(BF)
    d_mid = row_scatter(list(matmul("tc,dc->td", d_gu_low, gu).reshape(n_row, -1, model)))
    d_residual = d_top.reshape(-1, model) + rms_back(d_mid * norm2_gain, residual, scale_mid)
    d_res_low = d_residual.astype(BF)
    d_gated = matmul("td,cd->tc", d_res_low, full_out, BF)
    d_gated = d_gated.reshape(n_micro, n_tok, n_heads, head_dim).transpose(2, 0, 1, 3)
    d_gated = to_heads(d_gated).transpose(1, 0, 2, 3).reshape(n_micro, length, head_dim)

    mlp_out = row_scatter(list(matmul("tf,fd->td", act_low, down).reshape(n_row, -1, model)))
    out = (residual + mlp_out).astype(BF).reshape(n_micro, 1, n_tok, model)

    d_mixed, d_news, d_state, d_gate_pre, g_head = scan_back(
        prep, router, projected, par, gate_at, mixed, d_gated
    )
    d_ext, g_taps, g_par = mixer_grads(
        prep, router, projected, taps, par, width, news, state, d_mixed, d_news, d_state, d_gate_pre
    )
    if copies > 1:
        mine = (seq % copies == 0).astype(F32)
        d_ext = d_ext * mine.astype(BF)
        g_taps, g_par, g_head = g_taps * mine, g_par * mine, g_head * mine
    w_ext = jnp.concatenate([w_head, w_rt], axis=1)
    d_in_part = matmul("mtc,dc->mtd", d_ext, w_ext)
    g_norm1 = jnp.sum(d_in_part * x_all * scale_all, axis=(0, 1))
    d_in_part = d_in_part.astype(BF).reshape(n_micro, n_seq, n_tok, model).transpose(1, 0, 2, 3)
    d_in = lax.psum_scatter(d_in_part, "seq", scatter_dimension=0).astype(F32)
    x_own = tokens[:, 0].astype(F32)
    grad_tokens = d_residual.reshape(n_micro, n_tok, model) + rms_back(
        d_in * norm1_gain, x_own, rms_scale(x_own)
    )

    g_ext = matmul("mtd,mtc->dc", normed_in, d_ext)
    g_in = g_ext[:, : slots * head_dim].reshape(n_seq, n_row, cut, slots * head_dim)
    g_in = row_scatter([lax.dynamic_index_in_dim(g_in, row ^ j, 1, False) for j in range(n_row)])
    g_in = from_heads(g_in.astype(BF)).reshape(n_heads, cut, slots, head_dim)
    g_in = g_in.transpose(1, 2, 0, 3).reshape(cut, -1)
    grad_in = lax.all_gather(g_in, "row", axis=0, tiled=True).astype(F32)

    g_out = matmul("tc,td->cd", gated_out, d_res_low).reshape(model, n_row, -1)
    g_out = row_scatter([lax.dynamic_index_in_dim(g_out, row ^ j, 1, False) for j in range(n_row)])
    g_gu = matmul("td,tc->dc", mid_rows, d_gu_low, BF)
    g_down = matmul("tf,td->fd", act_low, d_top_rows, BF)
    g_wide = jnp.concatenate([g_gu, g_out.astype(BF)], axis=1)
    g_wide = lax.psum_scatter(g_wide, "seq", scatter_dimension=0, tiled=True)
    g_down = lax.psum_scatter(g_down, "seq", scatter_dimension=0, tiled=True)
    g_wide = lax.all_gather(g_wide, "row", axis=0)
    grad_down = lax.all_gather(g_down, "row", axis=0, tiled=True).astype(F32)
    grad_gu = g_wide[:, :, : 2 * n_units].reshape(n_row, -1, 2, n_seq, unit_cut)
    grad_gu = grad_gu.transpose(1, 2, 3, 0, 4).reshape(-1, 2 * hidden).astype(F32)
    grad_out = g_wide[:, :, 2 * n_units :].transpose(1, 0, 2).reshape(-1, model).astype(F32)

    g_norm2 = jnp.sum(d_mid * residual * scale_mid, axis=0)
    shared = jnp.concatenate([g_norm1, g_norm2, g_head[0]])
    by_head = jnp.concatenate(
        [
            g_taps[:n_taps].reshape(-1),
            g_ext[:, slots * head_dim : slots * head_dim + n_rt].T.reshape(-1),
            g_par[1, 2:3],
            g_par[2, 2:3],
        ]
    )
    size = shared.shape[0] + by_head.shape[0]
    packed = jnp.pad(jnp.concatenate([shared, by_head]), (0, -size % 1024)).reshape(-1, 1024)
    packed = lax.all_gather(row_sum(packed), "seq", axis=0).reshape(n_seq, -1)
    total = jnp.sum(packed[:, : shared.shape[0]], axis=0)
    heads = packed[::copies, shared.shape[0] : size]
    n_conv = n_taps * width
    conv_sum = heads[:, :n_conv].reshape(n_heads, n_taps, gate_at, head_dim)
    conv_sum = conv_sum.transpose(1, 2, 0, 3).reshape(n_taps, conv_width)
    router_sum = heads[:, n_conv : n_conv + n_rt * model].reshape(n_heads, n_rt, model)
    router_sum = router_sum.transpose(2, 1, 0).reshape(model, n_rt * n_heads)
    return (
        out,
        grad_tokens[:, None],
        total[:model],
        grad_in,
        router_sum,
        conv_sum,
        heads[:, -2],
        heads[:, -1],
        total[2 * model :],
        grad_out,
        total[model : 2 * model],
        grad_gu,
        grad_down,
    )


def solution(mesh):
    by_rows = P("seq", None)
    by_tokens = P(None, "row", "seq", None)
    return jax.shard_map(
        local,
        mesh=mesh,
        in_specs=(
            by_tokens, by_tokens, P(None, "row"), P(), by_rows, P(), P(), P(), P(), P(),
            by_rows, P(), by_rows, by_rows,
        ),
        out_specs=(
            by_tokens, by_tokens, P(), by_rows, P(), P(), P(), P(), P(),
            by_rows, P(), by_rows, by_rows,
        ),
        check_vma=False,
    )
```

time: 2070 us -> 659 us (0.32)
  waiting for transfers between devices: 1010 us -> 266 us
  other arithmetic: 411 us -> 45.3 us
  matrix products: 371 us -> 63.3 us
  local copies, waits for them, and re-layouts: 198 us -> 67.1 us
  Pallas kernels: 0 us -> 92.5 us
  blocking collectives: 39.8 us -> 81.6 us
    all_gather x12 -> x6, waiting for transfers between devices: 506 us -> 103 us  [the longest x1 35.6 us: local(): tokens_all = lax.all_gather(tokens[:, 0], 'seq', axis=0)]
    another operation x10, other arithmetic: 325 us -> 6.24 us  [the longest x4 3.32 us: row_scatter(): jnp.stack([parts[j].astype(BF) for j in away])]
    dot_general x130 -> x13, matrix products: 353 us -> 63.3 us  [matmul(): jnp.einsum(spec, left, right, preferred_element_type=F32).astype(kind)]
    reduce_scatter x4 -> x3, waiting for transfers between devices: 356 us -> 70.1 us  [the longest x1 70.1 us: local(): d_in = lax.psum_scatter(d_in_part, 'seq', scatter_dimension=0).astype(F32)]
    psum x2 -> x0, waiting for transfers between devices: 143 us -> none  [the longest x1 122 us: local(): lax.psum(small_total, ('row', 'seq'))]
    pallas_call x0 -> x4, Pallas kernels: none -> 92.5 us  [the longest x1 43.9 us: mixer_grads(): pl.pallas_call(partial(grads_kernel, count), grid=(n_micro, blocks), in_s...]
    while x108 -> x0, local copies, waits for them, and re-layouts: 46.1 us -> none
    ppermute x4 -> x16, waiting for transfers between devices: 5.03 us -> 50.2 us  [exchange(): return lax.ppermute(value, 'row', [(i, i ^ bit) for i in range(count)])]
  transfers between devices with their start and end apart: 22 -> 27, of which waited for: 14 -> 17; matrix products, arithmetic and copies ran while one was open for 36% -> 19% of each run, Pallas kernels for 0% -> 14%
where the time goes in v1:
time: 659 us; the launch traced here: 650 us
  waiting for transfers between devices  266 us (40%)
  Pallas kernels  92.5 us (14%)
  blocking collectives  81.6 us (12%)
  local copies, waits for them, and re-layouts  67.1 us (10%)
  matrix products  63.3 us (10%)
  other arithmetic  45.3 us (7%)
  starting transfers between devices  19.7 us (3%)
  between operations  15 us (2%)
    reduce_scatter x1, waiting for transfers between devices, local(): d_in = lax.psum_scatter(d_in_part, 'seq', scatter_dimension=0).astype(F32)  70.1 us
    dot_general x13, matrix products, matmul(): jnp.einsum(spec, left, right, preferred_element_type=F32).astype(kind)  63.3 us
    ppermute x16, waiting for transfers between devices, exchange(): return lax.ppermute(value, 'row', [(i, i ^ bit) for i in range(count)])  50.2 us
    pallas_call x1, Pallas kernels, mixer_grads(): pl.pallas_call(partial(grads_kernel, count), grid=(n_micro, blocks), in_s...  43.9 us
    all_gather x1, waiting for transfers between devices, local(): tokens_all = lax.all_gather(tokens[:, 0], 'seq', axis=0)  35.6 us
    all_gather x1, waiting for transfers between devices, local(): down = lax.all_gather(down_piece, 'seq', axis=0, tiled=True)  35.4 us
    all_gather x1, blocking collectives, local(): packed = lax.all_gather(row_sum(packed), 'seq', axis=0).reshape(n_seq, -1)  30.7 us
    all_to_all x1, blocking collectives, to_heads(): lax.all_to_all(jnp.repeat(value, copies, axis=0), 'seq', 0, 0, tiled=True)  27.5 us
  transfers between devices with their start and end apart: 27, of which 17 were waited for; matrix products, arithmetic and copies ran while one was open for 19% of the time, Pallas kernels for 14%

profile of v1, /device:TPU:0, one launch (start us, length us, event | category | flops | bytes accessed | tf_op | source)
XLA Modules:
  0.0 650.5 jit_solution(6015985173461270010)
XLA Ops:
  11.1 27.5 %all_to_all.20 = bf16[8,32,768]{2,1,0:T(8,128)(2,1)S(1)} all-to-all(bf16[8,32,768]{2,1,0:T(8,128)(2,1)S(1)} %reshape_broadcast_in_dim_reshape.3), channel_id=1, replica_groups=mesh['row'=4,'seq'=8] {'seq'}, dimensions={0} | all-to-all | bytes 786432 | tf_op jit(solution)/shard_map/all_to_all | solution.py:597
  40.2 6.2 collective-permute-done
  55.7 35.6 %all-gather.18.cloned.1.call-done = bf16[16,1,128,1024]{3,2,1,0:T(8,128)(2,1)} async-done(((bf16[2,1,128,1024]{3,2,1,0:T(8,128)(2,1)}), bf16[16,1,128,1024]{3,2,1,0:T(8,128)(2,1)}) %all-gather.18.cloned.1.call-update) | async-done | bytes 4194320 | tf_op jit(solution)/shard_map/all_gather | solution.py:603
  91.2 6.6 %bitcast_convert_fusion = f32[8,2,128,1024]{3,2,1,0:T(8,128)} fusion(bf16[8,2,128,1024]{3,2,1,0:T(8,128)(2,1)} %bitcast.318), kind=kLoop, calls=%fused_computation.11 | loop fusion | flops 2097152 | bytes 12582912 | tf_op jit(solution)/shard_map/convert_element_type | solution.py:648
  97.8 4.6 copy.103
  108.3 4.8 convolution_convert_fusion.1.proj_ref.halo_ref.gate_ref
  113.1 22.3 %mixer_prepare.1 = (f32[2,16,128,128]{3,2,1,0:T(8,128)}, f32[2,16,128,128]{3,2,1,0:T(8,128)}, f32[2,16,128,128]{3,2,1,0:T(8,128)}, f32[2,16,64,128]{3,2,1,0:T(8,...) custom-call(bf16[2,1024,768]{2,1,0:T(8,128)(2,1)} %convolution_convert_fusion.1.proj_ref.halo_ref.gate, ...), custom_call_target="tpu_custom_call" | custom-call | flops 5905580032 | bytes 13107200 | tf_op jit(solution)/shard_map/mixer_prepare/pallas_call | solution.py:396
  136.4 13.0 %mixer_scan.1 = (bf16[2,1024,128]{2,1,0:T(8,128)(2,1)S(1)}, f32[2,16,64,128]{3,2,1,0:T(8,128)S(1)}, f32[2,16,128,128]{3,2,1,0:T(8,128)}, f32[2,16,128,128]{3,2,1,0:T(8,128)}) custom-call(f32[2,16,128,128]{3,2,1,0:T(8,128)} %get-tuple-element.31.wmat_ref, f32[2,16,128,128]{3,2,1,0:T(8,128)} %get-tuple-element.32.umat_ref, ...), custom_call_target="tpu_custom_call" | custom-call | flops 1610612736 | bytes 13762560 | tf_op jit(solution)/shard_map/mixer_scan/pallas_call | solution.py:425
  150.3 4.1 all-to-all-start.1
  158.9 17.6 %all-to-all-done.1 = bf16[8,2,128,128]{3,2,1,0:T(8,128)(2,1)} async-done(((bf16[8,2,128,128]{3,2,1,0:T(8,128)(2,1)}), bf16[8,2,128,128]{3,2,1,0:T(8,128)(2,1)}, u32[]{:S(2)}, u32[]{:S(2)}) %all-to-all-start.1) | async-done | bytes 524320 | tf_op jit(solution)/shard_map/all_to_all | solution.py:600
  183.8 6.3 collective-permute-done.2
  194.7 14.4 %all-gather.12.cloned.1.call-done = bf16[1024,1408]{0,1:T(8,128)(2,1)} async-done(((bf16[128,1408]{0,1:T(8,128)(2,1)}), bf16[1024,1408]{0,1:T(8,128)(2,1)}) %all-gather.12.cloned.1.call-update) | async-done | bytes 2883600 | tf_op jit(solution)/shard_map/all_gather | solution.py:636
  209.1 8.5 %fusion.44 = f32[1024,1408]{1,0:T(8,128)} fusion(bf16[1024,1408]{0,1:T(8,128)(2,1)} %all-gather.12.cloned.1.call-done, bf16[256,1024]{1,0:T(8,128)(2,1)} %get-tuple-element.133, bf16[256,1024]{1,0:T(8,128)(2,1)} %bitcast.361, bf16[256,1024]{1,0:T(8,128)(2,1)} %get-tuple-element.132, bf16[256,1024]{1,0:T(8,128)(2,1)} %multiply_convert_fusion.3), kind=kOutput, calls=%fused_computation.115 | convolution fusion | flops 2961178624 | bytes 10747904 | tf_op jit(solution)/shard_map/td,dc->tc/dot_general | solution.py:564
  217.5 35.4 %all-gather.14.cloned.1.call-done = bf16[704,1024]{1,0:T(8,128)(2,1)} async-done(((bf16[88,1024]{1,0:T(8,128)(2,1)}), bf16[704,1024]{1,0:T(8,128)(2,1)}) %all-gather.14.cloned.1.call-update) | async-done | bytes 1441808 | tf_op jit(solution)/shard_map/all_gather | solution.py:637
  253.0 6.9 %multiply_convert_fusion.1 = (bf16[1024,704]{1,0:T(8,128)(2,1)S(1)}, bf16[1024,704]{1,0:T(8,128)(2,1)S(1)}, bf16[1024,704]{1,0:T(8,128)(2,1)S(1)}) fusion(f32[1024,1408]{1,0:T(8,128)} %fusion.44, bf16[704,1024]{1,0:T(8,128)(2,1)} %all-gather.14.cloned.1.call-done, bf16[256,1024]{1,0:T(8,128)(2,1)} %bitcast.359, bf16[256,1024]{1,0:T(8,128)(2,1)} %bitcast.42, ...), kind=kOutput, calls=%fused_computation.16 | convolution fusion | flops 1496317952 | bytes 13631488 | tf_op jit(solution)/shard_map/td,fd->tf/dot_general | solution.py:564
  265.8 3.8 fusion.62
  279.4 8.8 %collective-permute-done.9 = bf16[1,256,1024]{2,1,0:T(8,128)(2,1)S(1)} collective-permute-done((bf16[1,256,1024]{2,1,0:T(8,128)(2,1)}, bf16[1,256,1024]{2,1,0:T(8,128)(2,1)S(1)}, u32[]{:S(2)}, u32[]{:S(2)}) %collective-permute-start.9) | collective-permute-done | bytes 524320 | tf_op jit(solution)/shard_map/ppermute | solution.py:519
  289.9 9.2 %collective-permute-done.5 = bf16[1,256,1024]{2,1,0:T(8,128)(2,1)S(1)} collective-permute-done((bf16[1,256,1024]{2,1,0:T(8,128)(2,1)S(1)}, bf16[1,256,1024]{2,1,0:T(8,128)(2,1)S(1)}, u32[]{:S(2)}, u32[]{:S(2)}) %collective-permute-start.5) | collective-permute-done | bytes 524320 | tf_op jit(solution)/shard_map/ppermute | solution.py:519
  323.6 6.7 %convolution_convert_fusion = bf16[1024,1408]{1,0:T(8,128)(2,1)} fusion(bf16[1024,704]{1,0:T(8,128)(2,1)} %copy-done.46, bf16[1024,704]{1,0:T(8,128)(2,1)S(1)} %copy-done.45, bf16[256,1024]{1,0:T(8,128)(2,1)S(1)} %copy-done.33, bf16[256,1024]{1,0:T(8,128)(2,1)S(1)} %bitcast.362, bf16[256,1024]{1,0:T(8,128)(2,1)S(1)} %copy-done.32, ...), kind=kOutput, calls=%fused_computation.13 | convolution fusion | flops 2968387584 | bytes 7864320 | tf_op jit(solution)/shard_map/td,tc->dc/dot_general | solution.py:564
  332.9 3.7 collective-permute-done.15
  347.5 4.8 convolution_convert_fusion.2
  352.3 22.6 %all-to-all-done.2 = bf16[8,2,128,128]{3,2,1,0:T(8,128)(2,1)S(1)} async-done(((bf16[8,2,128,128]{3,2,1,0:T(8,128)(2,1)}), bf16[8,2,128,128]{3,2,1,0:T(8,128)(2,1)S(1)}, u32[]{:S(2)}, u32[]{:S(2)}) %all-to-all-start.2) | async-done | bytes 524320 | tf_op jit(solution)/shard_map/all_to_all | solution.py:597
  375.0 13.2 %mixer_scan_back.1 = (f32[2,16,64,128]{3,2,1,0:T(8,128)S(1)}, f32[2,16,128,128]{3,2,1,0:T(8,128)}, f32[2,16,128,128]{3,2,1,0:T(8,128)}, bf16[2,1024,128]{2,1,0:T(8,128)(2,1)S(1)}, f32[8,128]{1,0:T(8,128)S(1)}) custom-call(f32[2,16,128,128]{3,2,1,0:T(8,128)} %get-tuple-element.31.wmat_ref, f32[2,16,64,128]{3,2,1,0:T(8,128)S(1)} %get-tuple-element.33.seen_ref, ...), custom_call_target="tpu_custom_call" | custom-call | flops 1610612736 | bytes 13762560 | tf_op jit(solution)/shard_map/mixer_scan_back/pallas_call | solution.py:457
  388.2 43.9 %mixer_grads.1 = (bf16[2,1024,896]{2,1,0:T(8,128)(2,1)}, f32[8,640]{1,0:T(8,128)S(1)}, f32[8,128]{1,0:T(8,128)S(1)}) custom-call(bf16[2,1024,768]{2,1,0:T(8,128)(2,1)} %convolution_convert_fusion.1.proj_ref.halo_ref.gate_ref, bf16[2,1024,768]{2,1,0:T(8,128)(2,1)} %convolution_convert_fusion.1.proj_ref.halo_ref.gate_ref, f32[2,1024,128]{2,1,0:T(8,128)S(1)} %copy-done.3, ...), custom_call_target="tpu_custom_call" | custom-call | flops 4294967296 | bytes 19660800 | tf_op jit(solution)/shard_map/mixer_grads/pallas_call | solution.py:495
  432.1 6.6 %convolution_bitcast_fusion = f32[1024,896]{1,0:T(8,128)S(1)} fusion(bf16[2,1024,1024]{2,1,0:T(8,128)(2,1)S(1)} %copy-done.9, bf16[2,1024,896]{2,1,0:T(8,128)(2,1)} %get-tuple-element.45), kind=kOutput, calls=%fused_computation.24 | convolution fusion | flops 3758096384 | bytes 11534336 | tf_op jit(solution)/shard_map/mtd,mtc->dc/dot_general | solution.py:564
  444.8 9.7 %collective-permute-done.13 = bf16[1,8,32,768]{3,2,1,0:T(8,128)(2,1)S(1)} collective-permute-done((bf16[1,8,32,768]{3,2,1,0:T(8,128)(2,1)S(1)}, bf16[1,8,32,768]{3,2,1,0:T(8,128)(2,1)S(1)}, u32[]{:S(2)}, u32[]{:S(2)}) %collective-permute-start.13) | collective-permute-done | bytes 393248 | tf_op jit(solution)/shard_map/ppermute | solution.py:519
  454.7 15.0 %all_to_all.21 = bf16[8,32,768]{2,1,0:T(8,128)(2,1)S(1)} all-to-all(bf16[8,32,768]{2,1,0:T(8,128)(2,1)S(1)} %fusion.38), channel_id=1, replica_groups=mesh['row'=4,'seq'=8] {'seq'}, dimensions={0} | all-to-all | bytes 786432 | tf_op jit(solution)/shard_map/all_to_all | solution.py:600
  471.6 9.7 %fusion.3 = (f32[1024]{0:T(1024)S(1)}, bf16[2,1024,1024]{2,1,0:T(8,128)(2,1)S(1)}) fusion(f32[8,2,128,1024]{3,2,0,1:T(8,128)} %copy-done.7, f32[2,1024]{1,0:T(2,128)S(1)} %bitcast.371, bf16[2,1024,896]{2,1,0:T(8,128)(2,1)} %get-tuple-element.45, bf16[1024,128]{1,0:T(8,128)(2,1)S(1)} %pad.12, bf16[1024,768]{1,0:T(8,128)(2,1)} %bitcast.351), kind=kOutput, calls=%fused_computation.5 | convolution fusion | flops 3770153984 | bytes 18100224 | tf_op jit(solution)/shard_map/mtc,dc->mtd/dot_general | solution.py:564
  493.1 30.7 %all-gather.1 = f32[64,1024]{1,0:T(8,128)S(1)} all-gather(f32[8,1024]{1,0:T(8,128)S(1)} %add.195), channel_id=3, replica_groups=mesh['row'=4,'seq'=8] {'seq'}, dimensions={0}, use_global_device_ids=true | all-gather | bytes 294912 | tf_op jit(solution)/shard_map/all_gather | solution.py:735
  527.0 8.4 %all_gather.39 = bf16[352,1024]{1,0:T(8,128)(2,1)S(1)} all-gather(bf16[88,1024]{1,0:T(8,128)(2,1)} %reduce-scatter.8.cloned.1.call-done), channel_id=1, replica_groups=mesh['row'=4,'seq'=8] {'row'}, dimensions={0}, use_global_device_ids=true | all-gather | bytes 901120 | tf_op jit(solution)/shard_map/all_gather | solution.py:718
  540.1 70.1 %reduce-scatter.4.cloned.1.call-done = bf16[1,2,128,1024]{3,2,1,0:T(8,128)(2,1)} async-done(((bf16[8,2,128,1024]{3,2,1,0:T(8,128)(2,1)}), bf16[1,2,128,1024]{3,2,1,0:T(8,128)(2,1)}) %reduce-scatter.4.cloned.1.call-update) | async-done | bytes 524304 | tf_op jit(solution)/shard_map/reduce_scatter | solution.py:697
  614.0 18.0 %all-gather.20.cloned.1.call-done = bf16[512,1664]{1,0:T(8,128)(2,1)} async-done(((bf16[128,1664]{1,0:T(8,128)(2,1)}), bf16[512,1664]{1,0:T(8,128)(2,1)}) %all-gather.20.cloned.1.call-update) | async-done | bytes 1703952 | tf_op jit(solution)/shard_map/all_gather | solution.py:717
  (264 shorter events, 136.7 us)
Async XLA Ops:
  7.2 151.0 %copy-start = (bf16[352,1024]{1,0:T(8,128)(2,1)S(1)}, bf16[352,1024]{1,0:T(8,128)(2,1)}, u32[]{:S(2)}) copy-start(bf16[352,1024]{1,0:T(8,128)(2,1)} %param.27) | copy-start | bytes 2162692
  7.2 84.0 %all-gather.18.cloned.1.call-start = ((), (), s32[]{:S(2)}) async-start(), calls=%async_computation.14 | async-start | bytes 4718592 | tf_op jit(solution)/shard_map/all_gather | solution.py:603
  7.9 170.0 %all-gather.10.cloned.1.call-start = ((), (), s32[]{:S(2)}) async-start(), calls=%async_computation.7 | async-start | bytes 2359296 | tf_op jit(solution)/shard_map/all_gather | solution.py:635
  8.7 200.4 %all-gather.12.cloned.1.call-start = ((), (), s32[]{:S(2)}) async-start(), calls=%async_computation.8 | async-start | bytes 3244032 | tf_op jit(solution)/shard_map/all_gather | solution.py:636
  38.6 7.8 %collective-permute-start = (bf16[1,8,32,768]{3,2,1,0:T(8,128)(2,1)S(1)}, bf16[1,8,32,768]{3,2,1,0:T(8,128)(2,1)S(1)}, u32[]{:S(2)}, u32[]{:S(2)}) collective-permute-start(bf16[1,8,32,768]{3,2,1,0:T(8,128)(2,1)S(1)} %bitcast.331), channel_id=1, source_target_pairs={{0,16},{8,24},{16,0},{24,8},{1,17},{9,25},{17,1},{25,9},{2,18},{10... | collective-permute-start | bytes 1179656 | tf_op jit(solution)/shard_map/ppermute | solution.py:519
  47.4 6.6 %collective-permute-start.1 = (bf16[2,8,32,768]{3,2,1,0:T(8,128)(2,1)}, bf16[2,8,32,768]{3,2,1,0:T(8,128)(2,1)}, u32[]{:S(2)}, u32[]{:S(2)}) collective-permute-start(bf16[2,8,32,768]{3,2,1,0:T(8,128)(2,1)} %pad_maximum_fusion.13), channel_id=1, source_target_pairs={{0,8},{8,0},{16,24},{24,16},{1,9},{9,1},{17,25},{25,17},{2,10},{10... | collective-permute-start | bytes 2359304 | tf_op jit(solution)/shard_map/ppermute | solution.py:519
  51.1 54.8 %copy-start.21 = (bf16[1024,3,1]{1,0,2:T(8,128)(2,1)}, bf16[1024,3,1]{1,0,2:T(8,128)(2,1)S(1)}, u32[]{:S(2)}) copy-start(bf16[1024,3,1]{1,0,2:T(8,128)(2,1)S(1)} %copy.135) | copy-start | bytes 18436
  150.3 26.2 %all-to-all-start.1 = ((bf16[8,2,128,128]{3,2,1,0:T(8,128)(2,1)}), bf16[8,2,128,128]{3,2,1,0:T(8,128)(2,1)}, u32[]{:S(2)}, u32[]{:S(2)}) async-start(bf16[8,2,128,128]{3,2,1,0:T(8,128)(2,1)} %bitcast.341), calls=%async_computation.1 | async-start | bytes 1048576 | tf_op jit(solution)/shard_map/all_to_all | solution.py:600
  154.5 98.5 %all-gather.14.cloned.1.call-start = ((), (), s32[]{:S(2)}) async-start(), calls=%async_computation.9 | async-start | bytes 1622016 | tf_op jit(solution)/shard_map/all_gather | solution.py:637
  156.6 25.7 %collective-permute-start.6 = (bf16[1,2,128,1024]{3,2,1,0:T(8,128)(2,1)}, bf16[1,2,128,1024]{3,2,1,0:T(8,128)(2,1)}, u32[]{:S(2)}, u32[]{:S(2)}) collective-permute-start(bf16[1,2,128,1024]{3,2,1,0:T(8,128)(2,1)} %fusion.33), channel_id=1, source_target_pairs={{0,16},{8,24},{16,0},{24,8},{1,17},{9,25},{17,1},{25,9},{2,18},{10... | collective-permute-start | bytes 1572872 | tf_op jit(solution)/shard_map/ppermute | solution.py:519
  158.9 325.0 %reduce-scatter.6.cloned.1.call-start = ((), (), s32[]{:S(2)}) async-start(), calls=%async_computation.12 | async-start | bytes 3833856 | tf_op jit(solution)/shard_map/reduce_scatter | solution.py:715
  180.8 9.2 %collective-permute-start.2 = (bf16[1,256,1024]{2,1,0:T(8,128)(2,1)S(1)}, bf16[1,256,1024]{2,1,0:T(8,128)(2,1)S(1)}, u32[]{:S(2)}, u32[]{:S(2)}) collective-permute-start(bf16[1,256,1024]{2,1,0:T(8,128)(2,1)S(1)} %fusion.81), channel_id=1, source_target_pairs={{0,16},{8,24},{16,0},{24,8},{1,17},{9,25},{17,1},{25,9},{2,18},{10... | collective-permute-start | bytes 1572872 | tf_op jit(solution)/shard_map/ppermute | solution.py:519
  183.7 7.6 %collective-permute-start.7 = (bf16[2,2,128,1024]{3,2,1,0:T(8,128)(2,1)S(1)}, bf16[2,2,128,1024]{3,2,1,0:T(8,128)(2,1)S(1)}, u32[]{:S(2)}, u32[]{:S(2)}) collective-permute-start(bf16[2,2,128,1024]{3,2,1,0:T(8,128)(2,1)S(1)} %pad_maximum_fusion.10), channel_id=1, source_target_pairs={{0,8},{8,0},{16,24},{24,16},{1,9},{9,1},{17,25},{25,17},{2,10},{10... | collective-permute-start | bytes 3145736 | tf_op jit(solution)/shard_map/ppermute | solution.py:519
  190.9 2.7 collective-permute-start.3
  191.3 61.7 %copy-start.27 = (bf16[256,1024]{1,0:T(8,128)(2,1)}, bf16[256,1024]{1,0:T(8,128)(2,1)S(1)}, u32[]{:S(2)}) copy-start(bf16[256,1024]{1,0:T(8,128)(2,1)S(1)} %fusion.34) | copy-start | bytes 1572868
  192.2 60.7 %copy-start.28 = (bf16[1,2,128,1024]{3,2,1,0:T(8,128)(2,1)}, bf16[1,2,128,1024]{3,2,1,0:T(8,128)(2,1)S(1)}, u32[]{:S(2)}) copy-start(bf16[1,2,128,1024]{3,2,1,0:T(8,128)(2,1)S(1)} %get-tuple-element.130) | copy-start | bytes 1572868
  263.6 7.2 %collective-permute-start.8 = (bf16[2,256,1024]{2,1,0:T(8,128)(2,1)S(1)}, bf16[2,256,1024]{2,1,0:T(8,128)(2,1)S(1)}, u32[]{:S(2)}, u32[]{:S(2)}) collective-permute-start(bf16[2,256,1024]{2,1,0:T(8,128)(2,1)S(1)} %pad_maximum_fusion.11), channel_id=1, source_target_pairs={{0,8},{8,0},{16,24},{24,16},{1,9},{9,1},{17,25},{25,17},{2,10},{10... | collective-permute-start | bytes 3145736 | tf_op jit(solution)/shard_map/ppermute | solution.py:519
  270.8 5.0 collective-permute-start.4
  273.3 14.9 %collective-permute-start.9 = (bf16[1,256,1024]{2,1,0:T(8,128)(2,1)}, bf16[1,256,1024]{2,1,0:T(8,128)(2,1)S(1)}, u32[]{:S(2)}, u32[]{:S(2)}) collective-permute-start(bf16[1,256,1024]{2,1,0:T(8,128)(2,1)} %fusion.24), channel_id=1, source_target_pairs={{0,16},{8,24},{16,0},{24,8},{1,17},{9,25},{17,1},{25,9},{2,18},{10... | collective-permute-start | bytes 1572872 | tf_op jit(solution)/shard_map/ppermute | solution.py:519
  278.8 20.3 %collective-permute-start.5 = (bf16[1,256,1024]{2,1,0:T(8,128)(2,1)S(1)}, bf16[1,256,1024]{2,1,0:T(8,128)(2,1)S(1)}, u32[]{:S(2)}, u32[]{:S(2)}) collective-permute-start(bf16[1,256,1024]{2,1,0:T(8,128)(2,1)S(1)} %fusion.27), channel_id=1, source_target_pairs={{0,16},{8,24},{16,0},{24,8},{1,17},{9,25},{17,1},{25,9},{2,18},{10... | collective-permute-start | bytes 1572872 | tf_op jit(solution)/shard_map/ppermute | solution.py:519
  313.3 5.7 collective-permute-start.14
  322.1 14.5 %collective-permute-start.15 = (bf16[1,1024,256]{2,1,0:T(8,128)(2,1)S(1)}, bf16[1,1024,256]{2,1,0:T(8,128)(2,1)}, u32[]{:S(2)}, u32[]{:S(2)}) collective-permute-start(bf16[1,1024,256]{2,1,0:T(8,128)(2,1)S(1)} %fusion.20), channel_id=1, source_target_pairs={{0,16},{8,24},{16,0},{24,8},{1,17},{9,25},{17,1},{25,9},{2,18},{10... | collective-permute-start | bytes 1572872 | tf_op jit(solution)/shard_map/ppermute | solution.py:519
  343.9 31.0 %all-to-all-start.2 = ((bf16[8,2,128,128]{3,2,1,0:T(8,128)(2,1)}), bf16[8,2,128,128]{3,2,1,0:T(8,128)(2,1)S(1)}, u32[]{:S(2)}, u32[]{:S(2)}) async-start(bf16[8,2,128,128]{3,2,1,0:T(8,128)(2,1)} %bitcast.343), calls=%async_computation.2 | async-start | bytes 1048576 | tf_op jit(solution)/shard_map/all_to_all | solution.py:597
  347.4 179.6 %reduce-scatter.8.cloned.1.call-start = ((), (), s32[]{:S(2)}) async-start(), calls=%async_computation.13 | async-start | bytes 1622016 | tf_op jit(solution)/shard_map/reduce_scatter | solution.py:716
  352.3 184.4 %all-gather.16.cloned.1.call-start = ((), (), s32[]{:S(2)}) async-start(), calls=%async_computation.11 | async-start | bytes 1966080 | tf_op jit(solution)/shard_map/all_gather | solution.py:708
  440.6 2.4 collective-permute-start.12
  443.3 11.2 %collective-permute-start.13 = (bf16[1,8,32,768]{3,2,1,0:T(8,128)(2,1)S(1)}, bf16[1,8,32,768]{3,2,1,0:T(8,128)(2,1)S(1)}, u32[]{:S(2)}, u32[]{:S(2)}) collective-permute-start(bf16[1,8,32,768]{3,2,1,0:T(8,128)(2,1)S(1)} %fusion.35), channel_id=1, source_target_pairs={{0,16},{8,24},{16,0},{24,8},{1,17},{9,25},{17,1},{25,9},{2,18},{10... | collective-permute-start | bytes 1179656 | tf_op jit(solution)/shard_map/ppermute | solution.py:519
  471.5 138.8 %reduce-scatter.4.cloned.1.call-start = ((), (), s32[]{:S(2)}) async-start(), calls=%async_computation.10 | async-start | bytes 4718592 | tf_op jit(solution)/shard_map/reduce_scatter | solution.py:697
  483.8 148.2 %all-gather.20.cloned.1.call-start = ((), (), s32[]{:S(2)}) async-start(), calls=%async_computation.15 | async-start | bytes 2129920 | tf_op jit(solution)/shard_map/all_gather | solution.py:717
  487.9 1.3 collective-permute-start.10
  489.1 3.9 collective-permute-start.11
  536.7 73.6 %copy-start.17 = (bf16[2,1,128,1024]{3,2,1,0:T(8,128)(2,1)S(1)}, bf16[2,1,128,1024]{3,2,1,0:T(8,128)(2,1)}, u32[]{:S(2)}) copy-start(bf16[2,1,128,1024]{3,2,1,0:T(8,128)(2,1)} %param.14) | copy-start | bytes 1572868
  (42 other events, 405.9 us)
Sparse Core Ops, SparseCore 0:
  10.2 81.0 all-gather.17
  93.4 47.6 all-gather.9
  143.1 65.9 all-gather.11
  211.7 41.2 all-gather.13
  340.7 86.7 reduce-scatter.5
  431.7 65.7 reduce-scatter.7
  499.7 18.4 all-gather.15
  522.3 87.9 reduce-scatter.3
  611.8 20.1 all-gather.19

commit v2 on v1

--- a/solution.py
+++ b/solution.py
@@ -376,33 +376,57 @@
     return pltpu.CompilerParams(dimension_semantics=semantics, vmem_limit_bytes=VMEM_BYTES)
 
 
-def cost(chunks, dots, size):
+def cost(chunks, per_chunk):
     return pl.CostEstimate(
-        flops=chunks * dots * 2 * 128**3, transcendentals=chunks * 128 * 1024, bytes_accessed=size
+        flops=int(chunks * per_chunk * 1.1e9), transcendentals=0, bytes_accessed=1 << 20
     )
+
+
+def launch(kernel, in_specs, earlier, **options):
+    n_in = len(in_specs)
+
+    def body(*refs):
+        kernel(*refs[:n_in], *refs[n_in + len(earlier) :])
+
+    specs = list(in_specs) + [pl.BlockSpec(memory_space=pl.ANY)] * len(earlier)
+    called = pl.pallas_call(body, in_specs=specs, **options)
+    return lambda *operands: called(*operands, *earlier)
+
+
+def fence(value, *earlier):
+    anywhere = pl.BlockSpec(memory_space=pl.ANY)
+    return pl.pallas_call(
+        lambda *refs: None,
+        in_specs=[anywhere] * (1 + len(earlier)),
+        out_specs=anywhere,
+        out_shape=jax.ShapeDtypeStruct(value.shape, value.dtype),
+        input_output_aliases={0: 0},
+        name="fence",
+    )(value, *earlier)
 
 
 def whole(shape):
     return pl.BlockSpec(shape, lambda *_: (0,) * len(shape))
 
 
-def prepare(projected, router, taps, par, width, count=8):
+def prepare(projected, router, taps, par, width, earlier=(), count=8):
     n_micro, length, full = projected.shape
     steps = length // (count * CH)
     chunks = length // CH
     size = count * CH
     per = lambda *tail: pl.BlockSpec((1, count) + tail, lambda m, i: (m, i, 0, 0))
     made = lambda kind, *tail: jax.ShapeDtypeStruct((n_micro, chunks) + tail, kind)
-    return pl.pallas_call(
+    return launch(
         partial(prep_kernel, count),
-        grid=(n_micro, steps),
-        in_specs=[
+        [
             pl.BlockSpec((1, size, full), lambda m, i: (m, i, 0)),
             pl.BlockSpec((1, HALO, full), lambda m, i: (m, jnp.maximum(i * (size // HALO) - 1, 0), 0)),
             pl.BlockSpec((1, size, LANES), lambda m, i: (m, i, 0)),
             whole(taps.shape),
             whole(par.shape),
         ],
+        earlier,
+        grid=(n_micro, steps),
         out_specs=[per(ST, ST), per(ST, 128), per(ST, 128), per(CH, ST), per(CH, 128), per(ST, 128)],
         out_shape=[
             made(F32, ST, ST), made(F32, ST, 128), made(F32, ST, 128), made(F32, CH, ST),
@@ -410,27 +434,28 @@
         ],
         scratch_shapes=[pltpu.VMEM((size + 8, width), F32)],
         compiler_params=params("arbitrary", "arbitrary"),
-        cost_estimate=cost(n_micro * chunks, 44, n_micro * chunks * 400 * 1024),
+        cost_estimate=cost(n_micro * chunks, 0.75),
         name="mixer_prepare",
     )(projected, projected, router, taps, par)
 
 
-def scan_states(prep, router, projected, par, gate_at, count=4):
+def scan_states(prep, router, projected, par, gate_at, earlier=(), count=4):
     _, wmat, umat, seen, q, k = prep
     n_micro, chunks = wmat.shape[:2]
     length = chunks * CH
     size = count * CH
     per = lambda *tail: pl.BlockSpec((n_micro, count) + tail, lambda i: (0, i, 0, 0))
     made = lambda kind, *tail: jax.ShapeDtypeStruct((n_micro, chunks) + tail, kind)
-    return pl.pallas_call(
+    return launch(
         partial(scan_kernel, n_micro, count),
-        grid=(chunks // count,),
-        in_specs=[
+        [
             per(ST, 128), per(ST, 128), per(CH, ST), per(CH, 128), per(ST, 128),
             pl.BlockSpec((n_micro, size, LANES), lambda i: (0, i, 0)),
             pl.BlockSpec((n_micro, size, 128), lambda i: (0, i, gate_at)),
             whole(par.shape),
         ],
+        earlier,
+        grid=(chunks // count,),
         out_specs=[
             pl.BlockSpec((n_micro, size, 128), lambda i: (0, i, 0)),
             per(CH, 128), per(ST, 128), per(128, 128),
@@ -441,12 +466,12 @@
         ],
         scratch_shapes=[pltpu.VMEM((n_micro, 128, 128), F32)],
         compiler_params=params("arbitrary"),
-        cost_estimate=cost(n_micro * chunks, 12, n_micro * chunks * 420 * 1024),
+        cost_estimate=cost(n_micro * chunks, 0.5),
         name="mixer_scan",
     )(wmat, umat, seen, q, k, router, projected, par)
 
 
-def scan_back(prep, router, projected, par, gate_at, mixed, d_out, count=4):
+def scan_back(prep, router, projected, par, gate_at, mixed, d_out, earlier=(), count=4):
     _, wmat, _, seen, q, k = prep
     n_micro, chunks = wmat.shape[:2]
     length = chunks * CH
@@ -454,10 +479,9 @@
     blocks = chunks // count
     per = lambda *tail: pl.BlockSpec((n_micro, count) + tail, lambda i: (0, blocks - 1 - i, 0, 0))
     made = lambda kind, *tail: jax.ShapeDtypeStruct((n_micro, chunks) + tail, kind)
-    return pl.pallas_call(
+    return launch(
         partial(scan_back_kernel, n_micro, count),
-        grid=(blocks,),
-        in_specs=[
+        [
             per(ST, 128), per(CH, ST), per(CH, 128), per(ST, 128),
             pl.BlockSpec((n_micro, size, LANES), lambda i: (0, blocks - 1 - i, 0)),
             pl.BlockSpec((n_micro, size, 128), lambda i: (0, blocks - 1 - i, gate_at)),
@@ -465,6 +489,8 @@
             per(CH, 128),
             pl.BlockSpec((n_micro, size, 128), lambda i: (0, blocks - 1 - i, 0)),
         ],
+        earlier,
+        grid=(blocks,),
         out_specs=[
             per(CH, 128), per(ST, 128), per(128, 128),
             pl.BlockSpec((n_micro, size, 128), lambda i: (0, blocks - 1 - i, 0)),
@@ -477,12 +503,15 @@
         ],
         scratch_shapes=[pltpu.VMEM((n_micro, 128, 128), F32)],
         compiler_params=params("arbitrary"),
-        cost_estimate=cost(n_micro * chunks, 12, n_micro * chunks * 420 * 1024),
+        cost_estimate=cost(n_micro * chunks, 0.5),
         name="mixer_scan_back",
     )(wmat, seen, q, k, router, projected, par, mixed, d_out)
 
 
-def mixer_grads(prep, router, projected, taps, par, width, news, state, d_mixed, d_news, d_state, d_gate, count=4):
+def mixer_grads(
+    prep, router, projected, taps, par, width, news, state, d_mixed, d_news, d_state, d_gate,
+    earlier=(), count=4,
+):
     solve, _, _, seen, _, _ = prep
     n_micro, chunks = solve.shape[:2]
     length = chunks * CH
@@ -492,15 +521,16 @@
     per = lambda *tail: pl.BlockSpec((1, count) + tail, lambda m, i: (m, blocks - 1 - i, 0, 0))
     rows = lambda n: pl.BlockSpec((1, size, n), lambda m, i: (m, blocks - 1 - i, 0))
     before = lambda m, i: (m, jnp.maximum((blocks - 1 - i) * (size // HALO) - 1, 0), 0)
-    return pl.pallas_call(
+    return launch(
         partial(grads_kernel, count),
-        grid=(n_micro, blocks),
-        in_specs=[
+        [
             rows(full), pl.BlockSpec((1, HALO, full), before), rows(LANES),
             whole(taps.shape), whole(par.shape),
             per(ST, ST), per(CH, ST), per(ST, 128), per(128, 128),
             per(CH, 128), per(ST, 128), per(128, 128), rows(LANES),
         ],
+        earlier,
+        grid=(n_micro, blocks),
         out_specs=[rows(width + 2 * LANES), whole((8, width)), whole((8, LANES))],
         out_shape=[
             jax.ShapeDtypeStruct((n_micro, length, width + 2 * LANES), BF),
@@ -509,45 +539,431 @@
         ],
         scratch_shapes=[pltpu.VMEM((size + 8, width), F32), pltpu.VMEM((size + 8, width), F32)],
         compiler_params=params("arbitrary", "arbitrary"),
-        cost_estimate=cost(n_micro * chunks, 32, n_micro * chunks * 600 * 1024),
+        cost_estimate=cost(n_micro * chunks, 1.4),
         name="mixer_grads",
     )(projected, projected, router, taps, par, solve, seen, news, state, d_mixed, d_news, d_state, d_gate)
 
 
-def exchange(value, bit):
-    count = lax.axis_size("row")
-    return lax.ppermute(value, "row", [(i, i ^ bit) for i in range(count)])
-
-
-def row_bits():
-    count = lax.axis_size("row")
+def project_kernel(x_ref, gain_ref, weight_ref, router_weight_ref, normed_ref, out_ref, router_ref):
+    x = x_ref[0].astype(F32)
+    scale = lax.rsqrt(jnp.mean(x * x, axis=-1, keepdims=True) + EPS_NORM)
+    normed = (x * scale * gain_ref[...]).astype(BF)
+    normed_ref[0] = normed
+    out_ref[0] = dot(normed, weight_ref[...]).astype(BF)
+    router_ref[0] = dot(normed, router_weight_ref[...])
+
+
+def project(x, gain, weight, router_weight, earlier=(), size=256):
+    n_micro, length, model = x.shape
+    full = weight.shape[1]
+    rows = lambda n: pl.BlockSpec((1, size, n), lambda m, i: (m, i, 0))
+    return launch(
+        project_kernel,
+        [rows(model), whole((1, model)), whole(weight.shape), whole(router_weight.shape)],
+        earlier,
+        grid=(n_micro, length // size),
+        out_specs=[rows(model), rows(full), rows(LANES)],
+        out_shape=[
+            jax.ShapeDtypeStruct((n_micro, length, model), BF),
+            jax.ShapeDtypeStruct((n_micro, length, full), BF),
+            jax.ShapeDtypeStruct((n_micro, length, LANES), F32),
+        ],
+        compiler_params=params("arbitrary", "arbitrary"),
+        cost_estimate=cost(n_micro * length // CH, 0.35),
+        name="project",
+    )(x, gain[None], weight, router_weight)
+
+
+def ring_add_kernel(table, ahead_ref, behind_ref, up_ref, low_ref, up_out, low_out):
+    up_out[...] = (ahead_ref[...].astype(F32) + up_ref[0, 0].astype(F32)).astype(up_out.dtype)
+    low_out[...] = (behind_ref[...].astype(F32) + low_ref[0, 0].astype(F32)).astype(low_out.dtype)
+
+
+def ring_add(table, step, ahead, behind, parts, kind, earlier=()):
+    rows, model = ahead.shape
+    one = pl.BlockSpec((rows, model), lambda i, table: (0, 0))
+    part = lambda m: pl.BlockSpec((1, 1, rows, model), lambda i, table: (m, table[2 * step + m], 0, 0))
+    made = jax.ShapeDtypeStruct((rows, model), kind)
+    n_in = 5
+
+    def body(*refs):
+        ring_add_kernel(*refs[:n_in], *refs[n_in + len(earlier) :])
+
+    return pl.pallas_call(
+        body,
+        grid_spec=pltpu.PrefetchScalarGridSpec(
+            num_scalar_prefetch=1,
+            grid=(1,),
+            in_specs=[one, one, part(0), part(1)] + [pl.BlockSpec(memory_space=pl.ANY)] * len(earlier),
+            out_specs=[one, one],
+        ),
+        out_shape=[made, made],
+        compiler_params=params("arbitrary"),
+        cost_estimate=cost(1, 1.0),
+        name="ring_add",
+    )(table, ahead, behind, parts, parts, *earlier)
+
+
+def input_grads_kernel(normed_ref, d_ext_ref, w_ext_ref, gain_ref, out_ref, lines_ref):
+    total = dot(normed_ref[0], d_ext_ref[0], 0, 0)
+    for m in range(1, normed_ref.shape[0]):
+        total = total + dot(normed_ref[m], d_ext_ref[m], 0, 0)
+    full = out_ref.shape[1]
+    out_ref[...] = total[:, :full].astype(BF)
+    norm = jnp.sum(total * w_ext_ref[...].astype(F32), axis=1, keepdims=True)
+    lane = lax.broadcasted_iota(jnp.int32, (total.shape[0], LANES), 1)
+    tail = jnp.where(lane == 3, norm, total[:, full:])
+    lines = tail.T[:8]
+    row = lax.broadcasted_iota(jnp.int32, lines.shape, 0)
+    lines_ref[...] = jnp.where(row == 3, lines / gain_ref[...], lines)
+
+
+def input_grads(normed, d_ext, w_ext, gain, full, earlier=(), size=128):
+    n_micro, length, model = normed.shape
+    wide = d_ext.shape[2]
+    return launch(
+        input_grads_kernel,
+        [
+            pl.BlockSpec((n_micro, length, size), lambda i: (0, 0, i)),
+            whole(d_ext.shape),
+            pl.BlockSpec((size, wide), lambda i: (i, 0)),
+            pl.BlockSpec((1, size), lambda i: (0, i)),
+        ],
+        earlier,
+        grid=(model // size,),
+        out_specs=[
+            pl.BlockSpec((size, full), lambda i: (i, 0)),
+            pl.BlockSpec((8, size), lambda i: (0, i)),
+        ],
+        out_shape=[
+            jax.ShapeDtypeStruct((model, full), BF),
+            jax.ShapeDtypeStruct((8, model), F32),
+        ],
+        compiler_params=params("arbitrary"),
+        cost_estimate=cost(1, 7.0),
+        name="input_grads",
+    )(normed, d_ext, w_ext, gain[None])
+
+
+def place_heads_kernel(n_heads, slots, where, *refs):
+    parts, out_ref = refs[:-1], refs[-1]
+    for j, part in enumerate(parts):
+        at = where[0] ^ j
+        for slot in range(slots):
+            for h in range(n_heads):
+                to = (slot * n_heads + h) * LANES
+                value = part[h, :, slot * LANES : (slot + 1) * LANES]
+                out_ref[at, :, to : to + LANES] = value.astype(F32)
+
+
+def place_heads(where, parts, slots):
+    n_heads, cut, full = parts[0].shape
+    shape = (len(parts), cut, full * n_heads)
+    return pl.pallas_call(
+        partial(place_heads_kernel, n_heads, slots),
+        grid_spec=pltpu.PrefetchScalarGridSpec(
+            num_scalar_prefetch=1,
+            grid=(1,),
+            in_specs=[pl.BlockSpec(part.shape, lambda i, where: (0, 0, 0)) for part in parts],
+            out_specs=pl.BlockSpec(shape, lambda i, where: (0, 0, 0)),
+        ),
+        out_shape=jax.ShapeDtypeStruct(shape, F32),
+        compiler_params=params("arbitrary"),
+        cost_estimate=cost(1, 3.0),
+        name="place_heads",
+    )(where, *parts).reshape(-1, full * n_heads)
+
+
+def place_units_kernel(unit_cut, unit_pad, n_seq, where, *refs):
+    parts, out_ref = refs[:-1], refs[-1]
+    n_row = len(parts)
+    group = unit_cut * n_row
+    hidden = group * n_seq
+    for block in range(hidden // LANES):
+        low = (block * LANES // group) * unit_pad // LANES * LANES
+        high = ((block * LANES + LANES - 1) // group + 1) * unit_pad
+        high = min(n_seq * unit_pad, -(-high // LANES) * LANES)
+        col = lax.broadcasted_iota(jnp.int32, (high - low, LANES), 1) + block * LANES
+        row = lax.broadcasted_iota(jnp.int32, (high - low, LANES), 0) + low
+        inner = lax.rem(col, group)
+        owner = lax.div(inner, unit_cut)
+        unit = lax.div(col, group) * unit_pad + lax.rem(inner, unit_cut)
+        total = [0.0, 0.0]
+        for j, part in enumerate(parts):
+            chosen = jnp.where((unit == row) & (owner == (where[0] ^ j)), 1.0, 0.0).astype(BF)
+            for half in range(2):
+                total[half] = total[half] + dot(part[half, :, low:high], chosen)
+        for half in range(2):
+            to = half * hidden + block * LANES
+            out_ref[:, to : to + LANES] = total[half]
+
+
+def place_units(where, parts, unit_cut, unit_pad, n_seq):
+    rows = parts[0].shape[1]
+    shape = (rows, 2 * unit_cut * n_seq * len(parts))
+    return pl.pallas_call(
+        partial(place_units_kernel, unit_cut, unit_pad, n_seq),
+        grid_spec=pltpu.PrefetchScalarGridSpec(
+            num_scalar_prefetch=1,
+            grid=(1,),
+            in_specs=[pl.BlockSpec(part.shape, lambda i, where: (0, 0, 0)) for part in parts],
+            out_specs=pl.BlockSpec(shape, lambda i, where: (0, 0)),
+        ),
+        out_shape=jax.ShapeDtypeStruct(shape, F32),
+        compiler_params=params("arbitrary"),
+        cost_estimate=cost(1, 5.0),
+        name="place_units",
+    )(where, *parts)
+
+
+def place_rows_kernel(where, *refs):
+    parts, out_ref = refs[:-1], refs[-1]
+    for j, part in enumerate(parts):
+        out_ref[where[0] ^ j] = part[: out_ref.shape[1]].astype(F32)
+
+
+def place_rows(where, parts, keep):
+    width = parts[0].shape[1]
+    shape = (len(parts), keep, width)
+    return pl.pallas_call(
+        place_rows_kernel,
+        grid_spec=pltpu.PrefetchScalarGridSpec(
+            num_scalar_prefetch=1,
+            grid=(1,),
+            in_specs=[pl.BlockSpec(part.shape, lambda i, where: (0, 0)) for part in parts],
+            out_specs=pl.BlockSpec(shape, lambda i, where: (0, 0, 0)),
+        ),
+        out_shape=jax.ShapeDtypeStruct(shape, F32),
+        compiler_params=params("arbitrary"),
+        cost_estimate=cost(1, 2.0),
+        name="place_rows",
+    )(where, *parts).reshape(-1, width)
+
+
+def feed_kernel(n_seq, first, mid_ref, d_top_ref, w_ref, act_ref, d_gu_ref, d_mid_ref, down_ref):
+    n_units = act_ref.shape[1]
+    model = mid_ref.shape[1]
+    per = n_units // n_seq
+
+    @pl.when(pl.program_id(0) == 0)
+    def _():
+        lines = w_ref[:, 2 * n_units :].reshape(n_seq, model // n_seq, model)
+        down_ref[...] = lines[:, first : first + per].reshape(n_units, model)
+
+    w_gate = w_ref[:, :n_units]
+    w_up = w_ref[:, n_units : 2 * n_units]
+    mid = mid_ref[...]
+    gate = dot(mid, w_gate)
+    up = dot(mid, w_up)
+    d_act = dot(d_top_ref[...], down_ref[...], 1, 1)
+    sig = jax.nn.sigmoid(gate)
+    silu = gate * sig
+    act_ref[...] = (silu * up).astype(BF)
+    d_gate = (d_act * up * sig * (1.0 + gate * (1.0 - sig))).astype(BF)
+    d_up = (d_act * silu).astype(BF)
+    d_gu_ref[0] = d_gate
+    d_gu_ref[1] = d_up
+    d_mid_ref[...] = (dot(d_gate, w_gate, 1, 1) + dot(d_up, w_up, 1, 1)).astype(BF)
+
+
+def feed(mid, d_top, weights, n_units, n_seq, first, size=256):
+    tokens, model = mid.shape
+    rows = lambda n: pl.BlockSpec((size, n), lambda i: (i, 0))
+    return pl.pallas_call(
+        partial(feed_kernel, n_seq, first),
+        grid=(tokens // size,),
+        in_specs=[rows(model), rows(model), whole(weights.shape)],
+        out_specs=[
+            rows(n_units), pl.BlockSpec((2, size, n_units), lambda i: (0, i, 0)),
+            rows(model), whole((n_units, model)),
+        ],
+        out_shape=[
+            jax.ShapeDtypeStruct((tokens, n_units), BF),
+            jax.ShapeDtypeStruct((2, tokens, n_units), BF),
+            jax.ShapeDtypeStruct((tokens, model), BF),
+            jax.ShapeDtypeStruct((n_units, model), BF),
+        ],
+        compiler_params=params("arbitrary"),
+        cost_estimate=cost(1, 14.0),
+        name="feed",
+    )(mid, d_top, weights)
+
+
+def times_kernel(left_ref, right_ref, out_ref):
+    out_ref[...] = dot(left_ref[...], right_ref[...]).astype(BF)
+
+
+def times(left, right, earlier=(), size=256):
+    tokens, inner = left.shape
+    rows = lambda n: pl.BlockSpec((size, n), lambda i: (i, 0))
+    return launch(
+        times_kernel,
+        [rows(inner), whole(right.shape)],
+        earlier,
+        grid=(tokens // size,),
+        out_specs=rows(right.shape[1]),
+        out_shape=jax.ShapeDtypeStruct((tokens, right.shape[1]), BF),
+        compiler_params=params("arbitrary"),
+        cost_estimate=cost(1, 3.0),
+        name="times",
+    )(left, right)
+
+
+def feed_grads(mid, d_gu, rows, earlier=()):
+    tokens, model = mid.shape
+    n_units = d_gu.shape[2]
+    size = max(rows, 128)
+    per = size // rows
+
+    def body(mid_ref, d_gu_ref, out_ref):
+        mid = mid_ref[...]
+        for half in range(2):
+            value = dot(mid, d_gu_ref[half], 0, 0).astype(BF)
+            for part in range(per):
+                out_ref[part, half] = value[part * rows : (part + 1) * rows]
+
+    return launch(
+        body,
+        [pl.BlockSpec((tokens, size), lambda i: (0, i)), whole(d_gu.shape)],
+        earlier,
+        grid=(model // size,),
+        out_specs=pl.BlockSpec((per, 2, rows, n_units), lambda i: (i, 0, 0, 0)),
+        out_shape=jax.ShapeDtypeStruct((model // rows, 2, rows, n_units), BF),
+        compiler_params=params("arbitrary"),
+        cost_estimate=cost(1, 6.0),
+        name="feed_grads",
+    )(mid, d_gu)
+
+
+def pick(stacked, at, axis=0):
+    return lax.dynamic_index_in_dim(stacked, at, axis, False, allow_negative_indices=False)
+
+
+def tie(value, *earlier):
+    for other in earlier:
+        first = lax.slice(other, (0,) * other.ndim, (1,) * other.ndim).reshape(())
+        value = value + (first * 0).astype(value.dtype)
+    return value
+
+
+def exchange(value, axis, bit):
+    count = lax.axis_size(axis)
+    return lax.ppermute(value, axis, [(i, i ^ bit) for i in range(count)])
+
+
+def bits(axis):
+    count = lax.axis_size(axis)
     return [1 << b for b in range(count.bit_length() - 1)]
 
 
 def row_gather(value):
     parts = {0: value}
-    for bit in reversed(row_bits()):
-        places = sorted(parts)
-        got = exchange(jnp.stack([parts[j] for j in places]), bit)
-        parts.update({j ^ bit: got[n] for n, j in enumerate(places)})
+    for bit in reversed(bits("row")):
+        parts.update({j ^ bit: exchange(part, "row", bit) for j, part in parts.items()})
     return [parts[j] for j in range(len(parts))]
 
 
 def row_scatter(parts):
     parts = dict(enumerate(parts))
-    for bit in row_bits():
-        away = [j for j in sorted(parts) if j & bit]
-        got = exchange(jnp.stack([parts[j].astype(BF) for j in away]), bit).astype(F32)
-        parts = {
-            j ^ bit: parts[j ^ bit].astype(F32) + got[n] for n, j in enumerate(away)
-        }
+    for bit in bits("row"):
+        got = {j ^ bit: exchange(parts[j].astype(BF), "row", bit) for j in parts if j & bit}
+        parts = {j: parts[j].astype(F32) + part.astype(F32) for j, part in got.items()}
     return parts[0]
 
 
-def row_sum(value):
-    for bit in row_bits():
-        value = value + exchange(value, bit)
-    return value
+def row_gather_chain(value, gate):
+    parts = {0: value}
+    for bit in reversed(bits("row")):
+        got = {j ^ bit: exchange(fence(part, gate), "row", bit) for j, part in parts.items()}
+        parts.update(got)
+        gate = yield list(got.values())
+    return [parts[j] for j in range(len(parts))], gate
+
+
+def row_scatter_chain(parts, gate):
+    parts = dict(enumerate(parts))
+    for bit in bits("row"):
+        got = {j: exchange(fence(parts[j].astype(BF), gate), "row", bit) for j in parts if j & bit}
+        gate = yield list(got.values())
+        parts = {j ^ bit: parts[j ^ bit].astype(F32) + part.astype(F32) for j, part in got.items()}
+    return parts[0], gate
+
+
+def row_sum_chain(value, gate):
+    for bit in bits("row"):
+        got = exchange(fence(value, gate), "row", bit)
+        gate = yield [got]
+        value = value + got
+    return value, gate
+
+
+def wait(rounds):
+    for _ in range(rounds):
+        gate = yield []
+    return gate
+
+
+def ring():
+    count, mine = lax.axis_size("seq"), lax.axis_index("seq")
+    order = list(range(0, count, 2)) + list(range(1, count, 2))[::-1]
+    half = mine >> 1
+    place = jnp.where((mine & 1) == 0, half, count - 1 - half)
+
+    def owner(k):
+        at = (place + (k % count)) & (count - 1)
+        return jnp.where(at < count // 2, 2 * at, 2 * count - 1 - 2 * at)
+
+    ahead = [(order[i], order[(i + 1) % count]) for i in range(count)]
+    behind = [(b, a) for a, b in ahead]
+    return count, owner, ahead, behind
+
+
+def ring_gather(value, earlier):
+    count, owner, ahead, behind = ring()
+    blocks = jnp.zeros(value.shape[:1] + (count,) + value.shape[1:], value.dtype)
+    put = lambda blocks, block, k: lax.dynamic_update_index_in_dim(
+        blocks, block, owner(k), 1, allow_negative_indices=False
+    )
+    blocks = put(blocks, value, 0)
+    there, back = value, value
+    for k in range(1, count // 2):
+        there = lax.ppermute(there, "seq", ahead)
+        back = lax.ppermute(back, "seq", behind)
+        if k == count // 4:
+            there = tie(there, earlier)
+        blocks = put(put(blocks, there, -k), back, k)
+    cut = value.shape[1] // 2
+    there = lax.ppermute(there[:, :cut], "seq", ahead)
+    back = lax.ppermute(back[:, cut:], "seq", behind)
+    return put(blocks, jnp.concatenate([there, back], axis=1), count // 2)
+
+
+def ring_scatter(parts, chains):
+    count, owner, ahead, behind = ring()
+    steps = jnp.arange(2, count + 1, dtype=jnp.int32)
+    table = owner(jnp.stack([-steps, steps], axis=1).reshape(-1))
+    there, back = pick(parts[0], owner(-1)), pick(parts[1], owner(1))
+    gate, live, done = None, dict(chains), {}
+    for k in range(count - 1):
+        there = lax.ppermute(there, "seq", ahead)
+        back = lax.ppermute(back, "seq", behind)
+        kind = BF if k < count - 2 else F32
+        there, back = ring_add(table, k, there, back, parts, kind, advance(live, gate, done))
+        gate = there
+    while live:
+        advance(live, gate, done)
+    return jnp.concatenate([there, back], axis=0), done
+
+
+def advance(live, gate, done):
+    needed = []
+    for name in list(live):
+        try:
+            needed.extend(live[name].send(gate))
+        except StopIteration as end:
+            done[name] = end.value[0]
+            del live[name]
+    return needed
 
 
 def rms_scale(values):
@@ -583,11 +999,13 @@
     n_seq, n_row = lax.axis_size("seq"), lax.axis_size("row")
     seq, row = lax.axis_index("seq"), lax.axis_index("row")
     n_micro, _, n_tok, model = tokens.shape
+    micros = list(range(n_micro))
     n_heads = a_log.shape[0]
     head_dim = head_gain.shape[0]
     n_taps, conv_width = conv_weight.shape
     slots = w_in.shape[1] // (n_heads * head_dim)
     width = conv_width // n_heads
+    full = slots * head_dim
     length = n_tok * n_seq
     copies = n_seq // n_heads
     head = seq // copies
@@ -596,27 +1014,27 @@
     def to_heads(value):
         return lax.all_to_all(jnp.repeat(value, copies, axis=0), "seq", 0, 0, tiled=True)
 
+    def seq_parts(value):
+        return lax.all_to_all(value, "seq", 0, 0, tiled=True)
+
     def from_heads(value):
         got = lax.all_to_all(value, "seq", 0, 0, tiled=True)
         return got if copies == 1 else got[::copies]
 
-    tokens_all = lax.all_gather(tokens[:, 0], "seq", axis=0)
+    def in_order(parts, axis):
+        stacked = jnp.stack(parts)
+        return jnp.concatenate([pick(stacked, row ^ j) for j in range(n_row)], axis=axis)
+
     cut = w_in.shape[0] // n_row
-    w_piece = lax.dynamic_index_in_dim(
-        w_in.reshape(n_row, cut, slots, n_heads, head_dim), row, 0, False
-    )
-    w_piece = w_piece.transpose(2, 0, 1, 3).reshape(n_heads, cut, slots * head_dim)
-    w_pieces = jnp.stack(row_gather(to_heads(w_piece)))
-    w_head = jnp.stack(
-        [lax.dynamic_index_in_dim(w_pieces, row ^ j, 0, False) for j in range(n_row)], axis=1
-    ).reshape(model, slots * head_dim)
-    w_rt = lax.dynamic_index_in_dim(w_router.reshape(model, -1, n_heads), head, 2, False)
+    w_piece = pick(w_in.reshape(n_row, cut, slots, n_heads, head_dim), row)
+    w_got = to_heads(w_piece.transpose(2, 0, 1, 3).reshape(n_heads, cut, full))
+    w_head = in_order(row_gather(w_got[:, None]), 1).reshape(model, full)
+    w_rt = pick(w_router.reshape(model, -1, n_heads), head, 2)
     n_rt = w_rt.shape[1]
     w_rt = jnp.pad(w_rt, ((0, 0), (0, LANES - n_rt)))
-    taps = lax.dynamic_index_in_dim(
-        conv_weight.reshape(n_taps, gate_at, n_heads, head_dim), head, 2, False
-    ).reshape(n_taps, width)
-    taps = jnp.pad(taps, ((0, 8 - n_taps), (0, 0)))
+    w_ext = jnp.concatenate([w_head, w_rt], axis=1)
+    taps = pick(conv_weight.reshape(n_taps, gate_at, n_heads, head_dim), head, 2)
+    taps = jnp.pad(taps.reshape(n_taps, width), ((0, 8 - n_taps), (0, 0)))
     par = jnp.concatenate(
         [
             head_gain[None],
@@ -625,133 +1043,156 @@
             jnp.zeros((5, LANES), F32),
         ]
     )
+    position = seq * n_tok + jnp.arange(n_tok, dtype=jnp.int32)
+    live = (position[None, :] < row_lengths[:, :1]).astype(F32)[:, :, None]
+    d_top = (cotangent[:, 0].astype(F32) * live).reshape(-1, model)
+    d_rows = jnp.concatenate(row_gather(d_top.astype(BF)), axis=0)
+    x_own = tokens[:, 0].astype(F32).reshape(-1, model)
+
+    x_all = ring_gather(tokens[:, 0], w_got).reshape(n_micro, length, model)
+
+    out_cut = w_out.shape[0] // n_row
+    shard = w_out.shape[0]
     hidden = w_gu.shape[1] // 2
     unit_cut = hidden // n_seq // n_row
-    n_units = unit_cut * n_seq
-    gu_piece = lax.dynamic_index_in_dim(
-        w_gu.reshape(-1, 2, n_seq, n_row, unit_cut), row, 3, False
-    ).reshape(-1, 2 * n_units)
+    unit_pad = -(-unit_cut // 16) * 16
+    n_units = unit_pad * n_seq
+    gu_piece = pick(w_gu.reshape(shard, 2, n_seq, n_row, unit_cut), row, 3)
+    gu_piece = jnp.pad(gu_piece, ((0, 0), (0, 0), (0, 0), (0, unit_pad - unit_cut)))
     down_piece = lax.dynamic_slice_in_dim(w_down, row * unit_cut, unit_cut, 0)
-    full_out = lax.all_gather(w_out, "seq", axis=0, tiled=True)
-    gu = lax.all_gather(gu_piece, "seq", axis=0, tiled=True)
-    down = lax.all_gather(down_piece, "seq", axis=0, tiled=True)
-
-    position = seq * n_tok + jnp.arange(n_tok, dtype=jnp.int32)
-    live = (position[None, :] < row_lengths[:, :1]).astype(F32)[:, :, None]
-    d_top = cotangent[:, 0].astype(F32) * live
-    d_top_low = d_top.astype(BF)
-    d_top_rows = jnp.concatenate(
-        [part.reshape(-1, model) for part in row_gather(d_top_low)], axis=0
+    down_piece = jnp.pad(down_piece, ((shard - unit_pad, unit_pad - unit_cut), (0, 0)))
+    weights = jnp.concatenate([gu_piece.reshape(shard, -1), down_piece], axis=1)
+    weights = fence(weights, x_all)
+    weights_all = lax.all_gather(weights, "seq", axis=0, tiled=True)
+
+    normed_in, projected, router = project(x_all, norm1_gain, w_head, w_rt, [d_rows, weights])
+    out_piece = lax.dynamic_slice_in_dim(w_out, row * out_cut, out_cut, 0)
+    out_piece = jnp.broadcast_to(out_piece[None], (n_seq,) + out_piece.shape)
+    out_got = lax.all_to_all(fence(out_piece, projected), "seq", 0, 0, tiled=True)
+    prep = prepare(projected, router, taps, par, width)
+    full_out = in_order([part[:, None] for part in row_gather(fence(out_got, prep[0]))], 1)
+    full_out = full_out.reshape(model, model)
+    sent, *kept = scan_states(prep, router, projected, par, gate_at)
+    gated = sent.reshape(n_micro, n_seq, n_tok, head_dim).transpose(1, 0, 2, 3)
+    gated = from_heads(gated).transpose(1, 2, 0, 3).reshape(-1, model)
+
+    residual = x_own + matmul("tc,cd->td", gated, full_out)
+    scale_mid = rms_scale(residual)
+    mid_rows = jnp.concatenate(
+        row_gather((residual * scale_mid * norm2_gain).astype(BF)), axis=0
     )
-    d_act = matmul("td,fd->tf", d_top_rows, down)
-
-    x_all = tokens_all.transpose(1, 0, 2, 3).reshape(n_micro, length, model).astype(F32)
-    scale_all = rms_scale(x_all)
-    normed_in = (x_all * scale_all * norm1_gain).astype(BF)
-    projected = matmul("mtd,dc->mtc", normed_in, w_head, BF)
-    router = matmul("mtd,dc->mtc", normed_in, w_rt)
-    prep = prepare(projected, router, taps, par, width)
-    gated, mixed, news, state = scan_states(prep, router, projected, par, gate_at)
-
-    gated_out = from_heads(
-        gated.reshape(n_micro, n_seq, n_tok, head_dim).transpose(1, 0, 2, 3)
+    act, d_gu, d_mid, down = feed(
+        mid_rows, d_rows, weights_all, n_units, n_seq, shard - unit_pad
     )
-    gated_out = gated_out.transpose(1, 2, 0, 3).reshape(n_micro * n_tok, model)
-    x_vals = tokens[:, 0].reshape(-1, model).astype(F32)
-    residual = x_vals + matmul("tc,cd->td", gated_out, full_out)
-    scale_mid = rms_scale(residual)
-    normed_mid = (residual * scale_mid * norm2_gain).astype(BF)
-    mid_rows = jnp.concatenate(row_gather(normed_mid), axis=0)
-    gate_up = matmul("td,dc->tc", mid_rows, gu)
-    gate_part = gate_up[:, :n_units]
-    up_part = gate_up[:, n_units:]
-    gate_sig = jax.nn.sigmoid(gate_part)
-    act_low = (gate_part * gate_sig * up_part).astype(BF)
-    d_gate = d_act * up_part * gate_sig * (1.0 + gate_part * (1.0 - gate_sig))
-    d_up = d_act * gate_part * gate_sig
-    d_gu_low = jnp.concatenate([d_gate, d_up], axis=1).astype(BF)
-    d_mid = row_scatter(list(matmul("tc,dc->td", d_gu_low, gu).reshape(n_row, -1, model)))
-    d_residual = d_top.reshape(-1, model) + rms_back(d_mid * norm2_gain, residual, scale_mid)
-    d_res_low = d_residual.astype(BF)
-    d_gated = matmul("td,cd->tc", d_res_low, full_out, BF)
-    d_gated = d_gated.reshape(n_micro, n_tok, n_heads, head_dim).transpose(2, 0, 1, 3)
+    d_mid = row_scatter(list(d_mid.reshape(n_row, -1, model)))
+
+    def row_parts(value, axis):
+        return [pick(value, row ^ j, axis) for j in range(n_row)]
+
+    g_gu = feed_grads(mid_rows, d_gu, shard)
+    g_gu_sum = lax.psum_scatter(g_gu, "seq", scatter_dimension=0, tiled=True)[0]
+    g_down = matmul("tf,td->fd", act, d_rows, BF)
+    g_down_sum = lax.psum_scatter(g_down, "seq", scatter_dimension=0, tiled=True)
+
+    d_mid = tie(d_mid, g_gu, g_down)
+    g_norm2 = jnp.sum(d_mid * residual * scale_mid, axis=0)
+    d_residual = d_top + rms_back(d_mid * norm2_gain, residual, scale_mid)
+    d_low = d_residual.astype(BF)
+    d_sent = matmul("td,cd->tc", d_low, full_out, BF)
+    d_gated = d_sent.reshape(n_micro, n_tok, n_heads, head_dim).transpose(2, 0, 1, 3)
     d_gated = to_heads(d_gated).transpose(1, 0, 2, 3).reshape(n_micro, length, head_dim)
 
-    mlp_out = row_scatter(list(matmul("tf,fd->td", act_low, down).reshape(n_row, -1, model)))
-    out = (residual + mlp_out).astype(BF).reshape(n_micro, 1, n_tok, model)
-
+    mlp = times(act, down, [d_sent])
+    out = (residual + row_scatter(list(mlp.reshape(n_row, -1, model)))).astype(BF)
+    out = out.reshape(n_micro, 1, n_tok, model)
+    g_out = matmul("tc,td->cd", tie(gated, d_sent), d_low).reshape(n_seq, n_row, out_cut, model)
+    g_out = row_scatter(row_parts(g_out, 1)).astype(BF)
+
+    mixed, news, state = kept
     d_mixed, d_news, d_state, d_gate_pre, g_head = scan_back(
         prep, router, projected, par, gate_at, mixed, d_gated
     )
     d_ext, g_taps, g_par = mixer_grads(
-        prep, router, projected, taps, par, width, news, state, d_mixed, d_news, d_state, d_gate_pre
+        prep, router, projected, taps, par, width,
+        news, state, d_mixed, d_news, d_state, d_gate_pre,
     )
     if copies > 1:
         mine = (seq % copies == 0).astype(F32)
         d_ext = d_ext * mine.astype(BF)
         g_taps, g_par, g_head = g_taps * mine, g_par * mine, g_head * mine
-    w_ext = jnp.concatenate([w_head, w_rt], axis=1)
-    d_in_part = matmul("mtc,dc->mtd", d_ext, w_ext)
-    g_norm1 = jnp.sum(d_in_part * x_all * scale_all, axis=(0, 1))
-    d_in_part = d_in_part.astype(BF).reshape(n_micro, n_seq, n_tok, model).transpose(1, 0, 2, 3)
-    d_in = lax.psum_scatter(d_in_part, "seq", scatter_dimension=0).astype(F32)
-    x_own = tokens[:, 0].astype(F32)
-    grad_tokens = d_residual.reshape(n_micro, n_tok, model) + rms_back(
-        d_in * norm1_gain, x_own, rms_scale(x_own)
+    d_in = matmul("mtc,dc->mtd", d_ext, w_ext, BF).reshape(n_micro, n_seq, n_tok, model)
+    g_in, in_lines = input_grads(normed_in, d_ext, w_ext, norm1_gain, full, [d_in])
+    where = row.astype(jnp.int32).reshape(1)
+
+    def input_chain():
+        gate = yield [g_in]
+        parts = row_parts(g_in.reshape(n_seq, n_row, cut, full), 1)
+        part, gate = yield from row_scatter_chain(parts, gate)
+        got = from_heads(fence(part.astype(BF), gate))
+        gate = yield from wait(1)
+        gate = yield [got]
+        return (yield from row_gather_chain(got, gate))
+
+    def small_chain():
+        gate = yield from wait(1)
+        padded = lambda value: jnp.pad(value, ((0, 0), (0, model - value.shape[1])))
+        scalars = jnp.concatenate([g_head[:1], g_par[1:2], g_par[2:3]], axis=1)
+        packed = [in_lines[: n_rt + 1], g_norm2[None], padded(scalars), padded(g_taps[:n_taps])]
+        packed, gate = yield from row_sum_chain(jnp.concatenate(packed), gate)
+        gate = yield from wait(1)
+        packed = jnp.broadcast_to(packed[None], (n_seq,) + packed.shape)
+        got = lax.all_to_all(fence(packed, gate), "seq", 0, 0, tiled=True)
+        gate = yield from wait(1)
+        gate = yield [got]
+        return got, gate
+
+    def output_chain():
+        gate = yield from wait(1)
+        got = seq_parts(fence(g_out, gate))
+        gate = yield from wait(1)
+        gate = yield [got]
+        got = jnp.sum(got.astype(F32), axis=0).astype(BF)
+        return (yield from row_gather_chain(got, gate))
+
+    def feed_chain(value, rounds):
+        gate = yield from wait(rounds)
+        return (yield from row_gather_chain(value, gate))
+
+    d_in, done = ring_scatter(
+        d_in,
+        {
+            "input": input_chain(),
+            "small": small_chain(),
+            "output": output_chain(),
+            "down": feed_chain(g_down_sum, 1),
+            "gu": feed_chain(g_gu_sum, 4),
+        },
     )
-
-    g_ext = matmul("mtd,mtc->dc", normed_in, d_ext)
-    g_in = g_ext[:, : slots * head_dim].reshape(n_seq, n_row, cut, slots * head_dim)
-    g_in = row_scatter([lax.dynamic_index_in_dim(g_in, row ^ j, 1, False) for j in range(n_row)])
-    g_in = from_heads(g_in.astype(BF)).reshape(n_heads, cut, slots, head_dim)
-    g_in = g_in.transpose(1, 2, 0, 3).reshape(cut, -1)
-    grad_in = lax.all_gather(g_in, "row", axis=0, tiled=True).astype(F32)
-
-    g_out = matmul("tc,td->cd", gated_out, d_res_low).reshape(model, n_row, -1)
-    g_out = row_scatter([lax.dynamic_index_in_dim(g_out, row ^ j, 1, False) for j in range(n_row)])
-    g_gu = matmul("td,tc->dc", mid_rows, d_gu_low, BF)
-    g_down = matmul("tf,td->fd", act_low, d_top_rows, BF)
-    g_wide = jnp.concatenate([g_gu, g_out.astype(BF)], axis=1)
-    g_wide = lax.psum_scatter(g_wide, "seq", scatter_dimension=0, tiled=True)
-    g_down = lax.psum_scatter(g_down, "seq", scatter_dimension=0, tiled=True)
-    g_wide = lax.all_gather(g_wide, "row", axis=0)
-    grad_down = lax.all_gather(g_down, "row", axis=0, tiled=True).astype(F32)
-    grad_gu = g_wide[:, :, : 2 * n_units].reshape(n_row, -1, 2, n_seq, unit_cut)
-    grad_gu = grad_gu.transpose(1, 2, 3, 0, 4).reshape(-1, 2 * hidden).astype(F32)
-    grad_out = g_wide[:, :, 2 * n_units :].transpose(1, 0, 2).reshape(-1, model).astype(F32)
-
-    g_norm2 = jnp.sum(d_mid * residual * scale_mid, axis=0)
-    shared = jnp.concatenate([g_norm1, g_norm2, g_head[0]])
-    by_head = jnp.concatenate(
-        [
-            g_taps[:n_taps].reshape(-1),
-            g_ext[:, slots * head_dim : slots * head_dim + n_rt].T.reshape(-1),
-            g_par[1, 2:3],
-            g_par[2, 2:3],
-        ]
-    )
-    size = shared.shape[0] + by_head.shape[0]
-    packed = jnp.pad(jnp.concatenate([shared, by_head]), (0, -size % 1024)).reshape(-1, 1024)
-    packed = lax.all_gather(row_sum(packed), "seq", axis=0).reshape(n_seq, -1)
-    total = jnp.sum(packed[:, : shared.shape[0]], axis=0)
-    heads = packed[::copies, shared.shape[0] : size]
-    n_conv = n_taps * width
-    conv_sum = heads[:, :n_conv].reshape(n_heads, n_taps, gate_at, head_dim)
+    grad_tokens = d_residual + rms_back(d_in * norm1_gain, x_own, rms_scale(x_own))
+    grad_tokens = grad_tokens.reshape(n_micro, 1, n_tok, model)
+    grad_out = place_rows(where, done["output"], out_cut)
+    grad_down = place_rows(where, done["down"], unit_cut)
+    grad_gu = place_units(where, done["gu"], unit_cut, unit_pad, n_seq)
+    grad_in = place_heads(where, done["input"], slots)
+    small = done["small"]
+
+    total = jnp.sum(small[:, n_rt : n_rt + 3], axis=0)
+    heads = small[::copies]
+    conv_sum = heads[:, n_rt + 3 :, :width].reshape(n_heads, n_taps, gate_at, head_dim)
     conv_sum = conv_sum.transpose(1, 2, 0, 3).reshape(n_taps, conv_width)
-    router_sum = heads[:, n_conv : n_conv + n_rt * model].reshape(n_heads, n_rt, model)
-    router_sum = router_sum.transpose(2, 1, 0).reshape(model, n_rt * n_heads)
+    router_sum = heads[:, :n_rt].transpose(2, 1, 0).reshape(model, n_rt * n_heads)
     return (
         out,
-        grad_tokens[:, None],
-        total[:model],
+        grad_tokens,
+        total[0],
         grad_in,
         router_sum,
         conv_sum,
-        heads[:, -2],
-        heads[:, -1],
-        total[2 * model :],
+        heads[:, n_rt + 2, LANES + 2],
+        heads[:, n_rt + 2, 2 * LANES + 2],
+        total[2, :head_dim],
         grad_out,
-        total[model : 2 * model],
+        total[1],
         grad_gu,
         grad_down,
     )

time: 659 us -> 490 us (0.74)
  waiting for transfers between devices: 266 us -> 98 us
  blocking collectives: 81.6 us -> 0 us
  Pallas kernels: 92.5 us -> 162 us
  starting transfers between devices: 19.7 us -> 76.3 us
  matrix products: 63.3 us -> 15.4 us
  local copies, waits for them, and re-layouts: 67.1 us -> 78.7 us
  other arithmetic: 45.3 us -> 34 us
    all_gather x6 -> x1, waiting for transfers between devices: 103 us -> 0.01 us  [local(): weights_all = lax.all_gather(weights, 'seq', axis=0, tiled=True)]
    reduce_scatter x3 -> x2, waiting for transfers between devices: 70.1 us -> 0.01 us  [the longest x1 0.01 us: local(): lax.psum_scatter(g_down, 'seq', scatter_dimension=0, tiled=True)]
    pallas_call x4 -> x43, Pallas kernels: 92.5 us -> 162 us  [the longest x8 123 us: launch(): return lambda *operands: called(*operands, *earlier)]
    dot_general x13 -> x5, matrix products: 63.3 us -> 15.4 us  [matmul(): jnp.einsum(spec, left, right, preferred_element_type=F32).astype(kind)]
    all_to_all x2 -> x0, blocking collectives: 42.4 us -> none  [the longest x1 27.5 us: to_heads(): lax.all_to_all(jnp.repeat(value, copies, axis=0), 'seq', 0, 0, tiled=True)]
    all_gather x2 -> x0, blocking collectives: 39.1 us -> none  [the longest x1 30.7 us: local(): packed = lax.all_gather(row_sum(packed), 'seq', axis=0).reshape(n_seq, -1)]
    ppermute x16 -> x60, starting transfers between devices: 11.7 us -> 41.1 us  [the longest x38 16.7 us: exchange(): return lax.ppermute(value, axis, [(i, i ^ bit) for i in range(count)])]
    all_to_all x1 -> x2, waiting for transfers between devices: 22.6 us -> 0.01 us  [to_heads(): lax.all_to_all(jnp.repeat(value, copies, axis=0), 'seq', 0, 0, tiled=True)]
  transfers between devices with their start and end apart: 27 -> 70, of which waited for: 17 -> 21; matrix products, arithmetic and copies ran while one was open for 19% -> 20% of each run, Pallas kernels for 14% -> 29%
where the time goes in v2:
time: 490 us; the launch traced here: 482 us
  Pallas kernels  162 us (33%)
  waiting for transfers between devices  98 us (20%)
  local copies, waits for them, and re-layouts  78.7 us (16%)
  starting transfers between devices  76.3 us (16%)
  other arithmetic  34 us (7%)
  between operations  17.7 us (4%)
  matrix products  15.4 us (3%)
    pallas_call x8, Pallas kernels, launch(): return lambda *operands: called(*operands, *earlier)  123 us
    ppermute x38, waiting for transfers between devices, exchange(): return lax.ppermute(value, axis, [(i, i ^ bit) for i in range(count)])  41.8 us
    unnamed x159, local copies, waits for them, and re-layouts  41.3 us
    all_to_all x2, waiting for transfers between devices, from_heads(): got = lax.all_to_all(value, 'seq', 0, 0, tiled=True)  27.8 us
    ppermute x38, starting transfers between devices, exchange(): return lax.ppermute(value, axis, [(i, i ^ bit) for i in range(count)])  16.7 us
    pallas_call x1, Pallas kernels, feed(): pl.pallas_call(partial(feed_kernel, n_seq, first), grid=(tokens // size,)...  16.2 us
    dot_general x5, matrix products, matmul(): jnp.einsum(spec, left, right, preferred_element_type=F32).astype(kind)  15.4 us
    pallas_call x7, Pallas kernels, ring_add(): pl.pallas_call(body, grid_spec=pltpu.PrefetchScalarGridSpec(num_scalar_pr...  13.6 us
  transfers between devices with their start and end apart: 70, of which 21 were waited for; matrix products, arithmetic and copies ran while one was open for 20% of the time, Pallas kernels for 29%

profile of v2, /device:TPU:0, one launch (start us, length us, event | category | flops | bytes accessed | tf_op | source)
XLA Modules:
  0.0 482.4 jit_solution(796796061914122645)
XLA Ops:
  7.2 3.1 collective-permute-start
  17.4 5.8 %all-to-all-start = ((bf16[8,32,768]{2,1,0:T(8,128)(2,1)}), bf16[8,32,768]{2,1,0:T(8,128)(2,1)S(1)}, u32[]{:S(2)}, u32[]{:S(2)}) async-start(bf16[8,32,768]{2,1,0:T(8,128)(2,1)} %reshape_broadcast_in_dim_reshape.3), calls=%async_computation | async-start | bytes 786432 | tf_op jit(solution)/shard_map/all_to_all | solution.py:1015
  40.8 5.9 %collective-permute-done.2 = bf16[2,128,1024]{2,1,0:T(8,128)(2,1)S(1)} collective-permute-done((bf16[2,128,1024]{2,1,0:T(8,128)(2,1)}, bf16[2,128,1024]{2,1,0:T(8,128)(2,1)S(1)}, u32[]{:S(2)}, u32[]{:S(2)}) %collective-permute-start.2) | collective-permute-done | bytes 524320 | tf_op jit(solution)/shard_map/ppermute | solution.py:930
  51.2 2.9 pad_maximum_fusion.refs_4_.d_top_ref
  54.9 5.6 %collective-permute-done.9 = bf16[8,1,32,768]{3,2,0,1:T(8,128)(2,1)S(1)} collective-permute-done((bf16[8,1,32,768]{3,2,0,1:T(8,128)(2,1)S(1)}, bf16[8,1,32,768]{3,2,0,1:T(8,128)(2,1)S(1)}, u32[]{:S(2)}, u32[]{:S(2)}) %collective-permute-start.9) | collective-permute-done | bytes 393248 | tf_op jit(solution)/shard_map/ppermute | solution.py:851
  64.8 4.5 collective-permute-done.6
  72.8 9.7 %project.1 = (bf16[2,1024,1024]{2,1,0:T(8,128)(2,1)}, bf16[2,1024,768]{2,1,0:T(8,128)(2,1)}, f32[2,1024,128]{2,1,0:T(8,128)S(1)}) custom-call(bf16[2,1024,1024]{2,1,0:T(8,128)(2,1)} %bitcast.19.refs_1_.refs_0_, f32[1,1024]{1,0:T(1,128)S(1)} %bitcast.243, bf16[1024,768]{1,0:T(8,128)(2,1)S(1)} %bitcast.231, bf16[1024,128]{1,0:T(8,128)(2,1)S(1)} %pad.24.refs_3_, ...), custom_call_target="tpu_custom_call" | custom-call | flops 12320000000 | bytes 1048576 | tf_op jit(solution)/shard_map/project/pallas_call | solution.py:393
  83.4 4.8 all-to-all-start.2
  88.2 22.2 %mixer_prepare.1 = (f32[2,16,128,128]{3,2,1,0:T(8,128)}, f32[2,16,128,128]{3,2,1,0:T(8,128)}, f32[2,16,128,128]{3,2,1,0:T(8,128)}, f32[2,16,64,128]{3,2,1,0:T(8,...) custom-call(bf16[2,1024,768]{2,1,0:T(8,128)(2,1)} %get-tuple-element.54.refs_0_.refs_1_.refs_6_.refs_5, ...), custom_call_target="tpu_custom_call" | custom-call | flops 26400000000 | bytes 1048576 | tf_op jit(solution)/shard_map/mixer_prepare/pallas_call | solution.py:393
  117.4 13.0 %mixer_scan.1 = (bf16[2,1024,128]{2,1,0:T(8,128)(2,1)S(1)}, f32[2,16,64,128]{3,2,1,0:T(8,128)S(1)}, f32[2,16,128,128]{3,2,1,0:T(8,128)}, f32[2,16,128,128]{3,2,1,0:T(8,128)}) custom-call(f32[2,16,128,128]{3,2,1,0:T(8,128)} %get-tuple-element.56.refs_0_, f32[2,16,128,128]{3,2,1,0:T(8,128)} %get-tuple-element.57.refs_1_, f32[2,16,64,128]{3,2,1,0:T(8,128)S(1)} %copy-done.41, ...), custom_call_target="tpu_custom_call" | custom-call | flops 17600000000 | bytes 1048576 | tf_op jit(solution)/shard_map/mixer_scan/pallas_call | solution.py:393
  131.6 4.1 all-to-all-start.1
  136.5 27.8 %all-to-all-done.1 = bf16[8,2,128,128]{3,2,1,0:T(8,128)(2,1)S(1)} async-done(((bf16[8,2,128,128]{3,2,1,0:T(8,128)(2,1)}), bf16[8,2,128,128]{3,2,1,0:T(8,128)(2,1)S(1)}, u32[]{:S(2)}, u32[]{:S(2)}) %all-to-all-start.1) | async-done | bytes 524320 | tf_op jit(solution)/shard_map/all_to_all | solution.py:1021
  169.8 11.7 %collective-permute-done.18 = bf16[256,1024]{1,0:T(8,128)(2,1)S(1)} collective-permute-done((bf16[256,1024]{1,0:T(8,128)(2,1)S(1)}, bf16[256,1024]{1,0:T(8,128)(2,1)S(1)}, u32[]{:S(2)}, u32[]{:S(2)}) %collective-permute-start.18) | collective-permute-done | bytes 524320 | tf_op jit(solution)/shard_map/ppermute | solution.py:851
  184.8 16.2 %feed.1 = (bf16[1024,768]{1,0:T(8,128)(2,1)S(1)}, bf16[2,1024,768]{2,1,0:T(8,128)(2,1)}, bf16[1024,1024]{1,0:T(8,128)(2,1)}, bf16[768,1024]{1,0:T(8,128)(2,1)S(1)}) custom-call(bf16[1024,1024]{1,0:T(8,128)(2,1)} %pad_maximum_fusion.3.mid_ref.refs_0_, bf16[1024,1024]{1,0:T(8,128)(2,1)} %pad_maximum_fusion.refs_4_.d_top_ref, ...), custom_call_target="tpu_custom_call" | custom-call | flops 15399999488 | bytes 1048576 | tf_op jit(solution)/shard_map/feed/pallas_call | solution.py:772
  205.9 5.0 %convolution_convert_fusion.1 = bf16[768,1024]{1,0:T(8,128)(2,1)} fusion(bf16[1024,768]{1,0:T(8,128)(2,1)} %copy-done.34, bf16[256,1024]{1,0:T(8,128)(2,1)} %collective-permute-done.13, bf16[256,1024]{1,0:T(8,128)(2,1)} %collective-permute-done.12, bf16[256,1024]{1,0:T(8,128)(2,1)} %collective-permute-done.11, bf16[256,1024]{1,0:T(8,128)(2,1)} %copy-done.61), kind=kOutput, calls=%fused_computation.7 | convolution fusion | flops 1619787776 | bytes 5242880 | tf_op jit(solution)/shard_map/tf,td->fd/dot_general | solution.py:980
  216.6 8.4 %feed_grads.1 = bf16[8,2,128,768]{3,2,1,0:T(8,128)(2,1)} custom-call(bf16[1024,1024]{1,0:T(8,128)(2,1)S(1)} %copy-done.9, bf16[2,1024,768]{2,1,0:T(8,128)(2,1)} %get-tuple-element.66.refs_1_), custom_call_target="tpu_custom_call" | custom-call | flops 6600000000 | bytes 1048576 | tf_op jit(solution)/shard_map/feed_grads/pallas_call | solution.py:393
  235.5 4.1 all-to-all-start.3
  252.1 3.3 times.1
  261.4 13.2 %mixer_scan_back.1 = (f32[2,16,64,128]{3,2,1,0:T(8,128)S(1)}, f32[2,16,128,128]{3,2,1,0:T(8,128)}, f32[2,16,128,128]{3,2,1,0:T(8,128)}, bf16[2,1024,128]{2,1,0:T(8,128)(2,1)S(1)}, f32[8,128]{1,0:T(8,128)S(1)}) custom-call(f32[2,16,128,128]{3,2,1,0:T(8,128)} %get-tuple-element.56.refs_0_, f32[2,16,64,128]{3,2,1,0:T(8,128)S(1)} %copy-done.42, ...), custom_call_target="tpu_custom_call" | custom-call | flops 17600000000 | bytes 1048576 | tf_op jit(solution)/shard_map/mixer_scan_back/pallas_call | solution.py:393
  274.6 43.7 %mixer_grads.1 = (bf16[2,1024,896]{2,1,0:T(8,128)(2,1)}, f32[8,640]{1,0:T(8,128)S(1)}, f32[8,128]{1,0:T(8,128)S(1)}) custom-call(bf16[2,1024,768]{2,1,0:T(8,128)(2,1)} %get-tuple-element.54.refs_0_.refs_1_.refs_6_.refs_5_, bf16[2,1024,768]{2,1,0:T(8,128)(2,1)} %get-tuple-element.54.refs_0_.refs_1_.refs_6_.refs_5_, f32[2,1024,128]{2,1,0:T(8,128)S(1)} %copy-done.39, ...), custom_call_target="tpu_custom_call" | custom-call | flops 49280000000 | bytes 1048576 | tf_op jit(solution)/shard_map/mixer_grads/pallas_call | solution.py:393
  318.3 6.9 %convolution_convert_fusion = bf16[2,1024,1024]{2,1,0:T(8,128)(2,1)S(1)} fusion(bf16[2,1024,896]{2,1,0:T(8,128)(2,1)} %get-tuple-element.74.refs_1_, bf16[1024,128]{1,0:T(8,128)(2,1)S(1)} %pad.24.refs_3_, bf16[1024,768]{1,0:T(8,128)(2,1)S(1)} %bitcast.233), kind=kOutput, calls=%fused_computation | convolution fusion | flops 3763863552 | bytes 9699328 | tf_op jit(solution)/shard_map/mtc,dc->mtd/dot_general | solution.py:980
  329.7 9.8 %input_grads.1 = (bf16[1024,768]{1,0:T(8,128)(2,1)S(1)}, f32[8,1024]{1,0:T(8,128)S(1)}) custom-call(bf16[2,1024,1024]{2,1,0:T(8,128)(2,1)} %get-tuple-element.75.refs_0_, bf16[2,1024,896]{2,1,0:T(8,128)(2,1)} %get-tuple-element.74.refs_1_, bf16[1024,896]{1,0:T(8,128)(2,1)S(1)} %copy-done.10, f32[1,1024]{1,0:T(1,128)S(1)} %bitcast.244, ...), custom_call_target="tpu_custom_call" | custom-call | flops 7699999744 | bytes 1048576 | tf_op jit(solution)/shard_map/input_grads/pallas_call | solution.py:393
  346.7 2.6 fusion.6.refs_0_
  349.3 5.2 %all-to-all-start.4 = ((bf16[8,32,1024]{2,1,0:T(8,128)(2,1)}), bf16[8,32,1024]{2,1,0:T(8,128)(2,1)S(1)}, u32[]{:S(2)}, u32[]{:S(2)}) async-start(bf16[8,32,1024]{2,1,0:T(8,128)(2,1)} %fence.32), calls=%async_computation.5 | async-start | bytes 1048576 | tf_op jit(solution)/shard_map/all_to_all | solution.py:1018
  358.3 3.3 collective-permute-done.29.refs_2_
  376.6 4.5 collective-permute-done.35.refs_2_
  387.3 4.7 all-to-all-start.5
  399.0 9.5 %collective-permute-done.45.refs_5_.refs_2_ = bf16[32,1024]{1,0:T(8,128)(2,1)S(1)} collective-permute-done((bf16[32,1024]{1,0:T(8,128)(2,1)}, bf16[32,1024]{1,0:T(8,128)(2,1)S(1)}, u32[]{:S(2)}, u32[]{:S(2)}) %collective-permute-start.45) | collective-permute-done | bytes 65568 | tf_op jit(solution)/shard_map/ppermute | solution.py:851
  412.4 5.7 %all-to-all-start.6 = ((f32[8,10,1024]{2,1,0:T(8,128)}), f32[8,10,1024]{2,1,0:T(8,128)S(1)}, u32[]{:S(2)}, u32[]{:S(2)}) async-start(f32[8,10,1024]{2,1,0:T(8,128)} %fence.41), calls=%async_computation.8 | async-start | bytes 1048576 | tf_op jit(solution)/shard_map/all_to_all | solution.py:1144
  432.1 7.2 %collective-permute-done.50.refs_8_.refs_2_ = bf16[2,128,768]{2,1,0:T(8,128)(2,1)S(1)} collective-permute-done((bf16[2,128,768]{2,1,0:T(8,128)(2,1)}, bf16[2,128,768]{2,1,0:T(8,128)(2,1)S(1)}, u32[]{:S(2)}, u32[]{:S(2)}) %collective-permute-start.50) | collective-permute-done | bytes 393248 | tf_op jit(solution)/shard_map/ppermute | solution.py:851
  460.3 4.3 place_units.1
  465.3 3.1 collective-permute-done.57.refs_2_
  (422 shorter events, 183.0 us)
Async XLA Ops:
  7.2 25.3 %collective-permute-start = (bf16[2,128,1024]{2,1,0:T(8,128)(2,1)}, bf16[2,128,1024]{2,1,0:T(8,128)(2,1)}, u32[]{:S(2)}, u32[]{:S(2)}) collective-permute-start(bf16[2,128,1024]{2,1,0:T(8,128)(2,1)} %bitcast.263), channel_id=1, source_target_pairs={{0,2},{2,4},{4,6},{6,7},{7,5},{5,3},{3,1},{1,0},{8,10},{10,12},{12... | collective-permute-start | bytes 1572872 | tf_op jit(solution)/shard_map/ppermute | solution.py:930
  10.3 25.5 %collective-permute-start.1 = (bf16[2,128,1024]{2,1,0:T(8,128)(2,1)}, bf16[2,128,1024]{2,1,0:T(8,128)(2,1)}, u32[]{:S(2)}, u32[]{:S(2)}) collective-permute-start(bf16[2,128,1024]{2,1,0:T(8,128)(2,1)} %bitcast.264), channel_id=1, source_target_pairs={{2,0},{4,2},{6,4},{7,6},{5,7},{3,5},{1,3},{0,1},{10,8},{12,10},{14... | collective-permute-start | bytes 1572872 | tf_op jit(solution)/shard_map/ppermute | solution.py:931
  12.2 23.6 %collective-permute-start.12 = (bf16[256,1024]{1,0:T(8,128)(2,1)S(1)}, bf16[256,1024]{1,0:T(8,128)(2,1)}, u32[]{:S(2)}, u32[]{:S(2)}) collective-permute-start(bf16[256,1024]{1,0:T(8,128)(2,1)S(1)} %fusion.3), channel_id=1, source_target_pairs={{0,16},{8,24},{16,0},{24,8},{1,17},{9,25},{17,1},{25,9},{2,18},{10... | collective-permute-start | bytes 1572872 | tf_op jit(solution)/shard_map/ppermute | solution.py:851
  14.2 36.9 %collective-permute-start.11 = (bf16[256,1024]{1,0:T(8,128)(2,1)S(1)}, bf16[256,1024]{1,0:T(8,128)(2,1)}, u32[]{:S(2)}, u32[]{:S(2)}) collective-permute-start(bf16[256,1024]{1,0:T(8,128)(2,1)S(1)} %fusion.3), channel_id=1, source_target_pairs={{0,8},{8,0},{16,24},{24,16},{1,9},{9,1},{17,25},{25,17},{2,10},{10... | collective-permute-start | bytes 1572872 | tf_op jit(solution)/shard_map/ppermute | solution.py:851
  17.4 22.3 %all-to-all-start = ((bf16[8,32,768]{2,1,0:T(8,128)(2,1)}), bf16[8,32,768]{2,1,0:T(8,128)(2,1)S(1)}, u32[]{:S(2)}, u32[]{:S(2)}) async-start(bf16[8,32,768]{2,1,0:T(8,128)(2,1)} %reshape_broadcast_in_dim_reshape.3), calls=%async_computation | async-start | bytes 786432 | tf_op jit(solution)/shard_map/all_to_all | solution.py:1015
  23.2 161.7 %all-gather.2.cloned.1.call-start = ((), (), s32[]{:S(2)}) async-start(), calls=%async_computation.9 | async-start | bytes 5898240 | tf_op jit(solution)/shard_map/all_gather | solution.py:1066
  32.5 14.3 %collective-permute-start.2 = (bf16[2,128,1024]{2,1,0:T(8,128)(2,1)}, bf16[2,128,1024]{2,1,0:T(8,128)(2,1)S(1)}, u32[]{:S(2)}, u32[]{:S(2)}) collective-permute-start(bf16[2,128,1024]{2,1,0:T(8,128)(2,1)} %collective-permute-done), channel_id=1, source_target_pairs={{0,2},{2,4},{4,6},{6,7},{7,5},{5,3},{3,1},{1,0},{8,10},{10,12},{12... | collective-permute-start | bytes 1572872 | tf_op jit(solution)/shard_map/ppermute | solution.py:930
  35.8 15.3 %collective-permute-start.13 = (bf16[256,1024]{1,0:T(8,128)(2,1)}, bf16[256,1024]{1,0:T(8,128)(2,1)}, u32[]{:S(2)}, u32[]{:S(2)}) collective-permute-start(bf16[256,1024]{1,0:T(8,128)(2,1)} %collective-permute-done.12), channel_id=1, source_target_pairs={{0,8},{8,0},{16,24},{24,16},{1,9},{9,1},{17,25},{25,17},{2,10},{10... | collective-permute-start | bytes 1572872 | tf_op jit(solution)/shard_map/ppermute | solution.py:851
  51.2 20.2 %collective-permute-start.8 = (bf16[8,1,32,768]{3,2,0,1:T(8,128)(2,1)S(1)}, bf16[8,1,32,768]{3,2,0,1:T(8,128)(2,1)S(1)}, u32[]{:S(2)}, u32[]{:S(2)}) collective-permute-start(bf16[8,1,32,768]{3,2,0,1:T(8,128)(2,1)S(1)} %bitcast.278), channel_id=1, source_target_pairs={{0,8},{8,0},{16,24},{24,16},{1,9},{9,1},{17,25},{25,17},{2,10},{10... | collective-permute-start | bytes 1179656 | tf_op jit(solution)/shard_map/ppermute | solution.py:851
  83.4 31.7 %all-to-all-start.2 = ((bf16[8,32,1024]{2,1,0:T(8,128)(2,1)}), bf16[8,32,1024]{2,1,0:T(8,128)(2,1)}, u32[]{:S(2)}, u32[]{:S(2)}) async-start(bf16[8,32,1024]{2,1,0:T(8,128)(2,1)} %fence.24), calls=%async_computation.2 | async-start | bytes 1048576 | tf_op jit(solution)/shard_map/all_to_all | solution.py:1071
  115.1 20.9 %collective-permute-start.15 = (bf16[8,32,1024]{2,1,0:T(8,128)(2,1)}, bf16[8,32,1024]{2,1,0:T(8,128)(2,1)}, u32[]{:S(2)}, u32[]{:S(2)}) collective-permute-start(bf16[8,32,1024]{2,1,0:T(8,128)(2,1)} %fence.25), channel_id=1, source_target_pairs={{0,16},{8,24},{16,0},{24,8},{1,17},{9,25},{17,1},{25,9},{2,18},{10... | collective-permute-start | bytes 1572872 | tf_op jit(solution)/shard_map/ppermute | solution.py:851
  131.6 32.7 %all-to-all-start.1 = ((bf16[8,2,128,128]{3,2,1,0:T(8,128)(2,1)}), bf16[8,2,128,128]{3,2,1,0:T(8,128)(2,1)S(1)}, u32[]{:S(2)}, u32[]{:S(2)}) async-start(bf16[8,2,128,128]{3,2,1,0:T(8,128)(2,1)} %bitcast.225), calls=%async_computation.1 | async-start | bytes 1048576 | tf_op jit(solution)/shard_map/all_to_all | solution.py:1021
  135.7 218.8 %reduce-scatter.3.cloned.1.call-start = ((), (), s32[]{:S(2)}) async-start(), calls=%async_computation.10 | async-start | bytes 1769472 | tf_op jit(solution)/shard_map/reduce_scatter | solution.py:1095
  135.9 28.8 %collective-permute-start.14 = (bf16[8,32,1024]{2,1,0:T(8,128)(2,1)}, bf16[8,32,1024]{2,1,0:T(8,128)(2,1)S(1)}, u32[]{:S(2)}, u32[]{:S(2)}) collective-permute-start(bf16[8,32,1024]{2,1,0:T(8,128)(2,1)} %fence.25), channel_id=1, source_target_pairs={{0,8},{8,0},{16,24},{24,16},{1,9},{9,1},{17,25},{25,17},{2,10},{10... | collective-permute-start | bytes 1572872 | tf_op jit(solution)/shard_map/ppermute | solution.py:851
  136.0 28.7 %collective-permute-start.16 = (bf16[8,32,1024]{2,1,0:T(8,128)(2,1)}, bf16[8,32,1024]{2,1,0:T(8,128)(2,1)}, u32[]{:S(2)}, u32[]{:S(2)}) collective-permute-start(bf16[8,32,1024]{2,1,0:T(8,128)(2,1)} %collective-permute-done.15), channel_id=1, source_target_pairs={{0,8},{8,0},{16,24},{24,16},{1,9},{9,1},{17,25},{25,17},{2,10},{10... | collective-permute-start | bytes 1572872 | tf_op jit(solution)/shard_map/ppermute | solution.py:851
  212.0 15.4 %collective-permute-start.20 = (bf16[256,1024]{1,0:T(8,128)(2,1)}, bf16[256,1024]{1,0:T(8,128)(2,1)}, u32[]{:S(2)}, u32[]{:S(2)}) collective-permute-start(bf16[256,1024]{1,0:T(8,128)(2,1)} %get-tuple-element.161), channel_id=1, source_target_pairs={{0,8},{8,0},{16,24},{24,16},{1,9},{9,1},{17,25},{25,17},{2,10},{10... | collective-permute-start | bytes 1572872 | tf_op jit(solution)/shard_map/ppermute | solution.py:851
  214.7 14.3 %collective-permute-start.22 = (bf16[256,1024]{1,0:T(8,128)(2,1)}, bf16[256,1024]{1,0:T(8,128)(2,1)}, u32[]{:S(2)}, u32[]{:S(2)}) collective-permute-start(bf16[256,1024]{1,0:T(8,128)(2,1)} %add_convert_fusion.2), channel_id=1, source_target_pairs={{0,16},{8,24},{16,0},{24,8},{1,17},{9,25},{17,1},{25,9},{2,18},{10... | collective-permute-start | bytes 1572872 | tf_op jit(solution)/shard_map/ppermute | solution.py:851
  235.5 22.6 %all-to-all-start.3 = ((bf16[8,2,128,128]{3,2,1,0:T(8,128)(2,1)}), bf16[8,2,128,128]{3,2,1,0:T(8,128)(2,1)}, u32[]{:S(2)}, u32[]{:S(2)}) async-start(bf16[8,2,128,128]{3,2,1,0:T(8,128)(2,1)} %bitcast.272), calls=%async_computation.3 | async-start | bytes 1048576 | tf_op jit(solution)/shard_map/all_to_all | solution.py:1015
  239.6 187.1 %reduce-scatter.5.cloned.1.call-start = ((), (), s32[]{:S(2)}) async-start(), calls=%async_computation.11 | async-start | bytes 3538944 | tf_op jit(solution)/shard_map/reduce_scatter | solution.py:1093
  248.7 97.2 %collective-permute-start.38 = (bf16[8,32,1024]{2,1,0:T(8,128)(2,1)}, bf16[8,32,1024]{2,1,0:T(8,128)(2,1)}, u32[]{:S(2)}, u32[]{:S(2)}) collective-permute-start(bf16[8,32,1024]{2,1,0:T(8,128)(2,1)} %get-tuple-element.155), channel_id=1, source_target_pairs={{0,8},{8,0},{16,24},{24,16},{1,9},{9,1},{17,25},{25,17},{2,10},{10... | collective-permute-start | bytes 1572872 | tf_op jit(solution)/shard_map/ppermute | solution.py:851
  257.6 88.4 %collective-permute-start.40 = (bf16[8,32,1024]{2,1,0:T(8,128)(2,1)}, bf16[8,32,1024]{2,1,0:T(8,128)(2,1)}, u32[]{:S(2)}, u32[]{:S(2)}) collective-permute-start(bf16[8,32,1024]{2,1,0:T(8,128)(2,1)} %fusion.4), channel_id=1, source_target_pairs={{0,16},{8,24},{16,0},{24,8},{1,17},{9,25},{17,1},{25,9},{2,18},{10... | collective-permute-start | bytes 1572872 | tf_op jit(solution)/shard_map/ppermute | solution.py:851
  343.4 14.9 %collective-permute-start.28 = (bf16[128,1024]{1,0:T(8,128)(2,1)S(1)}, bf16[128,1024]{1,0:T(8,128)(2,1)}, u32[]{:S(2)}, u32[]{:S(2)}) collective-permute-start(bf16[128,1024]{1,0:T(8,128)(2,1)S(1)} %get-tuple-element.77.refs_1_), channel_id=1, source_target_pairs={{0,2},{2,4},{4,6},{6,7},{7,5},{5,3},{3,1},{1,0},{8,10},{10,12},{12... | collective-permute-start | bytes 786440 | tf_op jit(solution)/shard_map/ppermute | solution.py:948
  345.4 16.2 %collective-permute-start.31 = (bf16[8,32,768]{2,1,0:T(8,128)(2,1)}, bf16[8,32,768]{2,1,0:T(8,128)(2,1)S(1)}, u32[]{:S(2)}, u32[]{:S(2)}) collective-permute-start(bf16[8,32,768]{2,1,0:T(8,128)(2,1)} %fence.27), channel_id=1, source_target_pairs={{0,8},{8,0},{16,24},{24,16},{1,9},{9,1},{17,25},{25,17},{2,10},{10... | collective-permute-start | bytes 1179656 | tf_op jit(solution)/shard_map/ppermute | solution.py:851
  345.9 15.7 %collective-permute-start.30 = (bf16[8,32,768]{2,1,0:T(8,128)(2,1)}, bf16[8,32,768]{2,1,0:T(8,128)(2,1)S(1)}, u32[]{:S(2)}, u32[]{:S(2)}) collective-permute-start(bf16[8,32,768]{2,1,0:T(8,128)(2,1)} %fence.26), channel_id=1, source_target_pairs={{0,8},{8,0},{16,24},{24,16},{1,9},{9,1},{17,25},{25,17},{2,10},{10... | collective-permute-start | bytes 1179656 | tf_op jit(solution)/shard_map/ppermute | solution.py:851
  346.0 15.6 %collective-permute-start.29 = (bf16[128,1024]{1,0:T(8,128)(2,1)}, bf16[128,1024]{1,0:T(8,128)(2,1)}, u32[]{:S(2)}, u32[]{:S(2)}) collective-permute-start(bf16[128,1024]{1,0:T(8,128)(2,1)} %get-tuple-element.78), channel_id=1, source_target_pairs={{2,0},{4,2},{6,4},{7,6},{5,7},{3,5},{1,3},{0,1},{10,8},{12,10},{14... | collective-permute-start | bytes 786440 | tf_op jit(solution)/shard_map/ppermute | solution.py:949
  349.3 27.3 %all-to-all-start.4 = ((bf16[8,32,1024]{2,1,0:T(8,128)(2,1)}), bf16[8,32,1024]{2,1,0:T(8,128)(2,1)S(1)}, u32[]{:S(2)}, u32[]{:S(2)}) async-start(bf16[8,32,1024]{2,1,0:T(8,128)(2,1)} %fence.32), calls=%async_computation.5 | async-start | bytes 1048576 | tf_op jit(solution)/shard_map/all_to_all | solution.py:1018
  376.1 16.0 %collective-permute-start.24 = (bf16[256,1024]{1,0:T(8,128)(2,1)}, bf16[256,1024]{1,0:T(8,128)(2,1)}, u32[]{:S(2)}, u32[]{:S(2)}) collective-permute-start(bf16[256,1024]{1,0:T(8,128)(2,1)} %get-tuple-element.160), channel_id=1, source_target_pairs={{0,8},{8,0},{16,24},{24,16},{1,9},{9,1},{17,25},{25,17},{2,10},{10... | collective-permute-start | bytes 1572872 | tf_op jit(solution)/shard_map/ppermute | solution.py:851
  376.1 42.1 %collective-permute-start.23 = (bf16[256,1024]{1,0:T(8,128)(2,1)}, bf16[256,1024]{1,0:T(8,128)(2,1)}, u32[]{:S(2)}, u32[]{:S(2)}) collective-permute-start(bf16[256,1024]{1,0:T(8,128)(2,1)} %get-tuple-element.159), channel_id=1, source_target_pairs={{0,8},{8,0},{16,24},{24,16},{1,9},{9,1},{17,25},{25,17},{2,10},{10... | collective-permute-start | bytes 1572872 | tf_op jit(solution)/shard_map/ppermute | solution.py:851
  387.3 25.1 %all-to-all-start.5 = ((bf16[8,32,768]{2,1,0:T(8,128)(2,1)}), bf16[8,32,768]{2,1,0:T(8,128)(2,1)S(1)}, u32[]{:S(2)}, u32[]{:S(2)}) async-start(bf16[8,32,768]{2,1,0:T(8,128)(2,1)} %fence.36), calls=%async_computation.6 | async-start | bytes 786432 | tf_op jit(solution)/shard_map/all_to_all | solution.py:1021
  394.2 24.0 %collective-permute-start.25 = (bf16[256,1024]{1,0:T(8,128)(2,1)}, bf16[256,1024]{1,0:T(8,128)(2,1)}, u32[]{:S(2)}, u32[]{:S(2)}) collective-permute-start(bf16[256,1024]{1,0:T(8,128)(2,1)} %add_convert_fusion.1), channel_id=1, source_target_pairs={{0,16},{8,24},{16,0},{24,8},{1,17},{9,25},{17,1},{25,9},{2,18},{10... | collective-permute-start | bytes 1572872 | tf_op jit(solution)/shard_map/ppermute | solution.py:851
  412.4 18.9 %all-to-all-start.6 = ((f32[8,10,1024]{2,1,0:T(8,128)}), f32[8,10,1024]{2,1,0:T(8,128)S(1)}, u32[]{:S(2)}, u32[]{:S(2)}) async-start(f32[8,10,1024]{2,1,0:T(8,128)} %fence.41), calls=%async_computation.8 | async-start | bytes 1048576 | tf_op jit(solution)/shard_map/all_to_all | solution.py:1144
  424.6 15.5 %collective-permute-start.46 = (bf16[128,1024]{1,0:T(8,128)(2,1)S(1)}, bf16[128,1024]{1,0:T(8,128)(2,1)S(1)}, u32[]{:S(2)}, u32[]{:S(2)}) collective-permute-start(bf16[128,1024]{1,0:T(8,128)(2,1)S(1)} %copy-done.5), channel_id=1, source_target_pairs={{0,2},{2,4},{4,6},{6,7},{7,5},{5,3},{3,1},{1,0},{8,10},{10,12},{12... | collective-permute-start | bytes 786440 | tf_op jit(solution)/shard_map/ppermute | solution.py:948
  (107 other events, 681.7 us)
Sparse Core Ops, SparseCore 0:
  71.5 105.3 all-gather.1
  212.2 67.7 reduce-scatter.2
  284.0 78.4 reduce-scatter.4

commit v3 on v2

--- a/solution.py
+++ b/solution.py
@@ -15,7 +15,8 @@
 ST = 128
 HALO = 16
 LANES = 128
-VMEM_BYTES = 50 * 1024 * 1024
+VMEM_BYTES = 60 * 1024 * 1024
+SMALL_BYTES = 50 * 1024 * 1024
 
 
 def halves(value):
@@ -186,7 +187,9 @@
             mixed = jnp.exp(g_col[:CH]) * mm(q_ref[m, n], held) + mm(halves(seen_ref[m, n]), news_h)
             mixed_ref[m, n] = mixed
             gate = gate_ref[m, rows, :].astype(F32)
-            out_ref[m, rows, :] = (
+            tok = out_ref.shape[2]
+            at = slice(n * CH % tok, n * CH % tok + CH)
+            out_ref[n * CH // tok, m, at, :] = (
                 mixed * head_norm(mixed) * par[0:1] * (gate * jax.nn.sigmoid(gate))
             ).astype(BF)
     for m in range(n_micro):
@@ -211,7 +214,9 @@
             _, g_col, _, g_last, _ = gate_columns(router_ref[m, rows, :], par)
             mixed = mixed_ref[m, n]
             gate = gate_ref[m, rows, :].astype(F32)
-            d_out = d_out_ref[m, rows, :].astype(F32)
+            tok = d_out_ref.shape[2]
+            at = slice(n * CH % tok, n * CH % tok + CH)
+            d_out = d_out_ref[n * CH // tok, m, at, :].astype(F32)
             scale = head_norm(mixed)
             normed = mixed * scale
             sig = jax.nn.sigmoid(gate)
@@ -240,6 +245,11 @@
         state[m] = now[m]
 
 
+def in_step(chains):
+    while chains:
+        chains = [chain for chain in chains if next(chain, chain) is not chain]
+
+
 def unit_back(grad, value, scale):
     return scale * grad - value * scale**3 * jnp.sum(grad * value, axis=-1, keepdims=True)
 
@@ -276,9 +286,9 @@
     above = jnp.where(col >= row, 1.0, 0.0).astype(BF)
     lane = lax.broadcasted_iota(jnp.int32, (CH, LANES), 1)
     last = lax.broadcasted_iota(jnp.int32, (CH, LANES), 0) == CH - 1
-    g_alog = jnp.zeros((1, LANES), F32)
-    g_dt = jnp.zeros((1, LANES), F32)
-    for n in range(count):
+    sums = [jnp.zeros((1, LANES), F32), jnp.zeros((1, LANES), F32)]
+
+    def one(n):
         rows = slice(n * CH, (n + 1) * CH)
         conv = taps_sum(window, weight, n * CH)
         sig = jax.nn.sigmoid(conv)
@@ -290,8 +300,11 @@
         k = jnp.concatenate([k0n, k1n], axis=0).astype(BF)
         kf, qf = k.astype(F32), q.astype(F32)
         router = router_ref[0, rows, :]
+        yield
+        d_right = mm(halves(solve_ref[0, n]), halves(d_news_ref[0, n]), 0, 0)
         beta, g_col, g_row, g_last, decay = gate_columns(router, par)
         gaps = seen_decay(g_col, g_row, visible)
+        yield
         ratio = jnp.where(strict, twice(gaps), 0.0)
         grown = jnp.exp(g_col)
         left = jnp.exp(g_last - g_col)
@@ -302,28 +315,32 @@
         news_h = halves(news)
         d_mixed_h = halves(d_mixed_ref[0, n])
         d_state = d_state_ref[0, n]
-        d_right = mm(halves(solve_ref[0, n]), halves(d_news_ref[0, n]), 0, 0)
+        d_seen = mm(d_mixed_h, news_h, 1, 1)
+        yield
+        d_q_grown = grown[:CH] * mm(d_mixed_h, state_h, 1, 1)
         d_right_h = halves(d_right)
         d_lower = jnp.where(strict, -mm(d_right_h, news_h, 1, 1), 0.0)
+        yield
+        d_ends = left * mm(news_h, halves(d_state), 1, 1)
         d_pre = (1.0 - beta) * jnp.sum(d_right * news, axis=-1, keepdims=True)
         d_v = beta * d_right
+        yield
         d_grown_k = -beta * mm(d_right_h, state_h, 1, 1)
+        d_scores = halves(d_seen * gaps)
+        seen_both = d_seen * seen_ref[0, n]
+        yield
+        d_q = d_q_grown + mm(d_scores, k)
         d_k = grown * d_grown_k
         d_gram = beta * ratio * d_lower
         both = d_gram * gram
         d_g = jnp.sum(both, axis=-1, keepdims=True) + jnp.sum(d_k * kf, axis=-1, keepdims=True)
         d_g_row = -jnp.sum(both, axis=0, keepdims=True)
-        d_k = d_k + mm(halves(d_gram + d_gram.T), k)
-        d_seen = mm(d_mixed_h, news_h, 1, 1)
-        d_scores = halves(d_seen * gaps)
-        seen_both = d_seen * seen_ref[0, n]
-        d_q_grown = grown[:CH] * mm(d_mixed_h, state_h, 1, 1)
-        d_q = d_q_grown + mm(d_scores, k)
+        yield
+        d_k = d_k + mm(halves(d_gram + d_gram.T), k) + d_ends
+        d_g_q = jnp.sum(seen_both + d_q_grown * qf, axis=-1, keepdims=True)
+        yield
         d_k = d_k + mm(d_scores, q, 0, 0)
-        d_g_q = jnp.sum(seen_both + d_q_grown * qf, axis=-1, keepdims=True)
         d_g_row = d_g_row - jnp.sum(seen_both, axis=0, keepdims=True)
-        d_ends = left * mm(news_h, halves(d_state), 1, 1)
-        d_k = d_k + d_ends
         ends_sum = jnp.sum(d_ends * kf, axis=-1, keepdims=True)
         d_g = d_g - ends_sum
         d_last = jnp.sum(ends_sum, axis=0, keepdims=True) + jnp.exp(g_last) * jnp.sum(
@@ -332,7 +349,9 @@
         d_g_rows = jnp.broadcast_to(d_g_row, (LANES, ST)).T
         d_g_tok = d_g_q + d_g[:CH] + d_g[CH:] + d_g_rows[:CH] + d_g_rows[CH:]
         d_g_tok = d_g_tok + jnp.where(last, d_last, 0.0)
+        yield
         d_decay = exact_sum(above, d_g_tok)
+        yield
         d_soft = -jnp.exp(par[1:2]) * jax.nn.sigmoid(router + par[2:3]) * d_decay
         d_router = jnp.where(
             lane == 0,
@@ -342,10 +361,8 @@
         width = window.shape[1]
         d_ext_ref[0, rows, width : width + LANES] = d_gate_ref[0, rows, :]
         d_ext_ref[0, rows, width + LANES :] = d_router.astype(BF)
-        g_alog = g_alog + jnp.sum(
-            jnp.where(lane == 2, d_decay * decay, 0.0), axis=0, keepdims=True
-        )
-        g_dt = g_dt + jnp.sum(jnp.where(lane == 2, d_soft, 0.0), axis=0, keepdims=True)
+        sums[0] += jnp.sum(jnp.where(lane == 2, d_decay * decay, 0.0), axis=0, keepdims=True)
+        sums[1] += jnp.sum(jnp.where(lane == 2, d_soft, 0.0), axis=0, keepdims=True)
         d_act = jnp.concatenate(
             [
                 unit_back(d_q, act[:, 0:128], q_scale),
@@ -357,6 +374,9 @@
             axis=1,
         )
         d_window[rows, :] = d_act * (sig * (1.0 + conv * (1.0 - sig)))
+
+    in_step([one(n) for n in range(count)])
+    g_alog, g_dt = sums
     g_par_ref[1:2, :] += g_alog
     g_par_ref[2:3, :] += g_dt
     for n in range(count):
@@ -376,6 +396,10 @@
     return pltpu.CompilerParams(dimension_semantics=semantics, vmem_limit_bytes=VMEM_BYTES)
 
 
+def small_params(*semantics):
+    return pltpu.CompilerParams(dimension_semantics=semantics, vmem_limit_bytes=SMALL_BYTES)
+
+
 def cost(chunks, per_chunk):
     return pl.CostEstimate(
         flops=int(chunks * per_chunk * 1.1e9), transcendentals=0, bytes_accessed=1 << 20
@@ -394,6 +418,9 @@
 
 
 def fence(value, *earlier):
+    earlier = [other for other in earlier if other is not None]
+    if not earlier:
+        return value
     anywhere = pl.BlockSpec(memory_space=pl.ANY)
     return pl.pallas_call(
         lambda *refs: None,
@@ -439,7 +466,7 @@
     )(projected, projected, router, taps, par)
 
 
-def scan_states(prep, router, projected, par, gate_at, earlier=(), count=4):
+def scan_states(prep, router, projected, par, gate_at, n_tok, earlier=(), count=4):
     _, wmat, umat, seen, q, k = prep
     n_micro, chunks = wmat.shape[:2]
     length = chunks * CH
@@ -457,11 +484,11 @@
         earlier,
         grid=(chunks // count,),
         out_specs=[
-            pl.BlockSpec((n_micro, size, 128), lambda i: (0, i, 0)),
+            pl.BlockSpec((size // n_tok, n_micro, n_tok, 128), lambda i: (i, 0, 0, 0)),
             per(CH, 128), per(ST, 128), per(128, 128),
         ],
         out_shape=[
-            jax.ShapeDtypeStruct((n_micro, length, 128), BF),
+            jax.ShapeDtypeStruct((length // n_tok, n_micro, n_tok, 128), BF),
             made(F32, CH, 128), made(F32, ST, 128), made(F32, 128, 128),
         ],
         scratch_shapes=[pltpu.VMEM((n_micro, 128, 128), F32)],
@@ -477,6 +504,7 @@
     length = chunks * CH
     size = count * CH
     blocks = chunks // count
+    n_tok = d_out.shape[2]
     per = lambda *tail: pl.BlockSpec((n_micro, count) + tail, lambda i: (0, blocks - 1 - i, 0, 0))
     made = lambda kind, *tail: jax.ShapeDtypeStruct((n_micro, chunks) + tail, kind)
     return launch(
@@ -487,7 +515,9 @@
             pl.BlockSpec((n_micro, size, 128), lambda i: (0, blocks - 1 - i, gate_at)),
             whole(par.shape),
             per(CH, 128),
-            pl.BlockSpec((n_micro, size, 128), lambda i: (0, blocks - 1 - i, 0)),
+            pl.BlockSpec(
+                (size // n_tok, n_micro, n_tok, 128), lambda i: (blocks - 1 - i, 0, 0, 0)
+            ),
         ],
         earlier,
         grid=(blocks,),
@@ -503,7 +533,7 @@
         ],
         scratch_shapes=[pltpu.VMEM((n_micro, 128, 128), F32)],
         compiler_params=params("arbitrary"),
-        cost_estimate=cost(n_micro * chunks, 0.5),
+        cost_estimate=cost(n_micro * chunks, 0.4),
         name="mixer_scan_back",
     )(wmat, seen, q, k, router, projected, par, mixed, d_out)
 
@@ -539,13 +569,14 @@
         ],
         scratch_shapes=[pltpu.VMEM((size + 8, width), F32), pltpu.VMEM((size + 8, width), F32)],
         compiler_params=params("arbitrary", "arbitrary"),
-        cost_estimate=cost(n_micro * chunks, 1.4),
+        cost_estimate=cost(n_micro * chunks, 1.0),
         name="mixer_grads",
     )(projected, projected, router, taps, par, solve, seen, news, state, d_mixed, d_news, d_state, d_gate)
 
 
 def project_kernel(x_ref, gain_ref, weight_ref, router_weight_ref, normed_ref, out_ref, router_ref):
-    x = x_ref[0].astype(F32)
+    per, _, n_tok, model = x_ref.shape
+    x = x_ref[:, 0].reshape(per * n_tok, model).astype(F32)
     scale = lax.rsqrt(jnp.mean(x * x, axis=-1, keepdims=True) + EPS_NORM)
     normed = (x * scale * gain_ref[...]).astype(BF)
     normed_ref[0] = normed
@@ -554,12 +585,14 @@
 
 
 def project(x, gain, weight, router_weight, earlier=(), size=256):
-    n_micro, length, model = x.shape
+    n_seq, n_micro, n_tok, model = x.shape
+    length = n_seq * n_tok
     full = weight.shape[1]
+    blocks = pl.BlockSpec((size // n_tok, 1, n_tok, model), lambda m, i: (i, m, 0, 0))
     rows = lambda n: pl.BlockSpec((1, size, n), lambda m, i: (m, i, 0))
     return launch(
         project_kernel,
-        [rows(model), whole((1, model)), whole(weight.shape), whole(router_weight.shape)],
+        [blocks, whole((1, model)), whole(weight.shape), whole(router_weight.shape)],
         earlier,
         grid=(n_micro, length // size),
         out_specs=[rows(model), rows(full), rows(LANES)],
@@ -598,7 +631,7 @@
             out_specs=[one, one],
         ),
         out_shape=[made, made],
-        compiler_params=params("arbitrary"),
+        compiler_params=small_params("arbitrary"),
         cost_estimate=cost(1, 1.0),
         name="ring_add",
     )(table, ahead, behind, parts, parts, *earlier)
@@ -618,7 +651,7 @@
     lines_ref[...] = jnp.where(row == 3, lines / gain_ref[...], lines)
 
 
-def input_grads(normed, d_ext, w_ext, gain, full, earlier=(), size=128):
+def input_grads(normed, d_ext, w_ext, gain, full, earlier=(), size=256):
     n_micro, length, model = normed.shape
     wide = d_ext.shape[2]
     return launch(
@@ -645,33 +678,74 @@
     )(normed, d_ext, w_ext, gain[None])
 
 
-def place_heads_kernel(n_heads, slots, where, *refs):
-    parts, out_ref = refs[:-1], refs[-1]
+def place_heads_kernel(n_heads, copies, slots, cut, lines, where, *refs):
+    parts, out_ref, small_ref = refs[:-2], refs[-2], refs[-1]
     for j, part in enumerate(parts):
         at = where[0] ^ j
         for slot in range(slots):
             for h in range(n_heads):
                 to = (slot * n_heads + h) * LANES
-                value = part[h, :, slot * LANES : (slot + 1) * LANES]
+                value = part[h * copies, :cut, slot * LANES : (slot + 1) * LANES]
                 out_ref[at, :, to : to + LANES] = value.astype(F32)
-
-
-def place_heads(where, parts, slots):
-    n_heads, cut, full = parts[0].shape
-    shape = (len(parts), cut, full * n_heads)
-    return pl.pallas_call(
-        partial(place_heads_kernel, n_heads, slots),
+        for s in range(part.shape[0]):
+            high = part[s, cut : cut + lines].astype(F32)
+            low = part[s, cut + lines : cut + 2 * lines].astype(F32)
+            for r in range(len(parts)):
+
+                @pl.when(at == r)
+                def _(s=s, r=r, value=high + low):
+                    small_ref[s, r * lines : (r + 1) * lines] = value
+
+
+def place_heads(where, parts, n_heads, slots, cut, lines):
+    n_seq, rows, full = parts[0].shape
+    n_parts = len(parts)
+    shape = (n_parts, cut, full * n_heads)
+    small = (n_seq, n_parts * lines, full)
+    grad, values = pl.pallas_call(
+        partial(place_heads_kernel, n_heads, n_seq // n_heads, slots, cut, lines),
         grid_spec=pltpu.PrefetchScalarGridSpec(
             num_scalar_prefetch=1,
             grid=(1,),
             in_specs=[pl.BlockSpec(part.shape, lambda i, where: (0, 0, 0)) for part in parts],
-            out_specs=pl.BlockSpec(shape, lambda i, where: (0, 0, 0)),
+            out_specs=[
+                pl.BlockSpec(shape, lambda i, where: (0, 0, 0)),
+                pl.BlockSpec(small, lambda i, where: (0, 0, 0)),
+            ],
         ),
-        out_shape=jax.ShapeDtypeStruct(shape, F32),
-        compiler_params=params("arbitrary"),
+        out_shape=[jax.ShapeDtypeStruct(shape, F32), jax.ShapeDtypeStruct(small, F32)],
+        compiler_params=small_params("arbitrary"),
         cost_estimate=cost(1, 3.0),
         name="place_heads",
-    )(where, *parts).reshape(-1, full * n_heads)
+    )(where, *parts)
+    return grad.reshape(-1, full * n_heads), values
+
+
+def pack_kernel(lines, own_ref, got_ref, small_ref, out_ref):
+    n_seq, cut, full = own_ref.shape
+    rows = out_ref.shape[1]
+    tail = list(halves(small_ref[...]))
+    if rows > cut + 2 * lines:
+        tail.append(jnp.zeros((rows - cut - 2 * lines, full), BF))
+    tail = jnp.concatenate(tail, axis=0)
+    for s in range(n_seq):
+        out_ref[s, :cut] = (own_ref[s].astype(F32) + got_ref[s].astype(F32)).astype(BF)
+        out_ref[s, cut:] = tail
+
+
+def pack(own, got, small, rows, earlier=()):
+    n_seq, cut, full = own.shape
+    return launch(
+        partial(pack_kernel, small.shape[0]),
+        [whole(own.shape), whole(got.shape), whole(small.shape)],
+        earlier,
+        grid=(1,),
+        out_specs=whole((n_seq, rows, full)),
+        out_shape=jax.ShapeDtypeStruct((n_seq, rows, full), BF),
+        compiler_params=small_params("arbitrary"),
+        cost_estimate=cost(1, 1.5),
+        name="pack",
+    )(own, got, small)
 
 
 def place_units_kernel(unit_cut, unit_pad, n_seq, where, *refs):
@@ -692,25 +766,26 @@
         for j, part in enumerate(parts):
             chosen = jnp.where((unit == row) & (owner == (where[0] ^ j)), 1.0, 0.0).astype(BF)
             for half in range(2):
-                total[half] = total[half] + dot(part[half, :, low:high], chosen)
+                at = half * n_seq * unit_pad
+                total[half] = total[half] + dot(part[:, at + low : at + high], chosen)
         for half in range(2):
             to = half * hidden + block * LANES
             out_ref[:, to : to + LANES] = total[half]
 
 
 def place_units(where, parts, unit_cut, unit_pad, n_seq):
-    rows = parts[0].shape[1]
+    rows = parts[0].shape[0]
     shape = (rows, 2 * unit_cut * n_seq * len(parts))
     return pl.pallas_call(
         partial(place_units_kernel, unit_cut, unit_pad, n_seq),
         grid_spec=pltpu.PrefetchScalarGridSpec(
             num_scalar_prefetch=1,
             grid=(1,),
-            in_specs=[pl.BlockSpec(part.shape, lambda i, where: (0, 0, 0)) for part in parts],
+            in_specs=[pl.BlockSpec(part.shape, lambda i, where: (0, 0)) for part in parts],
             out_specs=pl.BlockSpec(shape, lambda i, where: (0, 0)),
         ),
         out_shape=jax.ShapeDtypeStruct(shape, F32),
-        compiler_params=params("arbitrary"),
+        compiler_params=small_params("arbitrary"),
         cost_estimate=cost(1, 5.0),
         name="place_units",
     )(where, *parts)
@@ -719,36 +794,60 @@
 def place_rows_kernel(where, *refs):
     parts, out_ref = refs[:-1], refs[-1]
     for j, part in enumerate(parts):
-        out_ref[where[0] ^ j] = part[: out_ref.shape[1]].astype(F32)
-
-
-def place_rows(where, parts, keep):
-    width = parts[0].shape[1]
-    shape = (len(parts), keep, width)
+        out_ref[where[0] ^ j] = part[...].astype(F32)
+
+
+def place_down_kernel(unit_pad, left, where, *refs):
+    parts, out_ref = refs[:-1], refs[-1]
+    _, keep, model = out_ref.shape
+    n_units = parts[0].shape[1] - left
+    rest = model - n_units
+    step = unit_pad * rest // n_units
+    for j, part in enumerate(parts):
+        at = where[0] ^ j
+        out_ref[at, :, :n_units] = part[:keep, left:].astype(F32)
+        for b in range(n_units // rest):
+            have = min(step, keep - b * step)
+            if have > 0:
+                value = part[unit_pad : unit_pad + have, left + b * rest : left + (b + 1) * rest]
+                out_ref[at, b * step : b * step + have, n_units:] = value.astype(F32)
+
+
+def place_rows(where, parts, shape, kernel=place_rows_kernel):
     return pl.pallas_call(
-        place_rows_kernel,
+        kernel,
         grid_spec=pltpu.PrefetchScalarGridSpec(
             num_scalar_prefetch=1,
             grid=(1,),
             in_specs=[pl.BlockSpec(part.shape, lambda i, where: (0, 0)) for part in parts],
-            out_specs=pl.BlockSpec(shape, lambda i, where: (0, 0, 0)),
+            out_specs=pl.BlockSpec((len(parts),) + shape, lambda i, where: (0, 0, 0)),
         ),
-        out_shape=jax.ShapeDtypeStruct(shape, F32),
-        compiler_params=params("arbitrary"),
+        out_shape=jax.ShapeDtypeStruct((len(parts),) + shape, F32),
+        compiler_params=small_params("arbitrary"),
         cost_estimate=cost(1, 2.0),
         name="place_rows",
-    )(where, *parts).reshape(-1, width)
-
-
-def feed_kernel(n_seq, first, mid_ref, d_top_ref, w_ref, act_ref, d_gu_ref, d_mid_ref, down_ref):
+    )(where, *parts).reshape(-1, shape[1])
+
+
+def place_down(where, parts, unit_pad, left, shape):
+    return place_rows(where, parts, shape, partial(place_down_kernel, unit_pad, left))
+
+
+def feed_kernel(n_seq, mid_ref, d_top_ref, w_ref, act_ref, d_gu_ref, down_ref, *d_mid_refs):
     n_units = act_ref.shape[1]
     model = mid_ref.shape[1]
     per = n_units // n_seq
 
     @pl.when(pl.program_id(0) == 0)
     def _():
-        lines = w_ref[:, 2 * n_units :].reshape(n_seq, model // n_seq, model)
-        down_ref[...] = lines[:, first : first + per].reshape(n_units, model)
+        lines = w_ref[:, 2 * n_units :].reshape(n_seq, model // n_seq, n_units)
+        rest = model - n_units
+        step = per * rest // n_units
+        for s in range(n_seq):
+            down_ref[s * per : (s + 1) * per, :n_units] = lines[s, :per]
+            for b in range(n_units // rest):
+                at = s * per + b * step
+                down_ref[at : at + step, n_units:] = lines[s, per:, b * rest : (b + 1) * rest]
 
     w_gate = w_ref[:, :n_units]
     w_up = w_ref[:, n_units : 2 * n_units]
@@ -763,87 +862,182 @@
     d_up = (d_act * silu).astype(BF)
     d_gu_ref[0] = d_gate
     d_gu_ref[1] = d_up
-    d_mid_ref[...] = (dot(d_gate, w_gate, 1, 1) + dot(d_up, w_up, 1, 1)).astype(BF)
-
-
-def feed(mid, d_top, weights, n_units, n_seq, first, size=256):
+    d_mid = (dot(d_gate, w_gate, 1, 1) + dot(d_up, w_up, 1, 1)).astype(BF)
+    for j, d_mid_ref in enumerate(d_mid_refs):
+
+        @pl.when(pl.program_id(0) == j)
+        def _(d_mid_ref=d_mid_ref):
+            d_mid_ref[...] = d_mid
+
+
+def feed(mid, d_top, weights, n_units, n_seq, n_parts):
     tokens, model = mid.shape
+    size = tokens // n_parts
     rows = lambda n: pl.BlockSpec((size, n), lambda i: (i, 0))
     return pl.pallas_call(
-        partial(feed_kernel, n_seq, first),
-        grid=(tokens // size,),
+        partial(feed_kernel, n_seq),
+        grid=(n_parts,),
         in_specs=[rows(model), rows(model), whole(weights.shape)],
         out_specs=[
             rows(n_units), pl.BlockSpec((2, size, n_units), lambda i: (0, i, 0)),
-            rows(model), whole((n_units, model)),
-        ],
+            whole((n_units, model)),
+        ] + [whole((size, model))] * n_parts,
         out_shape=[
             jax.ShapeDtypeStruct((tokens, n_units), BF),
             jax.ShapeDtypeStruct((2, tokens, n_units), BF),
-            jax.ShapeDtypeStruct((tokens, model), BF),
             jax.ShapeDtypeStruct((n_units, model), BF),
-        ],
+        ] + [jax.ShapeDtypeStruct((size, model), BF)] * n_parts,
         compiler_params=params("arbitrary"),
         cost_estimate=cost(1, 14.0),
         name="feed",
     )(mid, d_top, weights)
 
 
-def times_kernel(left_ref, right_ref, out_ref):
-    out_ref[...] = dot(left_ref[...], right_ref[...]).astype(BF)
-
-
-def times(left, right, earlier=(), size=256):
+def times_kernel(left_ref, right_ref, *out_refs):
+    value = dot(left_ref[...], right_ref[...]).astype(BF)
+    for j, out_ref in enumerate(out_refs):
+
+        @pl.when(pl.program_id(0) == j)
+        def _(out_ref=out_ref):
+            out_ref[...] = value
+
+
+def times(left, right, n_parts, earlier=()):
     tokens, inner = left.shape
-    rows = lambda n: pl.BlockSpec((size, n), lambda i: (i, 0))
+    size = tokens // n_parts
     return launch(
         times_kernel,
-        [rows(inner), whole(right.shape)],
+        [pl.BlockSpec((size, inner), lambda i: (i, 0)), whole(right.shape)],
         earlier,
-        grid=(tokens // size,),
-        out_specs=rows(right.shape[1]),
-        out_shape=jax.ShapeDtypeStruct((tokens, right.shape[1]), BF),
-        compiler_params=params("arbitrary"),
+        grid=(n_parts,),
+        out_specs=[whole((size, right.shape[1]))] * n_parts,
+        out_shape=[jax.ShapeDtypeStruct((size, right.shape[1]), BF)] * n_parts,
+        compiler_params=small_params("arbitrary"),
         cost_estimate=cost(1, 3.0),
         name="times",
     )(left, right)
 
 
-def feed_grads(mid, d_gu, rows, earlier=()):
+def feed_grads(mid, d_gu, g_down, n_seq, earlier=(), size=256):
     tokens, model = mid.shape
     n_units = d_gu.shape[2]
-    size = max(rows, 128)
-    per = size // rows
-
-    def body(mid_ref, d_gu_ref, out_ref):
+    shard, unit_pad = model // n_seq, n_units // n_seq
+    per = size // shard
+
+    def body(mid_ref, d_gu_ref, g_down_ref, out_ref):
         mid = mid_ref[...]
         for half in range(2):
             value = dot(mid, d_gu_ref[half], 0, 0).astype(BF)
-            for part in range(per):
-                out_ref[part, half] = value[part * rows : (part + 1) * rows]
+            out_ref[:, half * n_units : (half + 1) * n_units] = value
+        rest = model - n_units
+        step = unit_pad * rest // n_units
+        for part in range(per):
+            at, rows = part * shard, g_down_ref[part * unit_pad : (part + 1) * unit_pad]
+            out_ref[at : at + unit_pad, 2 * n_units :] = rows[:, :n_units]
+            for b in range(n_units // rest):
+                to = 2 * n_units + b * rest
+                out_ref[at + unit_pad : at + shard, to : to + rest] = rows[
+                    b * step : (b + 1) * step, n_units:
+                ]
 
     return launch(
         body,
-        [pl.BlockSpec((tokens, size), lambda i: (0, i)), whole(d_gu.shape)],
+        [
+            pl.BlockSpec((tokens, size), lambda i: (0, i)), whole(d_gu.shape),
+            pl.BlockSpec((per * unit_pad, model), lambda i: (i, 0)),
+        ],
         earlier,
         grid=(model // size,),
-        out_specs=pl.BlockSpec((per, 2, rows, n_units), lambda i: (i, 0, 0, 0)),
-        out_shape=jax.ShapeDtypeStruct((model // rows, 2, rows, n_units), BF),
+        out_specs=pl.BlockSpec((size, 3 * n_units), lambda i: (i, 0)),
+        out_shape=jax.ShapeDtypeStruct((model, 3 * n_units), BF),
         compiler_params=params("arbitrary"),
-        cost_estimate=cost(1, 6.0),
+        cost_estimate=cost(1, 7.0),
         name="feed_grads",
-    )(mid, d_gu)
+    )(mid, d_gu, g_down)
+
+
+def place_pieces_kernel(n_seq, where, *refs):
+    parts, out_ref = refs[:-1], refs[-1]
+    for j, part in enumerate(parts):
+        for s in range(n_seq):
+            out_ref[s, where[0] ^ j] = part[s]
+
+
+def place_pieces(where, parts):
+    n_seq, cut, width = parts[0].shape
+    shape = (n_seq, len(parts), cut, width)
+    return pl.pallas_call(
+        partial(place_pieces_kernel, n_seq),
+        grid_spec=pltpu.PrefetchScalarGridSpec(
+            num_scalar_prefetch=1,
+            grid=(1,),
+            in_specs=[pl.BlockSpec(part.shape, lambda i, where: (0, 0, 0)) for part in parts],
+            out_specs=pl.BlockSpec(shape, lambda i, where: (0, 0, 0, 0)),
+        ),
+        out_shape=jax.ShapeDtypeStruct(shape, BF),
+        compiler_params=small_params("arbitrary"),
+        cost_estimate=cost(1, 2.0),
+        name="place_pieces",
+    )(where, *parts).reshape(-1, width)
+
+
+def middle_kernel(copies, gated_ref, x_ref, w_ref, gain_ref, residual_ref, normed_ref, gated_out_ref):
+    n_heads = gated_ref.shape[0] // copies
+    total = x_ref[0].astype(F32)
+    for h in range(n_heads):
+        part = gated_ref[h * copies, 0]
+        gated_out_ref[0, :, h * LANES : (h + 1) * LANES] = part
+        total = total + dot(part, w_ref[h * LANES : (h + 1) * LANES])
+    scale = lax.rsqrt(jnp.mean(total * total, axis=-1, keepdims=True) + EPS_NORM)
+    residual_ref[0] = total
+    normed_ref[0] = (total * scale * gain_ref[...]).astype(BF)
+
+
+def middle(gated, x, w_out, gain, copies):
+    n_micro, n_tok, model = x.shape
+    n_seq = gated.shape[0]
+    rows = pl.BlockSpec((1, n_tok, model), lambda m: (m, 0, 0))
+    made = lambda kind: jax.ShapeDtypeStruct((n_micro, n_tok, model), kind)
+    return pl.pallas_call(
+        partial(middle_kernel, copies),
+        grid=(n_micro,),
+        in_specs=[
+            pl.BlockSpec((n_seq, 1, n_tok, LANES), lambda m: (0, m, 0, 0)),
+            rows, whole(w_out.shape), whole((1, model)),
+        ],
+        out_specs=[rows] * 3,
+        out_shape=[made(F32), made(BF), made(BF)],
+        compiler_params=small_params("arbitrary"),
+        cost_estimate=cost(1, 4.0),
+        name="middle",
+    )(gated, x, w_out, gain[None])
+
+
+def input_back_kernel(d_ext_ref, w_ref, out_ref):
+    value = dot(d_ext_ref[0], w_ref[...], 1, 1).astype(BF)
+    per, _, n_tok, _ = out_ref.shape
+    for part in range(per):
+        out_ref[part, 0] = value[part * n_tok : (part + 1) * n_tok]
+
+
+def input_back(d_ext, w_ext, n_tok, size=512):
+    n_micro, length, wide = d_ext.shape
+    model = w_ext.shape[0]
+    per = size // n_tok
+    return pl.pallas_call(
+        input_back_kernel,
+        grid=(n_micro, length // size),
+        in_specs=[pl.BlockSpec((1, size, wide), lambda m, s: (m, s, 0)), whole(w_ext.shape)],
+        out_specs=pl.BlockSpec((per, 1, n_tok, model), lambda m, s: (s, m, 0, 0)),
+        out_shape=jax.ShapeDtypeStruct((length // n_tok, n_micro, n_tok, model), BF),
+        compiler_params=params("arbitrary", "arbitrary"),
+        cost_estimate=cost(1, 7.0),
+        name="input_back",
+    )(d_ext, w_ext)
 
 
 def pick(stacked, at, axis=0):
     return lax.dynamic_index_in_dim(stacked, at, axis, False, allow_negative_indices=False)
-
-
-def tie(value, *earlier):
-    for other in earlier:
-        first = lax.slice(other, (0,) * other.ndim, (1,) * other.ndim).reshape(())
-        value = value + (first * 0).astype(value.dtype)
-    return value
 
 
 def exchange(value, axis, bit):
@@ -863,44 +1057,42 @@
     return [parts[j] for j in range(len(parts))]
 
 
-def row_scatter(parts):
+def row_gather_steps(value):
+    parts = {0: value}
+    for bit in reversed(bits("row")):
+        got = {j ^ bit: exchange(part, "row", bit) for j, part in parts.items()}
+        parts.update(got)
+        yield list(got.values())
+    return [parts[j] for j in range(len(parts))]
+
+
+def seq_scatter_steps(parts):
+    mine = lax.axis_index("seq")
+    for bit in reversed(bits("seq")):
+        parts = parts.reshape((2, bit) + parts.shape[1:])
+        side = (mine & bit) // bit
+        got = exchange(pick(parts, 1 - side).astype(BF), "seq", bit)
+        yield got
+        parts = pick(parts, side).astype(F32) + got.astype(F32)
+    return parts[0].astype(BF)
+
+
+def finish(steps):
+    try:
+        while True:
+            next(steps)
+    except StopIteration as end:
+        return end.value
+
+
+def row_scatter(parts, earlier=()):
     parts = dict(enumerate(parts))
     for bit in bits("row"):
         got = {j ^ bit: exchange(parts[j].astype(BF), "row", bit) for j in parts if j & bit}
+        if len(got) == 1:
+            got = {j: fence(part, *earlier) for j, part in got.items()}
         parts = {j: parts[j].astype(F32) + part.astype(F32) for j, part in got.items()}
     return parts[0]
-
-
-def row_gather_chain(value, gate):
-    parts = {0: value}
-    for bit in reversed(bits("row")):
-        got = {j ^ bit: exchange(fence(part, gate), "row", bit) for j, part in parts.items()}
-        parts.update(got)
-        gate = yield list(got.values())
-    return [parts[j] for j in range(len(parts))], gate
-
-
-def row_scatter_chain(parts, gate):
-    parts = dict(enumerate(parts))
-    for bit in bits("row"):
-        got = {j: exchange(fence(parts[j].astype(BF), gate), "row", bit) for j in parts if j & bit}
-        gate = yield list(got.values())
-        parts = {j ^ bit: parts[j ^ bit].astype(F32) + part.astype(F32) for j, part in got.items()}
-    return parts[0], gate
-
-
-def row_sum_chain(value, gate):
-    for bit in bits("row"):
-        got = exchange(fence(value, gate), "row", bit)
-        gate = yield [got]
-        value = value + got
-    return value, gate
-
-
-def wait(rounds):
-    for _ in range(rounds):
-        gate = yield []
-    return gate
 
 
 def ring():
@@ -920,50 +1112,22 @@
 
 def ring_gather(value, earlier):
     count, owner, ahead, behind = ring()
-    blocks = jnp.zeros(value.shape[:1] + (count,) + value.shape[1:], value.dtype)
+    blocks = jnp.zeros((count,) + value.shape, value.dtype)
     put = lambda blocks, block, k: lax.dynamic_update_index_in_dim(
-        blocks, block, owner(k), 1, allow_negative_indices=False
+        blocks, block, owner(k), 0, allow_negative_indices=False
     )
     blocks = put(blocks, value, 0)
     there, back = value, value
     for k in range(1, count // 2):
         there = lax.ppermute(there, "seq", ahead)
         back = lax.ppermute(back, "seq", behind)
-        if k == count // 4:
-            there = tie(there, earlier)
+        if k in earlier:
+            there = fence(there, *earlier[k])
         blocks = put(put(blocks, there, -k), back, k)
     cut = value.shape[1] // 2
     there = lax.ppermute(there[:, :cut], "seq", ahead)
     back = lax.ppermute(back[:, cut:], "seq", behind)
     return put(blocks, jnp.concatenate([there, back], axis=1), count // 2)
-
-
-def ring_scatter(parts, chains):
-    count, owner, ahead, behind = ring()
-    steps = jnp.arange(2, count + 1, dtype=jnp.int32)
-    table = owner(jnp.stack([-steps, steps], axis=1).reshape(-1))
-    there, back = pick(parts[0], owner(-1)), pick(parts[1], owner(1))
-    gate, live, done = None, dict(chains), {}
-    for k in range(count - 1):
-        there = lax.ppermute(there, "seq", ahead)
-        back = lax.ppermute(back, "seq", behind)
-        kind = BF if k < count - 2 else F32
-        there, back = ring_add(table, k, there, back, parts, kind, advance(live, gate, done))
-        gate = there
-    while live:
-        advance(live, gate, done)
-    return jnp.concatenate([there, back], axis=0), done
-
-
-def advance(live, gate, done):
-    needed = []
-    for name in list(live):
-        try:
-            needed.extend(live[name].send(gate))
-        except StopIteration as end:
-            done[name] = end.value[0]
-            del live[name]
-    return needed
 
 
 def rms_scale(values):
@@ -1025,10 +1189,12 @@
         stacked = jnp.stack(parts)
         return jnp.concatenate([pick(stacked, row ^ j) for j in range(n_row)], axis=axis)
 
+    where = jnp.stack([row, seq]).astype(jnp.int32)
+
     cut = w_in.shape[0] // n_row
     w_piece = pick(w_in.reshape(n_row, cut, slots, n_heads, head_dim), row)
     w_got = to_heads(w_piece.transpose(2, 0, 1, 3).reshape(n_heads, cut, full))
-    w_head = in_order(row_gather(w_got[:, None]), 1).reshape(model, full)
+    w_head = place_pieces(where, row_gather(w_got))
     w_rt = pick(w_router.reshape(model, -1, n_heads), head, 2)
     n_rt = w_rt.shape[1]
     w_rt = jnp.pad(w_rt, ((0, 0), (0, LANES - n_rt)))
@@ -1049,9 +1215,12 @@
     d_rows = jnp.concatenate(row_gather(d_top.astype(BF)), axis=0)
     x_own = tokens[:, 0].astype(F32).reshape(-1, model)
 
-    x_all = ring_gather(tokens[:, 0], w_got).reshape(n_micro, length, model)
+    x_all = ring_gather(
+        tokens[:, 0], {n_seq // 4: [w_got], n_seq // 2 - 1: [w_ext, w_rt, taps, par, d_rows]}
+    )
 
     out_cut = w_out.shape[0] // n_row
+    out_piece = lax.dynamic_slice_in_dim(w_out, row * out_cut, out_cut, 0)
     shard = w_out.shape[0]
     hidden = w_gu.shape[1] // 2
     unit_cut = hidden // n_seq // n_row
@@ -1060,53 +1229,54 @@
     gu_piece = pick(w_gu.reshape(shard, 2, n_seq, n_row, unit_cut), row, 3)
     gu_piece = jnp.pad(gu_piece, ((0, 0), (0, 0), (0, 0), (0, unit_pad - unit_cut)))
     down_piece = lax.dynamic_slice_in_dim(w_down, row * unit_cut, unit_cut, 0)
-    down_piece = jnp.pad(down_piece, ((shard - unit_pad, unit_pad - unit_cut), (0, 0)))
+    down_piece = jnp.pad(down_piece, ((0, unit_pad - unit_cut), (0, 0)))
+    beside = down_piece[:, n_units:]
+    beside = beside.reshape(n_units // beside.shape[1], -1, beside.shape[1])
+    beside = jnp.concatenate(list(beside), axis=1)
+    down_piece = jnp.concatenate([down_piece[:, :n_units], beside])
     weights = jnp.concatenate([gu_piece.reshape(shard, -1), down_piece], axis=1)
     weights = fence(weights, x_all)
     weights_all = lax.all_gather(weights, "seq", axis=0, tiled=True)
 
     normed_in, projected, router = project(x_all, norm1_gain, w_head, w_rt, [d_rows, weights])
-    out_piece = lax.dynamic_slice_in_dim(w_out, row * out_cut, out_cut, 0)
     out_piece = jnp.broadcast_to(out_piece[None], (n_seq,) + out_piece.shape)
-    out_got = lax.all_to_all(fence(out_piece, projected), "seq", 0, 0, tiled=True)
+    out_got = seq_parts(fence(out_piece, projected))
     prep = prepare(projected, router, taps, par, width)
-    full_out = in_order([part[:, None] for part in row_gather(fence(out_got, prep[0]))], 1)
-    full_out = full_out.reshape(model, model)
-    sent, *kept = scan_states(prep, router, projected, par, gate_at)
-    gated = sent.reshape(n_micro, n_seq, n_tok, head_dim).transpose(1, 0, 2, 3)
-    gated = from_heads(gated).transpose(1, 2, 0, 3).reshape(-1, model)
-
-    residual = x_own + matmul("tc,cd->td", gated, full_out)
+    full_out = place_pieces(where, row_gather(fence(out_got, prep[0])))
+    gated, *kept = scan_states(prep, router, projected, par, gate_at, n_tok)
+
+    residual, normed_mid, gated = middle(
+        seq_parts(gated), tokens[:, 0], full_out, norm2_gain, copies
+    )
+    residual, normed_mid, gated = (
+        value.reshape(-1, model) for value in (residual, normed_mid, gated)
+    )
     scale_mid = rms_scale(residual)
-    mid_rows = jnp.concatenate(
-        row_gather((residual * scale_mid * norm2_gain).astype(BF)), axis=0
+    mid_rows = jnp.concatenate(row_gather(normed_mid), axis=0)
+    act, d_gu, down, *d_mid = feed(
+        mid_rows, d_rows, weights_all, n_units, n_seq, n_row
     )
-    act, d_gu, d_mid, down = feed(
-        mid_rows, d_rows, weights_all, n_units, n_seq, shard - unit_pad
-    )
-    d_mid = row_scatter(list(d_mid.reshape(n_row, -1, model)))
+    g_down = matmul("tf,td->fd", act, d_rows, BF)
+    g_feed = feed_grads(mid_rows, d_gu, g_down, n_seq)
+    g_feed_sum = lax.psum_scatter(g_feed, "seq", scatter_dimension=0, tiled=True)
+    d_mid = row_scatter(d_mid, [g_feed])
 
     def row_parts(value, axis):
         return [pick(value, row ^ j, axis) for j in range(n_row)]
 
-    g_gu = feed_grads(mid_rows, d_gu, shard)
-    g_gu_sum = lax.psum_scatter(g_gu, "seq", scatter_dimension=0, tiled=True)[0]
-    g_down = matmul("tf,td->fd", act, d_rows, BF)
-    g_down_sum = lax.psum_scatter(g_down, "seq", scatter_dimension=0, tiled=True)
-
-    d_mid = tie(d_mid, g_gu, g_down)
     g_norm2 = jnp.sum(d_mid * residual * scale_mid, axis=0)
     d_residual = d_top + rms_back(d_mid * norm2_gain, residual, scale_mid)
     d_low = d_residual.astype(BF)
     d_sent = matmul("td,cd->tc", d_low, full_out, BF)
     d_gated = d_sent.reshape(n_micro, n_tok, n_heads, head_dim).transpose(2, 0, 1, 3)
-    d_gated = to_heads(d_gated).transpose(1, 0, 2, 3).reshape(n_micro, length, head_dim)
-
-    mlp = times(act, down, [d_sent])
-    out = (residual + row_scatter(list(mlp.reshape(n_row, -1, model)))).astype(BF)
-    out = out.reshape(n_micro, 1, n_tok, model)
-    g_out = matmul("tc,td->cd", tie(gated, d_sent), d_low).reshape(n_seq, n_row, out_cut, model)
-    g_out = row_scatter(row_parts(g_out, 1)).astype(BF)
+    d_gated = to_heads(d_gated)
+
+    mlp = times(act, down, n_row, [d_sent])
+    out = residual + row_scatter(mlp)
+    out = out.astype(BF).reshape(n_micro, 1, n_tok, model)
+    g_out_full = matmul("tc,td->cd", fence(gated, d_sent), d_low)
+    g_out = g_out_full
+    g_out = row_scatter(row_parts(g_out.reshape(n_seq, n_row, out_cut, model), 1)).astype(BF)
 
     mixed, news, state = kept
     d_mixed, d_news, d_state, d_gate_pre, g_head = scan_back(
@@ -1114,85 +1284,71 @@
     )
     d_ext, g_taps, g_par = mixer_grads(
         prep, router, projected, taps, par, width,
-        news, state, d_mixed, d_news, d_state, d_gate_pre,
+        news, state, d_mixed, d_news, d_state, d_gate_pre, [g_out, out],
     )
     if copies > 1:
         mine = (seq % copies == 0).astype(F32)
         d_ext = d_ext * mine.astype(BF)
         g_taps, g_par, g_head = g_taps * mine, g_par * mine, g_head * mine
-    d_in = matmul("mtc,dc->mtd", d_ext, w_ext, BF).reshape(n_micro, n_seq, n_tok, model)
-    g_in, in_lines = input_grads(normed_in, d_ext, w_ext, norm1_gain, full, [d_in])
-    where = row.astype(jnp.int32).reshape(1)
-
-    def input_chain():
-        gate = yield [g_in]
-        parts = row_parts(g_in.reshape(n_seq, n_row, cut, full), 1)
-        part, gate = yield from row_scatter_chain(parts, gate)
-        got = from_heads(fence(part.astype(BF), gate))
-        gate = yield from wait(1)
-        gate = yield [got]
-        return (yield from row_gather_chain(got, gate))
-
-    def small_chain():
-        gate = yield from wait(1)
-        padded = lambda value: jnp.pad(value, ((0, 0), (0, model - value.shape[1])))
-        scalars = jnp.concatenate([g_head[:1], g_par[1:2], g_par[2:3]], axis=1)
-        packed = [in_lines[: n_rt + 1], g_norm2[None], padded(scalars), padded(g_taps[:n_taps])]
-        packed, gate = yield from row_sum_chain(jnp.concatenate(packed), gate)
-        gate = yield from wait(1)
-        packed = jnp.broadcast_to(packed[None], (n_seq,) + packed.shape)
-        got = lax.all_to_all(fence(packed, gate), "seq", 0, 0, tiled=True)
-        gate = yield from wait(1)
-        gate = yield [got]
-        return got, gate
-
-    def output_chain():
-        gate = yield from wait(1)
-        got = seq_parts(fence(g_out, gate))
-        gate = yield from wait(1)
-        gate = yield [got]
-        got = jnp.sum(got.astype(F32), axis=0).astype(BF)
-        return (yield from row_gather_chain(got, gate))
-
-    def feed_chain(value, rounds):
-        gate = yield from wait(rounds)
-        return (yield from row_gather_chain(value, gate))
-
-    d_in, done = ring_scatter(
-        d_in,
-        {
-            "input": input_chain(),
-            "small": small_chain(),
-            "output": output_chain(),
-            "down": feed_chain(g_down_sum, 1),
-            "gu": feed_chain(g_gu_sum, 4),
-        },
-    )
+    d_in_part = input_back(d_ext, w_ext, n_tok).reshape(-1, model)
+    d_in = lax.psum_scatter(d_in_part, "seq", scatter_dimension=0, tiled=True)
+    g_in, in_lines = input_grads(normed_in, d_ext, w_ext, norm1_gain, full, [d_in_part])
+    fill = lambda value: jnp.pad(value, ((0, 0), (0, full - value.shape[1])))
+    scalars = jnp.concatenate([g_head[:1], g_par[1:2], g_par[2:3]], axis=1)
+    vectors = jnp.concatenate([in_lines[: n_rt + 1], g_norm2[None]]).reshape(-1, model // 2)
+    small = jnp.concatenate([fill(vectors), fill(scalars), fill(g_taps[:n_taps])])
+    n_vec = vectors.shape[0]
+    lines = -(-small.shape[0] // n_row)
+    small = jnp.pad(small, ((0, n_row * lines - small.shape[0]), (0, 0))).reshape(n_row, lines, full)
+
+    parts = dict(enumerate(row_parts(g_in.reshape(n_seq, n_row, cut, full), 1)))
+    smalls = dict(enumerate(row_parts(small, 0)))
+    for bit in bits("row"):
+        got = {j ^ bit: exchange(parts[j], "row", bit) for j in parts if j & bit}
+        got_small = {j ^ bit: exchange(smalls[j], "row", bit) for j in smalls if j & bit}
+        smalls = {j: smalls[j] + part for j, part in got_small.items()}
+        if len(got) > 1:
+            parts = {
+                j: (parts[j].astype(F32) + part.astype(F32)).astype(BF) for j, part in got.items()
+            }
+    g_out_steps = seq_scatter_steps(fence(g_out, parts[0]))
+    rows = cut + -(-2 * lines // 16) * 16
+    g_in_got = seq_parts(pack(parts[0], got[0], smalls[0], rows, [next(g_out_steps)]))
+    feed_steps = row_gather_steps(fence(g_feed_sum, got[0]))
+    g_in_got = fence(g_in_got, *next(feed_steps), next(g_out_steps))
+    in_steps = row_gather_steps(g_in_got)
+    first_in = next(in_steps)
+    g_out_sum = finish(g_out_steps)
+    g_feed_all = finish(feed_steps)
+    g_out_all = row_gather(g_out_sum)
+    grad_out = place_rows(where, g_out_all, (out_cut, model))
+    grad_down = place_down(where, g_feed_all, unit_pad, 2 * n_units, (unit_cut, model))
+    grad_gu = place_units(where, g_feed_all, unit_cut, unit_pad, n_seq)
+    g_in_all = finish(in_steps)
+    grad_in, small = place_heads(where, g_in_all, n_heads, slots, cut, lines)
+    d_in = fence(d_in, grad_in, grad_gu, grad_down, grad_out).astype(F32)
     grad_tokens = d_residual + rms_back(d_in * norm1_gain, x_own, rms_scale(x_own))
     grad_tokens = grad_tokens.reshape(n_micro, 1, n_tok, model)
-    grad_out = place_rows(where, done["output"], out_cut)
-    grad_down = place_rows(where, done["down"], unit_cut)
-    grad_gu = place_units(where, done["gu"], unit_cut, unit_pad, n_seq)
-    grad_in = place_heads(where, done["input"], slots)
-    small = done["small"]
-
-    total = jnp.sum(small[:, n_rt : n_rt + 3], axis=0)
+    total = jnp.sum(small[:, 2 * n_rt : n_vec + 1], axis=0)
+    norms = total[:4, : model // 2].reshape(2, model)
     heads = small[::copies]
-    conv_sum = heads[:, n_rt + 3 :, :width].reshape(n_heads, n_taps, gate_at, head_dim)
+    conv_sum = heads[:, n_vec + 1 : n_vec + 1 + n_taps, :width]
+    conv_sum = conv_sum.reshape(n_heads, n_taps, gate_at, head_dim)
     conv_sum = conv_sum.transpose(1, 2, 0, 3).reshape(n_taps, conv_width)
-    router_sum = heads[:, :n_rt].transpose(2, 1, 0).reshape(model, n_rt * n_heads)
+    router_sum = heads[:, : 2 * n_rt, : model // 2].reshape(n_heads, n_rt, model)
+    router_sum = router_sum.transpose(2, 1, 0).reshape(model, n_rt * n_heads)
     return (
         out,
         grad_tokens,
-        total[0],
+        norms[0],
         grad_in,
         router_sum,
         conv_sum,
-        heads[:, n_rt + 2, LANES + 2],
-        heads[:, n_rt + 2, 2 * LANES + 2],
-        total[2, :head_dim],
+        heads[:, n_vec, LANES + 2],
+        heads[:, n_vec, 2 * LANES + 2],
+        total[4, :head_dim],
         grad_out,
-        total[1],
+        norms[1],
         grad_gu,
         grad_down,
     )

time: 490 us -> 469 us (0.957)
  waiting for transfers between devices: 98 us -> 142 us
  local copies, waits for them, and re-layouts: 78.7 us -> 50.7 us
  starting transfers between devices: 76.3 us -> 53.5 us
  matrix products: 15.4 us -> 8.22 us
    ppermute x38 -> x39, waiting for transfers between devices: 41.8 us -> 79.5 us  [exchange(): return lax.ppermute(value, axis, [(i, i ^ bit) for i in range(count)])]
    all_to_all x4 -> x0, waiting for transfers between devices: 29.8 us -> none  [the longest x2 27.8 us: from_heads(): got = lax.all_to_all(value, 'seq', 0, 0, tiled=True)]
    all_to_all x1 -> x3, waiting for transfers between devices: 0.01 us -> 27.6 us  [seq_parts(): return lax.all_to_all(value, 'seq', 0, 0, tiled=True)]
    unnamed x159 -> x90, local copies, waits for them, and re-layouts: 41.3 us -> 17 us
    all_to_all x4 -> x0, starting transfers between devices: 19.3 us -> none  [the longest x2 8.75 us: from_heads(): got = lax.all_to_all(value, 'seq', 0, 0, tiled=True)]
    ppermute x14 -> x0, starting transfers between devices: 15.1 us -> none  [the longest x7 11.5 us: ring_scatter(): there = lax.ppermute(there, 'seq', ahead)]
    ppermute x14 -> x0, waiting for transfers between devices: 14.3 us -> none  [the longest x7 12.6 us: ring_scatter(): back = lax.ppermute(back, 'seq', behind)]
    all_to_all x2, waiting for transfers between devices: 0.01 us -> 12.4 us  [to_heads(): lax.all_to_all(jnp.repeat(value, copies, axis=0), 'seq', 0, 0, tiled=True)]
  transfers between devices with their start and end apart: 70 -> 55, of which waited for: 21 -> 21; matrix products, arithmetic and copies ran while one was open for 20% -> 15% of each run, Pallas kernels for 29% -> 31%
where the time goes in v3:
time: 469 us; the launch traced here: 462 us
  Pallas kernels  161 us (34%)
  waiting for transfers between devices  142 us (30%)
  starting transfers between devices  53.5 us (11%)
  local copies, waits for them, and re-layouts  50.7 us (11%)
  other arithmetic  31 us (7%)
  between operations  14.8 us (3%)
  matrix products  8.22 us (2%)
    pallas_call x9, Pallas kernels, launch(): return lambda *operands: called(*operands, *earlier)  119 us
    ppermute x39, waiting for transfers between devices, exchange(): return lax.ppermute(value, axis, [(i, i ^ bit) for i in range(count)])  79.5 us
    all_to_all x3, waiting for transfers between devices, seq_parts(): return lax.all_to_all(value, 'seq', 0, 0, tiled=True)  27.6 us
    ppermute x39, starting transfers between devices, exchange(): return lax.ppermute(value, axis, [(i, i ^ bit) for i in range(count)])  21.4 us
    pallas_call x1, Pallas kernels, feed(): pl.pallas_call(partial(feed_kernel, n_seq), grid=(n_parts,), in_specs=[ro...  17.5 us
    unnamed x90, local copies, waits for them, and re-layouts  17 us
    all_to_all x3, starting transfers between devices, seq_parts(): return lax.all_to_all(value, 'seq', 0, 0, tiled=True)  12.5 us
    all_to_all x2, waiting for transfers between devices, to_heads(): lax.all_to_all(jnp.repeat(value, copies, axis=0), 'seq', 0, 0, tiled=True)  12.4 us
  transfers between devices with their start and end apart: 55, of which 21 were waited for; matrix products, arithmetic and copies ran while one was open for 15% of the time, Pallas kernels for 31%

profile of v3, /device:TPU:0, one launch (start us, length us, event | category | flops | bytes accessed | tf_op | source)
XLA Modules:
  0.0 461.9 jit_solution(17803589194081811397)
XLA Ops:
  7.2 3.1 collective-permute-start
  18.1 5.8 %all-to-all-start = ((bf16[8,32,768]{2,1,0:T(8,128)(2,1)}), bf16[8,32,768]{2,1,0:T(8,128)(2,1)S(1)}, u32[]{:S(2)}, u32[]{:S(2)}) async-start(bf16[8,32,768]{2,1,0:T(8,128)(2,1)} %reshape_broadcast_in_dim_reshape.3), calls=%async_computation | async-start | bytes 786432 | tf_op jit(solution)/shard_map/all_to_all | solution.py:1179
  43.7 6.9 %collective-permute-done.2.refs_0_ = bf16[2,128,1024]{2,1,0:T(8,128)(2,1)S(1)} collective-permute-done((bf16[2,128,1024]{2,1,0:T(8,128)(2,1)}, bf16[2,128,1024]{2,1,0:T(8,128)(2,1)S(1)}, u32[]{:S(2)}, u32[]{:S(2)}) %collective-permute-start.2) | collective-permute-done | bytes 524320 | tf_op jit(solution)/shard_map/ppermute | solution.py:1122
  62.6 4.6 collective-permute-done.4.refs_0_
  76.7 3.8 collective-permute-done.13
  81.4 10.6 %project.1 = (bf16[2,1024,1024]{2,1,0:T(8,128)(2,1)}, bf16[2,1024,768]{2,1,0:T(8,128)(2,1)}, f32[2,1024,128]{2,1,0:T(8,128)}) custom-call(bf16[8,2,128,1024]{3,2,1,0:T(8,128)(2,1)} %fusion.20.refs_1_.refs_0_, f32[1,1024]{1,0:T(1,128)} %bitcast.252, bf16[1024,768]{1,0:T(8,128)(2,1)} %bitcast.209, bf16[1024,128]{1,0:T(8,128)(2,1)} %copy-done.24, ...), custom_call_target="tpu_custom_call" | custom-call | flops 12320000000 | bytes 1048576 | tf_op jit(solution)/shard_map/project/pallas_call | solution.py:417
  92.9 5.2 %all-to-all-start.2 = ((bf16[8,32,1024]{2,1,0:T(8,128)(2,1)}), bf16[8,32,1024]{2,1,0:T(8,128)(2,1)S(1)}, u32[]{:S(2)}, u32[]{:S(2)}) async-start(bf16[8,32,1024]{2,1,0:T(8,128)(2,1)} %fence.14), calls=%async_computation.2 | async-start | bytes 1048576 | tf_op jit(solution)/shard_map/all_to_all | solution.py:1182
  98.1 22.4 %mixer_prepare.1 = (f32[2,16,128,128]{3,2,1,0:T(8,128)}, f32[2,16,128,128]{3,2,1,0:T(8,128)}, f32[2,16,128,128]{3,2,1,0:T(8,128)}, f32[2,16,64,128]{3,2,1,0:T(8,...) custom-call(bf16[2,1024,768]{2,1,0:T(8,128)(2,1)} %get-tuple-element.52.refs_0_.refs_1_.refs_6_.refs_5_, ...), custom_call_target="tpu_custom_call" | custom-call | flops 26400000000 | bytes 1048576 | tf_op jit(solution)/shard_map/mixer_prepare/pallas_call | solution.py:417
  125.3 14.3 %mixer_scan.1 = (bf16[8,2,128,128]{3,2,1,0:T(8,128)(2,1)}, f32[2,16,64,128]{3,2,1,0:T(8,128)}, f32[2,16,128,128]{3,2,1,0:T(8,128)}, f32[2,16,128,128]{3,2,1,0:T(8,128)}) custom-call(f32[2,16,128,128]{3,2,1,0:T(8,128)} %get-tuple-element.54.refs_0_, f32[2,16,128,128]{3,2,1,0:T(8,128)} %get-tuple-element.55.refs_1_, ...), custom_call_target="tpu_custom_call" | custom-call | flops 17600000000 | bytes 1048576 | tf_op jit(solution)/shard_map/mixer_scan/pallas_call | solution.py:417
  139.6 3.5 all-to-all-start.1
  148.2 25.0 %all-to-all-done.1.gated_ref = bf16[8,2,128,128]{3,2,1,0:T(8,128)(2,1)S(1)} async-done(((bf16[8,2,128,128]{3,2,1,0:T(8,128)(2,1)}), bf16[8,2,128,128]{3,2,1,0:T(8,128)(2,1)S(1)}, u32[]{:S(2)}, u32[]{:S(2)}) %all-to-all-start.1) | async-done | bytes 524320 | tf_op jit(solution)/shard_map/all_to_all | solution.py:1182
  173.2 3.3 middle.1
  177.2 11.1 %collective-permute-done.18 = bf16[256,1024]{1,0:T(8,128)(2,1)S(1)} collective-permute-done((bf16[256,1024]{1,0:T(8,128)(2,1)S(1)}, bf16[256,1024]{1,0:T(8,128)(2,1)S(1)}, u32[]{:S(2)}, u32[]{:S(2)}) %collective-permute-start.18) | collective-permute-done | bytes 524320 | tf_op jit(solution)/shard_map/ppermute | solution.py:1045
  192.9 17.5 %feed.1 = (bf16[1024,768]{1,0:T(8,128)(2,1)}, bf16[2,1024,768]{2,1,0:T(8,128)(2,1)}, bf16[768,1024]{1,0:T(8,128)(2,1)}, bf16[256,1024]{1,0:T(8,128)(2,1)}, bf16[...) custom-call(bf16[1024,1024]{1,0:T(8,128)(2,1)} %pad_maximum_fusion.1.mid_ref.refs_0_, ...), custom_call_target="tpu_custom_call" | custom-call | flops 15399999488 | bytes 1048576 | tf_op jit(solution)/shard_map/feed/pallas_call | solution.py:877
  211.0 4.8 %convolution_convert_fusion.refs_2_ = bf16[768,1024]{1,0:T(8,128)(2,1)} fusion(bf16[1024,768]{1,0:T(8,128)(2,1)} %get-tuple-element.63.refs_0_, bf16[256,1024]{1,0:T(8,128)(2,1)S(1)} %copy-done.32, bf16[256,1024]{1,0:T(8,128)(2,1)} %collective-permute-done.9, bf16[256,1024]{1,0:T(8,128)(2,1)} %collective-permute-done.8, bf16[256,1024]{1,0:T(8,128)(2,1)} %fusion.1), kind=kOutput, calls=%fused_computation.3 | convolution fusion | flops 1619787776 | bytes 5242880 | tf_op jit(solution)/shard_map/tf,td->fd/dot_general | solution.py:1144
  215.8 8.0 %feed_grads.1.refs_1_ = bf16[1024,2304]{1,0:T(8,128)(2,1)} custom-call(bf16[1024,1024]{1,0:T(8,128)(2,1)} %pad_maximum_fusion.1.mid_ref.refs_0_, bf16[2,1024,768]{2,1,0:T(8,128)(2,1)} %get-tuple-element.69.refs_1_, bf16[768,1024]{1,0:T(8,128)(2,1)} %convolution_convert_fusion.refs_2_), custom_call_target="tpu_custom_call" | custom-call | flops 7699999744 | bytes 1048576 | tf_op jit(solution)/shard_map/feed_grads/pallas_call | solution.py:417
  227.0 12.1 %collective-permute-done.22.refs_0_ = bf16[256,1024]{1,0:T(8,128)(2,1)S(1)} collective-permute-done((bf16[256,1024]{1,0:T(8,128)(2,1)S(1)}, bf16[256,1024]{1,0:T(8,128)(2,1)S(1)}, u32[]{:S(2)}, u32[]{:S(2)}) %collective-permute-start.22) | collective-permute-done | bytes 524320 | tf_op jit(solution)/shard_map/ppermute | solution.py:1045
  251.4 4.1 all-to-all-start.3
  255.8 5.3 %times.1 = (bf16[256,1024]{1,0:T(8,128)(2,1)S(1)}, bf16[256,1024]{1,0:T(8,128)(2,1)S(1)}, bf16[256,1024]{1,0:T(8,128)(2,1)S(1)}, bf16[256,1024]{1,0:T(8,128)(2,1)}) custom-call(bf16[1024,768]{1,0:T(8,128)(2,1)} %get-tuple-element.63.refs_0_, bf16[768,1024]{1,0:T(8,128)(2,1)} %get-tuple-element.64.refs_1_, bf16[256,1024]{1,0:T(8,128)(2,1)S(1)} %copy-done.3), custom_call_target="tpu_custom_call" | custom-call | flops 3300000000 | bytes 1048576 | tf_op jit(solution)/shard_map/times/pallas_call | solution.py:417
  269.4 12.4 %all-to-all-done.3.refs_8_ = bf16[8,2,128,128]{3,2,1,0:T(8,128)(2,1)} async-done(((bf16[8,2,128,128]{3,2,1,0:T(8,128)(2,1)}), bf16[8,2,128,128]{3,2,1,0:T(8,128)(2,1)}, u32[]{:S(2)}, u32[]{:S(2)}) %all-to-all-start.3) | async-done | bytes 524320 | tf_op jit(solution)/shard_map/all_to_all | solution.py:1179
  281.8 13.3 %mixer_scan_back.1 = (f32[2,16,64,128]{3,2,1,0:T(8,128)}, f32[2,16,128,128]{3,2,1,0:T(8,128)}, f32[2,16,128,128]{3,2,1,0:T(8,128)}, bf16[2,1024,128]{2,1,0:T(8,128)(2,1)}, f32[8,128]{1,0:T(8,128)}) custom-call(f32[2,16,128,128]{3,2,1,0:T(8,128)} %get-tuple-element.54.refs_0_, f32[2,16,64,128]{3,2,1,0:T(8,128)} %get-tuple-element.56.refs_2_.refs_1_.refs_6_, ...), custom_call_target="tpu_custom_call" | custom-call | flops 14080000000 | bytes 1048576 | tf_op jit(solution)/shard_map/mixer_scan_back/pallas_call | solution.py:417
  300.0 34.7 %mixer_grads.1 = (bf16[2,1024,896]{2,1,0:T(8,128)(2,1)}, f32[8,640]{1,0:T(8,128)}, f32[8,128]{1,0:T(8,128)}) custom-call(bf16[2,1024,768]{2,1,0:T(8,128)(2,1)} %get-tuple-element.52.refs_0_.refs_1_.refs_6_.refs_5_, bf16[2,1024,768]{2,1,0:T(8,128)(2,1)} %get-tuple-element.52.refs_0_.refs_1_.refs_6_.refs_5_, ...), custom_call_target="tpu_custom_call" | custom-call | flops 35200000000 | bytes 1048576 | tf_op jit(solution)/shard_map/mixer_grads/pallas_call | solution.py:417
  334.8 8.3 %input_back.1 = bf16[8,2,128,1024]{3,2,1,0:T(8,128)(2,1)} custom-call(bf16[2,1024,896]{2,1,0:T(8,128)(2,1)} %get-tuple-element.82.d_ext_ref.refs_1_, bf16[1024,896]{1,0:T(8,128)(2,1)} %pad_maximum_fusion.2.refs_1_.w_ref.refs_2_), custom_call_target="tpu_custom_call" | custom-call | flops 7699999744 | bytes 1048576 | tf_op jit(solution)/shard_map/input_back/pallas_call | solution.py:1027
  343.8 9.0 %input_grads.1 = (bf16[1024,768]{1,0:T(8,128)(2,1)}, f32[8,1024]{1,0:T(8,128)}) custom-call(bf16[2,1024,1024]{2,1,0:T(8,128)(2,1)} %get-tuple-element.83.refs_0_, bf16[2,1024,896]{2,1,0:T(8,128)(2,1)} %get-tuple-element.82.d_ext_ref.refs_1_, bf16[1024,896]{1,0:T(8,128)(2,1)} %pad_maximum_fusion.2.refs_1_.w_ref.refs_2_, f32[1,1024]{1,0:T(1,128)} %bitcast.253, ...), custom_call_target="tpu_custom_call" | custom-call | flops 7699999744 | bytes 1048576 | tf_op jit(solution)/shard_map/input_grads/pallas_call | solution.py:417
  362.1 9.3 %collective-permute-done.34 = f32[4,768]{1,0:T(4,128)S(1)} collective-permute-done((f32[4,768]{1,0:T(4,128)S(1)}, f32[4,768]{1,0:T(4,128)S(1)}, u32[]{:S(2)}, u32[]{:S(2)}) %collective-permute-start.34) | collective-permute-done | bytes 12320 | tf_op jit(solution)/shard_map/ppermute | solution.py:1045
  371.4 16.4 %collective-permute-done.35.refs_3_ = bf16[4,32,1024]{2,1,0:T(8,128)(2,1)S(1)} collective-permute-done((bf16[4,32,1024]{2,1,0:T(8,128)(2,1)S(1)}, bf16[4,32,1024]{2,1,0:T(8,128)(2,1)S(1)}, u32[]{:S(2)}, u32[]{:S(2)}) %collective-permute-start.35) | collective-permute-done | bytes 262176 | tf_op jit(solution)/shard_map/ppermute | solution.py:1045
  389.7 3.8 all-to-all-start.4
  397.2 10.9 %collective-permute-done.37.refs_2_ = bf16[2,32,1024]{2,1,0:T(8,128)(2,1)S(1)} collective-permute-done((bf16[2,32,1024]{2,1,0:T(8,128)(2,1)S(1)}, bf16[2,32,1024]{2,1,0:T(8,128)(2,1)S(1)}, u32[]{:S(2)}, u32[]{:S(2)}) %collective-permute-start.37) | collective-permute-done | bytes 131104 | tf_op jit(solution)/shard_map/ppermute | solution.py:1045
  409.8 3.1 collective-permute-done.43
  420.5 11.0 %collective-permute-done.39.refs_2_ = bf16[8,48,768]{2,1,0:T(8,128)(2,1)S(1)} collective-permute-done((bf16[8,48,768]{2,1,0:T(8,128)(2,1)}, bf16[8,48,768]{2,1,0:T(8,128)(2,1)S(1)}, u32[]{:S(2)}, u32[]{:S(2)}) %collective-permute-start.39) | collective-permute-done | bytes 589856 | tf_op jit(solution)/shard_map/ppermute | solution.py:1045
  433.2 4.9 %place_units.1.refs_2_ = f32[128,5632]{1,0:T(8,128)} custom-call(s32[2]{0:T(128)S(1)} %pad_add_fusion.where, bf16[128,2304]{1,0:T(8,128)(2,1)S(1)} %copy-done.13, bf16[128,2304]{1,0:T(8,128)(2,1)S(1)} %collective-permute-done.41.refs_1_, bf16[128,2304]{1,0:T(8,128)(2,1)S(1)} %copy-done.15, bf16[128,2304]{1,0:T(8,128)(2,1)S(1)} %collective-permute-done.42.refs_3_), custom_call_target="tpu_custom_call" | custom-call | flops 5500000256 | bytes 1048576 | tf_op jit(solution)/shard_map/place_units/pallas_call | solution.py:779
  442.4 5.8 %reduce-scatter.3.cloned.1.call-done.refs_0_ = bf16[256,1024]{1,0:T(8,128)(2,1)} async-done(((bf16[2048,1024]{1,0:T(8,128)(2,1)}), bf16[256,1024]{1,0:T(8,128)(2,1)}) %reduce-scatter.3.cloned.1.call-update) | async-done | bytes 524304 | tf_op jit(solution)/shard_map/reduce_scatter | solution.py:1294
  (296 shorter events, 132.8 us)
Async XLA Ops:
  7.2 29.1 %collective-permute-start = (bf16[2,128,1024]{2,1,0:T(8,128)(2,1)}, bf16[2,128,1024]{2,1,0:T(8,128)(2,1)}, u32[]{:S(2)}, u32[]{:S(2)}) collective-permute-start(bf16[2,128,1024]{2,1,0:T(8,128)(2,1)} %bitcast.203), channel_id=1, source_target_pairs={{0,2},{2,4},{4,6},{6,7},{7,5},{5,3},{3,1},{1,0},{8,10},{10,12},{12... | collective-permute-start | bytes 1572872 | tf_op jit(solution)/shard_map/ppermute | solution.py:1122
  10.3 29.0 %collective-permute-start.1 = (bf16[2,128,1024]{2,1,0:T(8,128)(2,1)}, bf16[2,128,1024]{2,1,0:T(8,128)(2,1)}, u32[]{:S(2)}, u32[]{:S(2)}) collective-permute-start(bf16[2,128,1024]{2,1,0:T(8,128)(2,1)} %bitcast.204), channel_id=1, source_target_pairs={{2,0},{4,2},{6,4},{7,6},{5,7},{3,5},{1,3},{0,1},{10,8},{12,10},{14... | collective-permute-start | bytes 1572872 | tf_op jit(solution)/shard_map/ppermute | solution.py:1123
  13.0 26.4 %collective-permute-start.9 = (bf16[256,1024]{1,0:T(8,128)(2,1)}, bf16[256,1024]{1,0:T(8,128)(2,1)}, u32[]{:S(2)}, u32[]{:S(2)}) collective-permute-start(bf16[256,1024]{1,0:T(8,128)(2,1)} %fusion.1), channel_id=1, source_target_pairs={{0,16},{8,24},{16,0},{24,8},{1,17},{9,25},{17,1},{25,9},{2,18},{10... | collective-permute-start | bytes 1572872 | tf_op jit(solution)/shard_map/ppermute | solution.py:1045
  15.0 41.9 %collective-permute-start.8 = (bf16[256,1024]{1,0:T(8,128)(2,1)}, bf16[256,1024]{1,0:T(8,128)(2,1)}, u32[]{:S(2)}, u32[]{:S(2)}) collective-permute-start(bf16[256,1024]{1,0:T(8,128)(2,1)} %fusion.1), channel_id=1, source_target_pairs={{0,8},{8,0},{16,24},{24,16},{1,9},{9,1},{17,25},{25,17},{2,10},{10... | collective-permute-start | bytes 1572872 | tf_op jit(solution)/shard_map/ppermute | solution.py:1045
  18.1 23.2 %all-to-all-start = ((bf16[8,32,768]{2,1,0:T(8,128)(2,1)}), bf16[8,32,768]{2,1,0:T(8,128)(2,1)S(1)}, u32[]{:S(2)}, u32[]{:S(2)}) async-start(bf16[8,32,768]{2,1,0:T(8,128)(2,1)} %reshape_broadcast_in_dim_reshape.3), calls=%async_computation | async-start | bytes 786432 | tf_op jit(solution)/shard_map/all_to_all | solution.py:1179
  23.9 169.0 %all-gather.2.cloned.1.call-start = ((), (), s32[]{:S(2)}) async-start(), calls=%async_computation.7 | async-start | bytes 5308416 | tf_op jit(solution)/shard_map/all_gather | solution.py:1239
  36.3 14.3 %collective-permute-start.2 = (bf16[2,128,1024]{2,1,0:T(8,128)(2,1)}, bf16[2,128,1024]{2,1,0:T(8,128)(2,1)S(1)}, u32[]{:S(2)}, u32[]{:S(2)}) collective-permute-start(bf16[2,128,1024]{2,1,0:T(8,128)(2,1)} %collective-permute-done), channel_id=1, source_target_pairs={{0,2},{2,4},{4,6},{6,7},{7,5},{5,3},{3,1},{1,0},{8,10},{10,12},{12... | collective-permute-start | bytes 1572872 | tf_op jit(solution)/shard_map/ppermute | solution.py:1122
  39.3 14.0 %collective-permute-start.3 = (bf16[2,128,1024]{2,1,0:T(8,128)(2,1)}, bf16[2,128,1024]{2,1,0:T(8,128)(2,1)}, u32[]{:S(2)}, u32[]{:S(2)}) collective-permute-start(bf16[2,128,1024]{2,1,0:T(8,128)(2,1)} %collective-permute-done.1), channel_id=1, source_target_pairs={{2,0},{4,2},{6,4},{7,6},{5,7},{3,5},{1,3},{0,1},{10,8},{12,10},{14... | collective-permute-start | bytes 1572872 | tf_op jit(solution)/shard_map/ppermute | solution.py:1123
  39.4 17.8 %collective-permute-start.10 = (bf16[256,1024]{1,0:T(8,128)(2,1)}, bf16[256,1024]{1,0:T(8,128)(2,1)S(1)}, u32[]{:S(2)}, u32[]{:S(2)}) collective-permute-start(bf16[256,1024]{1,0:T(8,128)(2,1)} %collective-permute-done.9), channel_id=1, source_target_pairs={{0,8},{8,0},{16,24},{24,16},{1,9},{9,1},{17,25},{25,17},{2,10},{10... | collective-permute-start | bytes 1572872 | tf_op jit(solution)/shard_map/ppermute | solution.py:1045
  53.3 13.9 %collective-permute-start.4 = (bf16[2,128,1024]{2,1,0:T(8,128)(2,1)}, bf16[2,128,1024]{2,1,0:T(8,128)(2,1)}, u32[]{:S(2)}, u32[]{:S(2)}) collective-permute-start(bf16[2,128,1024]{2,1,0:T(8,128)(2,1)} %fence.11), channel_id=1, source_target_pairs={{0,2},{2,4},{4,6},{6,7},{7,5},{5,3},{3,1},{1,0},{8,10},{10,12},{12... | collective-permute-start | bytes 1572872 | tf_op jit(solution)/shard_map/ppermute | solution.py:1122
  56.9 14.7 %collective-permute-start.11 = (bf16[2,128,1024]{2,1,0:T(8,128)(2,1)}, bf16[2,128,1024]{2,1,0:T(8,128)(2,1)}, u32[]{:S(2)}, u32[]{:S(2)}) collective-permute-start(bf16[2,128,1024]{2,1,0:T(8,128)(2,1)} %collective-permute-done.3), channel_id=1, source_target_pairs={{2,0},{4,2},{6,4},{7,6},{5,7},{3,5},{1,3},{0,1},{10,8},{12,10},{14... | collective-permute-start | bytes 1572872 | tf_op jit(solution)/shard_map/ppermute | solution.py:1123
  92.9 30.1 %all-to-all-start.2 = ((bf16[8,32,1024]{2,1,0:T(8,128)(2,1)}), bf16[8,32,1024]{2,1,0:T(8,128)(2,1)S(1)}, u32[]{:S(2)}, u32[]{:S(2)}) async-start(bf16[8,32,1024]{2,1,0:T(8,128)(2,1)} %fence.14), calls=%async_computation.2 | async-start | bytes 1048576 | tf_op jit(solution)/shard_map/all_to_all | solution.py:1182
  123.8 19.6 %collective-permute-start.15 = (bf16[8,32,1024]{2,1,0:T(8,128)(2,1)}, bf16[8,32,1024]{2,1,0:T(8,128)(2,1)S(1)}, u32[]{:S(2)}, u32[]{:S(2)}) collective-permute-start(bf16[8,32,1024]{2,1,0:T(8,128)(2,1)} %fence.15.refs_0_), channel_id=1, source_target_pairs={{0,16},{8,24},{16,0},{24,8},{1,17},{9,25},{17,1},{25,9},{2,18},{10... | collective-permute-start | bytes 1572872 | tf_op jit(solution)/shard_map/ppermute | solution.py:1045
  139.6 33.6 %all-to-all-start.1 = ((bf16[8,2,128,128]{3,2,1,0:T(8,128)(2,1)}), bf16[8,2,128,128]{3,2,1,0:T(8,128)(2,1)S(1)}, u32[]{:S(2)}, u32[]{:S(2)}) async-start(bf16[8,2,128,128]{3,2,1,0:T(8,128)(2,1)} %get-tuple-element.59), calls=%async_computation.1 | async-start | bytes 1048576 | tf_op jit(solution)/shard_map/all_to_all | solution.py:1182
  143.1 252.6 %reduce-scatter.5.cloned.1.call-start = ((), (), s32[]{:S(2)}) async-start(), calls=%async_computation.9 | async-start | bytes 5308416 | tf_op jit(solution)/shard_map/reduce_scatter | solution.py:1261
  210.6 29.2 %collective-permute-start.20 = (bf16[256,1024]{1,0:T(8,128)(2,1)}, bf16[256,1024]{1,0:T(8,128)(2,1)S(1)}, u32[]{:S(2)}, u32[]{:S(2)}) collective-permute-start(bf16[256,1024]{1,0:T(8,128)(2,1)} %get-tuple-element.66), channel_id=1, source_target_pairs={{0,8},{8,0},{16,24},{24,16},{1,9},{9,1},{17,25},{25,17},{2,10},{10... | collective-permute-start | bytes 1572872 | tf_op jit(solution)/shard_map/ppermute | solution.py:1045
  225.0 14.0 %collective-permute-start.22 = (bf16[256,1024]{1,0:T(8,128)(2,1)S(1)}, bf16[256,1024]{1,0:T(8,128)(2,1)S(1)}, u32[]{:S(2)}, u32[]{:S(2)}) collective-permute-start(bf16[256,1024]{1,0:T(8,128)(2,1)S(1)} %add_convert_fusion.1), channel_id=1, source_target_pairs={{0,16},{8,24},{16,0},{24,8},{1,17},{9,25},{17,1},{25,9},{2,18},{10... | collective-permute-start | bytes 1572872 | tf_op jit(solution)/shard_map/ppermute | solution.py:1045
  251.4 30.4 %all-to-all-start.3 = ((bf16[8,2,128,128]{3,2,1,0:T(8,128)(2,1)}), bf16[8,2,128,128]{3,2,1,0:T(8,128)(2,1)}, u32[]{:S(2)}, u32[]{:S(2)}) async-start(bf16[8,2,128,128]{3,2,1,0:T(8,128)(2,1)} %bitcast.196), calls=%async_computation.3 | async-start | bytes 1048576 | tf_op jit(solution)/shard_map/all_to_all | solution.py:1179
  255.6 192.6 %reduce-scatter.3.cloned.1.call-start = ((), (), s32[]{:S(2)}) async-start(), calls=%async_computation.8 | async-start | bytes 4718592 | tf_op jit(solution)/shard_map/reduce_scatter | solution.py:1294
  262.5 32.7 %collective-permute-start.26 = (bf16[8,32,1024]{2,1,0:T(8,128)(2,1)}, bf16[8,32,1024]{2,1,0:T(8,128)(2,1)}, u32[]{:S(2)}, u32[]{:S(2)}) collective-permute-start(bf16[8,32,1024]{2,1,0:T(8,128)(2,1)} %get-tuple-element.134), channel_id=1, source_target_pairs={{0,8},{8,0},{16,24},{24,16},{1,9},{9,1},{17,25},{25,17},{2,10},{10... | collective-permute-start | bytes 1572872 | tf_op jit(solution)/shard_map/ppermute | solution.py:1045
  262.5 35.3 %collective-permute-start.23 = (bf16[256,1024]{1,0:T(8,128)(2,1)}, bf16[256,1024]{1,0:T(8,128)(2,1)}, u32[]{:S(2)}, u32[]{:S(2)}) collective-permute-start(bf16[256,1024]{1,0:T(8,128)(2,1)} %copy-done.18), channel_id=1, source_target_pairs={{0,8},{8,0},{16,24},{24,16},{1,9},{9,1},{17,25},{25,17},{2,10},{10... | collective-permute-start | bytes 1572872 | tf_op jit(solution)/shard_map/ppermute | solution.py:1045
  265.3 29.9 %collective-permute-start.28 = (bf16[8,32,1024]{2,1,0:T(8,128)(2,1)}, bf16[8,32,1024]{2,1,0:T(8,128)(2,1)}, u32[]{:S(2)}, u32[]{:S(2)}) collective-permute-start(bf16[8,32,1024]{2,1,0:T(8,128)(2,1)} %fusion.7), channel_id=1, source_target_pairs={{0,16},{8,24},{16,0},{24,8},{1,17},{9,25},{17,1},{25,9},{2,18},{10... | collective-permute-start | bytes 1572872 | tf_op jit(solution)/shard_map/ppermute | solution.py:1045
  269.1 28.7 %collective-permute-start.25 = (bf16[256,1024]{1,0:T(8,128)(2,1)S(1)}, bf16[256,1024]{1,0:T(8,128)(2,1)S(1)}, u32[]{:S(2)}, u32[]{:S(2)}) collective-permute-start(bf16[256,1024]{1,0:T(8,128)(2,1)S(1)} %add_convert_fusion), channel_id=1, source_target_pairs={{0,16},{8,24},{16,0},{24,8},{1,17},{9,25},{17,1},{25,9},{2,18},{10... | collective-permute-start | bytes 1572872 | tf_op jit(solution)/shard_map/ppermute | solution.py:1045
  359.9 27.9 %collective-permute-start.35 = (bf16[4,32,1024]{2,1,0:T(8,128)(2,1)S(1)}, bf16[4,32,1024]{2,1,0:T(8,128)(2,1)S(1)}, u32[]{:S(2)}, u32[]{:S(2)}) collective-permute-start(bf16[4,32,1024]{2,1,0:T(8,128)(2,1)S(1)} %dynamic-slice_bitcast_fusion.3), channel_id=1, source_target_pairs={{0,4},{1,5},{2,6},{3,7},{4,0},{5,1},{6,2},{7,3},{8,12},{9,13},{10,... | collective-permute-start | bytes 786440 | tf_op jit(solution)/shard_map/ppermute | solution.py:1045
  360.0 27.9 %collective-permute-start.31 = (bf16[8,32,768]{2,1,0:T(8,128)(2,1)S(1)}, bf16[8,32,768]{2,1,0:T(8,128)(2,1)S(1)}, u32[]{:S(2)}, u32[]{:S(2)}) collective-permute-start(bf16[8,32,768]{2,1,0:T(8,128)(2,1)S(1)} %get-tuple-element.136), channel_id=1, source_target_pairs={{0,16},{8,24},{16,0},{24,8},{1,17},{9,25},{17,1},{25,9},{2,18},{10... | collective-permute-start | bytes 1179656 | tf_op jit(solution)/shard_map/ppermute | solution.py:1045
  389.7 24.1 %all-to-all-start.4 = ((bf16[8,48,768]{2,1,0:T(8,128)(2,1)}), bf16[8,48,768]{2,1,0:T(8,128)(2,1)S(1)}, u32[]{:S(2)}, u32[]{:S(2)}) async-start(bf16[8,48,768]{2,1,0:T(8,128)(2,1)} %pack.1), calls=%async_computation.5 | async-start | bytes 1179648 | tf_op jit(solution)/shard_map/all_to_all | solution.py:1182
  393.7 14.4 %collective-permute-start.37 = (bf16[2,32,1024]{2,1,0:T(8,128)(2,1)S(1)}, bf16[2,32,1024]{2,1,0:T(8,128)(2,1)S(1)}, u32[]{:S(2)}, u32[]{:S(2)}) collective-permute-start(bf16[2,32,1024]{2,1,0:T(8,128)(2,1)S(1)} %fusion.24), channel_id=1, source_target_pairs={{0,2},{1,3},{2,0},{3,1},{4,6},{5,7},{6,4},{7,5},{8,10},{9,11},{10,... | collective-permute-start | bytes 393224 | tf_op jit(solution)/shard_map/ppermute | solution.py:1045
  395.7 18.2 %collective-permute-start.36 = (bf16[128,2304]{1,0:T(8,128)(2,1)}, bf16[128,2304]{1,0:T(8,128)(2,1)S(1)}, u32[]{:S(2)}, u32[]{:S(2)}) collective-permute-start(bf16[128,2304]{1,0:T(8,128)(2,1)} %fence.19.refs_0_), channel_id=1, source_target_pairs={{0,16},{8,24},{16,0},{24,8},{1,17},{9,25},{17,1},{25,9},{2,18},{10... | collective-permute-start | bytes 1769480 | tf_op jit(solution)/shard_map/ppermute | solution.py:1045
  413.9 17.6 %collective-permute-start.41 = (bf16[128,2304]{1,0:T(8,128)(2,1)}, bf16[128,2304]{1,0:T(8,128)(2,1)S(1)}, u32[]{:S(2)}, u32[]{:S(2)}) collective-permute-start(bf16[128,2304]{1,0:T(8,128)(2,1)} %fence.19.refs_0_), channel_id=1, source_target_pairs={{0,8},{8,0},{16,24},{24,16},{1,9},{9,1},{17,25},{25,17},{2,10},{10... | collective-permute-start | bytes 1769480 | tf_op jit(solution)/shard_map/ppermute | solution.py:1045
  415.5 16.0 %collective-permute-start.39 = (bf16[8,48,768]{2,1,0:T(8,128)(2,1)}, bf16[8,48,768]{2,1,0:T(8,128)(2,1)S(1)}, u32[]{:S(2)}, u32[]{:S(2)}) collective-permute-start(bf16[8,48,768]{2,1,0:T(8,128)(2,1)} %fence.20.refs_0_), channel_id=1, source_target_pairs={{0,16},{8,24},{16,0},{24,8},{1,17},{9,25},{17,1},{25,9},{2,18},{10... | collective-permute-start | bytes 1769480 | tf_op jit(solution)/shard_map/ppermute | solution.py:1045
  416.7 14.8 %collective-permute-start.42 = (bf16[128,2304]{1,0:T(8,128)(2,1)}, bf16[128,2304]{1,0:T(8,128)(2,1)S(1)}, u32[]{:S(2)}, u32[]{:S(2)}) collective-permute-start(bf16[128,2304]{1,0:T(8,128)(2,1)} %copy-done.14), channel_id=1, source_target_pairs={{0,8},{8,0},{16,24},{24,16},{1,9},{9,1},{17,25},{25,17},{2,10},{10... | collective-permute-start | bytes 1769480 | tf_op jit(solution)/shard_map/ppermute | solution.py:1045
  420.2 17.9 %collective-permute-start.38 = (bf16[8,48,768]{2,1,0:T(8,128)(2,1)S(1)}, bf16[8,48,768]{2,1,0:T(8,128)(2,1)S(1)}, u32[]{:S(2)}, u32[]{:S(2)}) collective-permute-start(bf16[8,48,768]{2,1,0:T(8,128)(2,1)S(1)} %copy-done.5), channel_id=1, source_target_pairs={{0,8},{8,0},{16,24},{24,16},{1,9},{9,1},{17,25},{25,17},{2,10},{10... | collective-permute-start | bytes 1769480 | tf_op jit(solution)/shard_map/ppermute | solution.py:1045
  (63 other events, 477.5 us)
Sparse Core Ops, SparseCore 0:
  81.5 98.9 all-gather.1
  223.9 104.6 reduce-scatter.4
  343.3 104.8 reduce-scatter.2

commit v4 on v3

--- a/solution.py
+++ b/solution.py
@@ -584,7 +584,7 @@
     router_ref[0] = dot(normed, router_weight_ref[...])
 
 
-def project(x, gain, weight, router_weight, earlier=(), size=256):
+def project(x, gain, weight, router_weight, earlier=(), size=512):
     n_seq, n_micro, n_tok, model = x.shape
     length = n_seq * n_tok
     full = weight.shape[1]
@@ -956,18 +956,19 @@
     )(mid, d_gu, g_down)
 
 
-def place_pieces_kernel(n_seq, where, *refs):
+def place_pieces_kernel(order, where, *refs):
     parts, out_ref = refs[:-1], refs[-1]
     for j, part in enumerate(parts):
-        for s in range(n_seq):
-            out_ref[s, where[0] ^ j] = part[s]
-
-
-def place_pieces(where, parts):
+        for n in range(part.shape[0]):
+            at = n if order is None else where[1] ^ order[n]
+            out_ref[at, where[0] ^ j] = part[n]
+
+
+def place_pieces(where, parts, order=None):
     n_seq, cut, width = parts[0].shape
     shape = (n_seq, len(parts), cut, width)
     return pl.pallas_call(
-        partial(place_pieces_kernel, n_seq),
+        partial(place_pieces_kernel, order),
         grid_spec=pltpu.PrefetchScalarGridSpec(
             num_scalar_prefetch=1,
             grid=(1,),
@@ -1036,6 +1037,85 @@
     )(d_ext, w_ext)
 
 
+def bottom_kernel(d_in_ref, d_residual_ref, x_ref, gain_ref, out_ref):
+    x = x_ref[0].astype(F32)
+    scale = lax.rsqrt(jnp.mean(x * x, axis=-1, keepdims=True) + EPS_NORM)
+    d_normed = d_in_ref[...].astype(F32) * gain_ref[...]
+    out_ref[0] = (
+        d_residual_ref[...]
+        + scale * d_normed
+        - x * scale**3 * jnp.mean(d_normed * x, axis=-1, keepdims=True)
+    )
+
+
+def bottom(d_in, d_residual, x, gain, earlier=()):
+    n_micro, n_tok, model = x.shape
+    rows = pl.BlockSpec((n_tok, model), lambda m: (m, 0))
+    block = pl.BlockSpec((1, n_tok, model), lambda m: (m, 0, 0))
+    return launch(
+        bottom_kernel,
+        [rows, rows, block, whole((1, model))],
+        earlier,
+        grid=(n_micro,),
+        out_specs=block,
+        out_shape=jax.ShapeDtypeStruct((n_micro, n_tok, model), F32),
+        compiler_params=small_params("arbitrary"),
+        cost_estimate=cost(1, 2.0),
+        name="bottom",
+    )(d_in, d_residual, x, gain[None])
+
+
+def turn_kernel(
+    own_ref, got_ref, d_top_ref, residual_ref, w_ref, gain_ref, d_residual_ref, d_low_ref, d_sent_ref, norm_ref
+):
+    @pl.when(pl.program_id(0) == 0)
+    def _():
+        norm_ref[...] = jnp.zeros_like(norm_ref)
+
+    residual = residual_ref[...]
+    scale = lax.rsqrt(jnp.mean(residual * residual, axis=-1, keepdims=True) + EPS_NORM)
+    d_mid = own_ref[...].astype(F32) + got_ref[...].astype(F32)
+    norm_ref[0:1, :] += jnp.sum(d_mid * residual * scale, axis=0, keepdims=True)
+    d_normed = d_mid * gain_ref[...]
+    d_residual = (
+        d_top_ref[...]
+        + scale * d_normed
+        - residual * scale**3 * jnp.mean(d_normed * residual, axis=-1, keepdims=True)
+    )
+    d_residual_ref[...] = d_residual
+    d_low = d_residual.astype(BF)
+    d_low_ref[...] = d_low
+    d_gated = dot(d_low, w_ref[...], 1, 1).astype(BF)
+    for h in range(d_sent_ref.shape[0]):
+        d_sent_ref[h, 0] = d_gated[:, h * LANES : (h + 1) * LANES]
+
+
+def turn(own, got, d_top, residual, w_out, gain, n_micro):
+    tokens, model = own.shape
+    n_tok = tokens // n_micro
+    n_heads = model // LANES
+    rows = pl.BlockSpec((n_tok, model), lambda m: (m, 0))
+    return pl.pallas_call(
+        turn_kernel,
+        grid=(n_micro,),
+        in_specs=[rows, rows, rows, rows, whole(w_out.shape), whole((1, model))],
+        out_specs=[
+            rows, rows,
+            pl.BlockSpec((n_heads, 1, n_tok, LANES), lambda m: (0, m, 0, 0)),
+            whole((8, model)),
+        ],
+        out_shape=[
+            jax.ShapeDtypeStruct((tokens, model), F32),
+            jax.ShapeDtypeStruct((tokens, model), BF),
+            jax.ShapeDtypeStruct((n_heads, n_micro, n_tok, LANES), BF),
+            jax.ShapeDtypeStruct((8, model), F32),
+        ],
+        compiler_params=small_params("arbitrary"),
+        cost_estimate=cost(1, 5.0),
+        name="turn",
+    )(own, got, d_top, residual, w_out, gain[None])
+
+
 def pick(stacked, at, axis=0):
     return lax.dynamic_index_in_dim(stacked, at, axis, False, allow_negative_indices=False)
 
@@ -1077,22 +1157,33 @@
     return parts[0].astype(BF)
 
 
-def finish(steps):
+def seq_gather_steps(value):
+    parts, order = value[None], [0]
+    for n, bit in enumerate(reversed(bits("seq"))):
+        parts = jnp.concatenate([parts, exchange(parts, "seq", bit)], axis=0)
+        order = order + [place ^ bit for place in order]
+        if n + 1 < len(bits("seq")):
+            sent = yield parts
+            parts = parts if sent is None else sent
+    return parts, order
+
+
+def finish(steps, value=None):
     try:
+        steps.send(value)
         while True:
             next(steps)
     except StopIteration as end:
         return end.value
 
 
-def row_scatter(parts, earlier=()):
+def row_scatter_halves(parts):
     parts = dict(enumerate(parts))
     for bit in bits("row"):
         got = {j ^ bit: exchange(parts[j].astype(BF), "row", bit) for j in parts if j & bit}
         if len(got) == 1:
-            got = {j: fence(part, *earlier) for j, part in got.items()}
+            return parts[0], got[0]
         parts = {j: parts[j].astype(F32) + part.astype(F32) for j, part in got.items()}
-    return parts[0]
 
 
 def ring():
@@ -1128,16 +1219,6 @@
     there = lax.ppermute(there[:, :cut], "seq", ahead)
     back = lax.ppermute(back[:, cut:], "seq", behind)
     return put(blocks, jnp.concatenate([there, back], axis=1), count // 2)
-
-
-def rms_scale(values):
-    return lax.rsqrt(jnp.mean(values * values, axis=-1, keepdims=True) + EPS_NORM)
-
-
-def rms_back(grad_norm, values, inv_scale):
-    return inv_scale * grad_norm - values * inv_scale**3 * jnp.mean(
-        grad_norm * values, axis=-1, keepdims=True
-    )
 
 
 def matmul(spec, left, right, kind=F32):
@@ -1213,14 +1294,16 @@
     live = (position[None, :] < row_lengths[:, :1]).astype(F32)[:, :, None]
     d_top = (cotangent[:, 0].astype(F32) * live).reshape(-1, model)
     d_rows = jnp.concatenate(row_gather(d_top.astype(BF)), axis=0)
-    x_own = tokens[:, 0].astype(F32).reshape(-1, model)
-
-    x_all = ring_gather(
-        tokens[:, 0], {n_seq // 4: [w_got], n_seq // 2 - 1: [w_ext, w_rt, taps, par, d_rows]}
-    )
 
     out_cut = w_out.shape[0] // n_row
     out_piece = lax.dynamic_slice_in_dim(w_out, row * out_cut, out_cut, 0)
+    out_steps = seq_gather_steps(out_piece)
+    out_got = next(out_steps)
+
+    x_all = ring_gather(
+        tokens[:, 0], {n_seq // 4: [w_got], n_seq // 2 - 1: [w_ext, w_rt, taps, par, d_rows, out_got]}
+    )
+
     shard = w_out.shape[0]
     hidden = w_gu.shape[1] // 2
     unit_cut = hidden // n_seq // n_row
@@ -1239,11 +1322,11 @@
     weights_all = lax.all_gather(weights, "seq", axis=0, tiled=True)
 
     normed_in, projected, router = project(x_all, norm1_gain, w_head, w_rt, [d_rows, weights])
-    out_piece = jnp.broadcast_to(out_piece[None], (n_seq,) + out_piece.shape)
-    out_got = seq_parts(fence(out_piece, projected))
+    out_got = out_steps.send(fence(out_got, projected))
     prep = prepare(projected, router, taps, par, width)
-    full_out = place_pieces(where, row_gather(fence(out_got, prep[0])))
+    out_got, order = finish(out_steps, fence(out_got, prep[0]))
     gated, *kept = scan_states(prep, router, projected, par, gate_at, n_tok)
+    full_out = place_pieces(where, row_gather(fence(out_got, gated)), order)
 
     residual, normed_mid, gated = middle(
         seq_parts(gated), tokens[:, 0], full_out, norm2_gain, copies
@@ -1251,7 +1334,6 @@
     residual, normed_mid, gated = (
         value.reshape(-1, model) for value in (residual, normed_mid, gated)
     )
-    scale_mid = rms_scale(residual)
     mid_rows = jnp.concatenate(row_gather(normed_mid), axis=0)
     act, d_gu, down, *d_mid = feed(
         mid_rows, d_rows, weights_all, n_units, n_seq, n_row
@@ -1259,24 +1341,21 @@
     g_down = matmul("tf,td->fd", act, d_rows, BF)
     g_feed = feed_grads(mid_rows, d_gu, g_down, n_seq)
     g_feed_sum = lax.psum_scatter(g_feed, "seq", scatter_dimension=0, tiled=True)
-    d_mid = row_scatter(d_mid, [g_feed])
+    d_mid_own, d_mid_got = row_scatter_halves(d_mid)
 
     def row_parts(value, axis):
         return [pick(value, row ^ j, axis) for j in range(n_row)]
 
-    g_norm2 = jnp.sum(d_mid * residual * scale_mid, axis=0)
-    d_residual = d_top + rms_back(d_mid * norm2_gain, residual, scale_mid)
-    d_low = d_residual.astype(BF)
-    d_sent = matmul("td,cd->tc", d_low, full_out, BF)
-    d_gated = d_sent.reshape(n_micro, n_tok, n_heads, head_dim).transpose(2, 0, 1, 3)
-    d_gated = to_heads(d_gated)
+    d_residual, d_low, d_sent, g_norm2 = turn(
+        d_mid_own, fence(d_mid_got, g_feed), d_top, residual, full_out, norm2_gain, n_micro
+    )
+    d_gated = to_heads(d_sent)
 
     mlp = times(act, down, n_row, [d_sent])
-    out = residual + row_scatter(mlp)
-    out = out.astype(BF).reshape(n_micro, 1, n_tok, model)
+    out_halves = row_scatter_halves(mlp)
     g_out_full = matmul("tc,td->cd", fence(gated, d_sent), d_low)
     g_out = g_out_full
-    g_out = row_scatter(row_parts(g_out.reshape(n_seq, n_row, out_cut, model), 1)).astype(BF)
+    g_out = row_scatter_halves(row_parts(g_out.reshape(n_seq, n_row, out_cut, model), 1))
 
     mixed, news, state = kept
     d_mixed, d_news, d_state, d_gate_pre, g_head = scan_back(
@@ -1284,7 +1363,7 @@
     )
     d_ext, g_taps, g_par = mixer_grads(
         prep, router, projected, taps, par, width,
-        news, state, d_mixed, d_news, d_state, d_gate_pre, [g_out, out],
+        news, state, d_mixed, d_news, d_state, d_gate_pre, [g_out[1], out_halves[1]],
     )
     if copies > 1:
         mine = (seq % copies == 0).astype(F32)
@@ -1295,7 +1374,7 @@
     g_in, in_lines = input_grads(normed_in, d_ext, w_ext, norm1_gain, full, [d_in_part])
     fill = lambda value: jnp.pad(value, ((0, 0), (0, full - value.shape[1])))
     scalars = jnp.concatenate([g_head[:1], g_par[1:2], g_par[2:3]], axis=1)
-    vectors = jnp.concatenate([in_lines[: n_rt + 1], g_norm2[None]]).reshape(-1, model // 2)
+    vectors = jnp.concatenate([in_lines[: n_rt + 1], g_norm2[:1]]).reshape(-1, model // 2)
     small = jnp.concatenate([fill(vectors), fill(scalars), fill(g_taps[:n_taps])])
     n_vec = vectors.shape[0]
     lines = -(-small.shape[0] // n_row)
@@ -1311,9 +1390,10 @@
             parts = {
                 j: (parts[j].astype(F32) + part.astype(F32)).astype(BF) for j, part in got.items()
             }
-    g_out_steps = seq_scatter_steps(fence(g_out, parts[0]))
+    g_out = g_out[0].astype(F32) + fence(g_out[1], parts[0]).astype(F32)
+    g_out_steps = seq_scatter_steps(g_out)
     rows = cut + -(-2 * lines // 16) * 16
-    g_in_got = seq_parts(pack(parts[0], got[0], smalls[0], rows, [next(g_out_steps)]))
+    g_in_got = seq_parts(pack(parts[0], got[0], smalls[0], rows))
     feed_steps = row_gather_steps(fence(g_feed_sum, got[0]))
     g_in_got = fence(g_in_got, *next(feed_steps), next(g_out_steps))
     in_steps = row_gather_steps(g_in_got)
@@ -1326,9 +1406,10 @@
     grad_gu = place_units(where, g_feed_all, unit_cut, unit_pad, n_seq)
     g_in_all = finish(in_steps)
     grad_in, small = place_heads(where, g_in_all, n_heads, slots, cut, lines)
-    d_in = fence(d_in, grad_in, grad_gu, grad_down, grad_out).astype(F32)
-    grad_tokens = d_residual + rms_back(d_in * norm1_gain, x_own, rms_scale(x_own))
-    grad_tokens = grad_tokens.reshape(n_micro, 1, n_tok, model)
+    before = [grad_in, grad_gu, grad_down, grad_out]
+    grad_tokens = bottom(d_in, d_residual, tokens[:, 0], norm1_gain, before)[:, None]
+    out = residual + out_halves[0].astype(F32) + out_halves[1].astype(F32)
+    out = out.astype(BF).reshape(n_micro, 1, n_tok, model)
     total = jnp.sum(small[:, 2 * n_rt : n_vec + 1], axis=0)
     norms = total[:4, : model // 2].reshape(2, model)
     heads = small[::copies]

time: 469 us -> 461 us (0.983)
  Pallas kernels: 161 us -> 167 us
  waiting for transfers between devices: 142 us -> 136 us
    all_to_all x3 -> x2, waiting for transfers between devices: 27.6 us -> 16.4 us  [seq_parts(): return lax.all_to_all(value, 'seq', 0, 0, tiled=True)]
    ppermute x39 -> x42, waiting for transfers between devices: 79.5 us -> 88.3 us  [exchange(): return lax.ppermute(value, axis, [(i, i ^ bit) for i in range(count)])]
    reduce_scatter x1, waiting for transfers between devices: 5.8 us -> 0.01 us  [local(): d_in = lax.psum_scatter(d_in_part, 'seq', scatter_dimension=0, tiled=True)]
    convert_element_type x5 -> x3, other arithmetic: 8.35 us -> 2.81 us  [row_scatter_halves(): parts[j].astype(BF)]
    all_to_all x3 -> x2, starting transfers between devices: 12.5 us -> 7.53 us  [seq_parts(): return lax.all_to_all(value, 'seq', 0, 0, tiled=True)]
    unnamed x90 -> x105, local copies, waits for them, and re-layouts: 17 us -> 18.7 us
    pallas_call x9 -> x10, Pallas kernels: 119 us -> 117 us  [launch(): return lambda *operands: called(*operands, *earlier)]
    ppermute x39 -> x42, starting transfers between devices: 21.4 us -> 22.3 us  [exchange(): return lax.ppermute(value, axis, [(i, i ^ bit) for i in range(count)])]
  transfers between devices with their start and end apart: 55 -> 57, of which waited for: 21 -> 19; matrix products, arithmetic and copies ran while one was open for 15% -> 15% of each run, Pallas kernels for 31% -> 31%
where the time goes in v4:
time: 461 us; the launch traced here: 454 us
  Pallas kernels  167 us (36%)
  waiting for transfers between devices  136 us (30%)
  local copies, waits for them, and re-layouts  51.5 us (11%)
  starting transfers between devices  50.3 us (11%)
  other arithmetic  28.3 us (6%)
  between operations  14.8 us (3%)
  matrix products  6.61 us (1%)
    pallas_call x10, Pallas kernels, launch(): return lambda *operands: called(*operands, *earlier)  117 us
    ppermute x42, waiting for transfers between devices, exchange(): return lax.ppermute(value, axis, [(i, i ^ bit) for i in range(count)])  88.3 us
    ppermute x42, starting transfers between devices, exchange(): return lax.ppermute(value, axis, [(i, i ^ bit) for i in range(count)])  22.3 us
    unnamed x105, local copies, waits for them, and re-layouts  18.7 us
    pallas_call x1, Pallas kernels, feed(): pl.pallas_call(partial(feed_kernel, n_seq), grid=(n_parts,), in_specs=[ro...  17.6 us
    all_to_all x2, waiting for transfers between devices, seq_parts(): return lax.all_to_all(value, 'seq', 0, 0, tiled=True)  16.4 us
    all_to_all x2, waiting for transfers between devices, to_heads(): lax.all_to_all(jnp.repeat(value, copies, axis=0), 'seq', 0, 0, tiled=True)  14.2 us
    dynamic_update_slice x7, local copies, waits for them, and re-layouts, ring_gather(): lax.dynamic_update_index_in_dim(blocks, block, owner(k), 0, allow_negativ...  12.2 us
  transfers between devices with their start and end apart: 57, of which 19 were waited for; matrix products, arithmetic and copies ran while one was open for 15% of the time, Pallas kernels for 31%

profile of v4, /device:TPU:0, one launch (start us, length us, event | category | flops | bytes accessed | tf_op | source)
XLA Modules:
  0.0 454.0 jit_solution(5023115570858587757)
XLA Ops:
  7.2 3.1 collective-permute-start
  17.1 5.8 %all-to-all-start = ((bf16[8,32,768]{2,1,0:T(8,128)(2,1)}), bf16[8,32,768]{2,1,0:T(8,128)(2,1)S(1)}, u32[]{:S(2)}, u32[]{:S(2)}) async-start(bf16[8,32,768]{2,1,0:T(8,128)(2,1)} %reshape_broadcast_in_dim_reshape.3), calls=%async_computation | async-start | bytes 786432 | tf_op jit(solution)/shard_map/all_to_all | solution.py:1260
  46.3 6.8 %collective-permute-done.2.refs_0_ = bf16[2,128,1024]{2,1,0:T(8,128)(2,1)S(1)} collective-permute-done((bf16[2,128,1024]{2,1,0:T(8,128)(2,1)}, bf16[2,128,1024]{2,1,0:T(8,128)(2,1)S(1)}, u32[]{:S(2)}, u32[]{:S(2)}) %collective-permute-start.2) | collective-permute-done | bytes 524320 | tf_op jit(solution)/shard_map/ppermute | solution.py:1213
  65.0 4.7 %collective-permute-done.4.refs_0_ = bf16[2,128,1024]{2,1,0:T(8,128)(2,1)} collective-permute-done((bf16[2,128,1024]{2,1,0:T(8,128)(2,1)}, bf16[2,128,1024]{2,1,0:T(8,128)(2,1)}, u32[]{:S(2)}, u32[]{:S(2)}) %collective-permute-start.4) | collective-permute-done | bytes 524320 | tf_op jit(solution)/shard_map/ppermute | solution.py:1213
  79.6 3.6 collective-permute-done.14
  84.2 9.1 %project.1 = (bf16[2,1024,1024]{2,1,0:T(8,128)(2,1)}, bf16[2,1024,768]{2,1,0:T(8,128)(2,1)}, f32[2,1024,128]{2,1,0:T(8,128)}) custom-call(bf16[8,2,128,1024]{3,2,1,0:T(8,128)(2,1)} %fusion.6.refs_1_.refs_0_, f32[1,1024]{1,0:T(1,128)} %bitcast.174, bf16[1024,768]{1,0:T(8,128)(2,1)} %bitcast.165, bf16[1024,128]{1,0:T(8,128)(2,1)} %copy-done.30, ...), custom_call_target="tpu_custom_call" | custom-call | flops 12320000000 | bytes 1048576 | tf_op jit(solution)/shard_map/project/pallas_call | solution.py:417
  93.5 22.3 %mixer_prepare.1 = (f32[2,16,128,128]{3,2,1,0:T(8,128)}, f32[2,16,128,128]{3,2,1,0:T(8,128)}, f32[2,16,128,128]{3,2,1,0:T(8,128)}, f32[2,16,64,128]{3,2,1,0:T(8,...) custom-call(bf16[2,1024,768]{2,1,0:T(8,128)(2,1)} %get-tuple-element.56.refs_0_.refs_1_.refs_6_.refs_5_, ...), custom_call_target="tpu_custom_call" | custom-call | flops 26400000000 | bytes 1048576 | tf_op jit(solution)/shard_map/mixer_prepare/pallas_call | solution.py:417
  118.3 14.4 %mixer_scan.1 = (bf16[8,2,128,128]{3,2,1,0:T(8,128)(2,1)}, f32[2,16,64,128]{3,2,1,0:T(8,128)}, f32[2,16,128,128]{3,2,1,0:T(8,128)}, f32[2,16,128,128]{3,2,1,0:T(8,128)}) custom-call(f32[2,16,128,128]{3,2,1,0:T(8,128)} %get-tuple-element.58.refs_0_, f32[2,16,128,128]{3,2,1,0:T(8,128)} %get-tuple-element.59.refs_1_, ...), custom_call_target="tpu_custom_call" | custom-call | flops 17600000000 | bytes 1048576 | tf_op jit(solution)/shard_map/mixer_scan/pallas_call | solution.py:417
  134.0 3.7 all-to-all-start.1
  138.0 7.8 %collective-permute-done.18.refs_2_ = bf16[8,32,1024]{2,1,0:T(8,128)(2,1)S(1)} collective-permute-done((bf16[8,32,1024]{2,1,0:T(8,128)(2,1)}, bf16[8,32,1024]{2,1,0:T(8,128)(2,1)S(1)}, u32[]{:S(2)}, u32[]{:S(2)}) %collective-permute-start.18) | collective-permute-done | bytes 524320 | tf_op jit(solution)/shard_map/ppermute | solution.py:1125
  150.8 16.4 %all-to-all-done.1.gated_ref = bf16[8,2,128,128]{3,2,1,0:T(8,128)(2,1)S(1)} async-done(((bf16[8,2,128,128]{3,2,1,0:T(8,128)(2,1)}), bf16[8,2,128,128]{3,2,1,0:T(8,128)(2,1)S(1)}, u32[]{:S(2)}, u32[]{:S(2)}) %all-to-all-start.1) | async-done | bytes 524320 | tf_op jit(solution)/shard_map/all_to_all | solution.py:1263
  167.1 3.3 middle.1
  173.6 9.1 %collective-permute-done.21 = bf16[256,1024]{1,0:T(8,128)(2,1)S(1)} collective-permute-done((bf16[256,1024]{1,0:T(8,128)(2,1)S(1)}, bf16[256,1024]{1,0:T(8,128)(2,1)S(1)}, u32[]{:S(2)}, u32[]{:S(2)}) %collective-permute-start.21) | collective-permute-done | bytes 524320 | tf_op jit(solution)/shard_map/ppermute | solution.py:1125
  186.0 17.6 %feed.1 = (bf16[1024,768]{1,0:T(8,128)(2,1)}, bf16[2,1024,768]{2,1,0:T(8,128)(2,1)}, bf16[768,1024]{1,0:T(8,128)(2,1)}, bf16[256,1024]{1,0:T(8,128)(2,1)}, bf16[...) custom-call(bf16[1024,1024]{1,0:T(8,128)(2,1)} %pad_maximum_fusion.1.mid_ref.refs_0_, ...), custom_call_target="tpu_custom_call" | custom-call | flops 15399999488 | bytes 1048576 | tf_op jit(solution)/shard_map/feed/pallas_call | solution.py:877
  203.6 4.8 %convolution_convert_fusion.refs_2_ = bf16[768,1024]{1,0:T(8,128)(2,1)} fusion(bf16[1024,768]{1,0:T(8,128)(2,1)} %get-tuple-element.67.refs_0_, bf16[256,1024]{1,0:T(8,128)(2,1)S(1)} %copy-done.41, bf16[256,1024]{1,0:T(8,128)(2,1)} %collective-permute-done.9, bf16[256,1024]{1,0:T(8,128)(2,1)} %collective-permute-done.8, bf16[256,1024]{1,0:T(8,128)(2,1)} %get-tuple-element.149), kind=kOutput, calls=%fused_computation.3 | convolution fusion | flops 1619787776 | bytes 5242880 | tf_op jit(solution)/shard_map/tf,td->fd/dot_general | solution.py:1225
  208.4 8.0 %feed_grads.1.refs_1_ = bf16[1024,2304]{1,0:T(8,128)(2,1)} custom-call(bf16[1024,1024]{1,0:T(8,128)(2,1)} %pad_maximum_fusion.1.mid_ref.refs_0_, bf16[2,1024,768]{2,1,0:T(8,128)(2,1)} %get-tuple-element.73.refs_1_, bf16[768,1024]{1,0:T(8,128)(2,1)} %convolution_convert_fusion.refs_2_), custom_call_target="tpu_custom_call" | custom-call | flops 7699999744 | bytes 1048576 | tf_op jit(solution)/shard_map/feed_grads/pallas_call | solution.py:417
  222.2 11.3 %collective-permute-done.25.refs_0_ = bf16[256,1024]{1,0:T(8,128)(2,1)S(1)} collective-permute-done((bf16[256,1024]{1,0:T(8,128)(2,1)S(1)}, bf16[256,1024]{1,0:T(8,128)(2,1)S(1)}, u32[]{:S(2)}, u32[]{:S(2)}) %collective-permute-start.25) | collective-permute-done | bytes 524320 | tf_op jit(solution)/shard_map/ppermute | solution.py:1125
  235.4 4.7 %turn.1 = (f32[256,1024]{1,0:T(8,128)S(1)}, bf16[256,1024]{1,0:T(8,128)(2,1)S(1)}, bf16[8,2,128,128]{3,2,1,0:T(8,128)(2,1)}, f32[8,1024]{1,0:T(8,128)S(1)}) custom-call(f32[256,1024]{1,0:T(8,128)S(1)} %convert_add_fusion.own_ref, bf16[256,1024]{1,0:T(8,128)(2,1)S(1)} %copy-done.22, f32[256,1024]{1,0:T(8,128)} %get-tuple-element.148.d_top_ref, ...), custom_call_target="tpu_custom_call" | custom-call | flops 5500000256 | bytes 1048576 | tf_op jit(solution)/shard_map/turn/pallas_call | solution.py:1098
  241.0 4.5 all-to-all-start.2
  249.8 4.5 times.1
  259.9 14.2 %all-to-all-done.2.refs_8_ = bf16[8,2,128,128]{3,2,1,0:T(8,128)(2,1)} async-done(((bf16[8,2,128,128]{3,2,1,0:T(8,128)(2,1)}), bf16[8,2,128,128]{3,2,1,0:T(8,128)(2,1)}, u32[]{:S(2)}, u32[]{:S(2)}) %all-to-all-start.2) | async-done | bytes 524320 | tf_op jit(solution)/shard_map/all_to_all | solution.py:1260
  274.1 13.3 %mixer_scan_back.1 = (f32[2,16,64,128]{3,2,1,0:T(8,128)}, f32[2,16,128,128]{3,2,1,0:T(8,128)}, f32[2,16,128,128]{3,2,1,0:T(8,128)}, bf16[2,1024,128]{2,1,0:T(8,128)(2,1)}, f32[8,128]{1,0:T(8,128)}) custom-call(f32[2,16,128,128]{3,2,1,0:T(8,128)} %get-tuple-element.58.refs_0_, f32[2,16,64,128]{3,2,1,0:T(8,128)} %get-tuple-element.60.refs_2_.refs_1_.refs_6_, ...), custom_call_target="tpu_custom_call" | custom-call | flops 14080000000 | bytes 1048576 | tf_op jit(solution)/shard_map/mixer_scan_back/pallas_call | solution.py:417
  288.4 34.7 %mixer_grads.1 = (bf16[2,1024,896]{2,1,0:T(8,128)(2,1)}, f32[8,640]{1,0:T(8,128)}, f32[8,128]{1,0:T(8,128)}) custom-call(bf16[2,1024,768]{2,1,0:T(8,128)(2,1)} %get-tuple-element.56.refs_0_.refs_1_.refs_6_.refs_5_, bf16[2,1024,768]{2,1,0:T(8,128)(2,1)} %get-tuple-element.56.refs_0_.refs_1_.refs_6_.refs_5_, ...), custom_call_target="tpu_custom_call" | custom-call | flops 35200000000 | bytes 1048576 | tf_op jit(solution)/shard_map/mixer_grads/pallas_call | solution.py:417
  323.1 8.3 %input_back.1 = bf16[8,2,128,1024]{3,2,1,0:T(8,128)(2,1)} custom-call(bf16[2,1024,896]{2,1,0:T(8,128)(2,1)} %get-tuple-element.88.d_ext_ref.refs_1_, bf16[1024,896]{1,0:T(8,128)(2,1)} %pad_maximum_fusion.2.refs_1_.w_ref.refs_2_), custom_call_target="tpu_custom_call" | custom-call | flops 7699999744 | bytes 1048576 | tf_op jit(solution)/shard_map/input_back/pallas_call | solution.py:1028
  333.2 9.0 %input_grads.1 = (bf16[1024,768]{1,0:T(8,128)(2,1)}, f32[8,1024]{1,0:T(8,128)}) custom-call(bf16[2,1024,1024]{2,1,0:T(8,128)(2,1)} %get-tuple-element.90.refs_0_, bf16[2,1024,896]{2,1,0:T(8,128)(2,1)} %get-tuple-element.88.d_ext_ref.refs_1_, bf16[1024,896]{1,0:T(8,128)(2,1)} %pad_maximum_fusion.2.refs_1_.w_ref.refs_2_, f32[1,1024]{1,0:T(1,128)} %bitcast.175, ...), custom_call_target="tpu_custom_call" | custom-call | flops 7699999744 | bytes 1048576 | tf_op jit(solution)/shard_map/input_grads/pallas_call | solution.py:417
  356.1 7.2 %collective-permute-done.33.refs_1_ = bf16[8,32,768]{2,1,0:T(8,128)(2,1)S(1)} collective-permute-done((bf16[8,32,768]{2,1,0:T(8,128)(2,1)}, bf16[8,32,768]{2,1,0:T(8,128)(2,1)S(1)}, u32[]{:S(2)}, u32[]{:S(2)}) %collective-permute-start.33) | collective-permute-done | bytes 393248 | tf_op jit(solution)/shard_map/ppermute | solution.py:1125
  364.3 3.8 all-to-all-start.3
  368.1 21.7 %collective-permute-done.39.refs_2_ = bf16[4,32,1024]{2,1,0:T(8,128)(2,1)} collective-permute-done((bf16[4,32,1024]{2,1,0:T(8,128)(2,1)}, bf16[4,32,1024]{2,1,0:T(8,128)(2,1)}, u32[]{:S(2)}, u32[]{:S(2)}) %collective-permute-start.39) | collective-permute-done | bytes 262176 | tf_op jit(solution)/shard_map/ppermute | solution.py:1125
  394.2 5.9 %collective-permute-done.45 = bf16[2,32,1024]{2,1,0:T(8,128)(2,1)} collective-permute-done((bf16[2,32,1024]{2,1,0:T(8,128)(2,1)S(1)}, bf16[2,32,1024]{2,1,0:T(8,128)(2,1)}, u32[]{:S(2)}, u32[]{:S(2)}) %collective-permute-start.45) | collective-permute-done | bytes 131104 | tf_op jit(solution)/shard_map/ppermute | solution.py:1125
  402.2 4.7 %collective-permute-done.37.refs_1_.refs_2_ = bf16[128,2304]{1,0:T(8,128)(2,1)S(1)} collective-permute-done((bf16[128,2304]{1,0:T(8,128)(2,1)}, bf16[128,2304]{1,0:T(8,128)(2,1)S(1)}, u32[]{:S(2)}, u32[]{:S(2)}) %collective-permute-start.37) | collective-permute-done | bytes 589856 | tf_op jit(solution)/shard_map/ppermute | solution.py:1125
  411.0 12.6 %collective-permute-done.48.refs_2_ = bf16[32,1024]{1,0:T(8,128)(2,1)S(1)} collective-permute-done((bf16[32,1024]{1,0:T(8,128)(2,1)S(1)}, bf16[32,1024]{1,0:T(8,128)(2,1)S(1)}, u32[]{:S(2)}, u32[]{:S(2)}) %collective-permute-start.48) | collective-permute-done | bytes 65568 | tf_op jit(solution)/shard_map/ppermute | solution.py:1125
  430.7 6.0 %place_units.1.refs_5_ = f32[128,5632]{1,0:T(8,128)} custom-call(s32[2]{0:T(128)S(1)} %pad_add_fusion.where, bf16[128,2304]{1,0:T(8,128)(2,1)S(1)} %copy-done.16, bf16[128,2304]{1,0:T(8,128)(2,1)} %collective-permute-done.43.refs_1_, bf16[128,2304]{1,0:T(8,128)(2,1)S(1)} %copy-done.18, bf16[128,2304]{1,0:T(8,128)(2,1)S(1)} %collective-permute-done.44.refs_3_), custom_call_target="tpu_custom_call" | custom-call | flops 5500000256 | bytes 1048576 | tf_op jit(solution)/shard_map/place_units/pallas_call | solution.py:779
  (307 shorter events, 132.6 us)
Async XLA Ops:
  7.2 32.1 %collective-permute-start = (bf16[2,128,1024]{2,1,0:T(8,128)(2,1)}, bf16[2,128,1024]{2,1,0:T(8,128)(2,1)}, u32[]{:S(2)}, u32[]{:S(2)}) collective-permute-start(bf16[2,128,1024]{2,1,0:T(8,128)(2,1)} %bitcast.160), channel_id=1, source_target_pairs={{0,2},{2,4},{4,6},{6,7},{7,5},{5,3},{3,1},{1,0},{8,10},{10,12},{12... | collective-permute-start | bytes 1572872 | tf_op jit(solution)/shard_map/ppermute | solution.py:1213
  10.3 31.2 %collective-permute-start.1 = (bf16[2,128,1024]{2,1,0:T(8,128)(2,1)}, bf16[2,128,1024]{2,1,0:T(8,128)(2,1)}, u32[]{:S(2)}, u32[]{:S(2)}) collective-permute-start(bf16[2,128,1024]{2,1,0:T(8,128)(2,1)} %bitcast.161), channel_id=1, source_target_pairs={{2,0},{4,2},{6,4},{7,6},{5,7},{3,5},{1,3},{0,1},{10,8},{12,10},{14... | collective-permute-start | bytes 1572872 | tf_op jit(solution)/shard_map/ppermute | solution.py:1214
  13.4 28.7 %collective-permute-start.9 = (bf16[256,1024]{1,0:T(8,128)(2,1)}, bf16[256,1024]{1,0:T(8,128)(2,1)}, u32[]{:S(2)}, u32[]{:S(2)}) collective-permute-start(bf16[256,1024]{1,0:T(8,128)(2,1)} %get-tuple-element.149), channel_id=1, source_target_pairs={{0,16},{8,24},{16,0},{24,8},{1,17},{9,25},{17,1},{25,9},{2,18},{10... | collective-permute-start | bytes 1572872 | tf_op jit(solution)/shard_map/ppermute | solution.py:1125
  15.3 43.8 %collective-permute-start.8 = (bf16[256,1024]{1,0:T(8,128)(2,1)}, bf16[256,1024]{1,0:T(8,128)(2,1)}, u32[]{:S(2)}, u32[]{:S(2)}) collective-permute-start(bf16[256,1024]{1,0:T(8,128)(2,1)} %get-tuple-element.149), channel_id=1, source_target_pairs={{0,8},{8,0},{16,24},{24,16},{1,9},{9,1},{17,25},{25,17},{2,10},{10... | collective-permute-start | bytes 1572872 | tf_op jit(solution)/shard_map/ppermute | solution.py:1125
  17.1 26.8 %all-to-all-start = ((bf16[8,32,768]{2,1,0:T(8,128)(2,1)}), bf16[8,32,768]{2,1,0:T(8,128)(2,1)S(1)}, u32[]{:S(2)}, u32[]{:S(2)}) async-start(bf16[8,32,768]{2,1,0:T(8,128)(2,1)} %reshape_broadcast_in_dim_reshape.3), calls=%async_computation | async-start | bytes 786432 | tf_op jit(solution)/shard_map/all_to_all | solution.py:1260
  22.9 163.1 %all-gather.2.cloned.1.call-start = ((), (), s32[]{:S(2)}) async-start(), calls=%async_computation.6 | async-start | bytes 5308416 | tf_op jit(solution)/shard_map/all_gather | solution.py:1322
  23.0 17.8 %collective-permute-start.11 = (bf16[1,32,1024]{2,1,0:T(8,128)(2,1)S(1)}, bf16[1,32,1024]{2,1,0:T(8,128)(2,1)S(1)}, u32[]{:S(2)}, u32[]{:S(2)}) collective-permute-start(bf16[1,32,1024]{2,1,0:T(8,128)(2,1)S(1)} %dynamic-slice_bitcast_fusion.3), channel_id=1, source_target_pairs={{0,4},{1,5},{2,6},{3,7},{4,0},{5,1},{6,2},{7,3},{8,12},{9,13},{10,... | collective-permute-start | bytes 196616 | tf_op jit(solution)/shard_map/ppermute | solution.py:1125
  39.3 13.7 %collective-permute-start.2 = (bf16[2,128,1024]{2,1,0:T(8,128)(2,1)}, bf16[2,128,1024]{2,1,0:T(8,128)(2,1)S(1)}, u32[]{:S(2)}, u32[]{:S(2)}) collective-permute-start(bf16[2,128,1024]{2,1,0:T(8,128)(2,1)} %collective-permute-done), channel_id=1, source_target_pairs={{0,2},{2,4},{4,6},{6,7},{7,5},{5,3},{3,1},{1,0},{8,10},{10,12},{12... | collective-permute-start | bytes 1572872 | tf_op jit(solution)/shard_map/ppermute | solution.py:1213
  41.4 14.3 %collective-permute-start.3 = (bf16[2,128,1024]{2,1,0:T(8,128)(2,1)}, bf16[2,128,1024]{2,1,0:T(8,128)(2,1)}, u32[]{:S(2)}, u32[]{:S(2)}) collective-permute-start(bf16[2,128,1024]{2,1,0:T(8,128)(2,1)} %collective-permute-done.1), channel_id=1, source_target_pairs={{2,0},{4,2},{6,4},{7,6},{5,7},{3,5},{1,3},{0,1},{10,8},{12,10},{14... | collective-permute-start | bytes 1572872 | tf_op jit(solution)/shard_map/ppermute | solution.py:1214
  42.0 17.6 %collective-permute-start.10 = (bf16[256,1024]{1,0:T(8,128)(2,1)}, bf16[256,1024]{1,0:T(8,128)(2,1)S(1)}, u32[]{:S(2)}, u32[]{:S(2)}) collective-permute-start(bf16[256,1024]{1,0:T(8,128)(2,1)} %collective-permute-done.9), channel_id=1, source_target_pairs={{0,8},{8,0},{16,24},{24,16},{1,9},{9,1},{17,25},{25,17},{2,10},{10... | collective-permute-start | bytes 1572872 | tf_op jit(solution)/shard_map/ppermute | solution.py:1125
  43.9 13.3 %collective-permute-start.6 = (bf16[8,32,768]{2,1,0:T(8,128)(2,1)S(1)}, bf16[8,32,768]{2,1,0:T(8,128)(2,1)S(1)}, u32[]{:S(2)}, u32[]{:S(2)}) collective-permute-start(bf16[8,32,768]{2,1,0:T(8,128)(2,1)S(1)} %all-to-all-done.refs_1_.refs_0_), channel_id=1, source_target_pairs={{0,16},{8,24},{16,0},{24,8},{1,17},{9,25},{17,1},{25,9},{2,18},{10... | collective-permute-start | bytes 1179656 | tf_op jit(solution)/shard_map/ppermute | solution.py:1125
  55.8 13.9 %collective-permute-start.4 = (bf16[2,128,1024]{2,1,0:T(8,128)(2,1)}, bf16[2,128,1024]{2,1,0:T(8,128)(2,1)}, u32[]{:S(2)}, u32[]{:S(2)}) collective-permute-start(bf16[2,128,1024]{2,1,0:T(8,128)(2,1)} %fence.11), channel_id=1, source_target_pairs={{0,2},{2,4},{4,6},{6,7},{7,5},{5,3},{3,1},{1,0},{8,10},{10,12},{12... | collective-permute-start | bytes 1572872 | tf_op jit(solution)/shard_map/ppermute | solution.py:1213
  59.1 14.7 %collective-permute-start.12 = (bf16[2,128,1024]{2,1,0:T(8,128)(2,1)}, bf16[2,128,1024]{2,1,0:T(8,128)(2,1)}, u32[]{:S(2)}, u32[]{:S(2)}) collective-permute-start(bf16[2,128,1024]{2,1,0:T(8,128)(2,1)} %collective-permute-done.3), channel_id=1, source_target_pairs={{2,0},{4,2},{6,4},{7,6},{5,7},{3,5},{1,3},{0,1},{10,8},{12,10},{14... | collective-permute-start | bytes 1572872 | tf_op jit(solution)/shard_map/ppermute | solution.py:1214
  93.2 22.5 %collective-permute-start.15 = (bf16[2,32,1024]{2,1,0:T(8,128)(2,1)}, bf16[2,32,1024]{2,1,0:T(8,128)(2,1)S(1)}, u32[]{:S(2)}, u32[]{:S(2)}) collective-permute-start(bf16[2,32,1024]{2,1,0:T(8,128)(2,1)} %fence.14), channel_id=1, source_target_pairs={{0,2},{1,3},{2,0},{3,1},{4,6},{5,7},{6,4},{7,5},{8,10},{9,11},{10,... | collective-permute-start | bytes 393224 | tf_op jit(solution)/shard_map/ppermute | solution.py:1125
  116.5 16.2 %collective-permute-start.16 = (bf16[4,32,1024]{2,1,0:T(8,128)(2,1)}, bf16[4,32,1024]{2,1,0:T(8,128)(2,1)S(1)}, u32[]{:S(2)}, u32[]{:S(2)}) collective-permute-start(bf16[4,32,1024]{2,1,0:T(8,128)(2,1)} %fence.15), channel_id=1, source_target_pairs={{0,1},{1,0},{2,3},{3,2},{4,5},{5,4},{6,7},{7,6},{8,9},{9,8},{10,11... | collective-permute-start | bytes 786440 | tf_op jit(solution)/shard_map/ppermute | solution.py:1125
  134.0 33.1 %all-to-all-start.1 = ((bf16[8,2,128,128]{3,2,1,0:T(8,128)(2,1)}), bf16[8,2,128,128]{3,2,1,0:T(8,128)(2,1)S(1)}, u32[]{:S(2)}, u32[]{:S(2)}) async-start(bf16[8,2,128,128]{3,2,1,0:T(8,128)(2,1)} %get-tuple-element.63.refs_1_), calls=%async_computation.1 | async-start | bytes 1048576 | tf_op jit(solution)/shard_map/all_to_all | solution.py:1263
  137.8 254.0 %reduce-scatter.5.cloned.1.call-start = ((), (), s32[]{:S(2)}) async-start(), calls=%async_computation.8 | async-start | bytes 5308416 | tf_op jit(solution)/shard_map/reduce_scatter | solution.py:1343
  219.5 14.0 %collective-permute-start.25 = (bf16[256,1024]{1,0:T(8,128)(2,1)S(1)}, bf16[256,1024]{1,0:T(8,128)(2,1)S(1)}, u32[]{:S(2)}, u32[]{:S(2)}) collective-permute-start(bf16[256,1024]{1,0:T(8,128)(2,1)S(1)} %add_convert_fusion.2), channel_id=1, source_target_pairs={{0,16},{8,24},{16,0},{24,8},{1,17},{9,25},{17,1},{25,9},{2,18},{10... | collective-permute-start | bytes 1572872 | tf_op jit(solution)/shard_map/ppermute | solution.py:1125
  241.0 33.1 %all-to-all-start.2 = ((bf16[8,2,128,128]{3,2,1,0:T(8,128)(2,1)}), bf16[8,2,128,128]{3,2,1,0:T(8,128)(2,1)}, u32[]{:S(2)}, u32[]{:S(2)}) async-start(bf16[8,2,128,128]{3,2,1,0:T(8,128)(2,1)} %get-tuple-element.74.refs_2_.refs_1_), calls=%async_computation.2 | async-start | bytes 1048576 | tf_op jit(solution)/shard_map/all_to_all | solution.py:1260
  245.5 198.1 %reduce-scatter.3.cloned.1.call-start = ((), (), s32[]{:S(2)}) async-start(), calls=%async_computation.7 | async-start | bytes 4718592 | tf_op jit(solution)/shard_map/reduce_scatter | solution.py:1373
  256.5 30.9 %collective-permute-start.30 = (bf16[8,32,1024]{2,1,0:T(8,128)(2,1)S(1)}, bf16[8,32,1024]{2,1,0:T(8,128)(2,1)S(1)}, u32[]{:S(2)}, u32[]{:S(2)}) collective-permute-start(bf16[8,32,1024]{2,1,0:T(8,128)(2,1)S(1)} %fusion.1), channel_id=1, source_target_pairs={{0,16},{8,24},{16,0},{24,8},{1,17},{9,25},{17,1},{25,9},{2,18},{10... | collective-permute-start | bytes 1572872 | tf_op jit(solution)/shard_map/ppermute | solution.py:1125
  259.1 28.3 %collective-permute-start.28 = (bf16[256,1024]{1,0:T(8,128)(2,1)S(1)}, bf16[256,1024]{1,0:T(8,128)(2,1)S(1)}, u32[]{:S(2)}, u32[]{:S(2)}) collective-permute-start(bf16[256,1024]{1,0:T(8,128)(2,1)S(1)} %add_convert_fusion.1), channel_id=1, source_target_pairs={{0,16},{8,24},{16,0},{24,8},{1,17},{9,25},{17,1},{25,9},{2,18},{10... | collective-permute-start | bytes 1572872 | tf_op jit(solution)/shard_map/ppermute | solution.py:1125
  332.5 20.9 %collective-permute-start.38 = (bf16[8,32,1024]{2,1,0:T(8,128)(2,1)S(1)}, bf16[8,32,1024]{2,1,0:T(8,128)(2,1)}, u32[]{:S(2)}, u32[]{:S(2)}) collective-permute-start(bf16[8,32,1024]{2,1,0:T(8,128)(2,1)S(1)} %copy-done.38), channel_id=1, source_target_pairs={{0,8},{8,0},{16,24},{24,16},{1,9},{9,1},{17,25},{25,17},{2,10},{10... | collective-permute-start | bytes 1572872 | tf_op jit(solution)/shard_map/ppermute | solution.py:1125
  356.1 33.7 %collective-permute-start.39 = (bf16[4,32,1024]{2,1,0:T(8,128)(2,1)}, bf16[4,32,1024]{2,1,0:T(8,128)(2,1)}, u32[]{:S(2)}, u32[]{:S(2)}) collective-permute-start(bf16[4,32,1024]{2,1,0:T(8,128)(2,1)} %fusion.7), channel_id=1, source_target_pairs={{0,4},{1,5},{2,6},{3,7},{4,0},{5,1},{6,2},{7,3},{8,12},{9,13},{10,... | collective-permute-start | bytes 786440 | tf_op jit(solution)/shard_map/ppermute | solution.py:1125
  364.3 37.9 %all-to-all-start.3 = ((bf16[8,48,768]{2,1,0:T(8,128)(2,1)}), bf16[8,48,768]{2,1,0:T(8,128)(2,1)S(1)}, u32[]{:S(2)}, u32[]{:S(2)}) async-start(bf16[8,48,768]{2,1,0:T(8,128)(2,1)} %pack.1), calls=%async_computation.4 | async-start | bytes 1179648 | tf_op jit(solution)/shard_map/all_to_all | solution.py:1263
  391.7 15.2 %collective-permute-start.37 = (bf16[128,2304]{1,0:T(8,128)(2,1)}, bf16[128,2304]{1,0:T(8,128)(2,1)S(1)}, u32[]{:S(2)}, u32[]{:S(2)}) collective-permute-start(bf16[128,2304]{1,0:T(8,128)(2,1)} %fence.19.refs_0_), channel_id=1, source_target_pairs={{0,16},{8,24},{16,0},{24,8},{1,17},{9,25},{17,1},{25,9},{2,18},{10... | collective-permute-start | bytes 1769480 | tf_op jit(solution)/shard_map/ppermute | solution.py:1125
  394.1 16.7 %collective-permute-start.26 = (bf16[256,1024]{1,0:T(8,128)(2,1)}, bf16[256,1024]{1,0:T(8,128)(2,1)}, u32[]{:S(2)}, u32[]{:S(2)}) collective-permute-start(bf16[256,1024]{1,0:T(8,128)(2,1)} %copy-done.25), channel_id=1, source_target_pairs={{0,8},{8,0},{16,24},{24,16},{1,9},{9,1},{17,25},{25,17},{2,10},{10... | collective-permute-start | bytes 1572872 | tf_op jit(solution)/shard_map/ppermute | solution.py:1125
  402.2 25.7 %collective-permute-start.43 = (bf16[128,2304]{1,0:T(8,128)(2,1)}, bf16[128,2304]{1,0:T(8,128)(2,1)}, u32[]{:S(2)}, u32[]{:S(2)}) collective-permute-start(bf16[128,2304]{1,0:T(8,128)(2,1)} %fence.19.refs_0_), channel_id=1, source_target_pairs={{0,8},{8,0},{16,24},{24,16},{1,9},{9,1},{17,25},{25,17},{2,10},{10... | collective-permute-start | bytes 1769480 | tf_op jit(solution)/shard_map/ppermute | solution.py:1125
  407.8 20.1 %collective-permute-start.41 = (bf16[8,48,768]{2,1,0:T(8,128)(2,1)}, bf16[8,48,768]{2,1,0:T(8,128)(2,1)S(1)}, u32[]{:S(2)}, u32[]{:S(2)}) collective-permute-start(bf16[8,48,768]{2,1,0:T(8,128)(2,1)} %fence.21.refs_0_), channel_id=1, source_target_pairs={{0,16},{8,24},{16,0},{24,8},{1,17},{9,25},{17,1},{25,9},{2,18},{10... | collective-permute-start | bytes 1769480 | tf_op jit(solution)/shard_map/ppermute | solution.py:1125
  408.4 19.5 %collective-permute-start.44 = (bf16[128,2304]{1,0:T(8,128)(2,1)}, bf16[128,2304]{1,0:T(8,128)(2,1)S(1)}, u32[]{:S(2)}, u32[]{:S(2)}) collective-permute-start(bf16[128,2304]{1,0:T(8,128)(2,1)} %copy-done.17), channel_id=1, source_target_pairs={{0,8},{8,0},{16,24},{24,16},{1,9},{9,1},{17,25},{25,17},{2,10},{10... | collective-permute-start | bytes 1769480 | tf_op jit(solution)/shard_map/ppermute | solution.py:1125
  409.4 14.3 %collective-permute-start.48 = (bf16[32,1024]{1,0:T(8,128)(2,1)S(1)}, bf16[32,1024]{1,0:T(8,128)(2,1)S(1)}, u32[]{:S(2)}, u32[]{:S(2)}) collective-permute-start(bf16[32,1024]{1,0:T(8,128)(2,1)S(1)} %fusion.9.refs_0_), channel_id=1, source_target_pairs={{0,16},{8,24},{16,0},{24,8},{1,17},{9,25},{17,1},{25,9},{2,18},{10... | collective-permute-start | bytes 196616 | tf_op jit(solution)/shard_map/ppermute | solution.py:1125
  410.8 15.2 %collective-permute-start.47 = (bf16[32,1024]{1,0:T(8,128)(2,1)S(1)}, bf16[32,1024]{1,0:T(8,128)(2,1)S(1)}, u32[]{:S(2)}, u32[]{:S(2)}) collective-permute-start(bf16[32,1024]{1,0:T(8,128)(2,1)S(1)} %fusion.9.refs_0_), channel_id=1, source_target_pairs={{0,8},{8,0},{16,24},{24,16},{1,9},{9,1},{17,25},{25,17},{2,10},{10... | collective-permute-start | bytes 196616 | tf_op jit(solution)/shard_map/ppermute | solution.py:1125
  (73 other events, 494.0 us)
Sparse Core Ops, SparseCore 0:
  84.3 89.2 all-gather.1
  216.5 107.8 reduce-scatter.4
  331.6 107.4 reduce-scatter.2

commit v5 on v4

--- a/solution.py
+++ b/solution.py
@@ -116,7 +116,7 @@
     count, proj_ref, halo_ref, router_ref, taps_ref, par_ref,
     solve_ref, wmat_ref, umat_ref, seen_ref, q_ref, k_ref, window,
 ):
-    fill_window(window, proj_ref, halo_ref, pl.program_id(1) == 0)
+    fill_window(window, proj_ref, halo_ref, pl.program_id(0) == 0)
     weight = taps_ref[...]
     par = par_ref[...]
     o_row, o_col = step_orders()
@@ -406,15 +406,18 @@
     )
 
 
-def launch(kernel, in_specs, earlier, **options):
+def launch(kernel, in_specs, earlier, onto=(), first_out=0, **options):
     n_in = len(in_specs)
+    others = list(earlier) + list(onto)
 
     def body(*refs):
-        kernel(*refs[:n_in], *refs[n_in + len(earlier) :])
-
-    specs = list(in_specs) + [pl.BlockSpec(memory_space=pl.ANY)] * len(earlier)
-    called = pl.pallas_call(body, in_specs=specs, **options)
-    return lambda *operands: called(*operands, *earlier)
+        kernel(*refs[:n_in], *refs[n_in + len(others) :])
+
+    specs = list(in_specs) + [pl.BlockSpec(memory_space=pl.ANY)] * len(others)
+    at = n_in + len(earlier)
+    aliases = {at + n: first_out + n for n in range(len(onto))}
+    called = pl.pallas_call(body, in_specs=specs, input_output_aliases=aliases, **options)
+    return lambda *operands: called(*operands, *others)
 
 
 def fence(value, *earlier):
@@ -436,64 +439,66 @@
     return pl.BlockSpec(shape, lambda *_: (0,) * len(shape))
 
 
-def prepare(projected, router, taps, par, width, earlier=(), count=8):
+def prepare(at, projected, router, taps, par, width, onto=(), earlier=(), count=8):
     n_micro, length, full = projected.shape
-    steps = length // (count * CH)
     chunks = length // CH
     size = count * CH
-    per = lambda *tail: pl.BlockSpec((1, count) + tail, lambda m, i: (m, i, 0, 0))
+    per = lambda *tail: pl.BlockSpec((1, count) + tail, lambda i: (at, i, 0, 0))
     made = lambda kind, *tail: jax.ShapeDtypeStruct((n_micro, chunks) + tail, kind)
     return launch(
         partial(prep_kernel, count),
         [
-            pl.BlockSpec((1, size, full), lambda m, i: (m, i, 0)),
-            pl.BlockSpec((1, HALO, full), lambda m, i: (m, jnp.maximum(i * (size // HALO) - 1, 0), 0)),
-            pl.BlockSpec((1, size, LANES), lambda m, i: (m, i, 0)),
+            pl.BlockSpec((1, size, full), lambda i: (at, i, 0)),
+            pl.BlockSpec((1, HALO, full), lambda i: (at, jnp.maximum(i * (size // HALO) - 1, 0), 0)),
+            pl.BlockSpec((1, size, LANES), lambda i: (at, i, 0)),
             whole(taps.shape),
             whole(par.shape),
         ],
         earlier,
-        grid=(n_micro, steps),
+        onto,
+        grid=(length // size,),
         out_specs=[per(ST, ST), per(ST, 128), per(ST, 128), per(CH, ST), per(CH, 128), per(ST, 128)],
         out_shape=[
             made(F32, ST, ST), made(F32, ST, 128), made(F32, ST, 128), made(F32, CH, ST),
             made(BF, CH, 128), made(BF, ST, 128),
         ],
         scratch_shapes=[pltpu.VMEM((size + 8, width), F32)],
-        compiler_params=params("arbitrary", "arbitrary"),
-        cost_estimate=cost(n_micro * chunks, 0.75),
+        compiler_params=params("arbitrary"),
+        cost_estimate=cost(chunks, 0.75),
         name="mixer_prepare",
     )(projected, projected, router, taps, par)
 
 
-def scan_states(prep, router, projected, par, gate_at, n_tok, earlier=(), count=4):
+def scan_states(at, prep, router, projected, par, gate_at, n_tok, onto=(), earlier=(), count=4):
     _, wmat, umat, seen, q, k = prep
     n_micro, chunks = wmat.shape[:2]
     length = chunks * CH
     size = count * CH
-    per = lambda *tail: pl.BlockSpec((n_micro, count) + tail, lambda i: (0, i, 0, 0))
+    per = lambda *tail: pl.BlockSpec((1, count) + tail, lambda i: (at, i, 0, 0))
     made = lambda kind, *tail: jax.ShapeDtypeStruct((n_micro, chunks) + tail, kind)
     return launch(
-        partial(scan_kernel, n_micro, count),
+        partial(scan_kernel, 1, count),
         [
             per(ST, 128), per(ST, 128), per(CH, ST), per(CH, 128), per(ST, 128),
-            pl.BlockSpec((n_micro, size, LANES), lambda i: (0, i, 0)),
-            pl.BlockSpec((n_micro, size, 128), lambda i: (0, i, gate_at)),
+            pl.BlockSpec((1, size, LANES), lambda i: (at, i, 0)),
+            pl.BlockSpec((1, size, 128), lambda i: (at, i, gate_at)),
             whole(par.shape),
         ],
         earlier,
+        onto,
+        1,
         grid=(chunks // count,),
         out_specs=[
-            pl.BlockSpec((size // n_tok, n_micro, n_tok, 128), lambda i: (i, 0, 0, 0)),
+            pl.BlockSpec((size // n_tok, 1, n_tok, 128), lambda i: (i, 0, 0, 0)),
             per(CH, 128), per(ST, 128), per(128, 128),
         ],
         out_shape=[
-            jax.ShapeDtypeStruct((length // n_tok, n_micro, n_tok, 128), BF),
+            jax.ShapeDtypeStruct((length // n_tok, 1, n_tok, 128), BF),
             made(F32, CH, 128), made(F32, ST, 128), made(F32, 128, 128),
         ],
-        scratch_shapes=[pltpu.VMEM((n_micro, 128, 128), F32)],
+        scratch_shapes=[pltpu.VMEM((1, 128, 128), F32)],
         compiler_params=params("arbitrary"),
-        cost_estimate=cost(n_micro * chunks, 0.5),
+        cost_estimate=cost(chunks, 0.5),
         name="mixer_scan",
     )(wmat, umat, seen, q, k, router, projected, par)
 
@@ -833,7 +838,19 @@
     return place_rows(where, parts, shape, partial(place_down_kernel, unit_pad, left))
 
 
-def feed_kernel(n_seq, mid_ref, d_top_ref, w_ref, act_ref, d_gu_ref, down_ref, *d_mid_refs):
+def feed_kernel(n_seq, n_parts, d_top_ref, w_ref, *refs):
+    part_refs, (mid_ref, act_ref, d_gu_ref, down_ref), d_mid_refs = (
+        refs[:-4 - n_parts], refs[-4 - n_parts : -n_parts], refs[-n_parts:]
+    )
+    per_step = len(part_refs) // n_parts
+    n_tok = part_refs[0].shape[0]
+    for j in range(n_parts):
+
+        @pl.when(pl.program_id(0) == j)
+        def _(j=j):
+            for m in range(per_step):
+                mid_ref[m * n_tok : (m + 1) * n_tok] = part_refs[j * per_step + m][...]
+
     n_units = act_ref.shape[1]
     model = mid_ref.shape[1]
     per = n_units // n_seq
@@ -871,18 +888,19 @@
 
 
 def feed(mid, d_top, weights, n_units, n_seq, n_parts):
-    tokens, model = mid.shape
+    tokens, model = d_top.shape
     size = tokens // n_parts
     rows = lambda n: pl.BlockSpec((size, n), lambda i: (i, 0))
     return pl.pallas_call(
-        partial(feed_kernel, n_seq),
+        partial(feed_kernel, n_seq, n_parts),
         grid=(n_parts,),
-        in_specs=[rows(model), rows(model), whole(weights.shape)],
+        in_specs=[rows(model), whole(weights.shape)] + [whole(part.shape) for part in mid],
         out_specs=[
-            rows(n_units), pl.BlockSpec((2, size, n_units), lambda i: (0, i, 0)),
+            rows(model), rows(n_units), pl.BlockSpec((2, size, n_units), lambda i: (0, i, 0)),
             whole((n_units, model)),
         ] + [whole((size, model))] * n_parts,
         out_shape=[
+            jax.ShapeDtypeStruct((tokens, model), BF),
             jax.ShapeDtypeStruct((tokens, n_units), BF),
             jax.ShapeDtypeStruct((2, tokens, n_units), BF),
             jax.ShapeDtypeStruct((n_units, model), BF),
@@ -890,7 +908,7 @@
         compiler_params=params("arbitrary"),
         cost_estimate=cost(1, 14.0),
         name="feed",
-    )(mid, d_top, weights)
+    )(d_top, weights, *mid)
 
 
 def times_kernel(left_ref, right_ref, *out_refs):
@@ -994,22 +1012,23 @@
     normed_ref[0] = (total * scale * gain_ref[...]).astype(BF)
 
 
-def middle(gated, x, w_out, gain, copies):
-    n_micro, n_tok, model = x.shape
+def middle(at, gated, x, w_out, gain, copies):
+    _, n_tok, model = x.shape
     n_seq = gated.shape[0]
-    rows = pl.BlockSpec((1, n_tok, model), lambda m: (m, 0, 0))
-    made = lambda kind: jax.ShapeDtypeStruct((n_micro, n_tok, model), kind)
+    rows = pl.BlockSpec((1, n_tok, model), lambda i: (0, 0, 0))
+    made = lambda kind: jax.ShapeDtypeStruct((1, n_tok, model), kind)
     return pl.pallas_call(
         partial(middle_kernel, copies),
-        grid=(n_micro,),
+        grid=(1,),
         in_specs=[
-            pl.BlockSpec((n_seq, 1, n_tok, LANES), lambda m: (0, m, 0, 0)),
-            rows, whole(w_out.shape), whole((1, model)),
+            pl.BlockSpec((n_seq, 1, n_tok, LANES), lambda i: (0, 0, 0, 0)),
+            pl.BlockSpec((1, n_tok, model), lambda i: (at, 0, 0)),
+            whole(w_out.shape), whole((1, model)),
         ],
         out_specs=[rows] * 3,
         out_shape=[made(F32), made(BF), made(BF)],
         compiler_params=small_params("arbitrary"),
-        cost_estimate=cost(1, 4.0),
+        cost_estimate=cost(1, 2.0),
         name="middle",
     )(gated, x, w_out, gain[None])
 
@@ -1142,7 +1161,9 @@
     for bit in reversed(bits("row")):
         got = {j ^ bit: exchange(part, "row", bit) for j, part in parts.items()}
         parts.update(got)
-        yield list(got.values())
+        earlier = yield list(got.values())
+        if earlier:
+            parts = {j: fence(part, *earlier) for j, part in parts.items()}
     return [parts[j] for j in range(len(parts))]
 
 
@@ -1323,19 +1344,24 @@
 
     normed_in, projected, router = project(x_all, norm1_gain, w_head, w_rt, [d_rows, weights])
     out_got = out_steps.send(fence(out_got, projected))
-    prep = prepare(projected, router, taps, par, width)
-    out_got, order = finish(out_steps, fence(out_got, prep[0]))
-    gated, *kept = scan_states(prep, router, projected, par, gate_at, n_tok)
-    full_out = place_pieces(where, row_gather(fence(out_got, gated)), order)
-
-    residual, normed_mid, gated = middle(
-        seq_parts(gated), tokens[:, 0], full_out, norm2_gain, copies
-    )
-    residual, normed_mid, gated = (
-        value.reshape(-1, model) for value in (residual, normed_mid, gated)
-    )
-    mid_rows = jnp.concatenate(row_gather(normed_mid), axis=0)
-    act, d_gu, down, *d_mid = feed(
+    prep, kept, sent = (), (), []
+    for m in micros:
+        prep = prepare(m, projected, router, taps, par, width, prep)
+        if m == 0:
+            out_got, order = finish(out_steps, fence(out_got, prep[0]))
+        gated, *kept = scan_states(
+            m, prep, router, projected, par, gate_at, n_tok, kept, sent[-1:]
+        )
+        sent.append(seq_parts(gated))
+        if m == 0:
+            full_out = place_pieces(where, row_gather(fence(out_got, gated)), order)
+
+    middles = [middle(m, sent[m], tokens[:, 0], full_out, norm2_gain, copies) for m in micros]
+    mid_rows = zip(*[row_gather(normed_mid[0]) for _, normed_mid, _ in middles])
+    mid_rows = [part for parts in mid_rows for part in parts]
+    residual = jnp.concatenate([value[0][0] for value in middles], axis=0)
+    gated = jnp.concatenate([value[2][0] for value in middles], axis=0)
+    mid_rows, act, d_gu, down, *d_mid = feed(
         mid_rows, d_rows, weights_all, n_units, n_seq, n_row
     )
     g_down = matmul("tf,td->fd", act, d_rows, BF)
@@ -1380,7 +1406,11 @@
     lines = -(-small.shape[0] // n_row)
     small = jnp.pad(small, ((0, n_row * lines - small.shape[0]), (0, 0))).reshape(n_row, lines, full)
 
-    parts = dict(enumerate(row_parts(g_in.reshape(n_seq, n_row, cut, full), 1)))
+    g_out = g_out[0].astype(F32) + fence(g_out[1], d_in_part).astype(F32)
+    g_out_steps = seq_scatter_steps(g_out)
+    moment = next(g_out_steps)
+    parts = row_parts(g_in.reshape(n_seq, n_row, cut, full), 1)
+    parts = {j: fence(part, moment) if j & 1 else part for j, part in enumerate(parts)}
     smalls = dict(enumerate(row_parts(small, 0)))
     for bit in bits("row"):
         got = {j ^ bit: exchange(parts[j], "row", bit) for j in parts if j & bit}
@@ -1390,10 +1420,8 @@
             parts = {
                 j: (parts[j].astype(F32) + part.astype(F32)).astype(BF) for j, part in got.items()
             }
-    g_out = g_out[0].astype(F32) + fence(g_out[1], parts[0]).astype(F32)
-    g_out_steps = seq_scatter_steps(g_out)
     rows = cut + -(-2 * lines // 16) * 16
-    g_in_got = seq_parts(pack(parts[0], got[0], smalls[0], rows))
+    g_in_got = seq_parts(pack(parts[0], got[0], smalls[0], rows, [next(g_out_steps)]))
     feed_steps = row_gather_steps(fence(g_feed_sum, got[0]))
     g_in_got = fence(g_in_got, *next(feed_steps), next(g_out_steps))
     in_steps = row_gather_steps(g_in_got)
@@ -1404,7 +1432,7 @@
     grad_out = place_rows(where, g_out_all, (out_cut, model))
     grad_down = place_down(where, g_feed_all, unit_pad, 2 * n_units, (unit_cut, model))
     grad_gu = place_units(where, g_feed_all, unit_cut, unit_pad, n_seq)
-    g_in_all = finish(in_steps)
+    g_in_all = finish(in_steps, [grad_gu, grad_down])
     grad_in, small = place_heads(where, g_in_all, n_heads, slots, cut, lines)
     before = [grad_in, grad_gu, grad_down, grad_out]
     grad_tokens = bottom(d_in, d_residual, tokens[:, 0], norm1_gain, before)[:, None]

time: 461 us -> 455 us (0.987)
  waiting for transfers between devices: 136 us -> 100 us
  local copies, waits for them, and re-layouts: 51.5 us -> 62.9 us
  starting transfers between devices: 50.3 us -> 60.3 us
  Pallas kernels: 167 us -> 175 us
    ppermute x42 -> x45, waiting for transfers between devices: 88.3 us -> 59 us  [exchange(): return lax.ppermute(value, axis, [(i, i ^ bit) for i in range(count)])]
    unnamed x105 -> x143, local copies, waits for them, and re-layouts: 18.7 us -> 32.2 us
    ppermute x3, waiting for transfers between devices: 1.69 us -> 8.71 us  [ring_gather(): back = lax.ppermute(back, 'seq', behind)]
    ppermute x42 -> x45, starting transfers between devices: 22.3 us -> 29 us  [exchange(): return lax.ppermute(value, axis, [(i, i ^ bit) for i in range(count)])]
    all_to_all x2, waiting for transfers between devices: 14.2 us -> 8.4 us  [to_heads(): lax.all_to_all(jnp.repeat(value, copies, axis=0), 'seq', 0, 0, tiled=True)]
    ppermute x3, waiting for transfers between devices: 11.4 us -> 6.07 us  [ring_gather(): there = lax.ppermute(there, 'seq', ahead)]
    all_to_all x2 -> x3, starting transfers between devices: 7.53 us -> 12.5 us  [seq_parts(): return lax.all_to_all(value, 'seq', 0, 0, tiled=True)]
    pallas_call x12 -> x15, Pallas kernels: 138 us -> 143 us  [the longest x12 123 us: launch(): return lambda *operands: called(*operands, *others)]
  transfers between devices with their start and end apart: 57 -> 61, of which waited for: 19 -> 23; matrix products, arithmetic and copies ran while one was open for 15% -> 13% of each run, Pallas kernels for 31% -> 33%
where the time goes in v5:
time: 455 us; the launch traced here: 447 us
  Pallas kernels  175 us (38%)
  waiting for transfers between devices  100 us (22%)
  local copies, waits for them, and re-layouts  62.9 us (14%)
  starting transfers between devices  60.3 us (13%)
  other arithmetic  27.6 us (6%)
  between operations  14.9 us (3%)
  matrix products  6.59 us (1%)
    pallas_call x12, Pallas kernels, launch(): return lambda *operands: called(*operands, *others)  123 us
    ppermute x45, waiting for transfers between devices, exchange(): return lax.ppermute(value, axis, [(i, i ^ bit) for i in range(count)])  59 us
    unnamed x143, local copies, waits for them, and re-layouts  32.2 us
    ppermute x45, starting transfers between devices, exchange(): return lax.ppermute(value, axis, [(i, i ^ bit) for i in range(count)])  29 us
    pallas_call x1, Pallas kernels, feed(): pl.pallas_call(partial(feed_kernel, n_seq, n_parts), grid=(n_parts,), in_...  18.3 us
    all_to_all x3, waiting for transfers between devices, seq_parts(): return lax.all_to_all(value, 'seq', 0, 0, tiled=True)  13.1 us
    all_to_all x3, starting transfers between devices, seq_parts(): return lax.all_to_all(value, 'seq', 0, 0, tiled=True)  12.5 us
    dynamic_update_slice x7, local copies, waits for them, and re-layouts, ring_gather(): lax.dynamic_update_index_in_dim(blocks, block, owner(k), 0, allow_negativ...  11.1 us
  transfers between devices with their start and end apart: 61, of which 23 were waited for; matrix products, arithmetic and copies ran while one was open for 13% of the time, Pallas kernels for 33%

profile of v5, /device:TPU:0, one launch (start us, length us, event | category | flops | bytes accessed | tf_op | source)
XLA Modules:
  0.0 447.0 jit_solution(11067461318391210407)
XLA Ops:
  17.2 5.8 %all-to-all-start = ((bf16[8,32,768]{2,1,0:T(8,128)(2,1)}), bf16[8,32,768]{2,1,0:T(8,128)(2,1)S(1)}, u32[]{:S(2)}, u32[]{:S(2)}) async-start(bf16[8,32,768]{2,1,0:T(8,128)(2,1)} %reshape_broadcast_in_dim_reshape.3), calls=%async_computation | async-start | bytes 786432 | tf_op jit(solution)/shard_map/all_to_all | solution.py:1281
  46.5 6.1 %collective-permute-done.2.refs_0_ = bf16[2,128,1024]{2,1,0:T(8,128)(2,1)S(1)} collective-permute-done((bf16[2,128,1024]{2,1,0:T(8,128)(2,1)}, bf16[2,128,1024]{2,1,0:T(8,128)(2,1)S(1)}, u32[]{:S(2)}, u32[]{:S(2)}) %collective-permute-start.2) | collective-permute-done | bytes 524320 | tf_op jit(solution)/shard_map/ppermute | solution.py:1234
  65.8 7.4 %collective-permute-done.12 = bf16[2,128,1024]{2,1,0:T(8,128)(2,1)S(1)} collective-permute-done((bf16[2,128,1024]{2,1,0:T(8,128)(2,1)}, bf16[2,128,1024]{2,1,0:T(8,128)(2,1)S(1)}, u32[]{:S(2)}, u32[]{:S(2)}) %collective-permute-start.12) | collective-permute-done | bytes 524320 | tf_op jit(solution)/shard_map/ppermute | solution.py:1235
  85.0 9.1 %project.1 = (bf16[2,1024,1024]{2,1,0:T(8,128)(2,1)}, bf16[2,1024,768]{2,1,0:T(8,128)(2,1)}, f32[2,1024,128]{2,1,0:T(8,128)}) custom-call(bf16[8,2,128,1024]{3,2,1,0:T(8,128)(2,1)} %fusion.6.refs_1_.refs_0_, f32[1,1024]{1,0:T(1,128)} %bitcast.180, bf16[1024,768]{1,0:T(8,128)(2,1)} %bitcast.175, bf16[1024,128]{1,0:T(8,128)(2,1)} %copy-done.41, ...), custom_call_target="tpu_custom_call" | custom-call | flops 12320000000 | bytes 1048576 | tf_op jit(solution)/shard_map/project/pallas_call | solution.py:420
  94.4 12.2 %mixer_prepare.2 = (f32[2,16,128,128]{3,2,1,0:T(8,128)}, f32[2,16,128,128]{3,2,1,0:T(8,128)}, f32[2,16,128,128]{3,2,1,0:T(8,128)}, f32[2,16,64,128]{3,2,1,0:T(8,...) custom-call(bf16[2,1024,768]{2,1,0:T(8,128)(2,1)} %get-tuple-element.70.refs_0_.refs_1_.refs_6_.refs_5_, ...), custom_call_target="tpu_custom_call" | custom-call | flops 13200000000 | bytes 1048576 | tf_op jit(solution)/shard_map/mixer_prepare/pallas_call | solution.py:420
  109.1 8.8 %mixer_scan.2 = (bf16[8,1,128,128]{3,2,1,0:T(8,128)(2,1)}, f32[2,16,64,128]{3,2,1,0:T(8,128)}, f32[2,16,128,128]{3,2,1,0:T(8,128)}, f32[2,16,128,128]{3,2,1,0:T(8,128)}) custom-call(f32[2,16,128,128]{3,2,1,0:T(8,128)} %get-tuple-element.72.refs_0_.refs_6_, f32[2,16,128,128]{3,2,1,0:T(8,128)} %get-tuple-element.73.refs_1_.refs_7_, ...), custom_call_target="tpu_custom_call" | custom-call | flops 8800000000 | bytes 1048576 | tf_op jit(solution)/shard_map/mixer_scan/pallas_call | solution.py:420
  118.0 4.0 all-to-all-start.1
  123.2 12.2 %mixer_prepare.3 = (f32[2,16,128,128]{3,2,1,0:T(8,128)}, f32[2,16,128,128]{3,2,1,0:T(8,128)}, f32[2,16,128,128]{3,2,1,0:T(8,128)}, f32[2,16,64,128]{3,2,1,0:T(8,...) custom-call(bf16[2,1024,768]{2,1,0:T(8,128)(2,1)} %get-tuple-element, ...), custom_call_target="tpu_custom_call", output_to_operand_aliasing={{0}: (5, {}), {1}: (6, {}), {2}: (7, {}), {3}: (8, {}), {4}... | custom-call | flops 13200000000 | bytes 1048576 | tf_op jit(solution)/shard_map/mixer_prepare/pallas_call | solution.py:420
  137.8 8.9 %mixer_scan.3 = (bf16[8,1,128,128]{3,2,1,0:T(8,128)(2,1)}, f32[2,16,64,128]{3,2,1,0:T(8,128)}, f32[2,16,128,128]{3,2,1,0:T(8,128)}, f32[2,16,128,128]{3,2,1,0:T(8,128)}) custom-call(f32[2,16,128,128]{3,2,1,0:T(8,128)} %get-tuple-element.80.refs_0_, ...), custom_call_target="tpu_custom_call", output_to_operand_aliasing={{1}: (9, {}), {2}: (10, {}), {3}: (11, {})} | custom-call | flops 8800000000 | bytes 1048576 | tf_op jit(solution)/shard_map/mixer_scan/pallas_call | solution.py:420
  146.7 5.0 %all-to-all-start.2 = ((bf16[8,1,128,128]{3,2,1,0:T(8,128)(2,1)}), bf16[8,1,128,128]{3,2,1,0:T(8,128)(2,1)S(1)}, u32[]{:S(2)}, u32[]{:S(2)}) async-start(bf16[8,1,128,128]{3,2,1,0:T(8,128)(2,1)} %get-tuple-element.88), calls=%async_computation.2 | async-start | bytes 524288 | tf_op jit(solution)/shard_map/all_to_all | solution.py:1284
  159.4 9.2 %all-to-all-done.2.gated_ref = bf16[8,1,128,128]{3,2,1,0:T(8,128)(2,1)S(1)} async-done(((bf16[8,1,128,128]{3,2,1,0:T(8,128)(2,1)}), bf16[8,1,128,128]{3,2,1,0:T(8,128)(2,1)S(1)}, u32[]{:S(2)}, u32[]{:S(2)}) %all-to-all-start.2) | async-done | bytes 262176 | tf_op jit(solution)/shard_map/all_to_all | solution.py:1284
  172.9 6.1 %collective-permute-done.23.refs_5_ = bf16[128,1024]{1,0:T(8,128)(2,1)S(1)} collective-permute-done((bf16[128,1024]{1,0:T(8,128)(2,1)S(1)}, bf16[128,1024]{1,0:T(8,128)(2,1)S(1)}, u32[]{:S(2)}, u32[]{:S(2)}) %collective-permute-start.23) | collective-permute-done | bytes 262176 | tf_op jit(solution)/shard_map/ppermute | solution.py:1144
  181.2 18.3 %feed.1 = (bf16[1024,1024]{1,0:T(8,128)(2,1)}, bf16[1024,768]{1,0:T(8,128)(2,1)}, bf16[2,1024,768]{2,1,0:T(8,128)(2,1)}, bf16[768,1024]{1,0:T(8,128)(2,1)}, bf16...) custom-call(bf16[1024,1024]{1,0:T(8,128)(2,1)} %pad_maximum_fusion.ref, ...), custom_call_target="tpu_custom_call" | custom-call | flops 15399999488 | bytes 1048576 | tf_op jit(solution)/shard_map/feed/pallas_call | solution.py:894
  199.5 4.8 %convolution_convert_fusion.refs_2_ = bf16[768,1024]{1,0:T(8,128)(2,1)} fusion(bf16[1024,768]{1,0:T(8,128)(2,1)} %get-tuple-element.92.refs_0_, bf16[256,1024]{1,0:T(8,128)(2,1)S(1)} %copy-done.55, bf16[256,1024]{1,0:T(8,128)(2,1)} %collective-permute-done.9, bf16[256,1024]{1,0:T(8,128)(2,1)} %collective-permute-done.8, bf16[256,1024]{1,0:T(8,128)(2,1)} %get-tuple-element.177), kind=kOutput, calls=%fused_computation.2 | convolution fusion | flops 1619787776 | bytes 5242880 | tf_op jit(solution)/shard_map/tf,td->fd/dot_general | solution.py:1246
  204.3 7.9 %feed_grads.1.refs_1_ = bf16[1024,2304]{1,0:T(8,128)(2,1)} custom-call(bf16[1024,1024]{1,0:T(8,128)(2,1)} %get-tuple-element.98.refs_0_, bf16[2,1024,768]{2,1,0:T(8,128)(2,1)} %get-tuple-element.99.refs_1_, bf16[768,1024]{1,0:T(8,128)(2,1)} %convolution_convert_fusion.refs_2_), custom_call_target="tpu_custom_call" | custom-call | flops 7699999744 | bytes 1048576 | tf_op jit(solution)/shard_map/feed_grads/pallas_call | solution.py:420
  218.6 10.3 %collective-permute-done.28.refs_0_ = bf16[256,1024]{1,0:T(8,128)(2,1)S(1)} collective-permute-done((bf16[256,1024]{1,0:T(8,128)(2,1)S(1)}, bf16[256,1024]{1,0:T(8,128)(2,1)S(1)}, u32[]{:S(2)}, u32[]{:S(2)}) %collective-permute-start.28) | collective-permute-done | bytes 524320 | tf_op jit(solution)/shard_map/ppermute | solution.py:1144
  232.0 4.7 %turn.1 = (f32[256,1024]{1,0:T(8,128)S(1)}, bf16[256,1024]{1,0:T(8,128)(2,1)S(1)}, bf16[8,2,128,128]{3,2,1,0:T(8,128)(2,1)}, f32[8,1024]{1,0:T(8,128)S(1)}) custom-call(f32[256,1024]{1,0:T(8,128)S(1)} %copy-done.10, bf16[256,1024]{1,0:T(8,128)(2,1)S(1)} %copy-done.22, f32[256,1024]{1,0:T(8,128)} %get-tuple-element.176.d_top_ref, ...), custom_call_target="tpu_custom_call" | custom-call | flops 5500000256 | bytes 1048576 | tf_op jit(solution)/shard_map/turn/pallas_call | solution.py:1117
  236.7 4.2 all-to-all-start.3
  241.1 5.3 %times.1 = (bf16[256,1024]{1,0:T(8,128)(2,1)S(1)}, bf16[256,1024]{1,0:T(8,128)(2,1)S(1)}, bf16[256,1024]{1,0:T(8,128)(2,1)S(1)}, bf16[256,1024]{1,0:T(8,128)(2,1)}) custom-call(bf16[1024,768]{1,0:T(8,128)(2,1)} %get-tuple-element.92.refs_0_, bf16[768,1024]{1,0:T(8,128)(2,1)} %get-tuple-element.93.refs_1_, ...), custom_call_target="tpu_custom_call" | custom-call | flops 3300000000 | bytes 1048576 | tf_op jit(solution)/shard_map/times/pallas_call | solution.py:420
  260.7 8.4 %all-to-all-done.3.refs_8_ = bf16[8,2,128,128]{3,2,1,0:T(8,128)(2,1)} async-done(((bf16[8,2,128,128]{3,2,1,0:T(8,128)(2,1)}), bf16[8,2,128,128]{3,2,1,0:T(8,128)(2,1)}, u32[]{:S(2)}, u32[]{:S(2)}) %all-to-all-start.3) | async-done | bytes 524320 | tf_op jit(solution)/shard_map/all_to_all | solution.py:1281
  269.1 13.3 %mixer_scan_back.1 = (f32[2,16,64,128]{3,2,1,0:T(8,128)}, f32[2,16,128,128]{3,2,1,0:T(8,128)}, f32[2,16,128,128]{3,2,1,0:T(8,128)}, bf16[2,1024,128]{2,1,0:T(8,128)(2,1)}, f32[8,128]{1,0:T(8,128)}) custom-call(f32[2,16,128,128]{3,2,1,0:T(8,128)} %get-tuple-element.80.refs_0_, f32[2,16,64,128]{3,2,1,0:T(8,128)} %get-tuple-element.82.refs_2_.refs_1_.refs_6_, ...), custom_call_target="tpu_custom_call" | custom-call | flops 14080000000 | bytes 1048576 | tf_op jit(solution)/shard_map/mixer_scan_back/pallas_call | solution.py:420
  283.2 34.8 %mixer_grads.1 = (bf16[2,1024,896]{2,1,0:T(8,128)(2,1)}, f32[8,640]{1,0:T(8,128)}, f32[8,128]{1,0:T(8,128)}) custom-call(bf16[2,1024,768]{2,1,0:T(8,128)(2,1)} %get-tuple-element.70.refs_0_.refs_1_.refs_6_.refs_5_, bf16[2,1024,768]{2,1,0:T(8,128)(2,1)} %get-tuple-element.70.refs_0_.refs_1_.refs_6_.refs_5_, ...), custom_call_target="tpu_custom_call" | custom-call | flops 35200000000 | bytes 1048576 | tf_op jit(solution)/shard_map/mixer_grads/pallas_call | solution.py:420
  318.0 8.4 %input_back.1 = bf16[8,2,128,1024]{3,2,1,0:T(8,128)(2,1)} custom-call(bf16[2,1024,896]{2,1,0:T(8,128)(2,1)} %get-tuple-element.116.d_ext_ref.refs_1_, bf16[1024,896]{1,0:T(8,128)(2,1)} %pad_maximum_fusion.1.refs_1_.w_ref.refs_2_), custom_call_target="tpu_custom_call" | custom-call | flops 7699999744 | bytes 1048576 | tf_op jit(solution)/shard_map/input_back/pallas_call | solution.py:1047
  334.2 9.2 %input_grads.1 = (bf16[1024,768]{1,0:T(8,128)(2,1)}, f32[8,1024]{1,0:T(8,128)}) custom-call(bf16[2,1024,1024]{2,1,0:T(8,128)(2,1)} %get-tuple-element.118.refs_0_, bf16[2,1024,896]{2,1,0:T(8,128)(2,1)} %get-tuple-element.116.d_ext_ref.refs_1_, bf16[1024,896]{1,0:T(8,128)(2,1)} %pad_maximum_fusion.1.refs_1_.w_ref.refs_2_, f32[1,1024]{1,0:T(1,128)} %bitcast.181, ...), custom_call_target="tpu_custom_call" | custom-call | flops 7699999744 | bytes 1048576 | tf_op jit(solution)/shard_map/input_grads/pallas_call | solution.py:420
  347.0 13.1 %collective-permute-done.35.refs_1_ = bf16[4,32,1024]{2,1,0:T(8,128)(2,1)S(1)} collective-permute-done((bf16[4,32,1024]{2,1,0:T(8,128)(2,1)S(1)}, bf16[4,32,1024]{2,1,0:T(8,128)(2,1)S(1)}, u32[]{:S(2)}, u32[]{:S(2)}) %collective-permute-start.35) | collective-permute-done | bytes 262176 | tf_op jit(solution)/shard_map/ppermute | solution.py:1144
  368.3 8.7 %collective-permute-done.38.refs_1_ = bf16[8,32,768]{2,1,0:T(8,128)(2,1)S(1)} collective-permute-done((bf16[8,32,768]{2,1,0:T(8,128)(2,1)S(1)}, bf16[8,32,768]{2,1,0:T(8,128)(2,1)S(1)}, u32[]{:S(2)}, u32[]{:S(2)}) %collective-permute-start.38) | collective-permute-done | bytes 393248 | tf_op jit(solution)/shard_map/ppermute | solution.py:1144
  384.4 3.5 all-to-all-start.4
  388.0 4.3 collective-permute-done.43.refs_1_.refs_2_
  394.9 5.4 %collective-permute-done.44.refs_2_ = bf16[1,32,1024]{2,1,0:T(8,128)(2,1)S(1)} collective-permute-done((bf16[1,32,1024]{2,1,0:T(8,128)(2,1)S(1)}, bf16[1,32,1024]{2,1,0:T(8,128)(2,1)S(1)}, u32[]{:S(2)}, u32[]{:S(2)}) %collective-permute-start.44) | collective-permute-done | bytes 65568 | tf_op jit(solution)/shard_map/ppermute | solution.py:1144
  407.0 6.3 %place_units.1.refs_1_.refs_5_ = f32[128,5632]{1,0:T(8,128)} custom-call(s32[2]{0:T(128)S(1)} %pad_add_fusion.where, bf16[128,2304]{1,0:T(8,128)(2,1)S(1)} %copy-done.11, bf16[128,2304]{1,0:T(8,128)(2,1)} %collective-permute-done.45.refs_1_, bf16[128,2304]{1,0:T(8,128)(2,1)} %collective-permute-done.43.refs_1_.refs_2_, ...), custom_call_target="tpu_custom_call" | custom-call | flops 5500000256 | bytes 1048576 | tf_op jit(solution)/shard_map/place_units/pallas_call | solution.py:784
  413.3 3.2 place_rows.2
  427.4 4.0 place_heads.1
  (361 shorter events, 159.4 us)
Async XLA Ops:
  10.5 31.5 %collective-permute-start.9 = (bf16[256,1024]{1,0:T(8,128)(2,1)}, bf16[256,1024]{1,0:T(8,128)(2,1)}, u32[]{:S(2)}, u32[]{:S(2)}) collective-permute-start(bf16[256,1024]{1,0:T(8,128)(2,1)} %get-tuple-element.177), channel_id=1, source_target_pairs={{0,16},{8,24},{16,0},{24,8},{1,17},{9,25},{17,1},{25,9},{2,18},{10... | collective-permute-start | bytes 1572872 | tf_op jit(solution)/shard_map/ppermute | solution.py:1144
  13.4 45.2 %collective-permute-start.8 = (bf16[256,1024]{1,0:T(8,128)(2,1)}, bf16[256,1024]{1,0:T(8,128)(2,1)}, u32[]{:S(2)}, u32[]{:S(2)}) collective-permute-start(bf16[256,1024]{1,0:T(8,128)(2,1)} %get-tuple-element.177), channel_id=1, source_target_pairs={{0,8},{8,0},{16,24},{24,16},{1,9},{9,1},{17,25},{25,17},{2,10},{10... | collective-permute-start | bytes 1572872 | tf_op jit(solution)/shard_map/ppermute | solution.py:1144
  13.4 26.0 %collective-permute-start = (bf16[2,128,1024]{2,1,0:T(8,128)(2,1)S(1)}, bf16[2,128,1024]{2,1,0:T(8,128)(2,1)}, u32[]{:S(2)}, u32[]{:S(2)}) collective-permute-start(bf16[2,128,1024]{2,1,0:T(8,128)(2,1)S(1)} %bitcast.165), channel_id=1, source_target_pairs={{0,2},{2,4},{4,6},{6,7},{7,5},{5,3},{3,1},{1,0},{8,10},{10,12},{12... | collective-permute-start | bytes 1572872 | tf_op jit(solution)/shard_map/ppermute | solution.py:1234
  15.0 27.0 %collective-permute-start.1 = (bf16[2,128,1024]{2,1,0:T(8,128)(2,1)S(1)}, bf16[2,128,1024]{2,1,0:T(8,128)(2,1)}, u32[]{:S(2)}, u32[]{:S(2)}) collective-permute-start(bf16[2,128,1024]{2,1,0:T(8,128)(2,1)S(1)} %bitcast.166), channel_id=1, source_target_pairs={{2,0},{4,2},{6,4},{7,6},{5,7},{3,5},{1,3},{0,1},{10,8},{12,10},{14... | collective-permute-start | bytes 1572872 | tf_op jit(solution)/shard_map/ppermute | solution.py:1235
  17.2 26.9 %all-to-all-start = ((bf16[8,32,768]{2,1,0:T(8,128)(2,1)}), bf16[8,32,768]{2,1,0:T(8,128)(2,1)S(1)}, u32[]{:S(2)}, u32[]{:S(2)}) async-start(bf16[8,32,768]{2,1,0:T(8,128)(2,1)} %reshape_broadcast_in_dim_reshape.3), calls=%async_computation | async-start | bytes 786432 | tf_op jit(solution)/shard_map/all_to_all | solution.py:1281
  23.0 158.1 %all-gather.2.cloned.1.call-start = ((), (), s32[]{:S(2)}) async-start(), calls=%async_computation.7 | async-start | bytes 5308416 | tf_op jit(solution)/shard_map/all_gather | solution.py:1343
  23.1 18.2 %collective-permute-start.11 = (bf16[1,32,1024]{2,1,0:T(8,128)(2,1)S(1)}, bf16[1,32,1024]{2,1,0:T(8,128)(2,1)S(1)}, u32[]{:S(2)}, u32[]{:S(2)}) collective-permute-start(bf16[1,32,1024]{2,1,0:T(8,128)(2,1)S(1)} %dynamic-slice_bitcast_fusion.3), channel_id=1, source_target_pairs={{0,4},{1,5},{2,6},{3,7},{4,0},{5,1},{6,2},{7,3},{8,12},{9,13},{10,... | collective-permute-start | bytes 196616 | tf_op jit(solution)/shard_map/ppermute | solution.py:1144
  39.4 13.1 %collective-permute-start.2 = (bf16[2,128,1024]{2,1,0:T(8,128)(2,1)}, bf16[2,128,1024]{2,1,0:T(8,128)(2,1)S(1)}, u32[]{:S(2)}, u32[]{:S(2)}) collective-permute-start(bf16[2,128,1024]{2,1,0:T(8,128)(2,1)} %collective-permute-done), channel_id=1, source_target_pairs={{0,2},{2,4},{4,6},{6,7},{7,5},{5,3},{3,1},{1,0},{8,10},{10,12},{12... | collective-permute-start | bytes 1572872 | tf_op jit(solution)/shard_map/ppermute | solution.py:1234
  42.0 18.6 %collective-permute-start.10 = (bf16[256,1024]{1,0:T(8,128)(2,1)}, bf16[256,1024]{1,0:T(8,128)(2,1)S(1)}, u32[]{:S(2)}, u32[]{:S(2)}) collective-permute-start(bf16[256,1024]{1,0:T(8,128)(2,1)} %collective-permute-done.9), channel_id=1, source_target_pairs={{0,8},{8,0},{16,24},{24,16},{1,9},{9,1},{17,25},{25,17},{2,10},{10... | collective-permute-start | bytes 1572872 | tf_op jit(solution)/shard_map/ppermute | solution.py:1144
  42.0 14.7 %collective-permute-start.3 = (bf16[2,128,1024]{2,1,0:T(8,128)(2,1)}, bf16[2,128,1024]{2,1,0:T(8,128)(2,1)}, u32[]{:S(2)}, u32[]{:S(2)}) collective-permute-start(bf16[2,128,1024]{2,1,0:T(8,128)(2,1)} %collective-permute-done.1), channel_id=1, source_target_pairs={{2,0},{4,2},{6,4},{7,6},{5,7},{3,5},{1,3},{0,1},{10,8},{12,10},{14... | collective-permute-start | bytes 1572872 | tf_op jit(solution)/shard_map/ppermute | solution.py:1235
  56.6 18.6 %collective-permute-start.4 = (bf16[2,128,1024]{2,1,0:T(8,128)(2,1)}, bf16[2,128,1024]{2,1,0:T(8,128)(2,1)}, u32[]{:S(2)}, u32[]{:S(2)}) collective-permute-start(bf16[2,128,1024]{2,1,0:T(8,128)(2,1)} %fence.15), channel_id=1, source_target_pairs={{0,2},{2,4},{4,6},{6,7},{7,5},{5,3},{3,1},{1,0},{8,10},{10,12},{12... | collective-permute-start | bytes 1572872 | tf_op jit(solution)/shard_map/ppermute | solution.py:1234
  58.6 14.5 %collective-permute-start.12 = (bf16[2,128,1024]{2,1,0:T(8,128)(2,1)}, bf16[2,128,1024]{2,1,0:T(8,128)(2,1)S(1)}, u32[]{:S(2)}, u32[]{:S(2)}) collective-permute-start(bf16[2,128,1024]{2,1,0:T(8,128)(2,1)} %collective-permute-done.3), channel_id=1, source_target_pairs={{2,0},{4,2},{6,4},{7,6},{5,7},{3,5},{1,3},{0,1},{10,8},{12,10},{14... | collective-permute-start | bytes 1572872 | tf_op jit(solution)/shard_map/ppermute | solution.py:1235
  107.8 14.1 %collective-permute-start.16 = (bf16[4,32,1024]{2,1,0:T(8,128)(2,1)}, bf16[4,32,1024]{2,1,0:T(8,128)(2,1)S(1)}, u32[]{:S(2)}, u32[]{:S(2)}) collective-permute-start(bf16[4,32,1024]{2,1,0:T(8,128)(2,1)} %fence.19), channel_id=1, source_target_pairs={{0,1},{1,0},{2,3},{3,2},{4,5},{5,4},{6,7},{7,6},{8,9},{9,8},{10,11... | collective-permute-start | bytes 786440 | tf_op jit(solution)/shard_map/ppermute | solution.py:1144
  118.0 19.1 %all-to-all-start.1 = ((bf16[8,1,128,128]{3,2,1,0:T(8,128)(2,1)}), bf16[8,1,128,128]{3,2,1,0:T(8,128)(2,1)S(1)}, u32[]{:S(2)}, u32[]{:S(2)}) async-start(bf16[8,1,128,128]{3,2,1,0:T(8,128)(2,1)} %get-tuple-element.77.refs_1_), calls=%async_computation.1 | async-start | bytes 524288 | tf_op jit(solution)/shard_map/all_to_all | solution.py:1284
  135.5 16.7 %collective-permute-start.17 = (bf16[8,32,1024]{2,1,0:T(8,128)(2,1)S(1)}, bf16[8,32,1024]{2,1,0:T(8,128)(2,1)S(1)}, u32[]{:S(2)}, u32[]{:S(2)}) collective-permute-start(bf16[8,32,1024]{2,1,0:T(8,128)(2,1)S(1)} %copy-done.6), channel_id=1, source_target_pairs={{0,8},{8,0},{16,24},{24,16},{1,9},{9,1},{17,25},{25,17},{2,10},{10... | collective-permute-start | bytes 1572872 | tf_op jit(solution)/shard_map/ppermute | solution.py:1144
  135.6 16.6 %collective-permute-start.19 = (bf16[8,32,1024]{2,1,0:T(8,128)(2,1)S(1)}, bf16[8,32,1024]{2,1,0:T(8,128)(2,1)}, u32[]{:S(2)}, u32[]{:S(2)}) collective-permute-start(bf16[8,32,1024]{2,1,0:T(8,128)(2,1)S(1)} %collective-permute-done.18.refs_2_), channel_id=1, source_target_pairs={{0,8},{8,0},{16,24},{24,16},{1,9},{9,1},{17,25},{25,17},{2,10},{10... | collective-permute-start | bytes 1572872 | tf_op jit(solution)/shard_map/ppermute | solution.py:1144
  146.7 21.9 %all-to-all-start.2 = ((bf16[8,1,128,128]{3,2,1,0:T(8,128)(2,1)}), bf16[8,1,128,128]{3,2,1,0:T(8,128)(2,1)S(1)}, u32[]{:S(2)}, u32[]{:S(2)}) async-start(bf16[8,1,128,128]{3,2,1,0:T(8,128)(2,1)} %get-tuple-element.88), calls=%async_computation.2 | async-start | bytes 524288 | tf_op jit(solution)/shard_map/all_to_all | solution.py:1284
  151.7 225.3 %reduce-scatter.5.cloned.1.call-start = ((), (), s32[]{:S(2)}) async-start(), calls=%async_computation.9 | async-start | bytes 5308416 | tf_op jit(solution)/shard_map/reduce_scatter | solution.py:1369
  157.7 15.2 %collective-permute-start.22 = (bf16[128,1024]{1,0:T(8,128)(2,1)S(1)}, bf16[128,1024]{1,0:T(8,128)(2,1)}, u32[]{:S(2)}, u32[]{:S(2)}) collective-permute-start(bf16[128,1024]{1,0:T(8,128)(2,1)S(1)} %bitcast.183), channel_id=1, source_target_pairs={{0,16},{8,24},{16,0},{24,8},{1,17},{9,25},{17,1},{25,9},{2,18},{10... | collective-permute-start | bytes 786440 | tf_op jit(solution)/shard_map/ppermute | solution.py:1144
  214.7 14.3 %collective-permute-start.28 = (bf16[256,1024]{1,0:T(8,128)(2,1)S(1)}, bf16[256,1024]{1,0:T(8,128)(2,1)S(1)}, u32[]{:S(2)}, u32[]{:S(2)}) collective-permute-start(bf16[256,1024]{1,0:T(8,128)(2,1)S(1)} %add_convert_fusion.2), channel_id=1, source_target_pairs={{0,16},{8,24},{16,0},{24,8},{1,17},{9,25},{17,1},{25,9},{2,18},{10... | collective-permute-start | bytes 1572872 | tf_op jit(solution)/shard_map/ppermute | solution.py:1144
  236.7 32.3 %all-to-all-start.3 = ((bf16[8,2,128,128]{3,2,1,0:T(8,128)(2,1)}), bf16[8,2,128,128]{3,2,1,0:T(8,128)(2,1)}, u32[]{:S(2)}, u32[]{:S(2)}) async-start(bf16[8,2,128,128]{3,2,1,0:T(8,128)(2,1)} %get-tuple-element.100.refs_2_.refs_1_), calls=%async_computation.3 | async-start | bytes 1048576 | tf_op jit(solution)/shard_map/all_to_all | solution.py:1281
  240.9 195.9 %reduce-scatter.3.cloned.1.call-start = ((), (), s32[]{:S(2)}) async-start(), calls=%async_computation.8 | async-start | bytes 4718592 | tf_op jit(solution)/shard_map/reduce_scatter | solution.py:1399
  256.3 26.1 %collective-permute-start.31 = (bf16[256,1024]{1,0:T(8,128)(2,1)}, bf16[256,1024]{1,0:T(8,128)(2,1)}, u32[]{:S(2)}, u32[]{:S(2)}) collective-permute-start(bf16[256,1024]{1,0:T(8,128)(2,1)} %add_convert_fusion.1), channel_id=1, source_target_pairs={{0,16},{8,24},{16,0},{24,8},{1,17},{9,25},{17,1},{25,9},{2,18},{10... | collective-permute-start | bytes 1572872 | tf_op jit(solution)/shard_map/ppermute | solution.py:1144
  259.6 22.8 %collective-permute-start.33 = (bf16[8,32,1024]{2,1,0:T(8,128)(2,1)}, bf16[8,32,1024]{2,1,0:T(8,128)(2,1)S(1)}, u32[]{:S(2)}, u32[]{:S(2)}) collective-permute-start(bf16[8,32,1024]{2,1,0:T(8,128)(2,1)} %fusion.1), channel_id=1, source_target_pairs={{0,16},{8,24},{16,0},{24,8},{1,17},{9,25},{17,1},{25,9},{2,18},{10... | collective-permute-start | bytes 1572872 | tf_op jit(solution)/shard_map/ppermute | solution.py:1144
  332.2 27.9 %collective-permute-start.35 = (bf16[4,32,1024]{2,1,0:T(8,128)(2,1)S(1)}, bf16[4,32,1024]{2,1,0:T(8,128)(2,1)S(1)}, u32[]{:S(2)}, u32[]{:S(2)}) collective-permute-start(bf16[4,32,1024]{2,1,0:T(8,128)(2,1)S(1)} %fusion.7), channel_id=1, source_target_pairs={{0,4},{1,5},{2,6},{3,7},{4,0},{5,1},{6,2},{7,3},{8,12},{9,13},{10,... | collective-permute-start | bytes 786440 | tf_op jit(solution)/shard_map/ppermute | solution.py:1144
  367.5 13.9 %collective-permute-start.42 = (bf16[2,32,1024]{2,1,0:T(8,128)(2,1)S(1)}, bf16[2,32,1024]{2,1,0:T(8,128)(2,1)S(1)}, u32[]{:S(2)}, u32[]{:S(2)}) collective-permute-start(bf16[2,32,1024]{2,1,0:T(8,128)(2,1)S(1)} %fusion.8), channel_id=1, source_target_pairs={{0,2},{1,3},{2,0},{3,1},{4,6},{5,7},{6,4},{7,5},{8,10},{9,11},{10,... | collective-permute-start | bytes 393224 | tf_op jit(solution)/shard_map/ppermute | solution.py:1144
  377.7 14.6 %collective-permute-start.43 = (bf16[128,2304]{1,0:T(8,128)(2,1)}, bf16[128,2304]{1,0:T(8,128)(2,1)}, u32[]{:S(2)}, u32[]{:S(2)}) collective-permute-start(bf16[128,2304]{1,0:T(8,128)(2,1)} %fence.26.refs_0_), channel_id=1, source_target_pairs={{0,16},{8,24},{16,0},{24,8},{1,17},{9,25},{17,1},{25,9},{2,18},{10... | collective-permute-start | bytes 1769480 | tf_op jit(solution)/shard_map/ppermute | solution.py:1144
  384.4 18.8 %all-to-all-start.4 = ((bf16[8,48,768]{2,1,0:T(8,128)(2,1)}), bf16[8,48,768]{2,1,0:T(8,128)(2,1)S(1)}, u32[]{:S(2)}, u32[]{:S(2)}) async-start(bf16[8,48,768]{2,1,0:T(8,128)(2,1)} %copy-done.12), calls=%async_computation.5 | async-start | bytes 1179648 | tf_op jit(solution)/shard_map/all_to_all | solution.py:1284
  387.9 18.0 %collective-permute-start.45 = (bf16[128,2304]{1,0:T(8,128)(2,1)}, bf16[128,2304]{1,0:T(8,128)(2,1)}, u32[]{:S(2)}, u32[]{:S(2)}) collective-permute-start(bf16[128,2304]{1,0:T(8,128)(2,1)} %fence.26.refs_0_), channel_id=1, source_target_pairs={{0,8},{8,0},{16,24},{24,16},{1,9},{9,1},{17,25},{25,17},{2,10},{10... | collective-permute-start | bytes 1769480 | tf_op jit(solution)/shard_map/ppermute | solution.py:1144
  392.4 13.6 %collective-permute-start.46 = (bf16[128,2304]{1,0:T(8,128)(2,1)}, bf16[128,2304]{1,0:T(8,128)(2,1)}, u32[]{:S(2)}, u32[]{:S(2)}) collective-permute-start(bf16[128,2304]{1,0:T(8,128)(2,1)} %collective-permute-done.43.refs_1_.refs_2_), channel_id=1, source_target_pairs={{0,8},{8,0},{16,24},{24,16},{1,9},{9,1},{17,25},{25,17},{2,10},{10... | collective-permute-start | bytes 1769480 | tf_op jit(solution)/shard_map/ppermute | solution.py:1144
  394.7 29.0 %collective-permute-start.29 = (bf16[256,1024]{1,0:T(8,128)(2,1)}, bf16[256,1024]{1,0:T(8,128)(2,1)}, u32[]{:S(2)}, u32[]{:S(2)}) collective-permute-start(bf16[256,1024]{1,0:T(8,128)(2,1)} %copy-done.31), channel_id=1, source_target_pairs={{0,8},{8,0},{16,24},{24,16},{1,9},{9,1},{17,25},{25,17},{2,10},{10... | collective-permute-start | bytes 1572872 | tf_op jit(solution)/shard_map/ppermute | solution.py:1144
  404.0 13.7 %collective-permute-start.48 = (bf16[8,48,768]{2,1,0:T(8,128)(2,1)}, bf16[8,48,768]{2,1,0:T(8,128)(2,1)S(1)}, u32[]{:S(2)}, u32[]{:S(2)}) collective-permute-start(bf16[8,48,768]{2,1,0:T(8,128)(2,1)} %fence.27.refs_0_), channel_id=1, source_target_pairs={{0,16},{8,24},{16,0},{24,8},{1,17},{9,25},{17,1},{25,9},{2,18},{10... | collective-permute-start | bytes 1769480 | tf_op jit(solution)/shard_map/ppermute | solution.py:1144
  (96 other events, 483.4 us)
Sparse Core Ops, SparseCore 0:
  85.1 88.0 all-gather.1
  212.3 106.0 reduce-scatter.4
  326.5 107.3 reduce-scatter.2

commit v6 on v5

--- a/solution.py
+++ b/solution.py
@@ -612,36 +612,6 @@
     )(x, gain[None], weight, router_weight)
 
 
-def ring_add_kernel(table, ahead_ref, behind_ref, up_ref, low_ref, up_out, low_out):
-    up_out[...] = (ahead_ref[...].astype(F32) + up_ref[0, 0].astype(F32)).astype(up_out.dtype)
-    low_out[...] = (behind_ref[...].astype(F32) + low_ref[0, 0].astype(F32)).astype(low_out.dtype)
-
-
-def ring_add(table, step, ahead, behind, parts, kind, earlier=()):
-    rows, model = ahead.shape
-    one = pl.BlockSpec((rows, model), lambda i, table: (0, 0))
-    part = lambda m: pl.BlockSpec((1, 1, rows, model), lambda i, table: (m, table[2 * step + m], 0, 0))
-    made = jax.ShapeDtypeStruct((rows, model), kind)
-    n_in = 5
-
-    def body(*refs):
-        ring_add_kernel(*refs[:n_in], *refs[n_in + len(earlier) :])
-
-    return pl.pallas_call(
-        body,
-        grid_spec=pltpu.PrefetchScalarGridSpec(
-            num_scalar_prefetch=1,
-            grid=(1,),
-            in_specs=[one, one, part(0), part(1)] + [pl.BlockSpec(memory_space=pl.ANY)] * len(earlier),
-            out_specs=[one, one],
-        ),
-        out_shape=[made, made],
-        compiler_params=small_params("arbitrary"),
-        cost_estimate=cost(1, 1.0),
-        name="ring_add",
-    )(table, ahead, behind, parts, parts, *earlier)
-
-
 def input_grads_kernel(normed_ref, d_ext_ref, w_ext_ref, gain_ref, out_ref, lines_ref):
     total = dot(normed_ref[0], d_ext_ref[0], 0, 0)
     for m in range(1, normed_ref.shape[0]):
@@ -936,21 +906,22 @@
     )(left, right)
 
 
-def feed_grads(mid, d_gu, g_down, n_seq, earlier=(), size=256):
+def feed_grads(mid, d_gu, act, d_top, n_seq, earlier=(), size=512):
     tokens, model = mid.shape
     n_units = d_gu.shape[2]
     shard, unit_pad = model // n_seq, n_units // n_seq
     per = size // shard
 
-    def body(mid_ref, d_gu_ref, g_down_ref, out_ref):
+    def body(mid_ref, d_gu_ref, act_ref, d_top_ref, out_ref):
         mid = mid_ref[...]
+        g_down = dot(act_ref[...], d_top_ref[...], 0, 0).astype(BF)
         for half in range(2):
             value = dot(mid, d_gu_ref[half], 0, 0).astype(BF)
             out_ref[:, half * n_units : (half + 1) * n_units] = value
         rest = model - n_units
         step = unit_pad * rest // n_units
         for part in range(per):
-            at, rows = part * shard, g_down_ref[part * unit_pad : (part + 1) * unit_pad]
+            at, rows = part * shard, g_down[part * unit_pad : (part + 1) * unit_pad]
             out_ref[at : at + unit_pad, 2 * n_units :] = rows[:, :n_units]
             for b in range(n_units // rest):
                 to = 2 * n_units + b * rest
@@ -962,7 +933,7 @@
         body,
         [
             pl.BlockSpec((tokens, size), lambda i: (0, i)), whole(d_gu.shape),
-            pl.BlockSpec((per * unit_pad, model), lambda i: (i, 0)),
+            pl.BlockSpec((tokens, per * unit_pad), lambda i: (0, i)), whole(d_top.shape),
         ],
         earlier,
         grid=(model // size,),
@@ -971,7 +942,7 @@
         compiler_params=params("arbitrary"),
         cost_estimate=cost(1, 7.0),
         name="feed_grads",
-    )(mid, d_gu, g_down)
+    )(mid, d_gu, act, d_top)
 
 
 def place_pieces_kernel(order, where, *refs):
@@ -1027,7 +998,7 @@
         ],
         out_specs=[rows] * 3,
         out_shape=[made(F32), made(BF), made(BF)],
-        compiler_params=small_params("arbitrary"),
+        compiler_params=params("arbitrary"),
         cost_estimate=cost(1, 2.0),
         name="middle",
     )(gated, x, w_out, gain[None])
@@ -1129,7 +1100,7 @@
             jax.ShapeDtypeStruct((n_heads, n_micro, n_tok, LANES), BF),
             jax.ShapeDtypeStruct((8, model), F32),
         ],
-        compiler_params=small_params("arbitrary"),
+        compiler_params=params("arbitrary"),
         cost_estimate=cost(1, 5.0),
         name="turn",
     )(own, got, d_top, residual, w_out, gain[None])
@@ -1364,8 +1335,7 @@
     mid_rows, act, d_gu, down, *d_mid = feed(
         mid_rows, d_rows, weights_all, n_units, n_seq, n_row
     )
-    g_down = matmul("tf,td->fd", act, d_rows, BF)
-    g_feed = feed_grads(mid_rows, d_gu, g_down, n_seq)
+    g_feed = feed_grads(mid_rows, d_gu, act, d_rows, n_seq)
     g_feed_sum = lax.psum_scatter(g_feed, "seq", scatter_dimension=0, tiled=True)
     d_mid_own, d_mid_got = row_scatter_halves(d_mid)
 

time: 455 us -> 450 us (0.989)
  local copies, waits for them, and re-layouts: 62.9 us -> 54.3 us
  Pallas kernels: 175 us -> 181 us
  matrix products: 6.59 us -> 1.88 us
    unnamed x143 -> x147, local copies, waits for them, and re-layouts: 32.2 us -> 21.6 us
    all_to_all x3, starting transfers between devices: 12.5 us -> 18.3 us  [seq_parts(): return lax.all_to_all(value, 'seq', 0, 0, tiled=True)]
    pallas_call x2, Pallas kernels: 1.63 us -> 6.91 us  [middle(): pl.pallas_call(partial(middle_kernel, copies), grid=(1,), in_specs=[pl.Bl...]
    dot_general x2 -> x1, matrix products: 6.59 us -> 1.88 us  [matmul(): jnp.einsum(spec, left, right, preferred_element_type=F32).astype(kind)]
  transfers between devices with their start and end apart: 61 -> 61, of which waited for: 23 -> 23; matrix products, arithmetic and copies ran while one was open for 13% -> 13% of each run, Pallas kernels for 33% -> 34%
where the time goes in v6:
time: 450 us; the launch traced here: 443 us
  Pallas kernels  181 us (40%)
  waiting for transfers between devices  101 us (22%)
  starting transfers between devices  64.2 us (14%)
  local copies, waits for them, and re-layouts  54.3 us (12%)
  other arithmetic  25.4 us (6%)
  between operations  15 us (3%)
    pallas_call x12, Pallas kernels, launch(): return lambda *operands: called(*operands, *others)  125 us
    ppermute x45, waiting for transfers between devices, exchange(): return lax.ppermute(value, axis, [(i, i ^ bit) for i in range(count)])  56.2 us
    ppermute x45, starting transfers between devices, exchange(): return lax.ppermute(value, axis, [(i, i ^ bit) for i in range(count)])  27.1 us
    unnamed x147, local copies, waits for them, and re-layouts  21.6 us
    all_to_all x3, starting transfers between devices, seq_parts(): return lax.all_to_all(value, 'seq', 0, 0, tiled=True)  18.3 us
    pallas_call x1, Pallas kernels, feed(): pl.pallas_call(partial(feed_kernel, n_seq, n_parts), grid=(n_parts,), in_...  18.3 us
    all_to_all x3, waiting for transfers between devices, seq_parts(): return lax.all_to_all(value, 'seq', 0, 0, tiled=True)  13.2 us
    all_to_all x2, waiting for transfers between devices, to_heads(): lax.all_to_all(jnp.repeat(value, copies, axis=0), 'seq', 0, 0, tiled=True)  12.2 us
  transfers between devices with their start and end apart: 61, of which 23 were waited for; matrix products, arithmetic and copies ran while one was open for 13% of the time, Pallas kernels for 34%

profile of v6, /device:TPU:0, one launch (start us, length us, event | category | flops | bytes accessed | tf_op | source)
XLA Modules:
  0.0 443.2 jit_solution(1763842866187167721)
XLA Ops:
  17.2 5.8 %all-to-all-start = ((bf16[8,32,768]{2,1,0:T(8,128)(2,1)}), bf16[8,32,768]{2,1,0:T(8,128)(2,1)S(1)}, u32[]{:S(2)}, u32[]{:S(2)}) async-start(bf16[8,32,768]{2,1,0:T(8,128)(2,1)} %reshape_broadcast_in_dim_reshape.3), calls=%async_computation | async-start | bytes 786432 | tf_op jit(solution)/shard_map/all_to_all | solution.py:1252
  47.7 5.1 %collective-permute-done.2.refs_0_ = bf16[2,128,1024]{2,1,0:T(8,128)(2,1)S(1)} collective-permute-done((bf16[2,128,1024]{2,1,0:T(8,128)(2,1)}, bf16[2,128,1024]{2,1,0:T(8,128)(2,1)S(1)}, u32[]{:S(2)}, u32[]{:S(2)}) %collective-permute-start.2) | collective-permute-done | bytes 524320 | tf_op jit(solution)/shard_map/ppermute | solution.py:1205
  66.8 7.4 %collective-permute-done.12 = bf16[2,128,1024]{2,1,0:T(8,128)(2,1)S(1)} collective-permute-done((bf16[2,128,1024]{2,1,0:T(8,128)(2,1)}, bf16[2,128,1024]{2,1,0:T(8,128)(2,1)S(1)}, u32[]{:S(2)}, u32[]{:S(2)}) %collective-permute-start.12) | collective-permute-done | bytes 524320 | tf_op jit(solution)/shard_map/ppermute | solution.py:1206
  83.0 3.8 collective-permute-done.13
  87.6 9.1 %project.1 = (bf16[2,1024,1024]{2,1,0:T(8,128)(2,1)}, bf16[2,1024,768]{2,1,0:T(8,128)(2,1)}, f32[2,1024,128]{2,1,0:T(8,128)}) custom-call(bf16[8,2,128,1024]{3,2,1,0:T(8,128)(2,1)} %fusion.6.refs_1_.refs_0_, f32[1,1024]{1,0:T(1,128)} %bitcast.173, bf16[1024,768]{1,0:T(8,128)(2,1)} %bitcast.170, bf16[1024,128]{1,0:T(8,128)(2,1)} %copy-done.28, ...), custom_call_target="tpu_custom_call" | custom-call | flops 12320000000 | bytes 1048576 | tf_op jit(solution)/shard_map/project/pallas_call | solution.py:420
  97.0 12.2 %mixer_prepare.2 = (f32[2,16,128,128]{3,2,1,0:T(8,128)}, f32[2,16,128,128]{3,2,1,0:T(8,128)}, f32[2,16,128,128]{3,2,1,0:T(8,128)}, f32[2,16,64,128]{3,2,1,0:T(8,...) custom-call(bf16[2,1024,768]{2,1,0:T(8,128)(2,1)} %get-tuple-element.70.refs_0_.refs_1_.refs_6_.refs_5_, ...), custom_call_target="tpu_custom_call" | custom-call | flops 13200000000 | bytes 1048576 | tf_op jit(solution)/shard_map/mixer_prepare/pallas_call | solution.py:420
  111.3 8.8 %mixer_scan.2 = (bf16[8,1,128,128]{3,2,1,0:T(8,128)(2,1)}, f32[2,16,64,128]{3,2,1,0:T(8,128)}, f32[2,16,128,128]{3,2,1,0:T(8,128)}, f32[2,16,128,128]{3,2,1,0:T(8,128)}) custom-call(f32[2,16,128,128]{3,2,1,0:T(8,128)} %get-tuple-element.72.refs_0_.refs_6_, f32[2,16,128,128]{3,2,1,0:T(8,128)} %get-tuple-element.73.refs_1_.refs_7_, ...), custom_call_target="tpu_custom_call" | custom-call | flops 8800000000 | bytes 1048576 | tf_op jit(solution)/shard_map/mixer_scan/pallas_call | solution.py:420
  120.1 4.3 all-to-all-start.1
  125.5 12.2 %mixer_prepare.3 = (f32[2,16,128,128]{3,2,1,0:T(8,128)}, f32[2,16,128,128]{3,2,1,0:T(8,128)}, f32[2,16,128,128]{3,2,1,0:T(8,128)}, f32[2,16,64,128]{3,2,1,0:T(8,...) custom-call(bf16[2,1024,768]{2,1,0:T(8,128)(2,1)} %get-tuple-element, ...), custom_call_target="tpu_custom_call", output_to_operand_aliasing={{0}: (5, {}), {1}: (6, {}), {2}: (7, {}), {3}: (8, {}), {4}... | custom-call | flops 13200000000 | bytes 1048576 | tf_op jit(solution)/shard_map/mixer_prepare/pallas_call | solution.py:420
  139.9 8.9 %mixer_scan.3 = (bf16[8,1,128,128]{3,2,1,0:T(8,128)(2,1)}, f32[2,16,64,128]{3,2,1,0:T(8,128)}, f32[2,16,128,128]{3,2,1,0:T(8,128)}, f32[2,16,128,128]{3,2,1,0:T(8,128)}) custom-call(f32[2,16,128,128]{3,2,1,0:T(8,128)} %get-tuple-element.80.refs_0_, ...), custom_call_target="tpu_custom_call", output_to_operand_aliasing={{1}: (9, {}), {2}: (10, {}), {3}: (11, {})} | custom-call | flops 8800000000 | bytes 1048576 | tf_op jit(solution)/shard_map/mixer_scan/pallas_call | solution.py:420
  148.8 5.1 %all-to-all-start.2 = ((bf16[8,1,128,128]{3,2,1,0:T(8,128)(2,1)}), bf16[8,1,128,128]{3,2,1,0:T(8,128)(2,1)S(1)}, u32[]{:S(2)}, u32[]{:S(2)}) async-start(bf16[8,1,128,128]{3,2,1,0:T(8,128)(2,1)} %get-tuple-element.88), calls=%async_computation.2 | async-start | bytes 524288 | tf_op jit(solution)/shard_map/all_to_all | solution.py:1255
  156.4 3.5 middle.2
  161.7 9.1 %all-to-all-done.2.gated_ref = bf16[8,1,128,128]{3,2,1,0:T(8,128)(2,1)S(1)} async-done(((bf16[8,1,128,128]{3,2,1,0:T(8,128)(2,1)}), bf16[8,1,128,128]{3,2,1,0:T(8,128)(2,1)S(1)}, u32[]{:S(2)}, u32[]{:S(2)}) %all-to-all-start.2) | async-done | bytes 262176 | tf_op jit(solution)/shard_map/all_to_all | solution.py:1255
  171.5 3.5 middle.3
  177.0 6.1 %collective-permute-done.23.refs_5_ = bf16[128,1024]{1,0:T(8,128)(2,1)S(1)} collective-permute-done((bf16[128,1024]{1,0:T(8,128)(2,1)}, bf16[128,1024]{1,0:T(8,128)(2,1)S(1)}, u32[]{:S(2)}, u32[]{:S(2)}) %collective-permute-start.23) | collective-permute-done | bytes 262176 | tf_op jit(solution)/shard_map/ppermute | solution.py:1115
  185.4 18.3 %feed.1 = (bf16[1024,1024]{1,0:T(8,128)(2,1)}, bf16[1024,768]{1,0:T(8,128)(2,1)}, bf16[2,1024,768]{2,1,0:T(8,128)(2,1)}, bf16[768,1024]{1,0:T(8,128)(2,1)}, bf16...) custom-call(bf16[1024,1024]{1,0:T(8,128)(2,1)} %pad_maximum_fusion.ref, ...), custom_call_target="tpu_custom_call" | custom-call | flops 15399999488 | bytes 1048576 | tf_op jit(solution)/shard_map/feed/pallas_call | solution.py:864
  203.7 9.9 %feed_grads.1.refs_1_ = bf16[1024,2304]{1,0:T(8,128)(2,1)} custom-call(bf16[1024,1024]{1,0:T(8,128)(2,1)} %get-tuple-element.98.refs_0_, bf16[2,1024,768]{2,1,0:T(8,128)(2,1)} %get-tuple-element.99.refs_1_, bf16[1024,768]{1,0:T(8,128)(2,1)} %get-tuple-element.92.refs_2_.refs_0_, bf16[1024,1024]{1,0:T(8,128)(2,1)} %pad_maximum_fusion.refs_5_.refs_4_.d_top_ref.refs_3_), custom_call_target="tpu_custom_call" | custom-call | flops 7699999744 | bytes 1048576 | tf_op jit(solution)/shard_map/feed_grads/pallas_call | solution.py:420
  219.9 10.2 %collective-permute-done.28.refs_0_ = bf16[256,1024]{1,0:T(8,128)(2,1)S(1)} collective-permute-done((bf16[256,1024]{1,0:T(8,128)(2,1)S(1)}, bf16[256,1024]{1,0:T(8,128)(2,1)S(1)}, u32[]{:S(2)}, u32[]{:S(2)}) %collective-permute-start.28) | collective-permute-done | bytes 524320 | tf_op jit(solution)/shard_map/ppermute | solution.py:1115
  230.9 5.1 %turn.1 = (f32[256,1024]{1,0:T(8,128)}, bf16[256,1024]{1,0:T(8,128)(2,1)}, bf16[8,2,128,128]{3,2,1,0:T(8,128)(2,1)}, f32[8,1024]{1,0:T(8,128)}) custom-call(f32[256,1024]{1,0:T(8,128)} %convert_add_fusion.own_ref, bf16[256,1024]{1,0:T(8,128)(2,1)} %fence.21.got_ref, f32[256,1024]{1,0:T(8,128)} %get-tuple-element.176.d_top_ref, ...), custom_call_target="tpu_custom_call" | custom-call | flops 5500000256 | bytes 1048576 | tf_op jit(solution)/shard_map/turn/pallas_call | solution.py:1088
  235.9 4.2 all-to-all-start.3
  241.4 4.6 %times.1 = (bf16[256,1024]{1,0:T(8,128)(2,1)S(1)}, bf16[256,1024]{1,0:T(8,128)(2,1)S(1)}, bf16[256,1024]{1,0:T(8,128)(2,1)S(1)}, bf16[256,1024]{1,0:T(8,128)(2,1)S(1)}) custom-call(bf16[1024,768]{1,0:T(8,128)(2,1)} %get-tuple-element.92.refs_2_.refs_0_, bf16[768,1024]{1,0:T(8,128)(2,1)} %get-tuple-element.93.refs_1_, bf16[8,2,128,128]{3,2,1,0:T(8,128)(2,1)S(1)} %copy-done.5), custom_call_target="tpu_custom_call" | custom-call | flops 3300000000 | bytes 1048576 | tf_op jit(solution)/shard_map/times/pallas_call | solution.py:420
  256.3 12.2 %all-to-all-done.3.refs_8_ = bf16[8,2,128,128]{3,2,1,0:T(8,128)(2,1)} async-done(((bf16[8,2,128,128]{3,2,1,0:T(8,128)(2,1)}), bf16[8,2,128,128]{3,2,1,0:T(8,128)(2,1)}, u32[]{:S(2)}, u32[]{:S(2)}) %all-to-all-start.3) | async-done | bytes 524320 | tf_op jit(solution)/shard_map/all_to_all | solution.py:1252
  268.5 13.3 %mixer_scan_back.1 = (f32[2,16,64,128]{3,2,1,0:T(8,128)}, f32[2,16,128,128]{3,2,1,0:T(8,128)}, f32[2,16,128,128]{3,2,1,0:T(8,128)}, bf16[2,1024,128]{2,1,0:T(8,128)(2,1)}, f32[8,128]{1,0:T(8,128)}) custom-call(f32[2,16,128,128]{3,2,1,0:T(8,128)} %get-tuple-element.80.refs_0_, f32[2,16,64,128]{3,2,1,0:T(8,128)} %get-tuple-element.82.refs_2_.refs_1_.refs_6_, ...), custom_call_target="tpu_custom_call" | custom-call | flops 14080000000 | bytes 1048576 | tf_op jit(solution)/shard_map/mixer_scan_back/pallas_call | solution.py:420
  282.8 34.8 %mixer_grads.1 = (bf16[2,1024,896]{2,1,0:T(8,128)(2,1)}, f32[8,640]{1,0:T(8,128)}, f32[8,128]{1,0:T(8,128)}) custom-call(bf16[2,1024,768]{2,1,0:T(8,128)(2,1)} %get-tuple-element.70.refs_0_.refs_1_.refs_6_.refs_5_, bf16[2,1024,768]{2,1,0:T(8,128)(2,1)} %get-tuple-element.70.refs_0_.refs_1_.refs_6_.refs_5_, ...), custom_call_target="tpu_custom_call" | custom-call | flops 35200000000 | bytes 1048576 | tf_op jit(solution)/shard_map/mixer_grads/pallas_call | solution.py:420
  317.6 8.4 %input_back.1 = bf16[8,2,128,1024]{3,2,1,0:T(8,128)(2,1)} custom-call(bf16[2,1024,896]{2,1,0:T(8,128)(2,1)} %get-tuple-element.116.d_ext_ref.refs_1_, bf16[1024,896]{1,0:T(8,128)(2,1)} %pad_maximum_fusion.1.refs_1_.w_ref.refs_2_), custom_call_target="tpu_custom_call" | custom-call | flops 7699999744 | bytes 1048576 | tf_op jit(solution)/shard_map/input_back/pallas_call | solution.py:1018
  330.7 9.0 %input_grads.1 = (bf16[1024,768]{1,0:T(8,128)(2,1)}, f32[8,1024]{1,0:T(8,128)}) custom-call(bf16[2,1024,1024]{2,1,0:T(8,128)(2,1)} %get-tuple-element.118.refs_0_, bf16[2,1024,896]{2,1,0:T(8,128)(2,1)} %get-tuple-element.116.d_ext_ref.refs_1_, bf16[1024,896]{1,0:T(8,128)(2,1)} %pad_maximum_fusion.1.refs_1_.w_ref.refs_2_, f32[1,1024]{1,0:T(1,128)} %bitcast.174, ...), custom_call_target="tpu_custom_call" | custom-call | flops 7699999744 | bytes 1048576 | tf_op jit(solution)/shard_map/input_grads/pallas_call | solution.py:420
  343.3 11.1 %collective-permute-done.35.refs_1_ = bf16[4,32,1024]{2,1,0:T(8,128)(2,1)S(1)} collective-permute-done((bf16[4,32,1024]{2,1,0:T(8,128)(2,1)S(1)}, bf16[4,32,1024]{2,1,0:T(8,128)(2,1)S(1)}, u32[]{:S(2)}, u32[]{:S(2)}) %collective-permute-start.35) | collective-permute-done | bytes 262176 | tf_op jit(solution)/shard_map/ppermute | solution.py:1115
  362.0 8.9 %collective-permute-done.38.refs_1_ = bf16[8,32,768]{2,1,0:T(8,128)(2,1)S(1)} collective-permute-done((bf16[8,32,768]{2,1,0:T(8,128)(2,1)S(1)}, bf16[8,32,768]{2,1,0:T(8,128)(2,1)S(1)}, u32[]{:S(2)}, u32[]{:S(2)}) %collective-permute-start.38) | collective-permute-done | bytes 393248 | tf_op jit(solution)/shard_map/ppermute | solution.py:1115
  374.5 8.9 %all-to-all-start.4 = ((bf16[8,48,768]{2,1,0:T(8,128)(2,1)}), bf16[8,48,768]{2,1,0:T(8,128)(2,1)S(1)}, u32[]{:S(2)}, u32[]{:S(2)}) async-start(bf16[8,48,768]{2,1,0:T(8,128)(2,1)} %pack.1), calls=%async_computation.5 | async-start | bytes 1179648 | tf_op jit(solution)/shard_map/all_to_all | solution.py:1255
  389.7 5.9 %collective-permute-done.44.refs_2_ = bf16[1,32,1024]{2,1,0:T(8,128)(2,1)S(1)} collective-permute-done((bf16[1,32,1024]{2,1,0:T(8,128)(2,1)S(1)}, bf16[1,32,1024]{2,1,0:T(8,128)(2,1)S(1)}, u32[]{:S(2)}, u32[]{:S(2)}) %collective-permute-start.44) | collective-permute-done | bytes 65568 | tf_op jit(solution)/shard_map/ppermute | solution.py:1115
  402.9 6.1 %place_units.1.refs_1_.refs_5_ = f32[128,5632]{1,0:T(8,128)} custom-call(s32[2]{0:T(128)S(1)} %pad_add_fusion.where, bf16[128,2304]{1,0:T(8,128)(2,1)S(1)} %copy-done.13, bf16[128,2304]{1,0:T(8,128)(2,1)} %collective-permute-done.45.refs_1_, bf16[128,2304]{1,0:T(8,128)(2,1)S(1)} %copy-done.15, bf16[128,2304]{1,0:T(8,128)(2,1)} %collective-permute-done.46.refs_3_), custom_call_target="tpu_custom_call" | custom-call | flops 5500000256 | bytes 1048576 | tf_op jit(solution)/shard_map/place_units/pallas_call | solution.py:754
  423.2 4.3 place_heads.1
  (364 shorter events, 148.2 us)
Async XLA Ops:
  10.4 32.7 %collective-permute-start.9 = (bf16[256,1024]{1,0:T(8,128)(2,1)}, bf16[256,1024]{1,0:T(8,128)(2,1)}, u32[]{:S(2)}, u32[]{:S(2)}) collective-permute-start(bf16[256,1024]{1,0:T(8,128)(2,1)} %get-tuple-element.177), channel_id=1, source_target_pairs={{0,16},{8,24},{16,0},{24,8},{1,17},{9,25},{17,1},{25,9},{2,18},{10... | collective-permute-start | bytes 1572872 | tf_op jit(solution)/shard_map/ppermute | solution.py:1115
  13.4 46.3 %collective-permute-start.8 = (bf16[256,1024]{1,0:T(8,128)(2,1)}, bf16[256,1024]{1,0:T(8,128)(2,1)}, u32[]{:S(2)}, u32[]{:S(2)}) collective-permute-start(bf16[256,1024]{1,0:T(8,128)(2,1)} %get-tuple-element.177), channel_id=1, source_target_pairs={{0,8},{8,0},{16,24},{24,16},{1,9},{9,1},{17,25},{25,17},{2,10},{10... | collective-permute-start | bytes 1572872 | tf_op jit(solution)/shard_map/ppermute | solution.py:1115
  13.4 26.2 %collective-permute-start = (bf16[2,128,1024]{2,1,0:T(8,128)(2,1)}, bf16[2,128,1024]{2,1,0:T(8,128)(2,1)}, u32[]{:S(2)}, u32[]{:S(2)}) collective-permute-start(bf16[2,128,1024]{2,1,0:T(8,128)(2,1)} %bitcast.164), channel_id=1, source_target_pairs={{0,2},{2,4},{4,6},{6,7},{7,5},{5,3},{3,1},{1,0},{8,10},{10,12},{12... | collective-permute-start | bytes 1572872 | tf_op jit(solution)/shard_map/ppermute | solution.py:1205
  15.0 28.2 %collective-permute-start.1 = (bf16[2,128,1024]{2,1,0:T(8,128)(2,1)}, bf16[2,128,1024]{2,1,0:T(8,128)(2,1)}, u32[]{:S(2)}, u32[]{:S(2)}) collective-permute-start(bf16[2,128,1024]{2,1,0:T(8,128)(2,1)} %bitcast.165), channel_id=1, source_target_pairs={{2,0},{4,2},{6,4},{7,6},{5,7},{3,5},{1,3},{0,1},{10,8},{12,10},{14... | collective-permute-start | bytes 1572872 | tf_op jit(solution)/shard_map/ppermute | solution.py:1206
  17.2 28.1 %all-to-all-start = ((bf16[8,32,768]{2,1,0:T(8,128)(2,1)}), bf16[8,32,768]{2,1,0:T(8,128)(2,1)S(1)}, u32[]{:S(2)}, u32[]{:S(2)}) async-start(bf16[8,32,768]{2,1,0:T(8,128)(2,1)} %reshape_broadcast_in_dim_reshape.3), calls=%async_computation | async-start | bytes 786432 | tf_op jit(solution)/shard_map/all_to_all | solution.py:1252
  23.0 161.7 %all-gather.2.cloned.1.call-start = ((), (), s32[]{:S(2)}) async-start(), calls=%async_computation.7 | async-start | bytes 5308416 | tf_op jit(solution)/shard_map/all_gather | solution.py:1314
  23.7 17.9 %collective-permute-start.11 = (bf16[1,32,1024]{2,1,0:T(8,128)(2,1)}, bf16[1,32,1024]{2,1,0:T(8,128)(2,1)}, u32[]{:S(2)}, u32[]{:S(2)}) collective-permute-start(bf16[1,32,1024]{2,1,0:T(8,128)(2,1)} %dynamic-slice_bitcast_fusion.3), channel_id=1, source_target_pairs={{0,4},{1,5},{2,6},{3,7},{4,0},{5,1},{6,2},{7,3},{8,12},{9,13},{10,... | collective-permute-start | bytes 196616 | tf_op jit(solution)/shard_map/ppermute | solution.py:1115
  39.6 13.1 %collective-permute-start.2 = (bf16[2,128,1024]{2,1,0:T(8,128)(2,1)}, bf16[2,128,1024]{2,1,0:T(8,128)(2,1)S(1)}, u32[]{:S(2)}, u32[]{:S(2)}) collective-permute-start(bf16[2,128,1024]{2,1,0:T(8,128)(2,1)} %collective-permute-done), channel_id=1, source_target_pairs={{0,2},{2,4},{4,6},{6,7},{7,5},{5,3},{3,1},{1,0},{8,10},{10,12},{12... | collective-permute-start | bytes 1572872 | tf_op jit(solution)/shard_map/ppermute | solution.py:1205
  43.1 18.6 %collective-permute-start.10 = (bf16[256,1024]{1,0:T(8,128)(2,1)}, bf16[256,1024]{1,0:T(8,128)(2,1)S(1)}, u32[]{:S(2)}, u32[]{:S(2)}) collective-permute-start(bf16[256,1024]{1,0:T(8,128)(2,1)} %collective-permute-done.9), channel_id=1, source_target_pairs={{0,8},{8,0},{16,24},{24,16},{1,9},{9,1},{17,25},{25,17},{2,10},{10... | collective-permute-start | bytes 1572872 | tf_op jit(solution)/shard_map/ppermute | solution.py:1115
  43.2 14.7 %collective-permute-start.3 = (bf16[2,128,1024]{2,1,0:T(8,128)(2,1)}, bf16[2,128,1024]{2,1,0:T(8,128)(2,1)}, u32[]{:S(2)}, u32[]{:S(2)}) collective-permute-start(bf16[2,128,1024]{2,1,0:T(8,128)(2,1)} %collective-permute-done.1), channel_id=1, source_target_pairs={{2,0},{4,2},{6,4},{7,6},{5,7},{3,5},{1,3},{0,1},{10,8},{12,10},{14... | collective-permute-start | bytes 1572872 | tf_op jit(solution)/shard_map/ppermute | solution.py:1206
  57.8 19.3 %collective-permute-start.4 = (bf16[2,128,1024]{2,1,0:T(8,128)(2,1)}, bf16[2,128,1024]{2,1,0:T(8,128)(2,1)S(1)}, u32[]{:S(2)}, u32[]{:S(2)}) collective-permute-start(bf16[2,128,1024]{2,1,0:T(8,128)(2,1)} %fence.15), channel_id=1, source_target_pairs={{0,2},{2,4},{4,6},{6,7},{7,5},{5,3},{3,1},{1,0},{8,10},{10,12},{12... | collective-permute-start | bytes 1572872 | tf_op jit(solution)/shard_map/ppermute | solution.py:1205
  59.7 14.5 %collective-permute-start.12 = (bf16[2,128,1024]{2,1,0:T(8,128)(2,1)}, bf16[2,128,1024]{2,1,0:T(8,128)(2,1)S(1)}, u32[]{:S(2)}, u32[]{:S(2)}) collective-permute-start(bf16[2,128,1024]{2,1,0:T(8,128)(2,1)} %collective-permute-done.3), channel_id=1, source_target_pairs={{2,0},{4,2},{6,4},{7,6},{5,7},{3,5},{1,3},{0,1},{10,8},{12,10},{14... | collective-permute-start | bytes 1572872 | tf_op jit(solution)/shard_map/ppermute | solution.py:1206
  96.7 13.9 %collective-permute-start.15 = (bf16[2,32,1024]{2,1,0:T(8,128)(2,1)}, bf16[2,32,1024]{2,1,0:T(8,128)(2,1)S(1)}, u32[]{:S(2)}, u32[]{:S(2)}) collective-permute-start(bf16[2,32,1024]{2,1,0:T(8,128)(2,1)} %fence.18), channel_id=1, source_target_pairs={{0,2},{1,3},{2,0},{3,1},{4,6},{5,7},{6,4},{7,5},{8,10},{9,11},{10,... | collective-permute-start | bytes 393224 | tf_op jit(solution)/shard_map/ppermute | solution.py:1115
  111.3 13.1 %collective-permute-start.16 = (bf16[4,32,1024]{2,1,0:T(8,128)(2,1)}, bf16[4,32,1024]{2,1,0:T(8,128)(2,1)S(1)}, u32[]{:S(2)}, u32[]{:S(2)}) collective-permute-start(bf16[4,32,1024]{2,1,0:T(8,128)(2,1)} %fence.19), channel_id=1, source_target_pairs={{0,1},{1,0},{2,3},{3,2},{4,5},{5,4},{6,7},{7,6},{8,9},{9,8},{10,11... | collective-permute-start | bytes 786440 | tf_op jit(solution)/shard_map/ppermute | solution.py:1115
  120.1 19.1 %all-to-all-start.1 = ((bf16[8,1,128,128]{3,2,1,0:T(8,128)(2,1)}), bf16[8,1,128,128]{3,2,1,0:T(8,128)(2,1)S(1)}, u32[]{:S(2)}, u32[]{:S(2)}) async-start(bf16[8,1,128,128]{3,2,1,0:T(8,128)(2,1)} %get-tuple-element.77.refs_1_), calls=%async_computation.1 | async-start | bytes 524288 | tf_op jit(solution)/shard_map/all_to_all | solution.py:1255
  137.7 16.7 %collective-permute-start.17 = (bf16[8,32,1024]{2,1,0:T(8,128)(2,1)S(1)}, bf16[8,32,1024]{2,1,0:T(8,128)(2,1)S(1)}, u32[]{:S(2)}, u32[]{:S(2)}) collective-permute-start(bf16[8,32,1024]{2,1,0:T(8,128)(2,1)S(1)} %copy-done.8), channel_id=1, source_target_pairs={{0,8},{8,0},{16,24},{24,16},{1,9},{9,1},{17,25},{25,17},{2,10},{10... | collective-permute-start | bytes 1572872 | tf_op jit(solution)/shard_map/ppermute | solution.py:1115
  137.8 16.6 %collective-permute-start.19 = (bf16[8,32,1024]{2,1,0:T(8,128)(2,1)S(1)}, bf16[8,32,1024]{2,1,0:T(8,128)(2,1)S(1)}, u32[]{:S(2)}, u32[]{:S(2)}) collective-permute-start(bf16[8,32,1024]{2,1,0:T(8,128)(2,1)S(1)} %collective-permute-done.18.refs_2_), channel_id=1, source_target_pairs={{0,8},{8,0},{16,24},{24,16},{1,9},{9,1},{17,25},{25,17},{2,10},{10... | collective-permute-start | bytes 1572872 | tf_op jit(solution)/shard_map/ppermute | solution.py:1115
  148.8 22.0 %all-to-all-start.2 = ((bf16[8,1,128,128]{3,2,1,0:T(8,128)(2,1)}), bf16[8,1,128,128]{3,2,1,0:T(8,128)(2,1)S(1)}, u32[]{:S(2)}, u32[]{:S(2)}) async-start(bf16[8,1,128,128]{3,2,1,0:T(8,128)(2,1)} %get-tuple-element.88), calls=%async_computation.2 | async-start | bytes 524288 | tf_op jit(solution)/shard_map/all_to_all | solution.py:1255
  153.9 217.0 %reduce-scatter.5.cloned.1.call-start = ((), (), s32[]{:S(2)}) async-start(), calls=%async_computation.9 | async-start | bytes 5308416 | tf_op jit(solution)/shard_map/reduce_scatter | solution.py:1339
  159.9 17.1 %collective-permute-start.22 = (bf16[128,1024]{1,0:T(8,128)(2,1)}, bf16[128,1024]{1,0:T(8,128)(2,1)S(1)}, u32[]{:S(2)}, u32[]{:S(2)}) collective-permute-start(bf16[128,1024]{1,0:T(8,128)(2,1)} %bitcast.219), channel_id=1, source_target_pairs={{0,16},{8,24},{16,0},{24,8},{1,17},{9,25},{17,1},{25,9},{2,18},{10... | collective-permute-start | bytes 786440 | tf_op jit(solution)/shard_map/ppermute | solution.py:1115
  216.0 14.0 %collective-permute-start.28 = (bf16[256,1024]{1,0:T(8,128)(2,1)S(1)}, bf16[256,1024]{1,0:T(8,128)(2,1)S(1)}, u32[]{:S(2)}, u32[]{:S(2)}) collective-permute-start(bf16[256,1024]{1,0:T(8,128)(2,1)S(1)} %add_convert_fusion.2), channel_id=1, source_target_pairs={{0,16},{8,24},{16,0},{24,8},{1,17},{9,25},{17,1},{25,9},{2,18},{10... | collective-permute-start | bytes 1572872 | tf_op jit(solution)/shard_map/ppermute | solution.py:1115
  235.9 32.6 %all-to-all-start.3 = ((bf16[8,2,128,128]{3,2,1,0:T(8,128)(2,1)}), bf16[8,2,128,128]{3,2,1,0:T(8,128)(2,1)}, u32[]{:S(2)}, u32[]{:S(2)}) async-start(bf16[8,2,128,128]{3,2,1,0:T(8,128)(2,1)} %get-tuple-element.100.refs_2_.refs_1_), calls=%async_computation.3 | async-start | bytes 1048576 | tf_op jit(solution)/shard_map/all_to_all | solution.py:1252
  240.1 192.9 %reduce-scatter.3.cloned.1.call-start = ((), (), s32[]{:S(2)}) async-start(), calls=%async_computation.8 | async-start | bytes 4718592 | tf_op jit(solution)/shard_map/reduce_scatter | solution.py:1369
  252.8 29.0 %collective-permute-start.31 = (bf16[256,1024]{1,0:T(8,128)(2,1)S(1)}, bf16[256,1024]{1,0:T(8,128)(2,1)S(1)}, u32[]{:S(2)}, u32[]{:S(2)}) collective-permute-start(bf16[256,1024]{1,0:T(8,128)(2,1)S(1)} %add_convert_fusion.1), channel_id=1, source_target_pairs={{0,16},{8,24},{16,0},{24,8},{1,17},{9,25},{17,1},{25,9},{2,18},{10... | collective-permute-start | bytes 1572872 | tf_op jit(solution)/shard_map/ppermute | solution.py:1115
  254.9 27.0 %collective-permute-start.33 = (bf16[8,32,1024]{2,1,0:T(8,128)(2,1)S(1)}, bf16[8,32,1024]{2,1,0:T(8,128)(2,1)S(1)}, u32[]{:S(2)}, u32[]{:S(2)}) collective-permute-start(bf16[8,32,1024]{2,1,0:T(8,128)(2,1)S(1)} %fusion.1), channel_id=1, source_target_pairs={{0,16},{8,24},{16,0},{24,8},{1,17},{9,25},{17,1},{25,9},{2,18},{10... | collective-permute-start | bytes 1572872 | tf_op jit(solution)/shard_map/ppermute | solution.py:1115
  330.6 23.9 %collective-permute-start.35 = (bf16[4,32,1024]{2,1,0:T(8,128)(2,1)S(1)}, bf16[4,32,1024]{2,1,0:T(8,128)(2,1)S(1)}, u32[]{:S(2)}, u32[]{:S(2)}) collective-permute-start(bf16[4,32,1024]{2,1,0:T(8,128)(2,1)S(1)} %fusion.7), channel_id=1, source_target_pairs={{0,4},{1,5},{2,6},{3,7},{4,0},{5,1},{6,2},{7,3},{8,12},{9,13},{10,... | collective-permute-start | bytes 786440 | tf_op jit(solution)/shard_map/ppermute | solution.py:1115
  371.6 14.6 %collective-permute-start.43 = (bf16[128,2304]{1,0:T(8,128)(2,1)}, bf16[128,2304]{1,0:T(8,128)(2,1)S(1)}, u32[]{:S(2)}, u32[]{:S(2)}) collective-permute-start(bf16[128,2304]{1,0:T(8,128)(2,1)} %fence.26.refs_0_), channel_id=1, source_target_pairs={{0,16},{8,24},{16,0},{24,8},{1,17},{9,25},{17,1},{25,9},{2,18},{10... | collective-permute-start | bytes 1769480 | tf_op jit(solution)/shard_map/ppermute | solution.py:1115
  374.5 24.3 %all-to-all-start.4 = ((bf16[8,48,768]{2,1,0:T(8,128)(2,1)}), bf16[8,48,768]{2,1,0:T(8,128)(2,1)S(1)}, u32[]{:S(2)}, u32[]{:S(2)}) async-start(bf16[8,48,768]{2,1,0:T(8,128)(2,1)} %pack.1), calls=%async_computation.5 | async-start | bytes 1179648 | tf_op jit(solution)/shard_map/all_to_all | solution.py:1255
  383.4 18.4 %collective-permute-start.45 = (bf16[128,2304]{1,0:T(8,128)(2,1)S(1)}, bf16[128,2304]{1,0:T(8,128)(2,1)}, u32[]{:S(2)}, u32[]{:S(2)}) collective-permute-start(bf16[128,2304]{1,0:T(8,128)(2,1)S(1)} %copy-done.13), channel_id=1, source_target_pairs={{0,8},{8,0},{16,24},{24,16},{1,9},{9,1},{17,25},{25,17},{2,10},{10... | collective-permute-start | bytes 1769480 | tf_op jit(solution)/shard_map/ppermute | solution.py:1115
  386.2 15.6 %collective-permute-start.46 = (bf16[128,2304]{1,0:T(8,128)(2,1)S(1)}, bf16[128,2304]{1,0:T(8,128)(2,1)}, u32[]{:S(2)}, u32[]{:S(2)}) collective-permute-start(bf16[128,2304]{1,0:T(8,128)(2,1)S(1)} %collective-permute-done.43.refs_1_.refs_2_), channel_id=1, source_target_pairs={{0,8},{8,0},{16,24},{24,16},{1,9},{9,1},{17,25},{25,17},{2,10},{10... | collective-permute-start | bytes 1769480 | tf_op jit(solution)/shard_map/ppermute | solution.py:1115
  389.6 30.0 %collective-permute-start.29 = (bf16[256,1024]{1,0:T(8,128)(2,1)}, bf16[256,1024]{1,0:T(8,128)(2,1)}, u32[]{:S(2)}, u32[]{:S(2)}) collective-permute-start(bf16[256,1024]{1,0:T(8,128)(2,1)} %copy-done.24), channel_id=1, source_target_pairs={{0,8},{8,0},{16,24},{24,16},{1,9},{9,1},{17,25},{25,17},{2,10},{10... | collective-permute-start | bytes 1572872 | tf_op jit(solution)/shard_map/ppermute | solution.py:1115
  399.6 14.5 %collective-permute-start.48 = (bf16[8,48,768]{2,1,0:T(8,128)(2,1)}, bf16[8,48,768]{2,1,0:T(8,128)(2,1)S(1)}, u32[]{:S(2)}, u32[]{:S(2)}) collective-permute-start(bf16[8,48,768]{2,1,0:T(8,128)(2,1)} %fence.27.refs_0_), channel_id=1, source_target_pairs={{0,16},{8,24},{16,0},{24,8},{1,17},{9,25},{17,1},{25,9},{2,18},{10... | collective-permute-start | bytes 1769480 | tf_op jit(solution)/shard_map/ppermute | solution.py:1115
  (98 other events, 540.1 us)
Sparse Core Ops, SparseCore 0:
  87.7 87.6 all-gather.1
  213.7 105.7 reduce-scatter.4
  326.1 103.7 reduce-scatter.2
